TPU v7x, 128 devices: a whole 4x4x4 slice. The times are simulated.
128 devices in a mesh: group: 4 (over z), tile: 32 (over y, x, core).
Axes of the slice: x: 4, y: 4, z: 4, core: 2. Of those that a mesh axis runs over, the one named last changes fastest.
Arguments:
- loads: float32 [1024, 8, 384], P(('group', 'tile')), may hold values from -6 to 6
- local_inverse: float32 [1024, 384, 384], P(('group', 'tile')), as said below
- schur: float32 [1024, 384, 384], P(('group', 'tile')), as said below
- corner_map: float32 [1024, 8, 384], P(('group', 'tile')), may hold values from -0.6 to 0.6
- corner_index: int32 [1024, 8], P(('group', 'tile')), may hold values from 0 to 8191, as said below
- partner: int32 [1024, 12], P(('group', 'tile')), may hold values from 0 to 287, as said below
- coarse_inverse: float32 [8192, 64], P(('group', 'tile')), as said below
Outputs:
- multipliers: float32 [1024, 8, 384], P(('group', 'tile'))
- residual: float32 [1024, 8, 384], P(('group', 'tile'))
- preconditioned: float32 [1024, 8, 384], P(('group', 'tile'))
Inputs may be any that keep to these rules, and one draw needn't show every extreme that they name: `partner`: the pairing of contact faces is symmetric: the mate of a face's mate is the face itself; every face has a mate on its own device or on the device of the tile one below or one above in the same group, tiles counted around the group; at most 2 * (12) faces of one device have mates on the tile above, and as many on the tile below, and some device reaches that number. `corner_index`: the corner dofs of one device name at most 4 coarse rows (counted with repeats) in the block of 64 rows of any one owner device; one owner block receives exactly 4 from every device. `local_inverse`: each block is symmetric and strictly diagonally dominant with a positive diagonal. `schur`: each block is symmetric and strictly diagonally dominant with a positive diagonal. `coarse_inverse`: each block of 64 rows is symmetric and strictly diagonally dominant with a positive diagonal.
All inputs are finite; a program needn't handle non-finite values.
Results may differ from a plain program's by a relative error of at most 0.0003.
Values sent between devices are 32-bit elements; how exact they have to be, the bound alone decides.
No kernel may reach another device: no remote copies, remote signals or barrier semaphores. Data moves between devices by JAX's collectives and lax.ppermute only.
A program may use at most 64 MiB of HBM per device.

v0:
```python
import jax
import jax.numpy as jnp
from jax import lax
from jax.sharding import PartitionSpec as P

ITERS = 2


highest = lax.Precision.HIGHEST


def padded(block, sides, width):
    for axis, dim in sides:
        count = lax.axis_size(axis)
        forward = [(i, i + 1) for i in range(count - 1)]
        forward.append((count - 1, 0))
        backward = [(target, source) for source, target in forward]
        low = lax.ppermute(
            lax.slice_in_dim(block, block.shape[dim] - width, None, axis=dim), axis, forward
        )
        high = lax.ppermute(lax.slice_in_dim(block, 0, width, axis=dim), axis, backward)
        block = jnp.concatenate([low, block, high], axis=dim)
    return block


def apply_blocks(matrices, vectors):
    return jnp.einsum("pij,pkj->pki", matrices, vectors, precision=highest)


def contact_jump(field, partner):
    count, cases_here, width = field.shape
    faces = partner.shape[1]
    pooled = padded(field, (("tile", 0),), count)
    blocked = pooled.reshape(3 * count, cases_here, faces, width // faces)
    other = blocked[partner // faces, :, partner % faces, :]
    return field - jnp.transpose(other, (0, 2, 1, 3)).reshape(field.shape)


def inner(first, second):
    return jnp.sum(first * second, axis=(0, 2))


def energy_sum(residual, preconditioned):
    return lax.psum(inner(residual, preconditioned), ("group", "tile"))


def shards(loads, local_inverse, schur, corner_map, corner_index, partner, coarse_inverse):
    count, cases_here, width = loads.shape
    owned_rows = coarse_inverse.shape[0]
    device_count = lax.axis_size(("group", "tile"))
    coarse_rows = owned_rows * device_count
    flat_index = corner_index.reshape(-1)
    onehot = (flat_index[:, None] == lax.iota(jnp.int32, coarse_rows)[None, :]).astype(jnp.float32)

    def coarse_term(field):
        contrib = jnp.einsum("pci,pki->kpc", corner_map, field, precision=highest).reshape(
            cases_here, -1
        )
        local_total = jnp.dot(contrib, onehot, precision=highest)
        owned = lax.psum_scatter(local_total, ("group", "tile"), scatter_dimension=1, tiled=True)
        solved = jnp.dot(owned, coarse_inverse.T, precision=highest)
        whole = lax.all_gather(solved, ("group", "tile"), axis=1, tiled=True)
        picked = jnp.dot(whole, onehot.T, precision=highest)
        picked = picked.reshape(cases_here, count, -1)
        return jnp.einsum("pci,kpc->pki", corner_map, picked, precision=highest)

    def operate(vectors):
        return contact_jump(apply_blocks(local_inverse, vectors), partner)

    def precondition(vectors):
        primal = apply_blocks(schur, vectors) + coarse_term(vectors)
        return 0.5 * contact_jump(primal, partner)

    rhs = operate(loads)
    multipliers = jnp.zeros_like(rhs)
    residual = rhs
    preconditioned = precondition(residual)
    direction = preconditioned
    energy_now = energy_sum(residual, preconditioned)
    for iteration in range(ITERS):
        image = operate(direction)
        curve = lax.psum(inner(direction, image), ("group", "tile"))
        step_size = energy_now / curve
        multipliers = multipliers + step_size[None, :, None] * direction
        residual = residual - step_size[None, :, None] * image
        preconditioned = precondition(residual)
        if iteration + 1 < ITERS:
            energy_new = energy_sum(residual, preconditioned)
            direction = preconditioned + (energy_new / energy_now)[None, :, None] * direction
            energy_now = energy_new
    return (multipliers, residual, preconditioned)


def solution(mesh):
    placed = (
        P(("group", "tile"), None, None),
        P(("group", "tile"), None, None),
        P(("group", "tile"), None, None),
        P(("group", "tile"), None, None),
        P(("group", "tile"), None),
        P(("group", "tile"), None),
        P(("group", "tile"), None),
    )
    return jax.shard_map(
        shards,
        mesh=mesh,
        in_specs=placed,
        out_specs=(
            P(("group", "tile"), None, None),
            P(("group", "tile"), None, None),
            P(("group", "tile"), None, None),
        ),
        check_vma=False,
    )
```

profile of v0, /device:TPU:1, one launch (start us, length us, event | category | flops | bytes accessed | tf_op | source)
XLA Modules:
  0.0 2339.8 jit_solution(1264541004633917394)
XLA Ops:
  7.2 6.6 fusion.25
  13.9 2.6 collective-permute-start
  16.7 1.5 collective-permute-done
  18.1 2.7 collective-permute-done.1
  20.9 0.5 reshape.64
  21.9 1.1 gather_fusion
  23.6 5.1 convolution_bitcast_fusion.2
  28.8 6.1 fusion.26
  34.9 634.6 %reduce-scatter.10.cloned.1.call-done = f32[64,8]{1,0:T(8,128)} async-done(((f32[8192,8]{1,0:T(8,128)}), f32[64,8]{1,0:T(8,128)}) %reduce-scatter.10.cloned.1.call-update) | async-done | bytes 2064
  669.5 0.9 convolution_bitcast_fusion.8
  670.5 40.1 %all-gather = f32[128,64,8]{1,2,0:T(8,128)S(1)} all-gather(f32[1,64,8]{1,2,0:T(8,128)S(1)} %convolution_bitcast_fusion.8), channel_id=1, replica_groups=mesh['group'=4,'tile'=32] {'group','tile'}, dimensions={0}, use_global_device_ids=true | all-gather | bytes 264192 | tf_op jit(solution)/shard_map/all_gather | solution.py:62
  710.8 1.1 fusion.2
  712.9 1.1 collective-permute-done.2
  714.0 2.5 collective-permute-done.3
  716.5 0.5 reshape.68
  717.5 1.1 gather_fusion.1
  718.9 6.1 fusion.9
  725.0 3.5 collective-permute-start.5
  728.5 0.7 collective-permute-done.4
  730.4 1.1 gather_fusion.2
  732.0 71.0 %all-reduce = (f32[8]{0:T(128)S(1)}, f32[8]{0:T(128)S(1)}) all-reduce(f32[8]{0:T(128)S(1)} %get-tuple-element.4, f32[8]{0:T(128)S(1)} %get-tuple-element.3), channel_id=1, replica_groups=mesh['group'=4,'tile'=32] {'group','tile'}, use_global_device_ids=true, to_apply=%region_2.3 | all-reduce | flops 16 | bytes 128 | tf_op jit(solution)/shard_map/psum | solution.py:44
  803.5 5.1 convolution_bitcast_fusion.1
  808.6 6.1 fusion.27
  814.7 628.8 %reduce-scatter.12.cloned.1.call-done = f32[64,8]{1,0:T(8,128)} async-done(((f32[8192,8]{1,0:T(8,128)}), f32[64,8]{1,0:T(8,128)}) %reduce-scatter.12.cloned.1.call-update) | async-done | bytes 2064
  1443.5 0.9 convolution_bitcast_fusion.7
  1444.5 39.9 %all-gather.1 = f32[128,64,8]{1,2,0:T(8,128)S(1)} all-gather(f32[1,64,8]{1,2,0:T(8,128)S(1)} %convolution_bitcast_fusion.7), channel_id=1, replica_groups=mesh['group'=4,'tile'=32] {'group','tile'}, dimensions={0}, use_global_device_ids=true | all-gather | bytes 264192 | tf_op jit(solution)/shard_map/all_gather | solution.py:62
  1484.7 1.1 fusion.1
  1486.8 1.1 collective-permute-done.6
  1487.9 2.5 collective-permute-done.7
  1491.4 1.1 gather_fusion.3
  1492.9 68.2 %psum.30 = f32[8]{0:T(128)S(1)} all-reduce(f32[8]{0:T(128)S(1)} %multiply_reduce_fusion.1), channel_id=1, replica_groups=mesh['group'=4,'tile'=32] {'group','tile'}, use_global_device_ids=true, to_apply=%region_7.8 | all-reduce | flops 8 | bytes 64 | tf_op jit(solution)/shard_map/psum | solution.py:44
  1561.2 6.1 fusion.28
  1567.3 2.0 collective-permute-start.8
  1569.3 1.6 collective-permute-done.8
  1570.9 2.7 collective-permute-done.9
  1574.6 1.1 gather_fusion.4
  1576.1 68.2 %psum.31 = f32[8]{0:T(128)S(1)} all-reduce(f32[8]{0:T(128)S(1)} %get-tuple-element.9), channel_id=1, replica_groups=mesh['group'=4,'tile'=32] {'group','tile'}, use_global_device_ids=true, to_apply=%region_9.10 | all-reduce | flops 8 | bytes 64 | tf_op jit(solution)/shard_map/psum | solution.py:82
  1644.3 0.7 multiply_subtract_fusion
  1645.4 5.1 convolution_bitcast_fusion
  1650.5 6.1 fusion.29
  1656.6 626.4 %reduce-scatter.14.cloned.1.call-done = f32[64,8]{1,0:T(8,128)} async-done(((f32[8192,8]{1,0:T(8,128)}), f32[64,8]{1,0:T(8,128)}) %reduce-scatter.14.cloned.1.call-update) | async-done | bytes 2064
  2283.0 0.9 convolution_bitcast_fusion.6
  2284.0 40.1 %all-gather.2 = f32[128,64,8]{1,2,0:T(8,128)S(1)} all-gather(f32[1,64,8]{1,2,0:T(8,128)S(1)} %convolution_bitcast_fusion.6), channel_id=1, replica_groups=mesh['group'=4,'tile'=32] {'group','tile'}, dimensions={0}, use_global_device_ids=true | all-gather | bytes 264192 | tf_op jit(solution)/shard_map/all_gather | solution.py:62
  2324.3 1.1 fusion
  2326.4 1.1 collective-permute-done.10
  2327.5 2.5 collective-permute-done.11
  2331.0 1.1 gather_fusion.5
  2332.4 0.7 subtract_multiply_fusion
  (88 shorter events, 12.4 us)
Async XLA Ops:
  7.2 16.1 copy-start
  7.2 9.3 copy-start.4
  7.2 9.4 copy-start.3
  7.2 662.3 %reduce-scatter.10.cloned.1.call-start = ((), (), s32[]{:S(2)}) async-start(), calls=%async_computation.3 | async-start | bytes 4227072
  13.9 4.3 collective-permute-start
  16.5 4.3 collective-permute-start.1
  28.7 640.8 %copy-start.2 = (f32[64,64]{1,0:T(8,128)S(1)}, f32[64,64]{1,0:T(8,128)}, u32[]{:S(2)}) copy-start(f32[64,64]{1,0:T(8,128)} %param.13) | copy-start | bytes 49156
  28.7 1414.8 %reduce-scatter.12.cloned.1.call-start = ((), (), s32[]{:S(2)}) async-start(), calls=%async_computation.4 | async-start | bytes 4227072
  712.3 1.7 collective-permute-start.2
  712.4 4.1 collective-permute-start.3
  725.0 4.2 collective-permute-start.4
  725.0 4.4 collective-permute-start.5
  808.6 1474.4 %reduce-scatter.14.cloned.1.call-start = ((), (), s32[]{:S(2)}) async-start(), calls=%async_computation.5 | async-start | bytes 4227072
  1486.2 1.7 collective-permute-start.6
  1486.3 4.1 collective-permute-start.7
  1567.3 3.6 collective-permute-start.8
  1569.3 4.3 collective-permute-start.9
  1645.0 5.5 copy-start.1
  2325.8 1.7 collective-permute-start.10
  2325.9 4.1 collective-permute-start.11
Sparse Core Ops, SparseCore 0:
  28.9 640.5 reduce-scatter.9
  808.7 634.7 reduce-scatter.11
  1650.6 632.3 reduce-scatter.13
where the time goes:
time: 2350 us; the launch traced here: 2340 us
  waiting for transfers between devices  1910 us (81%)
  blocking collectives  327 us (14%)
  matrix products  60.2 us (3%)
    unnamed x6, waiting for transfers between devices  1890 us
    psum x2, blocking collectives, energy_sum(): return lax.psum(inner(residual, preconditioned), ('group', 'tile'))  139 us
    all_gather x3, blocking collectives, coarse_term(): whole = lax.all_gather(solved, ('group', 'tile'), axis=1, tiled=True)  120 us
    psum x1, blocking collectives, shards(): curve = lax.psum(inner(direction, image), ('group', 'tile'))  68.2 us
  transfers between devices with their start and end apart: 15, of which 15 were waited for; matrix products, arithmetic and copies ran while one was open for 1% of the time, Pallas kernels for 0%

commit v1 on v0

v1 whole, which is shorter than its diff:
```python
import jax
import jax.numpy as jnp
from jax import lax
from jax.sharding import PartitionSpec as P

highest = lax.Precision.HIGHEST
GT = ("group", "tile")


def swap_lists(tiles):
    inner_swap = [(i, i ^ 1) for i in range(tiles)]
    outer_swap = [(i, (i - 1) % tiles if i % 2 == 0 else (i + 1) % tiles) for i in range(tiles)]
    return inner_swap, outer_swap


def apply_blocks(matrices, vectors):
    return jnp.einsum("pij,pkj->pki", matrices, vectors, precision=highest)


def inner(first, second):
    return jnp.sum(first * second, axis=(0, 2))


def shards(loads, local_inverse, schur, corner_map, corner_index, partner, coarse_inverse):
    count, cases, width = loads.shape
    faces = partner.shape[1]
    corners = corner_index.shape[1]
    slots = count * corners
    rows = coarse_inverse.shape[0]
    tiles = lax.axis_size("tile")
    devices = lax.axis_size(GT)
    inner_swap, outer_swap = swap_lists(tiles)
    same_core = [[2 * i + c for i in range(devices // 2)] for c in range(2)]
    tile = lax.axis_index("tile")
    core = tile % 2
    me = lax.axis_index("group") * tiles + tile

    def pool(x):
        a = lax.ppermute(x, "tile", inner_swap)
        b = lax.ppermute(x, "tile", outer_swap)
        return jnp.concatenate([a, x, b], axis=0)

    region = partner // (count * faces)
    region = jnp.where(core == 1, region, 2 - region)
    within = partner % (count * faces)
    mate_particle = region * count + within // faces
    mate_face = within % faces

    def jump(pooled):
        blocked = pooled.reshape(3 * count, cases, faces, width // faces)
        other = blocked[mate_particle, :, mate_face, :]
        return pooled[count : 2 * count] - jnp.transpose(other, (0, 2, 1, 3)).reshape(count, cases, width)

    card = jnp.concatenate(
        [coarse_inverse.reshape(-1), corner_index.reshape(-1).astype(jnp.float32), jnp.zeros((64,), jnp.float32)]
    )
    half = lax.all_to_all(
        jnp.broadcast_to(card[None], (devices // 2, card.shape[0])), GT, 0, 0, tiled=True, axis_index_groups=same_core
    )
    other_half = lax.ppermute(half, "tile", inner_swap)
    first = jnp.where(core == 0, half, other_half)
    second = jnp.where(core == 0, other_half, half)
    cards = jnp.stack([first, second], axis=1).reshape(devices, -1)
    all_inverse = cards[:, : rows * rows].reshape(devices * rows, rows)
    all_index = cards[:, rows * rows : rows * rows + slots].astype(jnp.int32)
    base = me - tile
    inner_tile = jnp.where(core == 0, tile + 1, tile - 1)
    outer_tile = jnp.where(core == 0, (tile + tiles - 1) % tiles, (tile + 1) % tiles)
    wanted = jnp.concatenate([all_index[base + inner_tile], all_index[me], all_index[base + outer_tile]])
    flat = all_index.reshape(-1)
    inverse_rows = all_inverse[wanted]
    onehot = (lax.iota(jnp.int32, rows)[:, None] == (flat % rows)[None, :]).astype(jnp.float32)
    spread = jnp.dot(inverse_rows, onehot, precision=highest)
    weights = jnp.where((wanted // rows)[:, None] == (flat // rows)[None, :], spread, 0.0)
    map_pool = pool(corner_map)

    def gather(field, sums):
        contrib = jnp.einsum("pci,pki->kpc", corner_map, field, precision=highest).reshape(-1)
        parts = jnp.concatenate([contrib] + sums + [jnp.zeros((128 - cases * len(sums),), jnp.float32)])
        got = lax.all_to_all(jnp.broadcast_to(parts[None], (devices, parts.shape[0])), GT, 0, 0, tiled=True)
        body = got[:, : cases * slots].reshape(devices, cases, slots)
        totals = jnp.sum(got[:, cases * slots :], axis=0)
        return body, [totals[i * cases : (i + 1) * cases] for i in range(len(sums))]

    def precondition(field, sums):
        body, totals = gather(field, sums)
        pooled = pool(apply_blocks(schur, field))
        g = jnp.transpose(body, (0, 2, 1)).reshape(devices * slots, cases)
        sol = jnp.dot(weights, g, precision=highest).reshape(3 * count, corners, cases)
        pooled = pooled + jnp.einsum("pci,pck->pki", map_pool, sol, precision=highest)
        return 0.5 * jump(pooled), totals

    def operate(field):
        return jump(pool(apply_blocks(local_inverse, field)))

    def by(s, x):
        return s[None, :, None] * x

    r0 = operate(loads)
    z0, _ = precondition(r0, [])
    w0 = operate(z0)
    y0, (rz0, pw0) = precondition(w0, [inner(r0, z0), inner(z0, w0)])
    a0 = rz0 / pw0
    r1 = r0 - by(a0, w0)
    z1 = z0 - by(a0, y0)
    v1 = operate(z1)
    y1, (rz1, zv, pv, zw) = precondition(v1, [inner(r1, z1), inner(z1, v1), inner(z0, v1), inner(z1, w0)])
    b0 = rz1 / rz0
    a1 = rz1 / (zv + b0 * (pv + zw) + b0 * b0 * pw0)
    multipliers = by(a0, z0) + by(a1, z1 + by(b0, z0))
    residual = r1 - by(a1, v1 + by(b0, w0))
    preconditioned = z1 - by(a1, y1 + by(b0, y0))
    return multipliers, residual, preconditioned


def solution(mesh):
    three = P(GT, None, None)
    two = P(GT, None)
    return jax.shard_map(
        shards,
        mesh=mesh,
        in_specs=(three, three, three, three, two, two, two),
        out_specs=(three, three, three),
        check_vma=False,
    )
```

time: 2350 us -> 321 us (0.14)
  waiting for transfers between devices: 1910 us -> 23.4 us
  blocking collectives: 327 us -> 0 us
  matrix products: 60.2 us -> 171 us
  starting transfers between devices: 9.9 us -> 68.4 us
  local copies, waits for them, and re-layouts: 15.5 us -> 49.2 us
    unnamed x6 -> x0, waiting for transfers between devices: 1890 us -> none
    psum x3 -> x0, blocking collectives: 207 us -> none  [the longest x2 139 us: energy_sum(): return lax.psum(inner(residual, preconditioned), ('group', 'tile'))]
    dot_general x12 -> x10, matrix products: 7.88 us -> 134 us  [the longest x3 129 us: precondition(): jnp.dot(weights, g, precision=highest).reshape(3 * count, corners, cases)]
    all_gather x3 -> x0, blocking collectives: 120 us -> none  [coarse_term(): whole = lax.all_gather(solved, ('group', 'tile'), axis=1, tiled=True)]
    all_to_all x0 -> x4, starting transfers between devices: none -> 44.9 us  [the longest x3 33 us: gather(): lax.all_to_all(jnp.broadcast_to(parts[None], (devices, parts.shape[0])),...]
  transfers between devices with their start and end apart: 15 -> 19, of which waited for: 15 -> 6; matrix products, arithmetic and copies ran while one was open for 1% -> 57% of each run, Pallas kernels for 0% -> 0%
where the time goes in v1:
time: 321 us; the launch traced here: 319 us
  matrix products  171 us (53%)
  starting transfers between devices  68.4 us (21%)
  local copies, waits for them, and re-layouts  49.2 us (15%)
  waiting for transfers between devices  23.4 us (7%)
  other arithmetic  5.23 us (2%)
    dot_general x3, matrix products, precondition(): jnp.dot(weights, g, precision=highest).reshape(3 * count, corners, cases)  129 us
    dot_general x6, matrix products, apply_blocks(): return jnp.einsum('pij,pkj->pki', matrices, vectors, precision=highest)  36.6 us
    all_to_all x3, starting transfers between devices, gather(): lax.all_to_all(jnp.broadcast_to(parts[None], (devices, parts.shape[0])),...  33 us
    all_to_all x3, waiting for transfers between devices, gather(): lax.all_to_all(jnp.broadcast_to(parts[None], (devices, parts.shape[0])),...  12.4 us
    gather x6, local copies, waits for them, and re-layouts, jump(): other = blocked[mate_particle, :, mate_face, :]  12.3 us
    ppermute x7, starting transfers between devices, pool(): a = lax.ppermute(x, 'tile', inner_swap)  12.3 us
    all_to_all x1, starting transfers between devices, shards(): lax.all_to_all(jnp.broadcast_to(card[None], (devices // 2, card.shape[0])...  12 us
    reshape x12, local copies, waits for them, and re-layouts, jump(): blocked = pooled.reshape(3 * count, cases, faces, width // faces)  11.1 us
  transfers between devices with their start and end apart: 19, of which 6 were waited for; matrix products, arithmetic and copies ran while one was open for 57% of the time, Pallas kernels for 0%

profile of v1, /device:TPU:1, one launch (start us, length us, event | category | flops | bytes accessed | tf_op | source)
XLA Modules:
  0.0 318.9 jit_solution(17115985827542096974)
XLA Ops:
  2.4 1.6 broadcast_in_dim.25
  3.9 12.0 %all-to-all-start = ((f32[64,1,4224]{2,1,0:T(1,128)}), f32[64,1,4224]{2,1,0:T(1,128)S(1)}, u32[]{:S(2)}, u32[]{:S(2)}) async-start(f32[64,1,4224]{2,1,0:T(1,128)} %broadcast_in_dim.25), calls=%async_computation | async-start | bytes 2162688 | tf_op jit(solution)/shard_map/all_to_all | solution.py:57
  15.9 6.1 %fusion.27 = f32[8,8,384]{2,1,0:T(8,128)S(1)} fusion(f32[8,8,384]{2,1,0:T(8,128)S(1)} %copy-done, f32[8,384,384]{2,1,0:T(8,128)} %param.8), kind=kOutput, calls=%fused_computation.101 | convolution fusion | flops 113246208 | bytes 4915200 | tf_op jit(solution)/shard_map/pij,pkj->pki/dot_general | solution.py:17
  22.0 2.2 collective-permute-start.1
  24.2 2.6 collective-permute-start
  26.8 7.0 %all-to-all-done = f32[64,1,4224]{2,1,0:T(1,128)S(1)} async-done(((f32[64,1,4224]{2,1,0:T(1,128)}), f32[64,1,4224]{2,1,0:T(1,128)S(1)}, u32[]{:S(2)}, u32[]{:S(2)}) %all-to-all-start) | async-done | bytes 1081376 | tf_op jit(solution)/shard_map/all_to_all | solution.py:57
  33.8 1.0 copy.88
  34.9 3.7 %collective-permute-start.4 = (f32[64,4224]{1,0:T(8,128)}, f32[64,4224]{1,0:T(8,128)}, u32[]{:S(2)}, u32[]{:S(2)}) collective-permute-start(f32[64,4224]{1,0:T(8,128)} %bitcast.97), channel_id=1, source_target_pairs={{0,1},{1,0},{2,3},{3,2},{4,5},{5,4},{6,7},{7,6},{8,9},{9,8},{10,11... | collective-permute-start | bytes 3244040 | tf_op jit(solution)/shard_map/ppermute | solution.py:60
  39.3 1.5 copy.54
  40.8 2.2 gather_fusion
  43.3 6.1 %fusion.28 = f32[8,8,384]{2,1,0:T(8,128)S(1)} fusion(f32[8,8,384]{2,1,0:T(8,128)S(1)} %sub.69, f32[8,384,384]{2,1,0:T(8,128)} %param.9), kind=kOutput, calls=%fused_computation.102 | convolution fusion | flops 113246208 | bytes 4915200 | tf_op jit(solution)/shard_map/pij,pkj->pki/dot_general | solution.py:17
  51.0 17.8 %all-to-all-start.1 = ((f32[128,1,640]{2,1,0:T(1,128)}), f32[128,1,640]{2,1,0:T(1,128)S(1)}, u32[]{:S(2)}, u32[]{:S(2)}) async-start(f32[128,1,640]{2,1,0:T(1,128)} %broadcast_in_dim.27), calls=%async_computation.1 | async-start | bytes 655360 | tf_op jit(solution)/shard_map/all_to_all | solution.py:80
  68.9 11.5 %all-to-all-done.1 = f32[128,1,640]{2,1,0:T(1,128)S(1)} async-done(((f32[128,1,640]{2,1,0:T(1,128)}), f32[128,1,640]{2,1,0:T(1,128)S(1)}, u32[]{:S(2)}, u32[]{:S(2)}) %all-to-all-start.1) | async-done | bytes 327712 | tf_op jit(solution)/shard_map/all_to_all | solution.py:80
  80.9 1.4 select_bitcast_fusion.1
  82.5 3.0 copy.56
  85.5 2.7 reshape.377
  88.3 1.6 slice.79
  89.9 4.6 %reshape.379 = f32[8192,64]{1,0:T(8,128)} reshape(f32[128,4096]{1,0:T(8,128)} %slice.79) | data formatting | bytes 4194304 | tf_op jit(solution)/shard_map/reshape | solution.py:64
  94.7 2.9 gather_fusion.1
  97.7 2.9 fusion
  100.5 41.7 %fusion.29 = f32[24,8,8]{1,2,0:T(8,128)S(1)} fusion(f32[24,8,8192]{2,1,0:T(8,128)S(1)} %fusion, f32[8192,8,1]{0,1,2:T(8,128)S(1)} %reshape.455), kind=kOutput, calls=%fused_computation.103 | convolution fusion | flops 150994944 | bytes 6559744 | tf_op jit(solution)/shard_map/dot_general | solution.py:89
  143.4 1.5 copy.61
  144.9 2.2 gather_fusion.2
  147.5 6.1 %fusion.6 = f32[8,8,384]{2,1,0:T(8,128)S(1)} fusion(f32[8,384,384]{2,1,0:T(8,128)} %param.8, f32[8,8,384]{2,1,0:T(8,128)S(1)} %slice_subtract_fusion.2), kind=kOutput, calls=%fused_computation.41 | convolution fusion | flops 113270784 | bytes 4915200 | tf_op jit(solution)/shard_map/pij,pkj->pki/dot_general | solution.py:17
  153.5 1.0 collective-permute-start.8
  154.6 1.1 collective-permute-start.7
  155.7 1.9 collective-permute-done.8
  158.2 1.5 copy.63
  159.6 2.2 gather_fusion.3
  163.7 7.6 %all-to-all-start.2 = ((f32[128,1,640]{2,1,0:T(1,128)}), f32[128,1,640]{2,1,0:T(1,128)S(1)}, u32[]{:S(2)}, u32[]{:S(2)}) async-start(f32[128,1,640]{2,1,0:T(1,128)} %broadcast_in_dim.29), calls=%async_computation.2 | async-start | bytes 655360 | tf_op jit(solution)/shard_map/all_to_all | solution.py:80
  171.3 6.1 %fusion.30 = f32[8,8,384]{2,1,0:T(8,128)S(1)} fusion(f32[8,8,384]{2,1,0:T(8,128)S(1)} %get-tuple-element.14, f32[8,384,384]{2,1,0:T(8,128)} %param.9), kind=kOutput, calls=%fused_computation.104 | convolution fusion | flops 113246208 | bytes 4915200 | tf_op jit(solution)/shard_map/pij,pkj->pki/dot_general | solution.py:17
  177.4 1.7 collective-permute-start.10
  179.0 3.7 %collective-permute-start.9 = (f32[8,8,384]{2,1,0:T(8,128)S(1)}, f32[8,8,384]{2,1,0:T(8,128)S(1)}, u32[]{:S(2)}, u32[]{:S(2)}) collective-permute-start(f32[8,8,384]{2,1,0:T(8,128)S(1)} %fusion.30), channel_id=1, source_target_pairs={{0,1},{1,0},{2,3},{3,2},{4,5},{5,4},{6,7},{7,6},{8,9},{9,8},{10,11... | collective-permute-start | bytes 294920 | tf_op jit(solution)/shard_map/ppermute | solution.py:39
  183.9 44.0 %fusion.31 = f32[24,8,8]{1,2,0:T(8,128)S(1)} fusion(f32[24,8,8192]{2,1,0:T(8,128)} %copy-done.2, f32[8192,8,1]{0,1,2:T(8,128)S(1)} %reshape.456), kind=kOutput, calls=%fused_computation.105 | convolution fusion | flops 150994944 | bytes 6559744 | tf_op jit(solution)/shard_map/dot_general | solution.py:89
  228.9 1.5 copy.69
  230.4 2.2 gather_fusion.4
  233.0 6.1 %fusion.32 = f32[8,8,384]{2,1,0:T(8,128)S(1)} fusion(f32[8,8,384]{2,1,0:T(8,128)S(1)} %multiply_subtract_fusion.2, f32[8,384,384]{2,1,0:T(8,128)} %param.8), kind=kOutput, calls=%fused_computation.106 | convolution fusion | flops 113246208 | bytes 4915200 | tf_op jit(solution)/shard_map/pij,pkj->pki/dot_general | solution.py:17
  240.1 1.1 collective-permute-start.11
  241.2 2.1 collective-permute-done.12
  243.8 1.5 copy.71
  245.3 2.2 gather_fusion.5
  249.5 7.6 %all-to-all-start.3 = ((f32[128,1,640]{2,1,0:T(1,128)}), f32[128,1,640]{2,1,0:T(1,128)S(1)}, u32[]{:S(2)}, u32[]{:S(2)}) async-start(f32[128,1,640]{2,1,0:T(1,128)} %broadcast_in_dim.31), calls=%async_computation.3 | async-start | bytes 655360 | tf_op jit(solution)/shard_map/all_to_all | solution.py:80
  257.1 6.1 %fusion.33 = f32[8,8,384]{2,1,0:T(8,128)S(1)} fusion(f32[8,8,384]{2,1,0:T(8,128)S(1)} %get-tuple-element.11, f32[8,384,384]{2,1,0:T(8,128)} %param.9), kind=kOutput, calls=%fused_computation.107 | convolution fusion | flops 113246208 | bytes 4915200 | tf_op jit(solution)/shard_map/pij,pkj->pki/dot_general | solution.py:17
  263.2 1.6 collective-permute-start.14
  264.8 3.6 %collective-permute-start.13 = (f32[8,8,384]{2,1,0:T(8,128)S(1)}, f32[8,8,384]{2,1,0:T(8,128)S(1)}, u32[]{:S(2)}, u32[]{:S(2)}) collective-permute-start(f32[8,8,384]{2,1,0:T(8,128)S(1)} %fusion.33), channel_id=1, source_target_pairs={{0,1},{1,0},{2,3},{3,2},{4,5},{5,4},{6,7},{7,6},{8,9},{9,8},{10,11... | collective-permute-start | bytes 294920 | tf_op jit(solution)/shard_map/ppermute | solution.py:39
  269.5 43.7 %fusion.34 = f32[24,8,8]{1,2,0:T(8,128)S(1)} fusion(f32[24,8,8192]{2,1,0:T(8,128)} %copy-done.2, f32[8192,8,1]{0,1,2:T(8,128)S(1)} %reshape.457), kind=kOutput, calls=%fused_computation.108 | convolution fusion | flops 150994944 | bytes 6559744 | tf_op jit(solution)/shard_map/dot_general | solution.py:89
  315.5 1.1 gather_fusion.6
  317.0 1.7 fusion.5
  (126 shorter events, 18.7 us)
Async XLA Ops:
  0.6 15.3 %copy-start = (f32[8,8,384]{2,1,0:T(8,128)S(1)}, f32[8,8,384]{2,1,0:T(8,128)}, u32[]{:S(2)}) copy-start(f32[8,8,384]{2,1,0:T(8,128)} %param.7) | copy-start | bytes 294916
  3.9 29.9 %all-to-all-start = ((f32[64,1,4224]{2,1,0:T(1,128)}), f32[64,1,4224]{2,1,0:T(1,128)S(1)}, u32[]{:S(2)}, u32[]{:S(2)}) async-start(f32[64,1,4224]{2,1,0:T(1,128)} %broadcast_in_dim.25), calls=%async_computation | async-start | bytes 2162688 | tf_op jit(solution)/shard_map/all_to_all | solution.py:57
  15.9 10.9 %copy-start.4 = (f32[8,8,384]{2,1,0:T(8,128)S(1)}, f32[8,8,384]{2,1,0:T(8,128)}, u32[]{:S(2)}) copy-start(f32[8,8,384]{2,1,0:T(8,128)} %param.10) | copy-start | bytes 294916
  22.0 16.5 %copy-start.11 = (s32[8,12]{1,0:T(8,128)S(1)}, s32[8,12]{1,0:T(8,128)}, u32[]{:S(2)}) copy-start(s32[8,12]{1,0:T(8,128)} %param.12) | copy-start | bytes 1156
  22.0 16.7 %collective-permute-start.1 = (f32[8,8,384]{2,1,0:T(8,128)S(1)}, f32[8,8,384]{2,1,0:T(8,128)S(1)}, u32[]{:S(2)}, u32[]{:S(2)}) collective-permute-start(f32[8,8,384]{2,1,0:T(8,128)S(1)} %fusion.27), channel_id=1, source_target_pairs={{0,31},{1,2},{2,1},{3,4},{4,3},{5,6},{6,5},{7,8},{8,7},{9,10},{10,... | collective-permute-start | bytes 294920 | tf_op jit(solution)/shard_map/ppermute | solution.py:40
  24.2 14.5 %collective-permute-start = (f32[8,8,384]{2,1,0:T(8,128)S(1)}, f32[8,8,384]{2,1,0:T(8,128)S(1)}, u32[]{:S(2)}, u32[]{:S(2)}) collective-permute-start(f32[8,8,384]{2,1,0:T(8,128)S(1)} %fusion.27), channel_id=1, source_target_pairs={{0,1},{1,0},{2,3},{3,2},{4,5},{5,4},{6,7},{7,6},{8,9},{9,8},{10,11... | collective-permute-start | bytes 294920 | tf_op jit(solution)/shard_map/ppermute | solution.py:39
  26.8 42.0 %collective-permute-start.5 = (f32[8,8,384]{2,1,0:T(8,128)S(1)}, f32[8,8,384]{2,1,0:T(8,128)S(1)}, u32[]{:S(2)}, u32[]{:S(2)}) collective-permute-start(f32[8,8,384]{2,1,0:T(8,128)S(1)} %copy-done.4), channel_id=1, source_target_pairs={{0,1},{1,0},{2,3},{3,2},{4,5},{5,4},{6,7},{7,6},{8,9},{9,8},{10,11... | collective-permute-start | bytes 294920 | tf_op jit(solution)/shard_map/ppermute | solution.py:39
  26.8 42.0 %collective-permute-start.6 = (f32[8,8,384]{2,1,0:T(8,128)S(1)}, f32[8,8,384]{2,1,0:T(8,128)S(1)}, u32[]{:S(2)}, u32[]{:S(2)}) collective-permute-start(f32[8,8,384]{2,1,0:T(8,128)S(1)} %copy-done.4), channel_id=1, source_target_pairs={{0,31},{1,2},{2,1},{3,4},{4,3},{5,6},{6,5},{7,8},{8,7},{9,10},{10,... | collective-permute-start | bytes 294920 | tf_op jit(solution)/shard_map/ppermute | solution.py:40
  34.9 46.1 %collective-permute-start.4 = (f32[64,4224]{1,0:T(8,128)}, f32[64,4224]{1,0:T(8,128)}, u32[]{:S(2)}, u32[]{:S(2)}) collective-permute-start(f32[64,4224]{1,0:T(8,128)} %bitcast.97), channel_id=1, source_target_pairs={{0,1},{1,0},{2,3},{3,2},{4,5},{5,4},{6,7},{7,6},{8,9},{9,8},{10,11... | collective-permute-start | bytes 3244040 | tf_op jit(solution)/shard_map/ppermute | solution.py:60
  49.4 92.9 %collective-permute-start.3 = (f32[8,8,384]{2,1,0:T(8,128)S(1)}, f32[8,8,384]{2,1,0:T(8,128)S(1)}, u32[]{:S(2)}, u32[]{:S(2)}) collective-permute-start(f32[8,8,384]{2,1,0:T(8,128)S(1)} %fusion.28), channel_id=1, source_target_pairs={{0,31},{1,2},{2,1},{3,4},{4,3},{5,6},{6,5},{7,8},{8,7},{9,10},{10,... | collective-permute-start | bytes 294920 | tf_op jit(solution)/shard_map/ppermute | solution.py:40
  49.4 92.9 %collective-permute-start.2 = (f32[8,8,384]{2,1,0:T(8,128)S(1)}, f32[8,8,384]{2,1,0:T(8,128)S(1)}, u32[]{:S(2)}, u32[]{:S(2)}) collective-permute-start(f32[8,8,384]{2,1,0:T(8,128)S(1)} %fusion.28), channel_id=1, source_target_pairs={{0,1},{1,0},{2,3},{3,2},{4,5},{5,4},{6,7},{7,6},{8,9},{9,8},{10,11... | collective-permute-start | bytes 294920 | tf_op jit(solution)/shard_map/ppermute | solution.py:39
  51.0 29.3 %all-to-all-start.1 = ((f32[128,1,640]{2,1,0:T(1,128)}), f32[128,1,640]{2,1,0:T(1,128)S(1)}, u32[]{:S(2)}, u32[]{:S(2)}) async-start(f32[128,1,640]{2,1,0:T(1,128)} %broadcast_in_dim.27), calls=%async_computation.1 | async-start | bytes 655360 | tf_op jit(solution)/shard_map/all_to_all | solution.py:80
  100.5 41.7 %copy-start.2 = (f32[24,8,8192]{2,1,0:T(8,128)}, f32[24,8,8192]{2,1,0:T(8,128)S(1)}, u32[]{:S(2)}) copy-start(f32[24,8,8192]{2,1,0:T(8,128)S(1)} %fusion) | copy-start | bytes 18874372
  153.5 4.1 %collective-permute-start.8 = (f32[8,8,384]{2,1,0:T(8,128)S(1)}, f32[8,8,384]{2,1,0:T(8,128)S(1)}, u32[]{:S(2)}, u32[]{:S(2)}) collective-permute-start(f32[8,8,384]{2,1,0:T(8,128)S(1)} %fusion.6), channel_id=1, source_target_pairs={{0,31},{1,2},{2,1},{3,4},{4,3},{5,6},{6,5},{7,8},{8,7},{9,10},{10,... | collective-permute-start | bytes 294920 | tf_op jit(solution)/shard_map/ppermute | solution.py:40
  154.6 3.0 collective-permute-start.7
  163.7 19.5 %all-to-all-start.2 = ((f32[128,1,640]{2,1,0:T(1,128)}), f32[128,1,640]{2,1,0:T(1,128)S(1)}, u32[]{:S(2)}, u32[]{:S(2)}) async-start(f32[128,1,640]{2,1,0:T(1,128)} %broadcast_in_dim.29), calls=%async_computation.2 | async-start | bytes 655360 | tf_op jit(solution)/shard_map/all_to_all | solution.py:80
  177.4 50.6 %collective-permute-start.10 = (f32[8,8,384]{2,1,0:T(8,128)S(1)}, f32[8,8,384]{2,1,0:T(8,128)S(1)}, u32[]{:S(2)}, u32[]{:S(2)}) collective-permute-start(f32[8,8,384]{2,1,0:T(8,128)S(1)} %fusion.30), channel_id=1, source_target_pairs={{0,31},{1,2},{2,1},{3,4},{4,3},{5,6},{6,5},{7,8},{8,7},{9,10},{10,... | collective-permute-start | bytes 294920 | tf_op jit(solution)/shard_map/ppermute | solution.py:40
  179.0 48.9 %collective-permute-start.9 = (f32[8,8,384]{2,1,0:T(8,128)S(1)}, f32[8,8,384]{2,1,0:T(8,128)S(1)}, u32[]{:S(2)}, u32[]{:S(2)}) collective-permute-start(f32[8,8,384]{2,1,0:T(8,128)S(1)} %fusion.30), channel_id=1, source_target_pairs={{0,1},{1,0},{2,3},{3,2},{4,5},{5,4},{6,7},{7,6},{8,9},{9,8},{10,11... | collective-permute-start | bytes 294920 | tf_op jit(solution)/shard_map/ppermute | solution.py:39
  227.9 19.8 %copy-start.9 = (f32[8]{0:T(128)}, f32[8]{0:T(128)S(1)}, u32[]{:S(2)}) copy-start(f32[8]{0:T(128)S(1)} %get-tuple-element.13) | copy-start | bytes 100
  232.9 6.2 %copy-start.7 = (f32[8,8,384]{2,1,0:T(8,128)}, f32[8,8,384]{2,1,0:T(8,128)S(1)}, u32[]{:S(2)}) copy-start(f32[8,8,384]{2,1,0:T(8,128)S(1)} %reshape.391) | copy-start | bytes 294916
  233.0 14.8 %copy-start.5 = (f32[8,8,384]{2,1,0:T(8,128)}, f32[8,8,384]{2,1,0:T(8,128)S(1)}, u32[]{:S(2)}) copy-start(f32[8,8,384]{2,1,0:T(8,128)S(1)} %multiply_subtract_fusion.2) | copy-start | bytes 294916
  239.2 4.1 %collective-permute-start.12 = (f32[8,8,384]{2,1,0:T(8,128)S(1)}, f32[8,8,384]{2,1,0:T(8,128)S(1)}, u32[]{:S(2)}, u32[]{:S(2)}) collective-permute-start(f32[8,8,384]{2,1,0:T(8,128)S(1)} %fusion.32), channel_id=1, source_target_pairs={{0,31},{1,2},{2,1},{3,4},{4,3},{5,6},{6,5},{7,8},{8,7},{9,10},{10,... | collective-permute-start | bytes 294920 | tf_op jit(solution)/shard_map/ppermute | solution.py:40
  240.1 3.1 collective-permute-start.11
  249.5 19.4 %all-to-all-start.3 = ((f32[128,1,640]{2,1,0:T(1,128)}), f32[128,1,640]{2,1,0:T(1,128)S(1)}, u32[]{:S(2)}, u32[]{:S(2)}) async-start(f32[128,1,640]{2,1,0:T(1,128)} %broadcast_in_dim.31), calls=%async_computation.3 | async-start | bytes 655360 | tf_op jit(solution)/shard_map/all_to_all | solution.py:80
  263.2 50.1 %collective-permute-start.14 = (f32[8,8,384]{2,1,0:T(8,128)S(1)}, f32[8,8,384]{2,1,0:T(8,128)S(1)}, u32[]{:S(2)}, u32[]{:S(2)}) collective-permute-start(f32[8,8,384]{2,1,0:T(8,128)S(1)} %fusion.33), channel_id=1, source_target_pairs={{0,31},{1,2},{2,1},{3,4},{4,3},{5,6},{6,5},{7,8},{8,7},{9,10},{10,... | collective-permute-start | bytes 294920 | tf_op jit(solution)/shard_map/ppermute | solution.py:40
  264.8 48.5 %collective-permute-start.13 = (f32[8,8,384]{2,1,0:T(8,128)S(1)}, f32[8,8,384]{2,1,0:T(8,128)S(1)}, u32[]{:S(2)}, u32[]{:S(2)}) collective-permute-start(f32[8,8,384]{2,1,0:T(8,128)S(1)} %fusion.33), channel_id=1, source_target_pairs={{0,1},{1,0},{2,3},{3,2},{4,5},{5,4},{6,7},{7,6},{8,9},{9,8},{10,11... | collective-permute-start | bytes 294920 | tf_op jit(solution)/shard_map/ppermute | solution.py:39
  313.8 0.7 copy-start.3
  315.0 3.7 %copy-start.1 = (f32[8,8,384]{2,1,0:T(8,128)S(1)}, f32[8,8,384]{2,1,0:T(8,128)}, u32[]{:S(2)}) copy-start(f32[8,8,384]{2,1,0:T(8,128)} %param.7) | copy-start | bytes 294916
  315.5 1.5 copy-start.6
  315.5 1.5 copy-start.8
  315.5 1.5 copy-start.10

commit v2 on v1

v2 whole, which is shorter than its diff:
```python
import functools

import jax
import jax.numpy as jnp
from jax import lax
from jax.experimental import pallas as pl
from jax.experimental.pallas import tpu as pltpu
from jax.sharding import PartitionSpec as P

GT = ("group", "tile")
F32 = jnp.float32
BF16 = jnp.bfloat16
NT = (((1,), (1,)), ((), ()))
VMEM = pl.BlockSpec(memory_space=pltpu.VMEM)
SMEM = pl.BlockSpec(memory_space=pltpu.SMEM)
PARAMS = pltpu.CompilerParams(vmem_limit_bytes=24 << 20)

COUNT, CASES, WIDTH, CORNERS, ROWS, FACES = 8, 8, 384, 8, 64, 12
CHUNKS = WIDTH // 128
TILES = COUNT * CHUNKS
SLOTS = COUNT * CORNERS
CARD = 40
PAY = 8


def call(kernel, outs, specs, scratch=()):
    return pl.pallas_call(
        kernel,
        in_specs=specs,
        out_specs=[VMEM] * len(outs),
        out_shape=outs,
        scratch_shapes=list(scratch),
        compiler_params=PARAMS,
    )


def shape(*dims):
    return jax.ShapeDtypeStruct(dims, F32)


def halves(x):
    high = x.astype(BF16)
    return high, (x - high.astype(F32)).astype(BF16)


def product(vector, matrix):
    vh, vl = halves(vector)
    mh, ml = halves(matrix)
    first = jnp.dot(jnp.concatenate([vh, vl], 0), mh, preferred_element_type=F32)
    return first[:8] + first[8:] + jnp.dot(vh, ml, preferred_element_type=F32)


def lanes(shape_=(8, 128)):
    return lax.broadcasted_iota(jnp.int32, shape_, 1)


def sublanes(shape_=(8, 128)):
    return lax.broadcasted_iota(jnp.int32, shape_, 0)


def put_tiles(ref, p, row):
    for c in range(CHUNKS):
        ref[p * CHUNKS + c] = row[:, c * 128 : (c + 1) * 128]


def get_row(tiles, p):
    return jnp.concatenate([tiles[p * CHUNKS + c] for c in range(CHUNKS)], axis=1)


def jump(pool, table):
    quarter = lanes() // 32
    out = []
    for t in range(TILES):
        p, c = divmod(t, CHUNKS)
        other = None
        for q in range(4):
            f = p * FACES + c * 4 + q
            face = pltpu.roll(pool[table[0, f]], table[1, f], 1)
            other = face if other is None else jnp.where(quarter == q, face, other)
        out.append(pool[TILES + t] - other)
    return out


def fill_pool(pool, a_ref, x_ref, b_ref):
    for e, ref in enumerate((a_ref, x_ref, b_ref)):
        for t in range(TILES):
            pool[e * TILES + t] = ref[t]


def card_kernel(inverse_ref, index_ref, card_ref):
    inverse = inverse_ref[...]
    block = jnp.concatenate([inverse[:32], inverse[32:]], axis=1)
    card_ref[:, 0:32, :] = jnp.broadcast_to(block[None], (card_ref.shape[0], 32, 128))
    row = index_row(index_ref)
    card_ref[:, 32:40, :] = jnp.broadcast_to(row[None], (card_ref.shape[0], 8, 128))


def index_row(index_ref):
    index = index_ref[...].astype(F32)
    wide = jnp.concatenate([index] * 16, axis=1)
    keep = lanes() // 8 == sublanes()
    return jnp.broadcast_to(jnp.sum(jnp.where(keep, wide, 0.0), axis=0, keepdims=True), (8, 128))


def start_kernel(loads_ref, index_ref, inverse_ref, out_ref):
    for p in range(COUNT):
        put_tiles(out_ref, p, product(loads_ref[p], inverse_ref[p]))
    out_ref[TILES] = index_row(index_ref)


def column_to_row(columns):
    lane, sub = lanes(), sublanes()
    row = jnp.zeros((8, 128), F32)
    for i, column in enumerate(columns):
        row = jnp.where(lane == i * 8 + sub, jnp.broadcast_to(column, (8, 128)), row)
    return jnp.sum(row, axis=0, keepdims=True)


def case_sum(first, second):
    total = first[0] * second[0]
    for t in range(1, TILES):
        total = total + first[t] * second[t]
    return jnp.sum(total, axis=1, keepdims=True)


def send(r, map_ref, columns, pay_ref):
    lane, sub = lanes(), sublanes()
    contrib = jnp.zeros((8, 128), F32)
    for p in range(COUNT):
        for j in range(CORNERS):
            part = r[p * CHUNKS] * map_ref[p, j : j + 1, 0:128]
            for c in range(1, CHUNKS):
                part = part + r[p * CHUNKS + c] * map_ref[p, j : j + 1, c * 128 : (c + 1) * 128]
            total = jnp.sum(part, axis=1, keepdims=True)
            contrib = jnp.where(lane == p * CORNERS + j, jnp.broadcast_to(total, (8, 128)), contrib)
    turned = pltpu.roll(pltpu.roll(contrib, 64, 1), 4, 0)
    pay = jnp.where(lane < 64, contrib, turned)
    if columns:
        pay = jnp.where(sub < 4, pay, jnp.broadcast_to(column_to_row(columns), (8, 128)))
    pay_ref[...] = jnp.broadcast_to(pay[None], pay_ref.shape)


def send_first_kernel(table, a_ref, x_ref, b_ref, map_ref, r_ref, pay_ref, pool):
    fill_pool(pool, a_ref, x_ref, b_ref)
    r = jump(pool, table)
    for t in range(TILES):
        r_ref[t] = r[t]
    send(r, map_ref, [], pay_ref)


def send_second_kernel(table, a_ref, x_ref, b_ref, map_ref, r0_ref, z0_ref, w_ref, pay_ref, pool):
    fill_pool(pool, a_ref, x_ref, b_ref)
    w = jump(pool, table)
    for t in range(TILES):
        w_ref[t] = w[t]
    send(w, map_ref, [case_sum(r0_ref, z0_ref), case_sum(z0_ref, w)], pay_ref)


def send_third_kernel(
    table, a_ref, x_ref, b_ref, map_ref, r1_ref, z1_ref, z0_ref, w0_ref, v_ref, pay_ref, pool
):
    fill_pool(pool, a_ref, x_ref, b_ref)
    v = jump(pool, table)
    for t in range(TILES):
        v_ref[t] = v[t]
    columns = [case_sum(r1_ref, z1_ref), case_sum(z1_ref, v), case_sum(z0_ref, v), case_sum(z1_ref, w0_ref)]
    send(v, map_ref, columns, pay_ref)


def product_kernel(x_ref, matrix_ref, out_ref):
    for p in range(COUNT):
        put_tiles(out_ref, p, product(get_row(x_ref, p), matrix_ref[p]))


def weights_kernel(core, wanted, own_ref, other_ref, out_ref, rows, names, index):
    mine = core[0]

    def pick(j, carry):
        row = wanted[j]
        owner = row // ROWS
        at = (owner // 2) * CARD + row % 32
        same = (owner % 2) == mine
        here = own_ref[pl.ds(at, 1), :]
        there = other_ref[pl.ds(at, 1), :]
        rows[pl.ds(j, 1), :] = jnp.where(same, here, there)
        names[pl.ds(j, 1), :] = jnp.full((1, 128), row, jnp.int32)
        return carry

    lax.fori_loop(0, 3 * SLOTS, pick, 0, unroll=8)
    chips = own_ref.shape[0] // CARD
    own = own_ref[pl.ds(32, chips, stride=CARD), :]
    other = other_ref[pl.ds(32, chips, stride=CARD), :]
    first = jnp.where(mine == 0, own, other)
    second = jnp.where(mine == 0, other, own)
    wide = lanes((chips, 128))
    index[...] = jnp.where(wide < 64, first, pltpu.roll(second, 64, 1)).astype(jnp.int32)
    lane = lanes((3 * SLOTS, 128))
    upper = (names[...] % ROWS) >= 32
    kept = jnp.where(upper == (lane >= 64), rows[...], 0.0)
    high, low = halves(kept)
    both = jnp.concatenate([high, low], axis=0)
    blocks = names[...] // ROWS

    def spread(q, carry):
        row = index[pl.ds(q, 1), :]
        onehot = (sublanes((128, 128)) % ROWS == row % ROWS).astype(F32).astype(BF16)
        full = jnp.dot(both, onehot, preferred_element_type=F32)
        hit = blocks == row // ROWS
        hit = jnp.concatenate([hit, hit], axis=0)
        at = pl.ds(pl.multiple_of(q * 128, 128), 128)
        out_ref[:, at] = jnp.where(hit, full, 0.0).astype(BF16)
        return carry

    lax.fori_loop(0, chips, spread, 0)


def coarse_into_pool(got_ref, weights_ref, maps, pool, gathered):
    lane, sub = lanes(), sublanes()
    straight = (sub < 4) == (lane < 64)
    sums = jnp.zeros((8, 128), F32)
    for q in range(got_ref.shape[0] // (2 * PAY)):
        first = got_ref[2 * q * PAY : 2 * q * PAY + 8, :]
        second = got_ref[(2 * q + 1) * PAY : (2 * q + 1) * PAY + 8, :]
        sums = sums + first + second
        pair = jnp.where(sub < 4, first, pltpu.roll(second, 4, 0))
        tile = jnp.where(straight, pair, pltpu.roll(pltpu.roll(pair, 64, 1), 4, 0))
        high, low = halves(tile)
        gathered[:, q * 128 : (q + 1) * 128] = jnp.concatenate([high, low], axis=0)
    out = lax.dot_general(weights_ref[...], gathered[...], NT, preferred_element_type=F32)
    count = 3 * SLOTS
    sol = out[:count] + out[count:]
    sol = sol.T
    sol = sol[:8] + sol[8:]
    own = lax.broadcasted_iota(jnp.int32, (64, 64), 0) // 8 == lax.broadcasted_iota(jnp.int32, (64, 64), 1) // 8
    for e, map_ref in enumerate(maps):
        part = sol[:, e * SLOTS : (e + 1) * SLOTS]
        spread = jnp.where(own, jnp.concatenate([part] * COUNT, axis=0), 0.0)
        sh, sl = halves(spread)
        ch, cl = halves(map_ref[...].reshape(SLOTS, WIDTH))
        two = jnp.dot(jnp.concatenate([sh, sl], axis=0), ch, preferred_element_type=F32)
        full = two[:64] + two[64:] + jnp.dot(sh, cl, preferred_element_type=F32)
        for p in range(COUNT):
            for c in range(CHUNKS):
                t = e * TILES + p * CHUNKS + c
                pool[t] = pool[t] + full[p * 8 : (p + 1) * 8, c * 128 : (c + 1) * 128]
    return sums


def totals(sums, count):
    lane, sub = lanes(), sublanes()
    row = jnp.broadcast_to(sums[4:5], (8, 128))
    return [
        jnp.broadcast_to(jnp.sum(jnp.where(lane == i * 8 + sub, row, 0.0), axis=1, keepdims=True), (8, 128))
        for i in range(count)
    ]


def solve_first_kernel(
    table, got_ref, weights_ref, am_ref, m_ref, bm_ref, a_ref, x_ref, b_ref, inverse_ref, z_ref, u_ref, pool, gathered
):
    fill_pool(pool, a_ref, x_ref, b_ref)
    coarse_into_pool(got_ref, weights_ref, (am_ref, m_ref, bm_ref), pool, gathered)
    z = [0.5 * t for t in jump(pool, table)]
    for t in range(TILES):
        z_ref[t] = z[t]
    for p in range(COUNT):
        put_tiles(u_ref, p, product(get_row(z, p), inverse_ref[p]))


def solve_second_kernel(
    table, got_ref, weights_ref, am_ref, m_ref, bm_ref, a_ref, x_ref, b_ref, inverse_ref, r0_ref, z0_ref, w0_ref,
    y_ref, r_ref, z_ref, scale_ref, u_ref, pool, gathered,
):
    fill_pool(pool, a_ref, x_ref, b_ref)
    sums = coarse_into_pool(got_ref, weights_ref, (am_ref, m_ref, bm_ref), pool, gathered)
    energy, curve = totals(sums, 2)
    step = energy / curve
    scale_ref[0] = energy
    scale_ref[1] = curve
    scale_ref[2] = step
    y = jump(pool, table)
    z = []
    for t in range(TILES):
        half = 0.5 * y[t]
        y_ref[t] = half
        r_ref[t] = r0_ref[t] - step * w0_ref[t]
        z.append(z0_ref[t] - step * half)
        z_ref[t] = z[t]
    for p in range(COUNT):
        put_tiles(u_ref, p, product(get_row(z, p), inverse_ref[p]))


def solve_third_kernel(
    table, got_ref, weights_ref, am_ref, m_ref, bm_ref, a_ref, x_ref, b_ref,
    scale_ref, z0_ref, w0_ref, y0_ref, r1_ref, z1_ref, v1_ref, multipliers_ref, residual_ref, preconditioned_ref,
    pool, gathered,
):
    fill_pool(pool, a_ref, x_ref, b_ref)
    sums = coarse_into_pool(got_ref, weights_ref, (am_ref, m_ref, bm_ref), pool, gathered)
    energy, zv, pv, zw = totals(sums, 4)
    first = scale_ref[2]
    grow = energy / scale_ref[0]
    second = energy / (zv + grow * (pv + zw) + grow * grow * scale_ref[1])
    y = jump(pool, table)
    for p in range(COUNT):
        for c in range(CHUNKS):
            t = p * CHUNKS + c
            at = slice(c * 128, (c + 1) * 128)
            multipliers_ref[p, :, at] = first * z0_ref[t] + second * (z1_ref[t] + grow * z0_ref[t])
            residual_ref[p, :, at] = r1_ref[t] - second * (v1_ref[t] + grow * w0_ref[t])
            preconditioned_ref[p, :, at] = z1_ref[t] - second * (0.5 * y[t] + grow * y0_ref[t])


def shards(loads, local_inverse, schur, corner_map, corner_index, partner, coarse_inverse):
    tiles = lax.axis_size("tile")
    devices = lax.axis_size(GT)
    inner_swap = [(i, i ^ 1) for i in range(tiles)]
    outer_swap = [(i, (i - 1) % tiles if i % 2 == 0 else (i + 1) % tiles) for i in range(tiles)]
    same_core = [[2 * i + c for i in range(devices // 2)] for c in range(2)]
    core = lax.axis_index("tile") % 2

    def both(x):
        return lax.ppermute(x, "tile", inner_swap), lax.ppermute(x, "tile", outer_swap)

    region = partner // (COUNT * FACES)
    region = jnp.where(core == 1, region, 2 - region)
    within = partner % (COUNT * FACES)
    face = within % FACES
    source = region * TILES + (within // FACES) * CHUNKS + face // 4
    turn = ((lax.iota(jnp.int32, FACES)[None, :] - face) % 4) * 32
    table = jnp.stack([source.reshape(-1), turn.reshape(-1)])

    field = shape(TILES, 8, 128)
    pool = pltpu.VMEM((3 * TILES, 8, 128), F32)
    gathered = pltpu.VMEM((16, devices * SLOTS), BF16)
    pay = shape(devices, PAY, 128)

    (card,) = call(card_kernel, [shape(devices // 2, CARD, 128)], [VMEM] * 2)(coarse_inverse, corner_index)
    own_cards = lax.all_to_all(card, GT, 0, 0, tiled=True, axis_index_groups=same_core)
    (u,) = call(start_kernel, [shape(TILES + 1, 8, 128)], [VMEM] * 3)(loads, corner_index, local_inverse)
    ua, ub = both(u)
    ma, mb = both(corner_map)
    maps = (ma, corner_map, mb)
    other_cards = lax.ppermute(own_cards, "tile", inner_swap)

    def spread(x):
        return lax.all_to_all(x, GT, 0, 0, tiled=True).reshape(devices * PAY, 128)

    def through(x):
        (q,) = call(product_kernel, [field], [VMEM] * 2)(x, schur)
        qa, qb = both(q)
        return qa, q, qb

    r0, parts = call(send_first_kernel, [field, pay], [SMEM] + [VMEM] * 4, [pool])(table, ua, u, ub, corner_map)
    got = spread(parts)
    wanted = jnp.concatenate(
        [ua[TILES, 0, :SLOTS].astype(jnp.int32), corner_index.reshape(-1), ub[TILES, 0, :SLOTS].astype(jnp.int32)]
    )
    (weights,) = call(
        lambda *refs: weights_kernel(*refs),
        [jax.ShapeDtypeStruct((6 * SLOTS, devices * SLOTS), BF16)],
        [SMEM] * 2 + [VMEM] * 2,
        [pltpu.VMEM((3 * SLOTS, 128), F32), pltpu.VMEM((3 * SLOTS, 128), jnp.int32),
         pltpu.VMEM((devices // 2, 128), jnp.int32)],
    )(core.reshape(1), wanted, own_cards.reshape(-1, 128), other_cards.reshape(-1, 128))
    pooled = through(r0)
    z0, u = call(solve_first_kernel, [field] * 2, [SMEM] + [VMEM] * 9, [pool, gathered])(
        table, got, weights, *maps, *pooled, local_inverse
    )
    ua, ub = both(u)
    w0, parts = call(send_second_kernel, [field, pay], [SMEM] + [VMEM] * 6, [pool])(
        table, ua, u, ub, corner_map, r0, z0
    )
    got = spread(parts)
    pooled = through(w0)
    y0, r1, z1, scale, u = call(
        solve_second_kernel, [field, field, field, shape(3, 8, 128), field], [SMEM] + [VMEM] * 12, [pool, gathered]
    )(table, got, weights, *maps, *pooled, local_inverse, r0, z0, w0)
    ua, ub = both(u)
    v1, parts = call(send_third_kernel, [field, pay], [SMEM] + [VMEM] * 8, [pool])(
        table, ua, u, ub, corner_map, r1, z1, z0, w0
    )
    got = spread(parts)
    pooled = through(v1)
    return tuple(
        call(solve_third_kernel, [shape(COUNT, CASES, WIDTH)] * 3, [SMEM] + [VMEM] * 15, [pool, gathered])(
            table, got, weights, *maps, *pooled, scale, z0, w0, y0, r1, z1, v1
        )
    )


def solution(mesh):
    three = P(GT, None, None)
    two = P(GT, None)
    return jax.shard_map(
        shards,
        mesh=mesh,
        in_specs=(three, three, three, three, two, two, two),
        out_specs=(three, three, three),
        check_vma=False,
    )
```

time: 321 us -> 170 us (0.53)
  matrix products: 171 us -> 0 us
  Pallas kernels: 0 us -> 37.9 us
  blocking collectives: 0 us -> 32.2 us
  starting transfers between devices: 68.4 us -> 40.7 us
  local copies, waits for them, and re-layouts: 49.2 us -> 29.1 us
  other arithmetic: 5.23 us -> 1.49 us
  waiting for transfers between devices: 23.4 us -> 27.1 us
    dot_general x16 -> x0, matrix products: 171 us -> none  [the longest x3 129 us: precondition(): jnp.dot(weights, g, precision=highest).reshape(3 * count, corners, cases)]
    pallas_call x0 -> x12, Pallas kernels: none -> 37.9 us  [the longest x1 14.9 us: shards(): call(lambda *refs: weights_kernel(*refs), [jax.ShapeDtypeStruct((6 * SLOT...]
    all_to_all x0 -> x1, blocking collectives: none -> 32.2 us  [shards(): lax.all_to_all(card, GT, 0, 0, tiled=True, axis_index_groups=same_core)]
    unnamed x27 -> x40, local copies, waits for them, and re-layouts: 1.82 us -> 28.9 us
    reshape x28 -> x1, local copies, waits for them, and re-layouts: 21.3 us -> 0.08 us  [shards(): corner_index.reshape(-1)]
    all_to_all x4 -> x3, starting transfers between devices: 44.9 us -> 26.3 us  [spread(): return lax.all_to_all(x, GT, 0, 0, tiled=True).reshape(devices * PAY, 128)]
    gather x7 -> x0, local copies, waits for them, and re-layouts: 15.2 us -> none  [the longest x6 12.3 us: jump(): other = blocked[mate_particle, :, mate_face, :]]
    ppermute x15, waiting for transfers between devices: 4.05 us -> 16.5 us  [the longest x7 15 us: both(): lax.ppermute(x, 'tile', outer_swap)]
  transfers between devices with their start and end apart: 19 -> 18, of which waited for: 6 -> 11; matrix products, arithmetic and copies ran while one was open for 57% -> 1% of each run, Pallas kernels for 0% -> 12%
where the time goes in v2:
time: 170 us; the launch traced here: 169 us
  starting transfers between devices  40.7 us (24%)
  Pallas kernels  37.9 us (22%)
  blocking collectives  32.2 us (19%)
  local copies, waits for them, and re-layouts  29.1 us (17%)
  waiting for transfers between devices  27.1 us (16%)
    all_to_all x1, blocking collectives, shards(): lax.all_to_all(card, GT, 0, 0, tiled=True, axis_index_groups=same_core)  32.2 us
    unnamed x40, local copies, waits for them, and re-layouts  28.9 us
    all_to_all x3, starting transfers between devices, spread(): return lax.all_to_all(x, GT, 0, 0, tiled=True).reshape(devices * PAY, 128)  26.3 us
    ppermute x7, waiting for transfers between devices, both(): lax.ppermute(x, 'tile', outer_swap)  15 us
    pallas_call x1, Pallas kernels, shards(): call(lambda *refs: weights_kernel(*refs), [jax.ShapeDtypeStruct((6 * SLOT...  14.9 us
    all_to_all x3, waiting for transfers between devices, spread(): return lax.all_to_all(x, GT, 0, 0, tiled=True).reshape(devices * PAY, 128)  10.6 us
    ppermute x7, starting transfers between devices, both(): lax.ppermute(x, 'tile', inner_swap)  8.3 us
    pallas_call x1, Pallas kernels, shards(): call(solve_first_kernel, [field] * 2, [SMEM] + [VMEM] * 9, [pool, gathered])  5.55 us
  transfers between devices with their start and end apart: 18, of which 11 were waited for; matrix products, arithmetic and copies ran while one was open for 1% of the time, Pallas kernels for 12%

profile of v2, /device:TPU:1, one launch (start us, length us, event | category | flops | bytes accessed | tf_op | source)
XLA Modules:
  0.0 169.4 jit_solution(15026383101125365355)
XLA Ops:
  0.7 0.7 copy-done.15
  1.4 0.8 copy-done.18
  2.3 32.2 %all_to_all.20 = f32[64,40,128]{2,1,0:T(8,128)S(1)} all-to-all(f32[64,40,128]{2,1,0:T(8,128)S(1)} %shard_map.96), channel_id=1, replica_groups={{0,2,4,6,8,10,12,14,16,18,20,22,24,26,28,30,32,34,36,38,40,42,44,46,48,..., dimensions={0} | all-to-all | bytes 2621440 | tf_op jit(solution)/shard_map/all_to_all | solution.py:339
  34.5 2.2 %collective-permute-start.2 = (f32[64,40,128]{2,1,0:T(8,128)S(1)}, f32[64,40,128]{2,1,0:T(8,128)S(1)}, u32[]{:S(2)}, u32[]{:S(2)}) collective-permute-start(f32[64,40,128]{2,1,0:T(8,128)S(1)} %all_to_all.20), channel_id=1, source_target_pairs={{0,1},{1,0},{2,3},{3,2},{4,5},{5,4},{6,7},{7,6},{8,9},{9,8},{10,11... | collective-permute-start | bytes 3932168 | tf_op jit(solution)/shard_map/ppermute | solution.py:344
  36.7 2.3 %copy-done.4 = f32[8,384,384]{2,1,0:T(8,128)S(1)} copy-done((f32[8,384,384]{2,1,0:T(8,128)S(1)}, f32[8,384,384]{2,1,0:T(8,128)}, u32[]{:S(2)}) %copy-start.4) | copy-done | bytes 4718616
  39.0 0.9 copy-done.14
  40.6 0.8 shard_map.94.x_ref
  42.4 0.9 collective-permute-start.4
  43.7 2.0 %collective-permute-done.1.b_ref = f32[25,8,128]{2,1,0:T(8,128)S(1)} collective-permute-done((f32[25,8,128]{2,1,0:T(8,128)S(1)}, f32[25,8,128]{2,1,0:T(8,128)S(1)}, u32[]{:S(2)}, u32[]{:S(2)}) %collective-permute-start.1) | collective-permute-done | bytes 102432 | tf_op jit(solution)/shard_map/ppermute | solution.py:323
  45.7 1.0 shard_map.95
  46.6 0.8 copy-done.11
  47.4 2.3 %copy-done.7 = f32[8,384,384]{2,1,0:T(8,128)S(1)} copy-done((f32[8,384,384]{2,1,0:T(8,128)S(1)}, f32[8,384,384]{2,1,0:T(8,128)}, u32[]{:S(2)}) %copy-start.7) | copy-done | bytes 4718616
  49.8 1.5 shard_map.98.x_ref
  51.2 3.7 %collective-permute-start.5 = (f32[24,8,128]{2,1,0:T(8,128)}, f32[24,8,128]{2,1,0:T(8,128)}, u32[]{:S(2)}, u32[]{:S(2)}) collective-permute-start(f32[24,8,128]{2,1,0:T(8,128)} %shard_map.98.x_ref), channel_id=1, source_target_pairs={{0,1},{1,0},{2,3},{3,2},{4,5},{5,4},{6,7},{7,6},{8,9},{9,8},{10,11... | collective-permute-start | bytes 294920 | tf_op jit(solution)/shard_map/ppermute | solution.py:323
  55.0 6.1 %all-to-all-start = ((f32[128,8,128]{2,1,0:T(8,128)}), f32[128,8,128]{2,1,0:T(8,128)S(1)}, u32[]{:S(2)}, u32[]{:S(2)}) async-start(f32[128,8,128]{2,1,0:T(8,128)} %copy-done.11), calls=%async_computation | async-start | bytes 1048576 | tf_op jit(solution)/shard_map/all_to_all | solution.py:347
  61.8 0.7 fusion.11
  62.6 14.9 %shard_map.97.weights_ref = bf16[384,8192]{1,0:T(8,128)(2,1)S(1)} custom-call(s32[1]{0:T(128)} %bitcast.1.refs_0_, s32[192]{0:T(256)S(1)} %pad_add_fusion.1.refs_1_, f32[2560,128]{1,0:T(8,128)S(1)} %bitcast.10, f32[2560,128]{1,0:T(8,128)S(1)} %bitcast.14), custom_call_target="tpu_custom_call" | custom-call | tf_op jit(solution)/shard_map/pallas_call | solution.py:359
  77.5 2.7 %copy-done = bf16[384,8192]{1,0:T(8,128)(2,1)} copy-done((bf16[384,8192]{1,0:T(8,128)(2,1)}, bf16[384,8192]{1,0:T(8,128)(2,1)S(1)}, u32[]{:S(2)}) %copy-start) | copy-done | bytes 6291480
  80.2 2.8 %copy-done.1 = bf16[384,8192]{1,0:T(8,128)(2,1)S(1)} copy-done((bf16[384,8192]{1,0:T(8,128)(2,1)S(1)}, bf16[384,8192]{1,0:T(8,128)(2,1)}, u32[]{:S(2)}) %copy-start.1) | copy-done | bytes 6291480
  83.0 2.3 %copy-done.5 = f32[8,384,384]{2,1,0:T(8,128)S(1)} copy-done((f32[8,384,384]{2,1,0:T(8,128)S(1)}, f32[8,384,384]{2,1,0:T(8,128)}, u32[]{:S(2)}) %copy-start.5) | copy-done | bytes 4718616
  85.3 5.6 %shard_map.99 = (f32[24,8,128]{2,1,0:T(8,128)S(1)}, f32[24,8,128]{2,1,0:T(8,128)S(1)}) custom-call(s32[2,96]{1,0:T(2,128)S(1)} %pad_add_fusion.table, f32[1024,128]{1,0:T(8,128)S(1)} %bitcast.11, bf16[384,8192]{1,0:T(8,128)(2,1)S(1)} %copy-done.1, f32[8,8,384]{2,1,0:T(8,128)S(1)} %collective-permute-done.3.am_ref, f32[8,8,384]{2,1,0:T(8,128)S(1)} %copy-done.10, ...), custom_call_target="tpu_custom_call" | custom-call | tf_op jit(solution)/shard_map/pallas_call | solution.py:367
  90.9 1.1 collective-permute-start.7
  92.0 0.7 collective-permute-start.8
  92.9 3.1 %collective-permute-done.8.b_ref = f32[24,8,128]{2,1,0:T(8,128)S(1)} collective-permute-done((f32[24,8,128]{2,1,0:T(8,128)S(1)}, f32[24,8,128]{2,1,0:T(8,128)S(1)}, u32[]{:S(2)}, u32[]{:S(2)}) %collective-permute-start.8) | collective-permute-done | bytes 98336 | tf_op jit(solution)/shard_map/ppermute | solution.py:323
  96.0 1.8 %shard_map.100 = (f32[24,8,128]{2,1,0:T(8,128)S(1)}, f32[128,8,128]{2,1,0:T(8,128)}) custom-call(s32[2,96]{1,0:T(2,128)S(1)} %pad_add_fusion.table, f32[24,8,128]{2,1,0:T(8,128)S(1)} %collective-permute-done.7.a_ref, f32[24,8,128]{2,1,0:T(8,128)S(1)} %get-tuple-element.18.x_ref, f32[24,8,128]{2,1,0:T(8,128)S(1)} %collective-permute-done.8.b_ref, ...), custom_call_target="tpu_custom_call" | custom-call | tf_op jit(solution)/shard_map/pallas_call | solution.py:371
  97.8 11.6 %all-to-all-start.2 = ((f32[128,8,128]{2,1,0:T(8,128)}), f32[128,8,128]{2,1,0:T(8,128)S(1)}, u32[]{:S(2)}, u32[]{:S(2)}) async-start(f32[128,8,128]{2,1,0:T(8,128)} %get-tuple-element.20), calls=%async_computation.2 | async-start | bytes 1048576 | tf_op jit(solution)/shard_map/all_to_all | solution.py:347
  109.4 2.3 %copy-done.8 = f32[8,384,384]{2,1,0:T(8,128)S(1)} copy-done((f32[8,384,384]{2,1,0:T(8,128)S(1)}, f32[8,384,384]{2,1,0:T(8,128)}, u32[]{:S(2)}) %copy-start.8) | copy-done | bytes 4718616
  111.8 0.8 shard_map.101.x_ref
  112.6 1.1 collective-permute-start.9
  113.7 0.8 collective-permute-start.10
  114.7 3.4 %collective-permute-done.10.b_ref = f32[24,8,128]{2,1,0:T(8,128)S(1)} collective-permute-done((f32[24,8,128]{2,1,0:T(8,128)S(1)}, f32[24,8,128]{2,1,0:T(8,128)S(1)}, u32[]{:S(2)}, u32[]{:S(2)}) %collective-permute-start.10) | collective-permute-done | bytes 98336 | tf_op jit(solution)/shard_map/ppermute | solution.py:323
  118.1 5.4 %all-to-all-done.2 = f32[128,8,128]{2,1,0:T(8,128)S(1)} async-done(((f32[128,8,128]{2,1,0:T(8,128)}), f32[128,8,128]{2,1,0:T(8,128)S(1)}, u32[]{:S(2)}, u32[]{:S(2)}) %all-to-all-start.2) | async-done | bytes 524320 | tf_op jit(solution)/shard_map/all_to_all | solution.py:347
  123.5 2.8 %copy-done.2 = bf16[384,8192]{1,0:T(8,128)(2,1)S(1)} copy-done((bf16[384,8192]{1,0:T(8,128)(2,1)S(1)}, bf16[384,8192]{1,0:T(8,128)(2,1)}, u32[]{:S(2)}) %copy-start.2) | copy-done | bytes 6291480
  126.3 2.3 %copy-done.6 = f32[8,384,384]{2,1,0:T(8,128)S(1)} copy-done((f32[8,384,384]{2,1,0:T(8,128)S(1)}, f32[8,384,384]{2,1,0:T(8,128)}, u32[]{:S(2)}) %copy-start.6) | copy-done | bytes 4718616
  128.6 5.1 %shard_map.102 = (f32[24,8,128]{2,1,0:T(8,128)S(1)}, f32[24,8,128]{2,1,0:T(8,128)S(1)}, f32[24,8,128]{2,1,0:T(8,128)S(1)}, f32[3,8,128]{2,1,0:T(8,128)S(1)}, f32[24,8,128]{2,1,0:T(8,128)S(1)}) custom-call(s32[2,96]{1,0:T(2,128)S(1)} %pad_add_fusion.table, f32[1024,128]{1,0:T(8,128)S(1)} %bitcast.13, bf16[384,8192]{1,0:T(8,128)(2,1)S(1)} %copy-done.2, ...), custom_call_target="tpu_custom_call" | custom-call | tf_op jit(solution)/shard_map/pallas_call | solution.py:376
  133.7 0.9 collective-permute-start.11
  134.6 0.9 collective-permute-done.11.a_ref
  135.5 3.1 %collective-permute-done.12.b_ref = f32[24,8,128]{2,1,0:T(8,128)S(1)} collective-permute-done((f32[24,8,128]{2,1,0:T(8,128)S(1)}, f32[24,8,128]{2,1,0:T(8,128)S(1)}, u32[]{:S(2)}, u32[]{:S(2)}) %collective-permute-start.12) | collective-permute-done | bytes 98336 | tf_op jit(solution)/shard_map/ppermute | solution.py:323
  138.6 1.8 %shard_map.103 = (f32[24,8,128]{2,1,0:T(8,128)S(1)}, f32[128,8,128]{2,1,0:T(8,128)}) custom-call(s32[2,96]{1,0:T(2,128)S(1)} %pad_add_fusion.table, f32[24,8,128]{2,1,0:T(8,128)S(1)} %collective-permute-done.11.a_ref, f32[24,8,128]{2,1,0:T(8,128)S(1)} %get-tuple-element.22.x_ref, f32[24,8,128]{2,1,0:T(8,128)S(1)} %collective-permute-done.12.b_ref, ...), custom_call_target="tpu_custom_call" | custom-call | tf_op jit(solution)/shard_map/pallas_call | solution.py:380
  140.4 8.6 %all-to-all-start.3 = ((f32[128,8,128]{2,1,0:T(8,128)}), f32[128,8,128]{2,1,0:T(8,128)S(1)}, u32[]{:S(2)}, u32[]{:S(2)}) async-start(f32[128,8,128]{2,1,0:T(8,128)} %get-tuple-element.25), calls=%async_computation.3 | async-start | bytes 1048576 | tf_op jit(solution)/shard_map/all_to_all | solution.py:347
  149.0 2.3 %copy-done.9 = f32[8,384,384]{2,1,0:T(8,128)S(1)} copy-done((f32[8,384,384]{2,1,0:T(8,128)S(1)}, f32[8,384,384]{2,1,0:T(8,128)}, u32[]{:S(2)}) %copy-start.9) | copy-done | bytes 4718616
  151.3 0.8 shard_map.104.x_ref
  152.1 1.1 collective-permute-start.13
  153.3 0.7 collective-permute-start.14
  154.2 3.4 %collective-permute-done.14.b_ref = f32[24,8,128]{2,1,0:T(8,128)S(1)} collective-permute-done((f32[24,8,128]{2,1,0:T(8,128)S(1)}, f32[24,8,128]{2,1,0:T(8,128)S(1)}, u32[]{:S(2)}, u32[]{:S(2)}) %collective-permute-start.14) | collective-permute-done | bytes 98336 | tf_op jit(solution)/shard_map/ppermute | solution.py:323
  157.6 5.2 %all-to-all-done.3 = f32[128,8,128]{2,1,0:T(8,128)S(1)} async-done(((f32[128,8,128]{2,1,0:T(8,128)}), f32[128,8,128]{2,1,0:T(8,128)S(1)}, u32[]{:S(2)}, u32[]{:S(2)}) %all-to-all-start.3) | async-done | bytes 524320 | tf_op jit(solution)/shard_map/all_to_all | solution.py:347
  162.8 2.8 %copy-done.3 = bf16[384,8192]{1,0:T(8,128)(2,1)S(1)} copy-done((bf16[384,8192]{1,0:T(8,128)(2,1)S(1)}, bf16[384,8192]{1,0:T(8,128)(2,1)}, u32[]{:S(2)}) %copy-start.3) | copy-done | bytes 6291480
  165.6 3.8 %shard_map.105 = (f32[8,8,384]{2,1,0:T(8,128)}, f32[8,8,384]{2,1,0:T(8,128)}, f32[8,8,384]{2,1,0:T(8,128)}) custom-call(s32[2,96]{1,0:T(2,128)S(1)} %pad_add_fusion.table, f32[1024,128]{1,0:T(8,128)S(1)} %bitcast.12, bf16[384,8192]{1,0:T(8,128)(2,1)S(1)} %copy-done.3, f32[8,8,384]{2,1,0:T(8,128)S(1)} %collective-permute-done.3.am_ref, ...), custom_call_target="tpu_custom_call" | custom-call | tf_op jit(solution)/shard_map/pallas_call | solution.py:386
  (49 shorter events, 3.6 us)
Async XLA Ops:
  0.6 41.6 %copy-start.10 = (f32[8,8,384]{2,1,0:T(8,128)S(1)}, f32[8,8,384]{2,1,0:T(8,128)}, u32[]{:S(2)}) copy-start(f32[8,8,384]{2,1,0:T(8,128)} %m_ref.5) | copy-start | bytes 294916
  0.6 0.7 copy-start.15
  1.4 0.8 copy-start.18
  2.1 41.2 %copy-start.17 = (s32[8,8]{1,0:T(8,128)S(1)}, s32[8,8]{1,0:T(8,128)}, u32[]{:S(2)}) copy-start(s32[8,8]{1,0:T(8,128)} %index_ref.3) | copy-start | bytes 772
  2.1 41.3 %copy-start.19 = (s32[8,12]{1,0:T(8,128)S(1)}, s32[8,12]{1,0:T(8,128)}, u32[]{:S(2)}) copy-start(s32[8,12]{1,0:T(8,128)} %param.12) | copy-start | bytes 1156
  34.5 28.1 %collective-permute-start.2 = (f32[64,40,128]{2,1,0:T(8,128)S(1)}, f32[64,40,128]{2,1,0:T(8,128)S(1)}, u32[]{:S(2)}, u32[]{:S(2)}) collective-permute-start(f32[64,40,128]{2,1,0:T(8,128)S(1)} %all_to_all.20), channel_id=1, source_target_pairs={{0,1},{1,0},{2,3},{3,2},{4,5},{5,4},{6,7},{7,6},{8,9},{9,8},{10,11... | collective-permute-start | bytes 3932168 | tf_op jit(solution)/shard_map/ppermute | solution.py:344
  36.7 2.3 %copy-start.4 = (f32[8,384,384]{2,1,0:T(8,128)S(1)}, f32[8,384,384]{2,1,0:T(8,128)}, u32[]{:S(2)}) copy-start(f32[8,384,384]{2,1,0:T(8,128)} %inverse_ref.7) | copy-start | bytes 14155780
  39.0 0.9 copy-start.14
  39.9 0.7 copy-start.16
  41.4 2.2 %collective-permute-start = (f32[25,8,128]{2,1,0:T(8,128)S(1)}, f32[25,8,128]{2,1,0:T(8,128)S(1)}, u32[]{:S(2)}, u32[]{:S(2)}) collective-permute-start(f32[25,8,128]{2,1,0:T(8,128)S(1)} %shard_map.94.x_ref), channel_id=1, source_target_pairs={{0,1},{1,0},{2,3},{3,2},{4,5},{5,4},{6,7},{7,6},{8,9},{9,8},{10,11... | collective-permute-start | bytes 307208 | tf_op jit(solution)/shard_map/ppermute | solution.py:323
  41.5 4.2 %collective-permute-start.1 = (f32[25,8,128]{2,1,0:T(8,128)S(1)}, f32[25,8,128]{2,1,0:T(8,128)S(1)}, u32[]{:S(2)}, u32[]{:S(2)}) collective-permute-start(f32[25,8,128]{2,1,0:T(8,128)S(1)} %shard_map.94.x_ref), channel_id=1, source_target_pairs={{0,31},{1,2},{2,1},{3,4},{4,3},{5,6},{6,5},{7,8},{8,7},{9,10},{10,... | collective-permute-start | bytes 307208 | tf_op jit(solution)/shard_map/ppermute | solution.py:323
  42.2 38.0 %collective-permute-start.3 = (f32[8,8,384]{2,1,0:T(8,128)S(1)}, f32[8,8,384]{2,1,0:T(8,128)S(1)}, u32[]{:S(2)}, u32[]{:S(2)}) collective-permute-start(f32[8,8,384]{2,1,0:T(8,128)S(1)} %copy-done.10), channel_id=1, source_target_pairs={{0,1},{1,0},{2,3},{3,2},{4,5},{5,4},{6,7},{7,6},{8,9},{9,8},{10,11... | collective-permute-start | bytes 294920 | tf_op jit(solution)/shard_map/ppermute | solution.py:323
  42.4 37.8 %collective-permute-start.4 = (f32[8,8,384]{2,1,0:T(8,128)S(1)}, f32[8,8,384]{2,1,0:T(8,128)S(1)}, u32[]{:S(2)}, u32[]{:S(2)}) collective-permute-start(f32[8,8,384]{2,1,0:T(8,128)S(1)} %copy-done.10), channel_id=1, source_target_pairs={{0,31},{1,2},{2,1},{3,4},{4,3},{5,6},{6,5},{7,8},{8,7},{9,10},{10,... | collective-permute-start | bytes 294920 | tf_op jit(solution)/shard_map/ppermute | solution.py:323
  43.6 11.3 %copy-start.12 = (f32[25,8,128]{2,1,0:T(8,128)}, f32[25,8,128]{2,1,0:T(8,128)S(1)}, u32[]{:S(2)}) copy-start(f32[25,8,128]{2,1,0:T(8,128)S(1)} %collective-permute-done.a_ref) | copy-start | bytes 307204
  45.7 9.3 %copy-start.13 = (f32[25,8,128]{2,1,0:T(8,128)}, f32[25,8,128]{2,1,0:T(8,128)S(1)}, u32[]{:S(2)}) copy-start(f32[25,8,128]{2,1,0:T(8,128)S(1)} %collective-permute-done.1.b_ref) | copy-start | bytes 307204
  46.6 0.8 copy-start.11
  47.4 2.3 %copy-start.7 = (f32[8,384,384]{2,1,0:T(8,128)S(1)}, f32[8,384,384]{2,1,0:T(8,128)}, u32[]{:S(2)}) copy-start(f32[8,384,384]{2,1,0:T(8,128)} %matrix_ref.5) | copy-start | bytes 14155780
  51.2 29.0 %collective-permute-start.5 = (f32[24,8,128]{2,1,0:T(8,128)}, f32[24,8,128]{2,1,0:T(8,128)}, u32[]{:S(2)}, u32[]{:S(2)}) collective-permute-start(f32[24,8,128]{2,1,0:T(8,128)} %shard_map.98.x_ref), channel_id=1, source_target_pairs={{0,1},{1,0},{2,3},{3,2},{4,5},{5,4},{6,7},{7,6},{8,9},{9,8},{10,11... | collective-permute-start | bytes 294920 | tf_op jit(solution)/shard_map/ppermute | solution.py:323
  55.0 25.2 %collective-permute-start.6 = (f32[24,8,128]{2,1,0:T(8,128)}, f32[24,8,128]{2,1,0:T(8,128)}, u32[]{:S(2)}, u32[]{:S(2)}) collective-permute-start(f32[24,8,128]{2,1,0:T(8,128)} %shard_map.98.x_ref), channel_id=1, source_target_pairs={{0,31},{1,2},{2,1},{3,4},{4,3},{5,6},{6,5},{7,8},{8,7},{9,10},{10,... | collective-permute-start | bytes 294920 | tf_op jit(solution)/shard_map/ppermute | solution.py:323
  55.0 25.2 %all-to-all-start = ((f32[128,8,128]{2,1,0:T(8,128)}), f32[128,8,128]{2,1,0:T(8,128)S(1)}, u32[]{:S(2)}, u32[]{:S(2)}) async-start(f32[128,8,128]{2,1,0:T(8,128)} %copy-done.11), calls=%async_computation | async-start | bytes 1048576 | tf_op jit(solution)/shard_map/all_to_all | solution.py:347
  77.5 2.7 %copy-start = (bf16[384,8192]{1,0:T(8,128)(2,1)}, bf16[384,8192]{1,0:T(8,128)(2,1)S(1)}, u32[]{:S(2)}) copy-start(bf16[384,8192]{1,0:T(8,128)(2,1)S(1)} %shard_map.97.weights_ref) | copy-start | bytes 18874372
  80.2 2.8 %copy-start.1 = (bf16[384,8192]{1,0:T(8,128)(2,1)S(1)}, bf16[384,8192]{1,0:T(8,128)(2,1)}, u32[]{:S(2)}) copy-start(bf16[384,8192]{1,0:T(8,128)(2,1)} %copy-done) | copy-start | bytes 18874372
  83.0 2.3 %copy-start.5 = (f32[8,384,384]{2,1,0:T(8,128)S(1)}, f32[8,384,384]{2,1,0:T(8,128)}, u32[]{:S(2)}) copy-start(f32[8,384,384]{2,1,0:T(8,128)} %inverse_ref.7) | copy-start | bytes 14155780
  90.9 2.0 %collective-permute-start.7 = (f32[24,8,128]{2,1,0:T(8,128)S(1)}, f32[24,8,128]{2,1,0:T(8,128)S(1)}, u32[]{:S(2)}, u32[]{:S(2)}) collective-permute-start(f32[24,8,128]{2,1,0:T(8,128)S(1)} %get-tuple-element.18.x_ref), channel_id=1, source_target_pairs={{0,1},{1,0},{2,3},{3,2},{4,5},{5,4},{6,7},{7,6},{8,9},{9,8},{10,11... | collective-permute-start | bytes 294920 | tf_op jit(solution)/shard_map/ppermute | solution.py:323
  92.0 4.0 %collective-permute-start.8 = (f32[24,8,128]{2,1,0:T(8,128)S(1)}, f32[24,8,128]{2,1,0:T(8,128)S(1)}, u32[]{:S(2)}, u32[]{:S(2)}) collective-permute-start(f32[24,8,128]{2,1,0:T(8,128)S(1)} %get-tuple-element.18.x_ref), channel_id=1, source_target_pairs={{0,31},{1,2},{2,1},{3,4},{4,3},{5,6},{6,5},{7,8},{8,7},{9,10},{10,... | collective-permute-start | bytes 294920 | tf_op jit(solution)/shard_map/ppermute | solution.py:323
  97.8 25.7 %all-to-all-start.2 = ((f32[128,8,128]{2,1,0:T(8,128)}), f32[128,8,128]{2,1,0:T(8,128)S(1)}, u32[]{:S(2)}, u32[]{:S(2)}) async-start(f32[128,8,128]{2,1,0:T(8,128)} %get-tuple-element.20), calls=%async_computation.2 | async-start | bytes 1048576 | tf_op jit(solution)/shard_map/all_to_all | solution.py:347
  109.4 2.3 %copy-start.8 = (f32[8,384,384]{2,1,0:T(8,128)S(1)}, f32[8,384,384]{2,1,0:T(8,128)}, u32[]{:S(2)}) copy-start(f32[8,384,384]{2,1,0:T(8,128)} %matrix_ref.5) | copy-start | bytes 14155780
  112.6 2.1 %collective-permute-start.9 = (f32[24,8,128]{2,1,0:T(8,128)S(1)}, f32[24,8,128]{2,1,0:T(8,128)S(1)}, u32[]{:S(2)}, u32[]{:S(2)}) collective-permute-start(f32[24,8,128]{2,1,0:T(8,128)S(1)} %shard_map.101.x_ref), channel_id=1, source_target_pairs={{0,1},{1,0},{2,3},{3,2},{4,5},{5,4},{6,7},{7,6},{8,9},{9,8},{10,11... | collective-permute-start | bytes 294920 | tf_op jit(solution)/shard_map/ppermute | solution.py:323
  113.7 4.3 %collective-permute-start.10 = (f32[24,8,128]{2,1,0:T(8,128)S(1)}, f32[24,8,128]{2,1,0:T(8,128)S(1)}, u32[]{:S(2)}, u32[]{:S(2)}) collective-permute-start(f32[24,8,128]{2,1,0:T(8,128)S(1)} %shard_map.101.x_ref), channel_id=1, source_target_pairs={{0,31},{1,2},{2,1},{3,4},{4,3},{5,6},{6,5},{7,8},{8,7},{9,10},{10,... | collective-permute-start | bytes 294920 | tf_op jit(solution)/shard_map/ppermute | solution.py:323
  123.5 2.8 %copy-start.2 = (bf16[384,8192]{1,0:T(8,128)(2,1)S(1)}, bf16[384,8192]{1,0:T(8,128)(2,1)}, u32[]{:S(2)}) copy-start(bf16[384,8192]{1,0:T(8,128)(2,1)} %copy-done) | copy-start | bytes 18874372
  126.3 2.3 %copy-start.6 = (f32[8,384,384]{2,1,0:T(8,128)S(1)}, f32[8,384,384]{2,1,0:T(8,128)}, u32[]{:S(2)}) copy-start(f32[8,384,384]{2,1,0:T(8,128)} %inverse_ref.7) | copy-start | bytes 14155780
  133.7 1.8 %collective-permute-start.11 = (f32[24,8,128]{2,1,0:T(8,128)S(1)}, f32[24,8,128]{2,1,0:T(8,128)S(1)}, u32[]{:S(2)}, u32[]{:S(2)}) collective-permute-start(f32[24,8,128]{2,1,0:T(8,128)S(1)} %get-tuple-element.22.x_ref), channel_id=1, source_target_pairs={{0,1},{1,0},{2,3},{3,2},{4,5},{5,4},{6,7},{7,6},{8,9},{9,8},{10,11... | collective-permute-start | bytes 294920 | tf_op jit(solution)/shard_map/ppermute | solution.py:323
  134.6 4.0 %collective-permute-start.12 = (f32[24,8,128]{2,1,0:T(8,128)S(1)}, f32[24,8,128]{2,1,0:T(8,128)S(1)}, u32[]{:S(2)}, u32[]{:S(2)}) collective-permute-start(f32[24,8,128]{2,1,0:T(8,128)S(1)} %get-tuple-element.22.x_ref), channel_id=1, source_target_pairs={{0,31},{1,2},{2,1},{3,4},{4,3},{5,6},{6,5},{7,8},{8,7},{9,10},{10,... | collective-permute-start | bytes 294920 | tf_op jit(solution)/shard_map/ppermute | solution.py:323
  140.4 22.4 %all-to-all-start.3 = ((f32[128,8,128]{2,1,0:T(8,128)}), f32[128,8,128]{2,1,0:T(8,128)S(1)}, u32[]{:S(2)}, u32[]{:S(2)}) async-start(f32[128,8,128]{2,1,0:T(8,128)} %get-tuple-element.25), calls=%async_computation.3 | async-start | bytes 1048576 | tf_op jit(solution)/shard_map/all_to_all | solution.py:347
  148.9 2.3 %copy-start.9 = (f32[8,384,384]{2,1,0:T(8,128)S(1)}, f32[8,384,384]{2,1,0:T(8,128)}, u32[]{:S(2)}) copy-start(f32[8,384,384]{2,1,0:T(8,128)} %matrix_ref.5) | copy-start | bytes 14155780
  152.1 2.1 %collective-permute-start.13 = (f32[24,8,128]{2,1,0:T(8,128)S(1)}, f32[24,8,128]{2,1,0:T(8,128)S(1)}, u32[]{:S(2)}, u32[]{:S(2)}) collective-permute-start(f32[24,8,128]{2,1,0:T(8,128)S(1)} %shard_map.104.x_ref), channel_id=1, source_target_pairs={{0,1},{1,0},{2,3},{3,2},{4,5},{5,4},{6,7},{7,6},{8,9},{9,8},{10,11... | collective-permute-start | bytes 294920 | tf_op jit(solution)/shard_map/ppermute | solution.py:323
  153.3 4.3 %collective-permute-start.14 = (f32[24,8,128]{2,1,0:T(8,128)S(1)}, f32[24,8,128]{2,1,0:T(8,128)S(1)}, u32[]{:S(2)}, u32[]{:S(2)}) collective-permute-start(f32[24,8,128]{2,1,0:T(8,128)S(1)} %shard_map.104.x_ref), channel_id=1, source_target_pairs={{0,31},{1,2},{2,1},{3,4},{4,3},{5,6},{6,5},{7,8},{8,7},{9,10},{10,... | collective-permute-start | bytes 294920 | tf_op jit(solution)/shard_map/ppermute | solution.py:323
  162.8 2.8 %copy-start.3 = (bf16[384,8192]{1,0:T(8,128)(2,1)S(1)}, bf16[384,8192]{1,0:T(8,128)(2,1)}, u32[]{:S(2)}) copy-start(bf16[384,8192]{1,0:T(8,128)(2,1)} %copy-done) | copy-start | bytes 18874372

commit v3 on v2

v3 whole, which is shorter than its diff:
```python
import jax
import jax.numpy as jnp
from jax import lax
from jax.experimental import pallas as pl
from jax.experimental.pallas import tpu as pltpu
from jax.sharding import PartitionSpec as P

GT = ("group", "tile")
F32 = jnp.float32
BF16 = jnp.bfloat16
NT = (((1,), (1,)), ((), ()))
VMEM = pl.BlockSpec(memory_space=pltpu.VMEM)
SMEM = pl.BlockSpec(memory_space=pltpu.SMEM)
ANY = pl.BlockSpec(memory_space=pl.ANY)
PARAMS = pltpu.CompilerParams(vmem_limit_bytes=24 << 20)

COUNT, CASES, WIDTH, CORNERS, ROWS, FACES = 8, 8, 384, 8, 64, 12
CHUNKS = WIDTH // 128
TILES = COUNT * CHUNKS
SLOTS = COUNT * CORNERS
CARD = 40
PARTS, PART = 8, 1024


def call(kernel, outs, specs, scratch=(), us=2):
    return pl.pallas_call(
        kernel,
        in_specs=specs,
        out_specs=[VMEM] * len(outs),
        out_shape=outs,
        scratch_shapes=list(scratch),
        compiler_params=PARAMS,
        cost_estimate=pl.CostEstimate(flops=us * 500_000_000, bytes_accessed=us * 3_000_000, transcendentals=0),
    )


def in_hbm(x):
    return pltpu.with_memory_space_constraint(x, pltpu.HBM)


def shape(*dims):
    return jax.ShapeDtypeStruct(dims, F32)


def halves(x):
    high = x.astype(BF16)
    return high, (x - high.astype(F32)).astype(BF16)


def product(vector, matrix):
    vh, vl = halves(vector)
    mh, ml = halves(matrix)
    first = jnp.dot(jnp.concatenate([vh, vl], 0), mh, preferred_element_type=F32)
    return first[:8] + first[8:] + jnp.dot(vh, ml, preferred_element_type=F32)


def lanes(shape_=(8, 128)):
    return lax.broadcasted_iota(jnp.int32, shape_, 1)


def sublanes(shape_=(8, 128)):
    return lax.broadcasted_iota(jnp.int32, shape_, 0)


def put_tiles(ref, p, row):
    for c in range(CHUNKS):
        ref[p * CHUNKS + c] = row[:, c * 128 : (c + 1) * 128]


def get_row(tiles, p):
    return jnp.concatenate([tiles[p * CHUNKS + c] for c in range(CHUNKS)], axis=1)


def jump(pool, table):
    quarter = lanes() // 32
    out = []
    for t in range(TILES):
        p, c = divmod(t, CHUNKS)
        other = None
        for q in range(4):
            f = c * 4 + q
            face = pltpu.roll(pool[table[p, f]], table[8 + p, f], 1)
            other = face if other is None else jnp.where(quarter == q, face, other)
        out.append(pool[TILES + t] - other)
    return out


def fill_pool(pool, a_ref, x_ref, b_ref):
    for e, ref in enumerate((a_ref, x_ref, b_ref)):
        for t in range(TILES):
            pool[e * TILES + t] = ref[t]


def card_kernel(core, inverse_ref, index_ref, partner_ref, card_ref, table_ref):
    inverse = inverse_ref[...]
    block = jnp.concatenate([inverse[:32], inverse[32:]], axis=1)
    card_ref[:, 0:32, :] = jnp.broadcast_to(block[None], (card_ref.shape[0], 32, 128))
    row = index_row(index_ref)
    card_ref[:, 32:40, :] = jnp.broadcast_to(row[None], (card_ref.shape[0], 8, 128))
    partner = partner_ref[...]
    region = (partner >= COUNT * FACES).astype(jnp.int32) + (partner >= 2 * COUNT * FACES).astype(jnp.int32)
    within = partner - region * (COUNT * FACES)
    particle = jnp.zeros_like(within)
    for p in range(1, COUNT):
        particle = particle + (within >= p * FACES).astype(jnp.int32)
    face = within - particle * FACES
    region = jnp.where(core[0] == 1, region, 2 - region)
    table_ref[0:8, 0:FACES] = region * TILES + particle * CHUNKS + (face >> 2)
    table_ref[8:16, 0:FACES] = ((lanes((COUNT, FACES)) - face) & 3) * 32


def index_row(index_ref):
    index = index_ref[...].astype(F32)
    wide = jnp.concatenate([index] * 16, axis=1)
    keep = lanes() // 8 == sublanes()
    return jnp.broadcast_to(jnp.sum(jnp.where(keep, wide, 0.0), axis=0, keepdims=True), (8, 128))


def fetch(source, held, sems, first=0):
    copies = [pltpu.make_async_copy(source.at[i], held.at[i], sems.at[first + i]) for i in range(source.shape[0])]
    for copy in copies:
        copy.start()
    return copies


def multiply(x, copies, held, out_ref):
    for p in range(COUNT):
        copies[p].wait()
        put_tiles(out_ref, p, product(get_row(x, p), held[p]))


def start_kernel(loads_ref, index_ref, inverse_ref, out_ref, held, sems):
    copies = fetch(inverse_ref, held, sems)
    out_ref[TILES] = index_row(index_ref)
    for p in range(COUNT):
        copies[p].wait()
        put_tiles(out_ref, p, product(loads_ref[p], held[p]))


def product_kernel(x_ref, matrix_ref, out_ref, held, sems):
    copies = fetch(matrix_ref, held, sems)
    multiply(x_ref, copies, held, out_ref)


def column_to_row(columns):
    lane, sub = lanes(), sublanes()
    row = jnp.zeros((8, 128), F32)
    for i, column in enumerate(columns):
        row = jnp.where(lane == i * 8 + sub, jnp.broadcast_to(column, (8, 128)), row)
    return jnp.sum(row, axis=0, keepdims=True)


def case_sum(first, second):
    total = first[0] * second[0]
    for t in range(1, TILES):
        total = total + first[t] * second[t]
    return jnp.sum(total, axis=1, keepdims=True)


def send(r, map_ref, columns, pay_ref):
    lane, sub = lanes(), sublanes()
    contrib = jnp.zeros((8, 128), F32)
    for p in range(COUNT):
        for j in range(CORNERS):
            part = r[p * CHUNKS] * map_ref[p, j : j + 1, 0:128]
            for c in range(1, CHUNKS):
                part = part + r[p * CHUNKS + c] * map_ref[p, j : j + 1, c * 128 : (c + 1) * 128]
            total = jnp.sum(part, axis=1, keepdims=True)
            contrib = jnp.where(lane == p * CORNERS + j, jnp.broadcast_to(total, (8, 128)), contrib)
    turned = pltpu.roll(pltpu.roll(contrib, 64, 1), 4, 0)
    pay = jnp.where(lane < 64, contrib, turned)
    if not columns:
        pair = jnp.where(sub < 4, pay, pltpu.roll(pay, 4, 0))
        for at in range(0, pay_ref.shape[0], 8):
            pay_ref[at : at + 8, :] = pair
        return
    pay = jnp.where(sub < 4, pay, jnp.broadcast_to(column_to_row(columns), (8, 128)))[0:5]
    for at in range(0, pay_ref.shape[0], 5):
        pay_ref[at : at + 5, :] = pay


def send_first_kernel(table, a_ref, x_ref, b_ref, map_ref, r_ref, pay_ref, pool):
    fill_pool(pool, a_ref, x_ref, b_ref)
    r = jump(pool, table)
    for t in range(TILES):
        r_ref[t] = r[t]
    send(r, map_ref, [], pay_ref)


def send_second_kernel(table, a_ref, x_ref, b_ref, map_ref, r0_ref, z0_ref, w_ref, pay_ref, pool):
    fill_pool(pool, a_ref, x_ref, b_ref)
    w = jump(pool, table)
    for t in range(TILES):
        w_ref[t] = w[t]
    send(w, map_ref, [case_sum(r0_ref, z0_ref), case_sum(z0_ref, w)], pay_ref)


def send_third_kernel(
    table, a_ref, x_ref, b_ref, map_ref, r1_ref, z1_ref, z0_ref, w0_ref, v_ref, pay_ref, pool
):
    fill_pool(pool, a_ref, x_ref, b_ref)
    v = jump(pool, table)
    for t in range(TILES):
        v_ref[t] = v[t]
    columns = [case_sum(r1_ref, z1_ref), case_sum(z1_ref, v), case_sum(z0_ref, v), case_sum(z1_ref, w0_ref)]
    send(v, map_ref, columns, pay_ref)


def weights_kernel(core, a_ref, x_ref, b_ref, own_ref, other_ref, out_ref, rows, names, index, wanted, built, sems):
    mine = core[0]
    copies = [
        pltpu.make_async_copy(ref.at[TILES], wanted.at[e], sems.at[e]) for e, ref in enumerate((a_ref, x_ref, b_ref))
    ]
    for copy in copies:
        copy.start()
    for copy in copies:
        copy.wait()

    def pick(j, carry):
        row = wanted[j >> 6, 0, j & 63].astype(jnp.int32)
        owner = row >> 6
        at = (owner >> 1) * CARD + (row & 31)
        same = (owner & 1) == mine
        here = own_ref[pl.ds(at, 1), :]
        there = other_ref[pl.ds(at, 1), :]
        rows[pl.ds(j, 1), :] = jnp.where(same, here, there)
        names[pl.ds(j, 1), :] = jnp.full((1, 128), row, jnp.int32)
        return carry

    lax.fori_loop(0, 3 * SLOTS, pick, 0, unroll=16)
    chips = own_ref.shape[0] // CARD
    own = own_ref[pl.ds(32, chips, stride=CARD), :]
    other = other_ref[pl.ds(32, chips, stride=CARD), :]
    first = jnp.where(mine == 0, own, other)
    second = jnp.where(mine == 0, other, own)
    wide = lanes((chips, 128))
    merged = jnp.where(wide < 64, first, pltpu.roll(second, 64, 1)).astype(jnp.int32)
    index[...] = merged
    lane = lanes((3 * SLOTS, 128))
    upper = (names[...] & 63) >= 32
    kept = jnp.where(upper == (lane >= 64), rows[...], 0.0)
    high, low = halves(kept)
    both = jnp.concatenate([high, low], axis=0)
    names[...] = names[...] >> 6
    place = sublanes((128, 256)) & 63

    def spread(q, carry):
        row = jnp.concatenate([index[pl.ds(2 * q, 1), :], index[pl.ds(2 * q + 1, 1), :]], axis=1)
        onehot = (place == (row & 63)).astype(F32).astype(BF16)
        full = jnp.dot(both, onehot, preferred_element_type=F32)
        block = row >> 6
        named = names[...]
        hit = jnp.concatenate([named, named], axis=1) == block
        at = pl.ds(pl.multiple_of((q & 3) * 256, 256), 256)
        built[q >> 2, 0 : 3 * SLOTS, at] = jnp.where(hit, full[: 3 * SLOTS], 0.0).astype(BF16)
        built[q >> 2, 3 * SLOTS :, at] = jnp.where(hit, full[3 * SLOTS :], 0.0).astype(BF16)
        return carry

    copies = []
    for part in range(PARTS):
        lax.fori_loop(part * 4, part * 4 + 4, spread, 0, unroll=4)
        copy = pltpu.make_async_copy(built.at[part], out_ref.at[part], sems.at[3 + part])
        copy.start()
        copies.append(copy)
    for copy in copies:
        copy.wait()


def coarse_into_pool(got_ref, copies, weights, maps, pool, gathered):
    lane, sub = lanes(), sublanes()
    straight = (sub < 4) == (lane < 64)
    sums = None
    senders = PARTS * PART // SLOTS
    rows = got_ref.shape[0] // senders
    if rows == 5:
        sums = jnp.sum(got_ref[pl.ds(4, senders, stride=5), :], axis=0, keepdims=True)
    for q in range(senders // 2):
        at = 2 * q * rows
        if rows == 4:
            pair = got_ref[at : at + 8, :]
        else:
            pair = jnp.concatenate([got_ref[at : at + 4, :], got_ref[at + 5 : at + 9, :]], axis=0)
        tile = jnp.where(straight, pair, pltpu.roll(pltpu.roll(pair, 64, 1), 4, 0))
        high, low = halves(tile)
        gathered[:, q * 128 : (q + 1) * 128] = jnp.concatenate([high, low], axis=0)
    out = None
    for c in range(PARTS):
        copies[c].wait()
        term = lax.dot_general(
            weights[c], gathered[:, c * PART : (c + 1) * PART], NT, preferred_element_type=F32
        )
        out = term if out is None else out + term
    count = 3 * SLOTS
    sol = out[:count] + out[count:]
    sol = sol.T
    sol = sol[:8] + sol[8:]
    own = lax.broadcasted_iota(jnp.int32, (64, 64), 0) // 8 == lax.broadcasted_iota(jnp.int32, (64, 64), 1) // 8
    for e, map_ref in enumerate(maps):
        part = sol[:, e * SLOTS : (e + 1) * SLOTS]
        spread = jnp.where(own, jnp.concatenate([part] * COUNT, axis=0), 0.0)
        sh, sl = halves(spread)
        ch, cl = halves(map_ref[...].reshape(SLOTS, WIDTH))
        two = jnp.dot(jnp.concatenate([sh, sl], axis=0), ch, preferred_element_type=F32)
        full = two[:64] + two[64:] + jnp.dot(sh, cl, preferred_element_type=F32)
        for p in range(COUNT):
            for c in range(CHUNKS):
                t = e * TILES + p * CHUNKS + c
                pool[t] = pool[t] + full[p * 8 : (p + 1) * 8, c * 128 : (c + 1) * 128]
    return sums


def totals(sums, count):
    lane, sub = lanes(), sublanes()
    row = jnp.broadcast_to(sums, (8, 128))
    return [
        jnp.broadcast_to(jnp.sum(jnp.where(lane == i * 8 + sub, row, 0.0), axis=1, keepdims=True), (8, 128))
        for i in range(count)
    ]


def solve_first_kernel(
    table, got_ref, weights_ref, am_ref, m_ref, bm_ref, a_ref, x_ref, b_ref, inverse_ref, z_ref, u_ref,
    pool, gathered, weights, held, sems,
):
    parts = fetch(weights_ref, weights, sems, COUNT)
    copies = fetch(inverse_ref, held, sems)
    fill_pool(pool, a_ref, x_ref, b_ref)
    coarse_into_pool(got_ref, parts, weights, (am_ref, m_ref, bm_ref), pool, gathered)
    z = [0.5 * t for t in jump(pool, table)]
    for t in range(TILES):
        z_ref[t] = z[t]
    multiply(z, copies, held, u_ref)


def solve_second_kernel(
    table, got_ref, weights_ref, am_ref, m_ref, bm_ref, a_ref, x_ref, b_ref, inverse_ref, r0_ref, z0_ref, w0_ref,
    y_ref, r_ref, z_ref, scale_ref, u_ref, pool, gathered, weights, held, sems,
):
    parts = fetch(weights_ref, weights, sems, COUNT)
    copies = fetch(inverse_ref, held, sems)
    fill_pool(pool, a_ref, x_ref, b_ref)
    sums = coarse_into_pool(got_ref, parts, weights, (am_ref, m_ref, bm_ref), pool, gathered)
    energy, curve = totals(sums, 2)
    step = energy / curve
    scale_ref[0] = energy
    scale_ref[1] = curve
    scale_ref[2] = step
    y = jump(pool, table)
    z = []
    for t in range(TILES):
        half = 0.5 * y[t]
        y_ref[t] = half
        r_ref[t] = r0_ref[t] - step * w0_ref[t]
        z.append(z0_ref[t] - step * half)
        z_ref[t] = z[t]
    multiply(z, copies, held, u_ref)


def solve_third_kernel(
    table, got_ref, weights_ref, am_ref, m_ref, bm_ref, a_ref, x_ref, b_ref,
    scale_ref, z0_ref, w0_ref, y0_ref, r1_ref, z1_ref, v1_ref, multipliers_ref, residual_ref, preconditioned_ref,
    pool, gathered, weights, sems,
):
    parts = fetch(weights_ref, weights, sems)
    fill_pool(pool, a_ref, x_ref, b_ref)
    sums = coarse_into_pool(got_ref, parts, weights, (am_ref, m_ref, bm_ref), pool, gathered)
    energy, zv, pv, zw = totals(sums, 4)
    first = scale_ref[2]
    grow = energy / scale_ref[0]
    second = energy / (zv + grow * (pv + zw) + grow * grow * scale_ref[1])
    y = jump(pool, table)
    for p in range(COUNT):
        for c in range(CHUNKS):
            t = p * CHUNKS + c
            at = slice(c * 128, (c + 1) * 128)
            multipliers_ref[p, :, at] = first * z0_ref[t] + second * (z1_ref[t] + grow * z0_ref[t])
            residual_ref[p, :, at] = r1_ref[t] - second * (v1_ref[t] + grow * w0_ref[t])
            preconditioned_ref[p, :, at] = z1_ref[t] - second * (0.5 * y[t] + grow * y0_ref[t])


def shards(loads, local_inverse, schur, corner_map, corner_index, partner, coarse_inverse):
    tiles = lax.axis_size("tile")
    devices = lax.axis_size(GT)
    inner_swap = [(i, i ^ 1) for i in range(tiles)]
    outer_swap = [(i, (i - 1) % tiles if i % 2 == 0 else (i + 1) % tiles) for i in range(tiles)]
    same_core = [[2 * i + c for i in range(devices // 2)] for c in range(2)]
    core = lax.axis_index("tile") % 2

    def both(x):
        return lax.ppermute(x, "tile", inner_swap), lax.ppermute(x, "tile", outer_swap)

    field = shape(TILES, 8, 128)
    pool = pltpu.VMEM((3 * TILES, 8, 128), F32)
    gathered = pltpu.VMEM((16, devices * SLOTS), BF16)
    pay = shape(devices * 5, 128)
    sems = pltpu.SemaphoreType.DMA((COUNT,))

    core = core.astype(jnp.int32).reshape(1)
    card, table = call(
        card_kernel,
        [shape(devices // 2, CARD, 128), jax.ShapeDtypeStruct((16, 128), jnp.int32)],
        [SMEM] + [VMEM] * 3,
        us=1,
    )(core, coarse_inverse, corner_index, partner)
    own_cards = lax.all_to_all(card, GT, 0, 0, tiled=True, axis_index_groups=same_core)
    held = pltpu.VMEM((COUNT, WIDTH, WIDTH), F32)
    solver = pltpu.VMEM((PARTS, 6 * SLOTS, PART), BF16)
    inverse, stiff = in_hbm(local_inverse), in_hbm(schur)
    (u,) = call(start_kernel, [shape(TILES + 1, 8, 128)], [VMEM, VMEM, ANY], [held, sems], us=4)(
        loads, corner_index, inverse
    )
    ua, ub = both(u)
    ma, mb = both(corner_map)
    maps = (ma, corner_map, mb)

    def spread(x):
        return lax.all_to_all(x.reshape(devices, -1), GT, 0, 0, tiled=True).reshape(-1, 128)

    def through(x):
        (q,) = call(product_kernel, [field], [VMEM, ANY], [held, sems], us=3)(x, stiff)
        qa, qb = both(q)
        return qa, q, qb

    r0, parts = call(send_first_kernel, [field, shape(devices * 4, 128)], [SMEM] + [VMEM] * 4, [pool])(
        table, ua, u, ub, corner_map
    )
    own_cards, parts = lax.optimization_barrier((own_cards, parts))
    other_cards = lax.ppermute(own_cards, "tile", inner_swap)
    got = spread(parts)
    pooled = through(r0)
    weights = pl.pallas_call(
        weights_kernel,
        in_specs=[SMEM] + [ANY] * 3 + [VMEM] * 2,
        out_specs=ANY,
        out_shape=pltpu.HBM((PARTS, 6 * SLOTS, PART), BF16),
        scratch_shapes=[
            pltpu.VMEM((3 * SLOTS, 128), F32),
            pltpu.VMEM((3 * SLOTS, 128), jnp.int32),
            pltpu.VMEM((devices // 2, 128), jnp.int32),
            pltpu.SMEM((3, 8, 128), F32),
            solver,
            pltpu.SemaphoreType.DMA((3 + PARTS,)),
        ],
        compiler_params=PARAMS,
        cost_estimate=pl.CostEstimate(flops=2_000_000_000, bytes_accessed=12_000_000, transcendentals=0),
    )(core, ua, u, ub, own_cards.reshape(-1, 128), other_cards.reshape(-1, 128))
    weights = in_hbm(weights)
    solve_sems = pltpu.SemaphoreType.DMA((COUNT + PARTS,))
    solve_scratch = [pool, gathered, solver, held, solve_sems]
    z0, u = call(
        solve_first_kernel, [field] * 2, [SMEM, VMEM, ANY] + [VMEM] * 6 + [ANY], solve_scratch, us=6
    )(table, got, weights, *maps, *pooled, inverse)
    ua, ub = both(u)
    w0, parts = call(send_second_kernel, [field, pay], [SMEM] + [VMEM] * 6, [pool])(
        table, ua, u, ub, corner_map, r0, z0
    )
    got = spread(parts)
    pooled = through(w0)
    y0, r1, z1, scale, u = call(
        solve_second_kernel,
        [field, field, field, shape(3, 8, 128), field],
        [SMEM, VMEM, ANY] + [VMEM] * 6 + [ANY] + [VMEM] * 3,
        solve_scratch,
        us=6,
    )(table, got, weights, *maps, *pooled, inverse, r0, z0, w0)
    ua, ub = both(u)
    v1, parts = call(send_third_kernel, [field, pay], [SMEM] + [VMEM] * 8, [pool])(
        table, ua, u, ub, corner_map, r1, z1, z0, w0
    )
    got = spread(parts)
    pooled = through(v1)
    return tuple(
        call(
            solve_third_kernel,
            [shape(COUNT, CASES, WIDTH)] * 3,
            [SMEM, VMEM, ANY] + [VMEM] * 13,
            [pool, gathered, solver, pltpu.SemaphoreType.DMA((PARTS,))],
            us=5,
        )(table, got, weights, *maps, *pooled, scale, z0, w0, y0, r1, z1, v1)
    )


def solution(mesh):
    three = P(GT, None, None)
    two = P(GT, None)
    return jax.shard_map(
        shards,
        mesh=mesh,
        in_specs=(three, three, three, three, two, two, two),
        out_specs=(three, three, three),
        check_vma=False,
    )
```

time: 170 us -> 147 us (0.86)
  blocking collectives: 32.2 us -> 0 us
  local copies, waits for them, and re-layouts: 29.1 us -> 9.19 us
  starting transfers between devices: 40.7 us -> 56 us
  Pallas kernels: 37.9 us -> 47 us
  waiting for transfers between devices: 27.1 us -> 33.4 us
    all_to_all x1 -> x0, blocking collectives: 32.2 us -> none  [shards(): lax.all_to_all(card, GT, 0, 0, tiled=True, axis_index_groups=same_core)]
    unnamed x40 -> x30, local copies, waits for them, and re-layouts: 28.9 us -> 9.19 us
    all_to_all x3 -> x4, starting transfers between devices: 26.3 us -> 39.8 us  [the longest x3 27.7 us: spread(): lax.all_to_all(x.reshape(devices, -1), GT, 0, 0, tiled=True)]
    ppermute x7, waiting for transfers between devices: 15 us -> 23.5 us  [both(): lax.ppermute(x, 'tile', outer_swap)]
    pallas_call x9, Pallas kernels: 29.3 us -> 34.8 us  [the longest x1 8.55 us: shards(): call(solve_first_kernel, [field] * 2, [SMEM, VMEM, ANY] + [VMEM] * 6 + [A...]
    pallas_call x1, Pallas kernels: 5.12 us -> 8.55 us  [shards(): call(solve_second_kernel, [field, field, field, shape(3, 8, 128), field],...]
    all_to_all x3 -> x4, waiting for transfers between devices: 10.6 us -> 7.74 us  [the longest x3 6.96 us: spread(): lax.all_to_all(x.reshape(devices, -1), GT, 0, 0, tiled=True)]
  transfers between devices with their start and end apart: 18 -> 19, of which waited for: 11 -> 12; matrix products, arithmetic and copies ran while one was open for 1% -> 0% of each run, Pallas kernels for 12% -> 12%
where the time goes in v3:
time: 147 us; the launch traced here: 146 us
  starting transfers between devices  56 us (38%)
  Pallas kernels  47 us (32%)
  waiting for transfers between devices  33.4 us (23%)
  local copies, waits for them, and re-layouts  9.19 us (6%)
    all_to_all x3, starting transfers between devices, spread(): lax.all_to_all(x.reshape(devices, -1), GT, 0, 0, tiled=True)  27.7 us
    ppermute x7, waiting for transfers between devices, both(): lax.ppermute(x, 'tile', outer_swap)  23.5 us
    all_to_all x1, starting transfers between devices, shards(): lax.all_to_all(card, GT, 0, 0, tiled=True, axis_index_groups=same_core)  12.1 us
    unnamed x30, local copies, waits for them, and re-layouts  9.19 us
    ppermute x7, starting transfers between devices, both(): lax.ppermute(x, 'tile', inner_swap)  9.16 us
    pallas_call x1, Pallas kernels, shards(): call(solve_first_kernel, [field] * 2, [SMEM, VMEM, ANY] + [VMEM] * 6 + [A...  8.55 us
    pallas_call x1, Pallas kernels, shards(): call(solve_second_kernel, [field, field, field, shape(3, 8, 128), field],...  8.55 us
    pallas_call x3, Pallas kernels, through(): call(product_kernel, [field], [VMEM, ANY], [held, sems], us=3)(x, stiff)  8.33 us
  transfers between devices with their start and end apart: 19, of which 12 were waited for; matrix products, arithmetic and copies ran while one was open for 0% of the time, Pallas kernels for 12%

profile of v3, /device:TPU:1, one launch (start us, length us, event | category | flops | bytes accessed | tf_op | source)
XLA Modules:
  0.0 146.5 jit_solution(11614335141623119937)
XLA Ops:
  0.7 0.7 copy-done.11
  1.4 0.7 copy-done.12
  2.1 0.7 copy-done.13
  2.8 1.3 shard_map.94
  4.0 12.1 %all-to-all-start = ((f32[64,40,128]{2,1,0:T(8,128)}), f32[64,40,128]{2,1,0:T(8,128)S(1)}, u32[]{:S(2)}, u32[]{:S(2)}) async-start(f32[64,40,128]{2,1,0:T(8,128)} %get-tuple-element.21), calls=%async_computation | async-start | bytes 2621440 | tf_op jit(solution)/shard_map/all_to_all | solution.py:405
  16.2 0.9 copy-done.10
  17.0 0.7 copy-done.14
  17.7 2.8 %shard_map.95.x_ref = f32[25,8,128]{2,1,0:T(8,128)S(1)} custom-call(f32[8,8,384]{2,1,0:T(8,128)S(1)} %copy-done.10, s32[8,8]{1,0:T(8,128)S(1)} %copy-done.14, f32[8,384,384]{2,1,0:T(8,128)} %inverse_ref.7), custom_call_target="tpu_custom_call" | custom-call | flops 2000000000 | bytes 12000000 | tf_op jit(solution)/shard_map/pallas_call | solution.py:409
  20.5 1.0 collective-permute-start
  21.6 1.3 collective-permute-start.1
  22.8 10.6 %collective-permute-done.1.b_ref = f32[25,8,128]{2,1,0:T(8,128)S(1)} collective-permute-done((f32[25,8,128]{2,1,0:T(8,128)S(1)}, f32[25,8,128]{2,1,0:T(8,128)S(1)}, u32[]{:S(2)}, u32[]{:S(2)}) %collective-permute-start.1) | collective-permute-done | bytes 102432 | tf_op jit(solution)/shard_map/ppermute | solution.py:390
  33.4 1.8 %shard_map.96 = (f32[24,8,128]{2,1,0:T(8,128)S(1)}, f32[512,128]{1,0:T(8,128)}) custom-call(s32[16,128]{1,0:T(8,128)S(1)} %get-tuple-element.20.table, f32[25,8,128]{2,1,0:T(8,128)S(1)} %collective-permute-done.a_ref, f32[25,8,128]{2,1,0:T(8,128)S(1)} %shard_map.95.x_ref, f32[25,8,128]{2,1,0:T(8,128)S(1)} %collective-permute-done.1.b_ref, ...), custom_call_target="tpu_custom_call" | custom-call | flops 1000000000 | bytes 6000000 | tf_op jit(solution)/shard_map/pallas_call | solution.py:424
  35.2 0.6 copy-done.1
  35.8 0.8 all-to-all-done
  36.6 3.3 %collective-permute-start.2 = (f32[64,40,128]{2,1,0:T(8,128)S(1)}, f32[64,40,128]{2,1,0:T(8,128)S(1)}, u32[]{:S(2)}, u32[]{:S(2)}) collective-permute-start(f32[64,40,128]{2,1,0:T(8,128)S(1)} %all-to-all-done), channel_id=1, source_target_pairs={{0,1},{1,0},{2,3},{3,2},{4,5},{5,4},{6,7},{7,6},{8,9},{9,8},{10,11... | collective-permute-start | bytes 3932168 | tf_op jit(solution)/shard_map/ppermute | solution.py:428
  39.9 8.5 %all-to-all-start.1 = ((f32[128,1,512]{2,1,0:T(1,128)}), f32[128,1,512]{2,1,0:T(1,128)S(1)}, u32[]{:S(2)}, u32[]{:S(2)}) async-start(f32[128,1,512]{2,1,0:T(1,128)} %bitcast.1), calls=%async_computation.1 | async-start | bytes 524288 | tf_op jit(solution)/shard_map/all_to_all | solution.py:417
  48.4 0.9 copy-done.2
  49.2 2.8 %shard_map.98.x_ref = f32[24,8,128]{2,1,0:T(8,128)S(1)} custom-call(f32[24,8,128]{2,1,0:T(8,128)S(1)} %copy-done.2, f32[8,384,384]{2,1,0:T(8,128)} %matrix_ref.5), custom_call_target="tpu_custom_call" | custom-call | flops 1500000000 | bytes 9000000 | tf_op jit(solution)/shard_map/pallas_call | solution.py:420
  52.0 1.1 collective-permute-start.5
  53.2 0.7 collective-permute-start.6
  53.9 5.3 %shard_map.97.weights_ref = bf16[8,384,1024]{2,1,0:T(8,128)(2,1)} custom-call(s32[1]{0:T(128)} %bitcast.core, f32[25,8,128]{2,1,0:T(8,128)S(1)} %collective-permute-done.a_ref, f32[25,8,128]{2,1,0:T(8,128)S(1)} %shard_map.95.x_ref, f32[25,8,128]{2,1,0:T(8,128)S(1)} %collective-permute-done.1.b_ref, f32[2560,128]{1,0:T(8,128)S(1)} %bitcast.9, ...), custom_call_target="tpu_custom_call" | custom-call | flops 2000000000 | bytes 12000000 | tf_op jit(solution)/shard_map/pallas_call | solution.py:431
  59.9 0.6 copy-done.8
  60.6 0.9 copy-done.5
  61.5 0.9 copy-done.7
  62.4 0.9 copy-done.9
  63.2 8.6 %shard_map.99 = (f32[24,8,128]{2,1,0:T(8,128)S(1)}, f32[24,8,128]{2,1,0:T(8,128)S(1)}) custom-call(s32[16,128]{1,0:T(8,128)S(1)} %get-tuple-element.20.table, f32[512,128]{1,0:T(8,128)S(1)} %bitcast.12, bf16[8,384,1024]{2,1,0:T(8,128)(2,1)} %shard_map.97.weights_ref, f32[8,8,384]{2,1,0:T(8,128)S(1)} %collective-permute-done.3.am_ref, ...), custom_call_target="tpu_custom_call" | custom-call | flops 3000000000 | bytes 18000000 | tf_op jit(solution)/shard_map/pallas_call | solution.py:450
  71.8 3.9 %collective-permute-start.7 = (f32[24,8,128]{2,1,0:T(8,128)S(1)}, f32[24,8,128]{2,1,0:T(8,128)S(1)}, u32[]{:S(2)}, u32[]{:S(2)}) collective-permute-start(f32[24,8,128]{2,1,0:T(8,128)S(1)} %get-tuple-element.26.x_ref), channel_id=1, source_target_pairs={{0,1},{1,0},{2,3},{3,2},{4,5},{5,4},{6,7},{7,6},{8,9},{9,8},{10,11... | collective-permute-start | bytes 294920 | tf_op jit(solution)/shard_map/ppermute | solution.py:390
  75.7 0.9 collective-permute-done.7.a_ref
  76.6 3.1 %collective-permute-done.8.b_ref = f32[24,8,128]{2,1,0:T(8,128)S(1)} collective-permute-done((f32[24,8,128]{2,1,0:T(8,128)S(1)}, f32[24,8,128]{2,1,0:T(8,128)S(1)}, u32[]{:S(2)}, u32[]{:S(2)}) %collective-permute-start.8) | collective-permute-done | bytes 98336 | tf_op jit(solution)/shard_map/ppermute | solution.py:390
  79.7 1.8 %shard_map.100 = (f32[24,8,128]{2,1,0:T(8,128)S(1)}, f32[640,128]{1,0:T(8,128)}) custom-call(s32[16,128]{1,0:T(8,128)S(1)} %get-tuple-element.20.table, f32[24,8,128]{2,1,0:T(8,128)S(1)} %collective-permute-done.7.a_ref, f32[24,8,128]{2,1,0:T(8,128)S(1)} %get-tuple-element.26.x_ref, f32[24,8,128]{2,1,0:T(8,128)S(1)} %collective-permute-done.8.b_ref, ...), custom_call_target="tpu_custom_call" | custom-call | flops 1000000000 | bytes 6000000 | tf_op jit(solution)/shard_map/pallas_call | solution.py:454
  81.5 8.7 %all-to-all-start.2 = ((f32[128,1,640]{2,1,0:T(1,128)}), f32[128,1,640]{2,1,0:T(1,128)S(1)}, u32[]{:S(2)}, u32[]{:S(2)}) async-start(f32[128,1,640]{2,1,0:T(1,128)} %bitcast.5), calls=%async_computation.2 | async-start | bytes 655360 | tf_op jit(solution)/shard_map/all_to_all | solution.py:417
  90.3 2.8 %shard_map.101.x_ref = f32[24,8,128]{2,1,0:T(8,128)S(1)} custom-call(f32[24,8,128]{2,1,0:T(8,128)S(1)} %get-tuple-element.29.x_ref.w0_ref, f32[8,384,384]{2,1,0:T(8,128)} %matrix_ref.5), custom_call_target="tpu_custom_call" | custom-call | flops 1500000000 | bytes 9000000 | tf_op jit(solution)/shard_map/pallas_call | solution.py:420
  93.1 1.1 collective-permute-start.9
  94.2 0.7 collective-permute-start.10
  95.1 3.4 %collective-permute-done.10.b_ref = f32[24,8,128]{2,1,0:T(8,128)S(1)} collective-permute-done((f32[24,8,128]{2,1,0:T(8,128)S(1)}, f32[24,8,128]{2,1,0:T(8,128)S(1)}, u32[]{:S(2)}, u32[]{:S(2)}) %collective-permute-start.10) | collective-permute-done | bytes 98336 | tf_op jit(solution)/shard_map/ppermute | solution.py:390
  98.5 3.5 %all-to-all-done.2 = f32[128,1,640]{2,1,0:T(1,128)S(1)} async-done(((f32[128,1,640]{2,1,0:T(1,128)}), f32[128,1,640]{2,1,0:T(1,128)S(1)}, u32[]{:S(2)}, u32[]{:S(2)}) %all-to-all-start.2) | async-done | bytes 327712 | tf_op jit(solution)/shard_map/all_to_all | solution.py:417
  102.0 8.6 %shard_map.102 = (f32[24,8,128]{2,1,0:T(8,128)S(1)}, f32[24,8,128]{2,1,0:T(8,128)S(1)}, f32[24,8,128]{2,1,0:T(8,128)S(1)}, f32[3,8,128]{2,1,0:T(8,128)S(1)}, f32[24,8,128]{2,1,0:T(8,128)S(1)}) custom-call(s32[16,128]{1,0:T(8,128)S(1)} %get-tuple-element.20.table, f32[640,128]{1,0:T(8,128)S(1)} %bitcast.11, bf16[8,384,1024]{2,1,0:T(8,128)(2,1)} %shard_map.97.weights_ref, ...), custom_call_target="tpu_custom_call" | custom-call | flops 3000000000 | bytes 18000000 | tf_op jit(solution)/shard_map/pallas_call | solution.py:459
  110.6 0.8 collective-permute-start.11
  111.7 0.7 collective-permute-done.11.a_ref
  112.3 3.1 %collective-permute-done.12.b_ref = f32[24,8,128]{2,1,0:T(8,128)S(1)} collective-permute-done((f32[24,8,128]{2,1,0:T(8,128)S(1)}, f32[24,8,128]{2,1,0:T(8,128)S(1)}, u32[]{:S(2)}, u32[]{:S(2)}) %collective-permute-start.12) | collective-permute-done | bytes 98336 | tf_op jit(solution)/shard_map/ppermute | solution.py:390
  115.4 1.8 %shard_map.103 = (f32[24,8,128]{2,1,0:T(8,128)S(1)}, f32[640,128]{1,0:T(8,128)}) custom-call(s32[16,128]{1,0:T(8,128)S(1)} %get-tuple-element.20.table, f32[24,8,128]{2,1,0:T(8,128)S(1)} %collective-permute-done.11.a_ref, f32[24,8,128]{2,1,0:T(8,128)S(1)} %get-tuple-element.30.x_ref, f32[24,8,128]{2,1,0:T(8,128)S(1)} %collective-permute-done.12.b_ref, ...), custom_call_target="tpu_custom_call" | custom-call | flops 1000000000 | bytes 6000000 | tf_op jit(solution)/shard_map/pallas_call | solution.py:467
  117.3 10.5 %all-to-all-start.3 = ((f32[128,1,640]{2,1,0:T(1,128)}), f32[128,1,640]{2,1,0:T(1,128)S(1)}, u32[]{:S(2)}, u32[]{:S(2)}) async-start(f32[128,1,640]{2,1,0:T(1,128)} %bitcast.7), calls=%async_computation.3 | async-start | bytes 655360 | tf_op jit(solution)/shard_map/all_to_all | solution.py:417
  127.8 2.8 %shard_map.104.x_ref = f32[24,8,128]{2,1,0:T(8,128)S(1)} custom-call(f32[24,8,128]{2,1,0:T(8,128)S(1)} %get-tuple-element.34.x_ref.v1_ref, f32[8,384,384]{2,1,0:T(8,128)} %matrix_ref.5), custom_call_target="tpu_custom_call" | custom-call | flops 1500000000 | bytes 9000000 | tf_op jit(solution)/shard_map/pallas_call | solution.py:420
  130.6 1.1 collective-permute-start.13
  131.7 0.7 collective-permute-start.14
  132.7 3.4 %collective-permute-done.14.b_ref = f32[24,8,128]{2,1,0:T(8,128)S(1)} collective-permute-done((f32[24,8,128]{2,1,0:T(8,128)S(1)}, f32[24,8,128]{2,1,0:T(8,128)S(1)}, u32[]{:S(2)}, u32[]{:S(2)}) %collective-permute-start.14) | collective-permute-done | bytes 98336 | tf_op jit(solution)/shard_map/ppermute | solution.py:390
  136.1 3.5 %all-to-all-done.3 = f32[128,1,640]{2,1,0:T(1,128)S(1)} async-done(((f32[128,1,640]{2,1,0:T(1,128)}), f32[128,1,640]{2,1,0:T(1,128)S(1)}, u32[]{:S(2)}, u32[]{:S(2)}) %all-to-all-start.3) | async-done | bytes 327712 | tf_op jit(solution)/shard_map/all_to_all | solution.py:417
  139.5 6.8 %shard_map.105 = (f32[8,8,384]{2,1,0:T(8,128)}, f32[8,8,384]{2,1,0:T(8,128)}, f32[8,8,384]{2,1,0:T(8,128)}) custom-call(s32[16,128]{1,0:T(8,128)S(1)} %get-tuple-element.20.table, f32[640,128]{1,0:T(8,128)S(1)} %bitcast.13, bf16[8,384,1024]{2,1,0:T(8,128)(2,1)} %shard_map.97.weights_ref, f32[8,8,384]{2,1,0:T(8,128)S(1)} %collective-permute-done.3.am_ref, ...), custom_call_target="tpu_custom_call" | custom-call | flops 2500000000 | bytes 15000000 | tf_op jit(solution)/shard_map/pallas_call | solution.py:473
  (32 shorter events, 1.4 us)
Async XLA Ops:
  0.6 0.8 copy-start.11
  1.4 0.7 copy-start.12
  2.1 0.7 copy-start.13
  4.0 29.3 %copy-start = (f32[8,8,384]{2,1,0:T(8,128)S(1)}, f32[8,8,384]{2,1,0:T(8,128)}, u32[]{:S(2)}) copy-start(f32[8,8,384]{2,1,0:T(8,128)} %m_ref.5) | copy-start | bytes 294916
  4.0 32.5 %all-to-all-start = ((f32[64,40,128]{2,1,0:T(8,128)}), f32[64,40,128]{2,1,0:T(8,128)S(1)}, u32[]{:S(2)}, u32[]{:S(2)}) async-start(f32[64,40,128]{2,1,0:T(8,128)} %get-tuple-element.21), calls=%async_computation | async-start | bytes 2621440 | tf_op jit(solution)/shard_map/all_to_all | solution.py:405
  16.1 0.9 copy-start.10
  17.0 0.7 copy-start.14
  20.5 2.3 %collective-permute-start = (f32[25,8,128]{2,1,0:T(8,128)S(1)}, f32[25,8,128]{2,1,0:T(8,128)S(1)}, u32[]{:S(2)}, u32[]{:S(2)}) collective-permute-start(f32[25,8,128]{2,1,0:T(8,128)S(1)} %shard_map.95.x_ref), channel_id=1, source_target_pairs={{0,1},{1,0},{2,3},{3,2},{4,5},{5,4},{6,7},{7,6},{8,9},{9,8},{10,11... | collective-permute-start | bytes 307208 | tf_op jit(solution)/shard_map/ppermute | solution.py:390
  21.6 11.8 %collective-permute-start.1 = (f32[25,8,128]{2,1,0:T(8,128)S(1)}, f32[25,8,128]{2,1,0:T(8,128)S(1)}, u32[]{:S(2)}, u32[]{:S(2)}) collective-permute-start(f32[25,8,128]{2,1,0:T(8,128)S(1)} %shard_map.95.x_ref), channel_id=1, source_target_pairs={{0,31},{1,2},{2,1},{3,4},{4,3},{5,6},{6,5},{7,8},{8,7},{9,10},{10,... | collective-permute-start | bytes 307208 | tf_op jit(solution)/shard_map/ppermute | solution.py:390
  35.2 0.6 copy-start.1
  36.6 17.3 %collective-permute-start.2 = (f32[64,40,128]{2,1,0:T(8,128)S(1)}, f32[64,40,128]{2,1,0:T(8,128)S(1)}, u32[]{:S(2)}, u32[]{:S(2)}) collective-permute-start(f32[64,40,128]{2,1,0:T(8,128)S(1)} %all-to-all-done), channel_id=1, source_target_pairs={{0,1},{1,0},{2,3},{3,2},{4,5},{5,4},{6,7},{7,6},{8,9},{9,8},{10,11... | collective-permute-start | bytes 3932168 | tf_op jit(solution)/shard_map/ppermute | solution.py:428
  39.9 19.4 %collective-permute-start.3 = (f32[8,8,384]{2,1,0:T(8,128)S(1)}, f32[8,8,384]{2,1,0:T(8,128)S(1)}, u32[]{:S(2)}, u32[]{:S(2)}) collective-permute-start(f32[8,8,384]{2,1,0:T(8,128)S(1)} %copy-done), channel_id=1, source_target_pairs={{0,1},{1,0},{2,3},{3,2},{4,5},{5,4},{6,7},{7,6},{8,9},{9,8},{10,11... | collective-permute-start | bytes 294920 | tf_op jit(solution)/shard_map/ppermute | solution.py:390
  39.9 19.4 %collective-permute-start.4 = (f32[8,8,384]{2,1,0:T(8,128)S(1)}, f32[8,8,384]{2,1,0:T(8,128)S(1)}, u32[]{:S(2)}, u32[]{:S(2)}) collective-permute-start(f32[8,8,384]{2,1,0:T(8,128)S(1)} %copy-done), channel_id=1, source_target_pairs={{0,31},{1,2},{2,1},{3,4},{4,3},{5,6},{6,5},{7,8},{8,7},{9,10},{10,... | collective-permute-start | bytes 294920 | tf_op jit(solution)/shard_map/ppermute | solution.py:390
  39.9 20.7 %all-to-all-start.1 = ((f32[128,1,512]{2,1,0:T(1,128)}), f32[128,1,512]{2,1,0:T(1,128)S(1)}, u32[]{:S(2)}, u32[]{:S(2)}) async-start(f32[128,1,512]{2,1,0:T(1,128)} %bitcast.1), calls=%async_computation.1 | async-start | bytes 524288 | tf_op jit(solution)/shard_map/all_to_all | solution.py:417
  48.3 0.9 copy-start.2
  52.0 7.2 %copy-start.4 = (f32[24,8,128]{2,1,0:T(8,128)}, f32[24,8,128]{2,1,0:T(8,128)S(1)}, u32[]{:S(2)}) copy-start(f32[24,8,128]{2,1,0:T(8,128)S(1)} %shard_map.98.x_ref) | copy-start | bytes 294916
  52.0 7.2 %collective-permute-start.5 = (f32[24,8,128]{2,1,0:T(8,128)S(1)}, f32[24,8,128]{2,1,0:T(8,128)S(1)}, u32[]{:S(2)}, u32[]{:S(2)}) collective-permute-start(f32[24,8,128]{2,1,0:T(8,128)S(1)} %shard_map.98.x_ref), channel_id=1, source_target_pairs={{0,1},{1,0},{2,3},{3,2},{4,5},{5,4},{6,7},{7,6},{8,9},{9,8},{10,11... | collective-permute-start | bytes 294920 | tf_op jit(solution)/shard_map/ppermute | solution.py:390
  53.2 6.7 %collective-permute-start.6 = (f32[24,8,128]{2,1,0:T(8,128)S(1)}, f32[24,8,128]{2,1,0:T(8,128)S(1)}, u32[]{:S(2)}, u32[]{:S(2)}) collective-permute-start(f32[24,8,128]{2,1,0:T(8,128)S(1)} %shard_map.98.x_ref), channel_id=1, source_target_pairs={{0,31},{1,2},{2,1},{3,4},{4,3},{5,6},{6,5},{7,8},{8,7},{9,10},{10,... | collective-permute-start | bytes 294920 | tf_op jit(solution)/shard_map/ppermute | solution.py:390
  59.3 0.6 copy-start.6
  59.9 0.6 copy-start.8
  60.6 0.9 copy-start.5
  61.5 0.9 copy-start.7
  62.4 0.9 copy-start.9
  63.2 16.5 %copy-start.3 = (f32[24,8,128]{2,1,0:T(8,128)S(1)}, f32[24,8,128]{2,1,0:T(8,128)}, u32[]{:S(2)}) copy-start(f32[24,8,128]{2,1,0:T(8,128)} %copy-done.1) | copy-start | bytes 294916
  71.8 4.8 %collective-permute-start.7 = (f32[24,8,128]{2,1,0:T(8,128)S(1)}, f32[24,8,128]{2,1,0:T(8,128)S(1)}, u32[]{:S(2)}, u32[]{:S(2)}) collective-permute-start(f32[24,8,128]{2,1,0:T(8,128)S(1)} %get-tuple-element.26.x_ref), channel_id=1, source_target_pairs={{0,1},{1,0},{2,3},{3,2},{4,5},{5,4},{6,7},{7,6},{8,9},{9,8},{10,11... | collective-permute-start | bytes 294920 | tf_op jit(solution)/shard_map/ppermute | solution.py:390
  75.7 4.0 %collective-permute-start.8 = (f32[24,8,128]{2,1,0:T(8,128)S(1)}, f32[24,8,128]{2,1,0:T(8,128)S(1)}, u32[]{:S(2)}, u32[]{:S(2)}) collective-permute-start(f32[24,8,128]{2,1,0:T(8,128)S(1)} %get-tuple-element.26.x_ref), channel_id=1, source_target_pairs={{0,31},{1,2},{2,1},{3,4},{4,3},{5,6},{6,5},{7,8},{8,7},{9,10},{10,... | collective-permute-start | bytes 294920 | tf_op jit(solution)/shard_map/ppermute | solution.py:390
  81.5 20.5 %all-to-all-start.2 = ((f32[128,1,640]{2,1,0:T(1,128)}), f32[128,1,640]{2,1,0:T(1,128)S(1)}, u32[]{:S(2)}, u32[]{:S(2)}) async-start(f32[128,1,640]{2,1,0:T(1,128)} %bitcast.5), calls=%async_computation.2 | async-start | bytes 655360 | tf_op jit(solution)/shard_map/all_to_all | solution.py:417
  93.1 2.1 %collective-permute-start.9 = (f32[24,8,128]{2,1,0:T(8,128)S(1)}, f32[24,8,128]{2,1,0:T(8,128)S(1)}, u32[]{:S(2)}, u32[]{:S(2)}) collective-permute-start(f32[24,8,128]{2,1,0:T(8,128)S(1)} %shard_map.101.x_ref), channel_id=1, source_target_pairs={{0,1},{1,0},{2,3},{3,2},{4,5},{5,4},{6,7},{7,6},{8,9},{9,8},{10,11... | collective-permute-start | bytes 294920 | tf_op jit(solution)/shard_map/ppermute | solution.py:390
  94.2 4.3 %collective-permute-start.10 = (f32[24,8,128]{2,1,0:T(8,128)S(1)}, f32[24,8,128]{2,1,0:T(8,128)S(1)}, u32[]{:S(2)}, u32[]{:S(2)}) collective-permute-start(f32[24,8,128]{2,1,0:T(8,128)S(1)} %shard_map.101.x_ref), channel_id=1, source_target_pairs={{0,31},{1,2},{2,1},{3,4},{4,3},{5,6},{6,5},{7,8},{8,7},{9,10},{10,... | collective-permute-start | bytes 294920 | tf_op jit(solution)/shard_map/ppermute | solution.py:390
  110.6 1.8 %collective-permute-start.11 = (f32[24,8,128]{2,1,0:T(8,128)S(1)}, f32[24,8,128]{2,1,0:T(8,128)S(1)}, u32[]{:S(2)}, u32[]{:S(2)}) collective-permute-start(f32[24,8,128]{2,1,0:T(8,128)S(1)} %get-tuple-element.30.x_ref), channel_id=1, source_target_pairs={{0,1},{1,0},{2,3},{3,2},{4,5},{5,4},{6,7},{7,6},{8,9},{9,8},{10,11... | collective-permute-start | bytes 294920 | tf_op jit(solution)/shard_map/ppermute | solution.py:390
  111.4 4.0 %collective-permute-start.12 = (f32[24,8,128]{2,1,0:T(8,128)S(1)}, f32[24,8,128]{2,1,0:T(8,128)S(1)}, u32[]{:S(2)}, u32[]{:S(2)}) collective-permute-start(f32[24,8,128]{2,1,0:T(8,128)S(1)} %get-tuple-element.30.x_ref), channel_id=1, source_target_pairs={{0,31},{1,2},{2,1},{3,4},{4,3},{5,6},{6,5},{7,8},{8,7},{9,10},{10,... | collective-permute-start | bytes 294920 | tf_op jit(solution)/shard_map/ppermute | solution.py:390
  117.3 22.3 %all-to-all-start.3 = ((f32[128,1,640]{2,1,0:T(1,128)}), f32[128,1,640]{2,1,0:T(1,128)S(1)}, u32[]{:S(2)}, u32[]{:S(2)}) async-start(f32[128,1,640]{2,1,0:T(1,128)} %bitcast.7), calls=%async_computation.3 | async-start | bytes 655360 | tf_op jit(solution)/shard_map/all_to_all | solution.py:417
  130.6 2.1 %collective-permute-start.13 = (f32[24,8,128]{2,1,0:T(8,128)S(1)}, f32[24,8,128]{2,1,0:T(8,128)S(1)}, u32[]{:S(2)}, u32[]{:S(2)}) collective-permute-start(f32[24,8,128]{2,1,0:T(8,128)S(1)} %shard_map.104.x_ref), channel_id=1, source_target_pairs={{0,1},{1,0},{2,3},{3,2},{4,5},{5,4},{6,7},{7,6},{8,9},{9,8},{10,11... | collective-permute-start | bytes 294920 | tf_op jit(solution)/shard_map/ppermute | solution.py:390
  131.7 4.3 %collective-permute-start.14 = (f32[24,8,128]{2,1,0:T(8,128)S(1)}, f32[24,8,128]{2,1,0:T(8,128)S(1)}, u32[]{:S(2)}, u32[]{:S(2)}) collective-permute-start(f32[24,8,128]{2,1,0:T(8,128)S(1)} %shard_map.104.x_ref), channel_id=1, source_target_pairs={{0,31},{1,2},{2,1},{3,4},{4,3},{5,6},{6,5},{7,8},{8,7},{9,10},{10,... | collective-permute-start | bytes 294920 | tf_op jit(solution)/shard_map/ppermute | solution.py:390

commit v4 on v3

--- a/solution.py
+++ b/solution.py
@@ -18,7 +18,7 @@
 CHUNKS = WIDTH // 128
 TILES = COUNT * CHUNKS
 SLOTS = COUNT * CORNERS
-CARD = 40
+CARD = 37
 PARTS, PART = 8, 1024
 
 
@@ -91,13 +91,7 @@
             pool[e * TILES + t] = ref[t]
 
 
-def card_kernel(core, inverse_ref, index_ref, partner_ref, card_ref, table_ref):
-    inverse = inverse_ref[...]
-    block = jnp.concatenate([inverse[:32], inverse[32:]], axis=1)
-    card_ref[:, 0:32, :] = jnp.broadcast_to(block[None], (card_ref.shape[0], 32, 128))
-    row = index_row(index_ref)
-    card_ref[:, 32:40, :] = jnp.broadcast_to(row[None], (card_ref.shape[0], 8, 128))
-    partner = partner_ref[...]
+def mate_places(core, partner, table_ref):
     region = (partner >= COUNT * FACES).astype(jnp.int32) + (partner >= 2 * COUNT * FACES).astype(jnp.int32)
     within = partner - region * (COUNT * FACES)
     particle = jnp.zeros_like(within)
@@ -109,15 +103,18 @@
     table_ref[8:16, 0:FACES] = ((lanes((COUNT, FACES)) - face) & 3) * 32
 
 
-def index_row(index_ref):
-    index = index_ref[...].astype(F32)
-    wide = jnp.concatenate([index] * 16, axis=1)
+def index_row(index):
+    wide = jnp.concatenate([index.astype(F32)] * 16, axis=1)
     keep = lanes() // 8 == sublanes()
     return jnp.broadcast_to(jnp.sum(jnp.where(keep, wide, 0.0), axis=0, keepdims=True), (8, 128))
 
 
+def copies_of(source, held, sems, first=0):
+    return [pltpu.make_async_copy(source.at[i], held.at[i], sems.at[first + i]) for i in range(source.shape[0])]
+
+
 def fetch(source, held, sems, first=0):
-    copies = [pltpu.make_async_copy(source.at[i], held.at[i], sems.at[first + i]) for i in range(source.shape[0])]
+    copies = copies_of(source, held, sems, first)
     for copy in copies:
         copy.start()
     return copies
@@ -129,12 +126,23 @@
         put_tiles(out_ref, p, product(get_row(x, p), held[p]))
 
 
-def start_kernel(loads_ref, index_ref, inverse_ref, out_ref, held, sems):
+def start_kernel(
+    core, loads_ref, index_ref, partner_ref, inverse_ref, out_ref, table_ref, loads, index, partner, held, sems
+):
+    small = [
+        pltpu.make_async_copy(source, to, sems.at[COUNT + i])
+        for i, (source, to) in enumerate(((loads_ref, loads), (index_ref, index), (partner_ref, partner)))
+    ]
+    for copy in small:
+        copy.start()
     copies = fetch(inverse_ref, held, sems)
-    out_ref[TILES] = index_row(index_ref)
+    for copy in small:
+        copy.wait()
+    out_ref[TILES] = index_row(index[...])
+    mate_places(core, partner[...], table_ref)
     for p in range(COUNT):
         copies[p].wait()
-        put_tiles(out_ref, p, product(loads_ref[p], held[p]))
+        put_tiles(out_ref, p, product(loads[p], held[p]))
 
 
 def product_kernel(x_ref, matrix_ref, out_ref, held, sems):
@@ -157,8 +165,8 @@
     return jnp.sum(total, axis=1, keepdims=True)
 
 
-def send(r, map_ref, columns, pay_ref):
-    lane, sub = lanes(), sublanes()
+def contributions(r, map_ref):
+    lane = lanes()
     contrib = jnp.zeros((8, 128), F32)
     for p in range(COUNT):
         for j in range(CORNERS):
@@ -168,23 +176,28 @@
             total = jnp.sum(part, axis=1, keepdims=True)
             contrib = jnp.where(lane == p * CORNERS + j, jnp.broadcast_to(total, (8, 128)), contrib)
     turned = pltpu.roll(pltpu.roll(contrib, 64, 1), 4, 0)
-    pay = jnp.where(lane < 64, contrib, turned)
-    if not columns:
-        pair = jnp.where(sub < 4, pay, pltpu.roll(pay, 4, 0))
-        for at in range(0, pay_ref.shape[0], 8):
-            pay_ref[at : at + 8, :] = pair
-        return
-    pay = jnp.where(sub < 4, pay, jnp.broadcast_to(column_to_row(columns), (8, 128)))[0:5]
+    return jnp.where(lane < 64, contrib, turned)
+
+
+def send(r, map_ref, columns, pay_ref):
+    pay = contributions(r, map_ref)
+    pay = jnp.where(sublanes() < 4, pay, jnp.broadcast_to(column_to_row(columns), (8, 128)))[0:5]
     for at in range(0, pay_ref.shape[0], 5):
         pay_ref[at : at + 5, :] = pay
 
 
-def send_first_kernel(table, a_ref, x_ref, b_ref, map_ref, r_ref, pay_ref, pool):
+def send_first_kernel(table, a_ref, x_ref, b_ref, map_ref, inverse_ref, r_ref, card_ref, pool):
     fill_pool(pool, a_ref, x_ref, b_ref)
     r = jump(pool, table)
     for t in range(TILES):
         r_ref[t] = r[t]
-    send(r, map_ref, [], pay_ref)
+    inverse = inverse_ref[...]
+    pay = contributions(r, map_ref)
+    card = jnp.concatenate([inverse[:32], inverse[32:]], axis=1)
+    tail = jnp.where(sublanes() < 1, x_ref[TILES], pltpu.roll(pay, 1, 0))[0:5]
+    for at in range(0, card_ref.shape[0], CARD):
+        card_ref[at : at + 32, :] = card
+        card_ref[at + 32 : at + CARD, :] = tail
 
 
 def send_second_kernel(table, a_ref, x_ref, b_ref, map_ref, r0_ref, z0_ref, w_ref, pay_ref, pool):
@@ -206,18 +219,9 @@
     send(v, map_ref, columns, pay_ref)
 
 
-def weights_kernel(core, a_ref, x_ref, b_ref, own_ref, other_ref, out_ref, rows, names, index, wanted, built, sems):
-    mine = core[0]
-    copies = [
-        pltpu.make_async_copy(ref.at[TILES], wanted.at[e], sems.at[e]) for e, ref in enumerate((a_ref, x_ref, b_ref))
-    ]
-    for copy in copies:
-        copy.start()
-    for copy in copies:
-        copy.wait()
-
+def gather_rows(mine, ids, own_ref, other_ref, rows, names):
     def pick(j, carry):
-        row = wanted[j >> 6, 0, j & 63].astype(jnp.int32)
+        row = ids[j >> 6, 0, j & 63].astype(jnp.int32)
         owner = row >> 6
         at = (owner >> 1) * CARD + (row & 31)
         same = (owner & 1) == mine
@@ -228,73 +232,32 @@
         return carry
 
     lax.fori_loop(0, 3 * SLOTS, pick, 0, unroll=16)
-    chips = own_ref.shape[0] // CARD
-    own = own_ref[pl.ds(32, chips, stride=CARD), :]
-    other = other_ref[pl.ds(32, chips, stride=CARD), :]
-    first = jnp.where(mine == 0, own, other)
-    second = jnp.where(mine == 0, other, own)
-    wide = lanes((chips, 128))
-    merged = jnp.where(wide < 64, first, pltpu.roll(second, 64, 1)).astype(jnp.int32)
-    index[...] = merged
-    lane = lanes((3 * SLOTS, 128))
-    upper = (names[...] & 63) >= 32
-    kept = jnp.where(upper == (lane >= 64), rows[...], 0.0)
-    high, low = halves(kept)
-    both = jnp.concatenate([high, low], axis=0)
-    names[...] = names[...] >> 6
-    place = sublanes((128, 256)) & 63
-
-    def spread(q, carry):
-        row = jnp.concatenate([index[pl.ds(2 * q, 1), :], index[pl.ds(2 * q + 1, 1), :]], axis=1)
-        onehot = (place == (row & 63)).astype(F32).astype(BF16)
-        full = jnp.dot(both, onehot, preferred_element_type=F32)
-        block = row >> 6
-        named = names[...]
-        hit = jnp.concatenate([named, named], axis=1) == block
-        at = pl.ds(pl.multiple_of((q & 3) * 256, 256), 256)
-        built[q >> 2, 0 : 3 * SLOTS, at] = jnp.where(hit, full[: 3 * SLOTS], 0.0).astype(BF16)
-        built[q >> 2, 3 * SLOTS :, at] = jnp.where(hit, full[3 * SLOTS :], 0.0).astype(BF16)
-        return carry
-
-    copies = []
-    for part in range(PARTS):
-        lax.fori_loop(part * 4, part * 4 + 4, spread, 0, unroll=4)
-        copy = pltpu.make_async_copy(built.at[part], out_ref.at[part], sems.at[3 + part])
-        copy.start()
-        copies.append(copy)
-    for copy in copies:
-        copy.wait()
-
-
-def coarse_into_pool(got_ref, copies, weights, maps, pool, gathered):
-    lane, sub = lanes(), sublanes()
-    straight = (sub < 4) == (lane < 64)
-    sums = None
-    senders = PARTS * PART // SLOTS
-    rows = got_ref.shape[0] // senders
-    if rows == 5:
-        sums = jnp.sum(got_ref[pl.ds(4, senders, stride=5), :], axis=0, keepdims=True)
-    for q in range(senders // 2):
-        at = 2 * q * rows
-        if rows == 4:
-            pair = got_ref[at : at + 8, :]
-        else:
-            pair = jnp.concatenate([got_ref[at : at + 4, :], got_ref[at + 5 : at + 9, :]], axis=0)
-        tile = jnp.where(straight, pair, pltpu.roll(pltpu.roll(pair, 64, 1), 4, 0))
-        high, low = halves(tile)
-        gathered[:, q * 128 : (q + 1) * 128] = jnp.concatenate([high, low], axis=0)
-    out = None
-    for c in range(PARTS):
-        copies[c].wait()
-        term = lax.dot_general(
-            weights[c], gathered[:, c * PART : (c + 1) * PART], NT, preferred_element_type=F32
-        )
-        out = term if out is None else out + term
+
+
+def place(pair, q, gathered):
+    straight = (sublanes() < 4) == (lanes() < 64)
+    tile = jnp.where(straight, pair, pltpu.roll(pltpu.roll(pair, 64, 1), 4, 0))
+    high, low = halves(tile)
+    gathered[:, q * 128 : (q + 1) * 128] = jnp.concatenate([high, low], axis=0)
+
+
+def unpack(got_ref, gathered):
+    for q in range(PARTS * PART // 128):
+        at = 10 * q
+        place(jnp.concatenate([got_ref[at : at + 4, :], got_ref[at + 5 : at + 9, :]], axis=0), q, gathered)
+    return jnp.sum(got_ref[pl.ds(4, PARTS * PART // SLOTS, stride=5), :], axis=0, keepdims=True)
+
+
+def partial_solve(weights, gathered, c):
+    return lax.dot_general(weights[c], gathered[:, c * PART : (c + 1) * PART], NT, preferred_element_type=F32)
+
+
+def into_pool(out, maps, pool):
     count = 3 * SLOTS
     sol = out[:count] + out[count:]
     sol = sol.T
     sol = sol[:8] + sol[8:]
-    own = lax.broadcasted_iota(jnp.int32, (64, 64), 0) // 8 == lax.broadcasted_iota(jnp.int32, (64, 64), 1) // 8
+    own = sublanes((64, 64)) // 8 == lanes((64, 64)) // 8
     for e, map_ref in enumerate(maps):
         part = sol[:, e * SLOTS : (e + 1) * SLOTS]
         spread = jnp.where(own, jnp.concatenate([part] * COUNT, axis=0), 0.0)
@@ -306,6 +269,18 @@
             for c in range(CHUNKS):
                 t = e * TILES + p * CHUNKS + c
                 pool[t] = pool[t] + full[p * 8 : (p + 1) * 8, c * 128 : (c + 1) * 128]
+
+
+def coarse_into_pool(got_ref, copies, weights, maps, pool, gathered, then=()):
+    sums = unpack(got_ref, gathered)
+    out = None
+    for c in range(PARTS):
+        copies[c].wait()
+        if then:
+            then[c].start()
+        term = partial_solve(weights, gathered, c)
+        out = term if out is None else out + term
+    into_pool(out, maps, pool)
     return sums
 
 
@@ -319,17 +294,68 @@
 
 
 def solve_first_kernel(
-    table, got_ref, weights_ref, am_ref, m_ref, bm_ref, a_ref, x_ref, b_ref, inverse_ref, z_ref, u_ref,
-    pool, gathered, weights, held, sems,
+    core, table, ia_ref, ix_ref, ib_ref, own_ref, other_ref, am_ref, m_ref, bm_ref, a_ref, x_ref, b_ref, inverse_ref,
+    z_ref, u_ref, weights_ref, pool, gathered, weights, held, sems, rows, names, index, ids,
 ):
-    parts = fetch(weights_ref, weights, sems, COUNT)
+    mine = core[0]
+    small = [
+        pltpu.make_async_copy(ref.at[TILES], ids.at[e], sems.at[COUNT + PARTS + e])
+        for e, ref in enumerate((ia_ref, ix_ref, ib_ref))
+    ]
+    for copy in small:
+        copy.start()
     copies = fetch(inverse_ref, held, sems)
+    for copy in small:
+        copy.wait()
+    gather_rows(mine, ids, own_ref, other_ref, rows, names)
     fill_pool(pool, a_ref, x_ref, b_ref)
-    coarse_into_pool(got_ref, parts, weights, (am_ref, m_ref, bm_ref), pool, gathered)
+    chips = PARTS * PART // 128
+    own = own_ref[pl.ds(32, chips, stride=CARD), :]
+    other = other_ref[pl.ds(32, chips, stride=CARD), :]
+    first = jnp.where(mine == 0, own, other)
+    second = jnp.where(mine == 0, other, own)
+    index[...] = jnp.where(lanes((chips, 128)) < 64, first, pltpu.roll(second, 64, 1)).astype(jnp.int32)
+    for q in range(chips):
+        at = q * CARD + 33
+        own, other = own_ref[at : at + 4, :], other_ref[at : at + 4, :]
+        first = jnp.where(mine == 0, own, other)
+        second = jnp.where(mine == 0, other, own)
+        place(jnp.concatenate([first, second], axis=0), q, gathered)
+    upper = (names[...] & 63) >= 32
+    kept = jnp.where(upper == (lanes((3 * SLOTS, 128)) >= 64), rows[...], 0.0)
+    high, low = halves(kept)
+    both = jnp.concatenate([high, low], axis=0)
+    names[...] = names[...] >> 6
+    spot = sublanes((128, 256)) & 63
+
+    def spread(q, carry):
+        row = jnp.concatenate([index[pl.ds(2 * q, 1), :], index[pl.ds(2 * q + 1, 1), :]], axis=1)
+        onehot = (spot == (row & 63)).astype(F32).astype(BF16)
+        full = jnp.dot(both, onehot, preferred_element_type=F32)
+        block = row >> 6
+        named = names[...]
+        hit = jnp.concatenate([named, named], axis=1) == block
+        at = pl.ds(pl.multiple_of((q & 3) * 256, 256), 256)
+        weights[q >> 2, 0 : 3 * SLOTS, at] = jnp.where(hit, full[: 3 * SLOTS], 0.0).astype(BF16)
+        weights[q >> 2, 3 * SLOTS :, at] = jnp.where(hit, full[3 * SLOTS :], 0.0).astype(BF16)
+        return carry
+
+    stores = []
+    out = None
+    for part in range(PARTS):
+        lax.fori_loop(part * 4, part * 4 + 4, spread, 0, unroll=4)
+        store = pltpu.make_async_copy(weights.at[part], weights_ref.at[part], sems.at[COUNT + part])
+        store.start()
+        stores.append(store)
+        term = partial_solve(weights, gathered, part)
+        out = term if out is None else out + term
+    into_pool(out, (am_ref, m_ref, bm_ref), pool)
     z = [0.5 * t for t in jump(pool, table)]
     for t in range(TILES):
         z_ref[t] = z[t]
     multiply(z, copies, held, u_ref)
+    for store in stores:
+        store.wait()
 
 
 def solve_second_kernel(
@@ -337,9 +363,9 @@
     y_ref, r_ref, z_ref, scale_ref, u_ref, pool, gathered, weights, held, sems,
 ):
     parts = fetch(weights_ref, weights, sems, COUNT)
-    copies = fetch(inverse_ref, held, sems)
+    copies = copies_of(inverse_ref, held, sems)
     fill_pool(pool, a_ref, x_ref, b_ref)
-    sums = coarse_into_pool(got_ref, parts, weights, (am_ref, m_ref, bm_ref), pool, gathered)
+    sums = coarse_into_pool(got_ref, parts, weights, (am_ref, m_ref, bm_ref), pool, gathered, copies)
     energy, curve = totals(sums, 2)
     step = energy / curve
     scale_ref[0] = energy
@@ -396,22 +422,24 @@
     sems = pltpu.SemaphoreType.DMA((COUNT,))
 
     core = core.astype(jnp.int32).reshape(1)
-    card, table = call(
-        card_kernel,
-        [shape(devices // 2, CARD, 128), jax.ShapeDtypeStruct((16, 128), jnp.int32)],
-        [SMEM] + [VMEM] * 3,
-        us=1,
-    )(core, coarse_inverse, corner_index, partner)
-    own_cards = lax.all_to_all(card, GT, 0, 0, tiled=True, axis_index_groups=same_core)
     held = pltpu.VMEM((COUNT, WIDTH, WIDTH), F32)
     solver = pltpu.VMEM((PARTS, 6 * SLOTS, PART), BF16)
     inverse, stiff = in_hbm(local_inverse), in_hbm(schur)
-    (u,) = call(start_kernel, [shape(TILES + 1, 8, 128)], [VMEM, VMEM, ANY], [held, sems], us=4)(
-        loads, corner_index, inverse
-    )
+    u, table = call(
+        start_kernel,
+        [shape(TILES + 1, 8, 128), jax.ShapeDtypeStruct((16, 128), jnp.int32)],
+        [SMEM] + [ANY] * 4,
+        [
+            pltpu.VMEM((COUNT, CASES, WIDTH), F32),
+            pltpu.VMEM((COUNT, CORNERS), jnp.int32),
+            pltpu.VMEM((COUNT, FACES), jnp.int32),
+            held,
+            pltpu.SemaphoreType.DMA((COUNT + 3,)),
+        ],
+        us=4,
+    )(core, in_hbm(loads), in_hbm(corner_index), in_hbm(partner), inverse)
     ua, ub = both(u)
-    ma, mb = both(corner_map)
-    maps = (ma, corner_map, mb)
+    indices = (ua, u, ub)
 
     def spread(x):
         return lax.all_to_all(x.reshape(devices, -1), GT, 0, 0, tiled=True).reshape(-1, 128)
@@ -421,35 +449,38 @@
         qa, qb = both(q)
         return qa, q, qb
 
-    r0, parts = call(send_first_kernel, [field, shape(devices * 4, 128)], [SMEM] + [VMEM] * 4, [pool])(
-        table, ua, u, ub, corner_map
+    r0, card = call(send_first_kernel, [field, shape(devices // 2 * CARD, 128)], [SMEM] + [VMEM] * 5, [pool])(
+        table, ua, u, ub, corner_map, coarse_inverse
     )
-    own_cards, parts = lax.optimization_barrier((own_cards, parts))
+    own_cards = lax.all_to_all(
+        card.reshape(devices // 2, -1), GT, 0, 0, tiled=True, axis_index_groups=same_core
+    ).reshape(-1, 128)
+    pooled = through(r0)
+    ma, mb = both(corner_map)
+    maps = (ma, corner_map, mb)
+    own_cards, pooled, maps = lax.optimization_barrier((own_cards, pooled, maps))
     other_cards = lax.ppermute(own_cards, "tile", inner_swap)
-    got = spread(parts)
-    pooled = through(r0)
-    weights = pl.pallas_call(
-        weights_kernel,
-        in_specs=[SMEM] + [ANY] * 3 + [VMEM] * 2,
-        out_specs=ANY,
-        out_shape=pltpu.HBM((PARTS, 6 * SLOTS, PART), BF16),
+    z0, u, weights = pl.pallas_call(
+        solve_first_kernel,
+        in_specs=[SMEM] * 2 + [ANY] * 3 + [VMEM] * 8 + [ANY],
+        out_specs=[VMEM, VMEM, ANY],
+        out_shape=[field, field, pltpu.HBM((PARTS, 6 * SLOTS, PART), BF16)],
         scratch_shapes=[
+            pool,
+            gathered,
+            solver,
+            held,
+            pltpu.SemaphoreType.DMA((COUNT + PARTS + 3,)),
             pltpu.VMEM((3 * SLOTS, 128), F32),
             pltpu.VMEM((3 * SLOTS, 128), jnp.int32),
             pltpu.VMEM((devices // 2, 128), jnp.int32),
             pltpu.SMEM((3, 8, 128), F32),
-            solver,
-            pltpu.SemaphoreType.DMA((3 + PARTS,)),
         ],
         compiler_params=PARAMS,
-        cost_estimate=pl.CostEstimate(flops=2_000_000_000, bytes_accessed=12_000_000, transcendentals=0),
-    )(core, ua, u, ub, own_cards.reshape(-1, 128), other_cards.reshape(-1, 128))
+        cost_estimate=pl.CostEstimate(flops=4_000_000_000, bytes_accessed=20_000_000, transcendentals=0),
+    )(core, table, *indices, own_cards, other_cards, *maps, *pooled, inverse)
     weights = in_hbm(weights)
-    solve_sems = pltpu.SemaphoreType.DMA((COUNT + PARTS,))
-    solve_scratch = [pool, gathered, solver, held, solve_sems]
-    z0, u = call(
-        solve_first_kernel, [field] * 2, [SMEM, VMEM, ANY] + [VMEM] * 6 + [ANY], solve_scratch, us=6
-    )(table, got, weights, *maps, *pooled, inverse)
+    solve_scratch = [pool, gathered, solver, held, pltpu.SemaphoreType.DMA((COUNT + PARTS,))]
     ua, ub = both(u)
     w0, parts = call(send_second_kernel, [field, pay], [SMEM] + [VMEM] * 6, [pool])(
         table, ua, u, ub, corner_map, r0, z0

time: 147 us -> 127 us (0.86)
  local copies, waits for them, and re-layouts: 9.19 us -> 0.01 us
  waiting for transfers between devices: 33.4 us -> 25.8 us
  Pallas kernels: 47 us -> 42.3 us
  starting transfers between devices: 56 us -> 57.5 us
    ppermute x7, waiting for transfers between devices: 23.5 us -> 10.1 us  [both(): lax.ppermute(x, 'tile', outer_swap)]
    ppermute x7, starting transfers between devices: 9.16 us -> 19.2 us  [both(): lax.ppermute(x, 'tile', inner_swap)]
    all_to_all x3 -> x2, starting transfers between devices: 27.7 us -> 17.8 us  [spread(): lax.all_to_all(x.reshape(devices, -1), GT, 0, 0, tiled=True)]
    unnamed x30 -> x4, local copies, waits for them, and re-layouts: 9.19 us -> 0.01 us
    ppermute x7, starting transfers between devices: 3.69 us -> 8.75 us  [both(): lax.ppermute(x, 'tile', outer_swap)]
    pallas_call x5 -> x3, Pallas kernels: 19.7 us -> 15 us  [the longest x1 9.98 us: shards(): pl.pallas_call(solve_first_kernel, in_specs=[SMEM] * 2 + [ANY] * 3 + [VME...]
    ppermute x1, starting transfers between devices: 3.29 us -> 0.01 us  [shards(): other_cards = lax.ppermute(own_cards, 'tile', inner_swap)]
    all_to_all x1, waiting for transfers between devices: 0.77 us -> 4.04 us  [shards(): lax.all_to_all(card.reshape(devices // 2, -1), GT, 0, 0, tiled=True, axis...]
  transfers between devices with their start and end apart: 19 -> 18, of which waited for: 12 -> 12; matrix products, arithmetic and copies ran while one was open for 0% -> 0% of each run, Pallas kernels for 12% -> 7%
where the time goes in v4:
time: 127 us
  starting transfers between devices  57.5 us (45%)
  Pallas kernels  42.3 us (33%)
  waiting for transfers between devices  25.8 us (20%)
    ppermute x7, starting transfers between devices, both(): lax.ppermute(x, 'tile', inner_swap)  19.2 us
    all_to_all x2, starting transfers between devices, spread(): lax.all_to_all(x.reshape(devices, -1), GT, 0, 0, tiled=True)  17.8 us
    all_to_all x1, starting transfers between devices, shards(): lax.all_to_all(card.reshape(devices // 2, -1), GT, 0, 0, tiled=True, axis...  11.8 us
    ppermute x7, waiting for transfers between devices, both(): lax.ppermute(x, 'tile', outer_swap)  10.1 us
    pallas_call x1, Pallas kernels, shards(): pl.pallas_call(solve_first_kernel, in_specs=[SMEM] * 2 + [ANY] * 3 + [VME...  9.98 us
    ppermute x7, starting transfers between devices, both(): lax.ppermute(x, 'tile', outer_swap)  8.75 us
    pallas_call x1, Pallas kernels, shards(): call(solve_second_kernel, [field, field, field, shape(3, 8, 128), field],...  8.55 us
    pallas_call x3, Pallas kernels, through(): call(product_kernel, [field], [VMEM, ANY], [held, sems], us=3)(x, stiff)  8.33 us
  transfers between devices with their start and end apart: 18, of which 12 were waited for; matrix products, arithmetic and copies ran while one was open for 0% of the time, Pallas kernels for 7%

profile of v4, /device:TPU:1, one launch (start us, length us, event | category | flops | bytes accessed | tf_op | source)
XLA Modules:
  0.0 126.6 jit_solution(10186526659493784047)
XLA Ops:
  0.6 0.0 copy-start
  0.7 2.9 %shard_map.94 = (f32[25,8,128]{2,1,0:T(8,128)S(1)}, s32[16,128]{1,0:T(8,128)S(1)}) custom-call(s32[1]{0:T(128)} %bitcast.core, f32[8,8,384]{2,1,0:T(8,128)} %loads_ref.1, s32[8,8]{1,0:T(8,128)} %index_ref.1, s32[8,12]{1,0:T(8,128)} %partner_ref.1, f32[8,384,384]{2,1,0:T(8,128)} %inverse_ref.7), custom_call_target="tpu_custom_call" | custom-call | flops 2000000000 | bytes 12000000 | tf_op jit(solution)/shard_map/pallas_call | solution.py:428
  3.6 2.7 %collective-permute-start.1 = (f32[25,8,128]{2,1,0:T(8,128)S(1)}, f32[25,8,128]{2,1,0:T(8,128)S(1)}, u32[]{:S(2)}, u32[]{:S(2)}) collective-permute-start(f32[25,8,128]{2,1,0:T(8,128)S(1)} %get-tuple-element.27.x_ref.ix_ref), channel_id=1, source_target_pairs={{0,31},{1,2},{2,1},{3,4},{4,3},{5,6},{6,5},{7,8},{8,7},{9,10},{10,... | collective-permute-start | bytes 307208 | tf_op jit(solution)/shard_map/ppermute | solution.py:416
  6.3 3.6 %collective-permute-start = (f32[25,8,128]{2,1,0:T(8,128)S(1)}, f32[25,8,128]{2,1,0:T(8,128)S(1)}, u32[]{:S(2)}, u32[]{:S(2)}) collective-permute-start(f32[25,8,128]{2,1,0:T(8,128)S(1)} %get-tuple-element.27.x_ref.ix_ref), channel_id=1, source_target_pairs={{0,1},{1,0},{2,3},{3,2},{4,5},{5,4},{6,7},{7,6},{8,9},{9,8},{10,11... | collective-permute-start | bytes 307208 | tf_op jit(solution)/shard_map/ppermute | solution.py:416
  9.8 0.0 collective-permute-done.1.b_ref.ib_ref
  9.8 0.9 collective-permute-done.a_ref.ia_ref
  10.8 0.0 copy-done.1
  10.8 2.1 %shard_map.95 = (f32[24,8,128]{2,1,0:T(8,128)S(1)}, f32[2368,128]{1,0:T(8,128)}) custom-call(s32[16,128]{1,0:T(8,128)S(1)} %get-tuple-element.26.table, f32[25,8,128]{2,1,0:T(8,128)S(1)} %collective-permute-done.a_ref.ia_ref, f32[25,8,128]{2,1,0:T(8,128)S(1)} %get-tuple-element.27.x_ref.ix_ref, f32[25,8,128]{2,1,0:T(8,128)S(1)} %collective-permute-done.1.b_ref.ib_ref, ...), custom_call_target="tpu_custom_call" | custom-call | flops 1000000000 | bytes 6000000 | tf_op jit(solution)/shard_map/pallas_call | solution.py:452
  12.9 11.8 %all-to-all-start = ((f32[64,1,4736]{2,1,0:T(1,128)}), f32[64,1,4736]{2,1,0:T(1,128)S(1)}, u32[]{:S(2)}, u32[]{:S(2)}) async-start(f32[64,1,4736]{2,1,0:T(1,128)} %bitcast.1), calls=%async_computation | async-start | bytes 2424832 | tf_op jit(solution)/shard_map/all_to_all | solution.py:455
  24.8 0.1 collective-permute-start.5
  24.8 4.7 %collective-permute-start.4 = (f32[8,8,384]{2,1,0:T(8,128)S(1)}, f32[8,8,384]{2,1,0:T(8,128)S(1)}, u32[]{:S(2)}, u32[]{:S(2)}) collective-permute-start(f32[8,8,384]{2,1,0:T(8,128)S(1)} %copy-done), channel_id=1, source_target_pairs={{0,1},{1,0},{2,3},{3,2},{4,5},{5,4},{6,7},{7,6},{8,9},{9,8},{10,11... | collective-permute-start | bytes 294920 | tf_op jit(solution)/shard_map/ppermute | solution.py:416
  29.6 2.8 %shard_map.96.x_ref = f32[24,8,128]{2,1,0:T(8,128)S(1)} custom-call(f32[24,8,128]{2,1,0:T(8,128)S(1)} %get-tuple-element.29.x_ref.r0_ref, f32[8,384,384]{2,1,0:T(8,128)} %matrix_ref.5), custom_call_target="tpu_custom_call" | custom-call | flops 1500000000 | bytes 9000000 | tf_op jit(solution)/shard_map/pallas_call | solution.py:448
  32.4 0.1 collective-permute-start.3
  32.4 1.0 collective-permute-start.2
  33.4 5.6 %collective-permute-done.5.bm_ref = f32[8,8,384]{2,1,0:T(8,128)S(1)} collective-permute-done((f32[8,8,384]{2,1,0:T(8,128)S(1)}, f32[8,8,384]{2,1,0:T(8,128)S(1)}, u32[]{:S(2)}, u32[]{:S(2)}) %collective-permute-start.5) | collective-permute-done | bytes 98336 | tf_op jit(solution)/shard_map/ppermute | solution.py:416
  39.0 0.0 collective-permute-done.4.am_ref
  39.0 1.5 %collective-permute-done.3.b_ref = f32[24,8,128]{2,1,0:T(8,128)S(1)} collective-permute-done((f32[24,8,128]{2,1,0:T(8,128)S(1)}, f32[24,8,128]{2,1,0:T(8,128)S(1)}, u32[]{:S(2)}, u32[]{:S(2)}) %collective-permute-start.3) | collective-permute-done | bytes 98336 | tf_op jit(solution)/shard_map/ppermute | solution.py:416
  40.5 0.0 collective-permute-done.2.a_ref
  40.5 4.0 %all-to-all-done = f32[64,1,4736]{2,1,0:T(1,128)S(1)} async-done(((f32[64,1,4736]{2,1,0:T(1,128)}), f32[64,1,4736]{2,1,0:T(1,128)S(1)}, u32[]{:S(2)}, u32[]{:S(2)}) %all-to-all-start) | async-done | bytes 1212448 | tf_op jit(solution)/shard_map/all_to_all | solution.py:455
  44.5 0.0 collective-permute-start.6
  44.5 2.9 %collective-permute-done.6.other_ref = f32[2368,128]{1,0:T(8,128)S(1)} collective-permute-done((f32[2368,128]{1,0:T(8,128)S(1)}, f32[2368,128]{1,0:T(8,128)S(1)}, u32[]{:S(2)}, u32[]{:S(2)}) %collective-permute-start.6) | collective-permute-done | bytes 1212448 | tf_op jit(solution)/shard_map/ppermute | solution.py:462
  47.4 10.0 %shard_map.97 = (f32[24,8,128]{2,1,0:T(8,128)S(1)}, f32[24,8,128]{2,1,0:T(8,128)S(1)}, bf16[8,384,1024]{2,1,0:T(8,128)(2,1)}) custom-call(s32[1]{0:T(128)} %bitcast.core, s32[16,128]{1,0:T(8,128)S(1)} %get-tuple-element.26.table, f32[25,8,128]{2,1,0:T(8,128)S(1)} %collective-permute-done.a_ref.ia_ref, f32[25,8,128]{2,1,0:T(8,128)S(1)} %get-tuple-element.27.x_ref.ix_ref, ...), custom_call_target="tpu_custom_call" | custom-call | flops 4000000000 | bytes 20000000 | tf_op jit(solution)/shard_map/pallas_call | solution.py:463
  57.4 1.3 %collective-permute-start.8 = (f32[24,8,128]{2,1,0:T(8,128)S(1)}, f32[24,8,128]{2,1,0:T(8,128)S(1)}, u32[]{:S(2)}, u32[]{:S(2)}) collective-permute-start(f32[24,8,128]{2,1,0:T(8,128)S(1)} %get-tuple-element.37.x_ref), channel_id=1, source_target_pairs={{0,31},{1,2},{2,1},{3,4},{4,3},{5,6},{6,5},{7,8},{8,7},{9,10},{10,... | collective-permute-start | bytes 294920 | tf_op jit(solution)/shard_map/ppermute | solution.py:416
  58.8 0.0 collective-permute-start.7
  58.8 2.8 %collective-permute-done.8.b_ref = f32[24,8,128]{2,1,0:T(8,128)S(1)} collective-permute-done((f32[24,8,128]{2,1,0:T(8,128)S(1)}, f32[24,8,128]{2,1,0:T(8,128)S(1)}, u32[]{:S(2)}, u32[]{:S(2)}) %collective-permute-start.8) | collective-permute-done | bytes 98336 | tf_op jit(solution)/shard_map/ppermute | solution.py:416
  61.5 0.0 collective-permute-done.7.a_ref
  61.5 1.8 %shard_map.98 = (f32[24,8,128]{2,1,0:T(8,128)S(1)}, f32[640,128]{1,0:T(8,128)}) custom-call(s32[16,128]{1,0:T(8,128)S(1)} %get-tuple-element.26.table, f32[24,8,128]{2,1,0:T(8,128)S(1)} %collective-permute-done.7.a_ref, f32[24,8,128]{2,1,0:T(8,128)S(1)} %get-tuple-element.37.x_ref, f32[24,8,128]{2,1,0:T(8,128)S(1)} %collective-permute-done.8.b_ref, ...), custom_call_target="tpu_custom_call" | custom-call | flops 1000000000 | bytes 6000000 | tf_op jit(solution)/shard_map/pallas_call | solution.py:485
  63.4 7.5 %all-to-all-start.1 = ((f32[128,1,640]{2,1,0:T(1,128)}), f32[128,1,640]{2,1,0:T(1,128)S(1)}, u32[]{:S(2)}, u32[]{:S(2)}) async-start(f32[128,1,640]{2,1,0:T(1,128)} %bitcast.3), calls=%async_computation.1 | async-start | bytes 655360 | tf_op jit(solution)/shard_map/all_to_all | solution.py:445
  70.9 2.8 %shard_map.99.x_ref = f32[24,8,128]{2,1,0:T(8,128)S(1)} custom-call(f32[24,8,128]{2,1,0:T(8,128)S(1)} %get-tuple-element.41.x_ref.w0_ref, f32[8,384,384]{2,1,0:T(8,128)} %matrix_ref.5), custom_call_target="tpu_custom_call" | custom-call | flops 1500000000 | bytes 9000000 | tf_op jit(solution)/shard_map/pallas_call | solution.py:448
  73.7 1.7 %collective-permute-start.10 = (f32[24,8,128]{2,1,0:T(8,128)S(1)}, f32[24,8,128]{2,1,0:T(8,128)S(1)}, u32[]{:S(2)}, u32[]{:S(2)}) collective-permute-start(f32[24,8,128]{2,1,0:T(8,128)S(1)} %shard_map.99.x_ref), channel_id=1, source_target_pairs={{0,31},{1,2},{2,1},{3,4},{4,3},{5,6},{6,5},{7,8},{8,7},{9,10},{10,... | collective-permute-start | bytes 294920 | tf_op jit(solution)/shard_map/ppermute | solution.py:416
  75.4 3.6 %collective-permute-start.9 = (f32[24,8,128]{2,1,0:T(8,128)S(1)}, f32[24,8,128]{2,1,0:T(8,128)S(1)}, u32[]{:S(2)}, u32[]{:S(2)}) collective-permute-start(f32[24,8,128]{2,1,0:T(8,128)S(1)} %shard_map.99.x_ref), channel_id=1, source_target_pairs={{0,1},{1,0},{2,3},{3,2},{4,5},{5,4},{6,7},{7,6},{8,9},{9,8},{10,11... | collective-permute-start | bytes 294920 | tf_op jit(solution)/shard_map/ppermute | solution.py:416
  79.0 0.0 collective-permute-done.10.b_ref
  79.0 0.9 collective-permute-done.9.a_ref
  79.9 2.6 %all-to-all-done.1 = f32[128,1,640]{2,1,0:T(1,128)S(1)} async-done(((f32[128,1,640]{2,1,0:T(1,128)}), f32[128,1,640]{2,1,0:T(1,128)S(1)}, u32[]{:S(2)}, u32[]{:S(2)}) %all-to-all-start.1) | async-done | bytes 327712 | tf_op jit(solution)/shard_map/all_to_all | solution.py:445
  82.5 8.6 %shard_map.100 = (f32[24,8,128]{2,1,0:T(8,128)S(1)}, f32[24,8,128]{2,1,0:T(8,128)S(1)}, f32[24,8,128]{2,1,0:T(8,128)S(1)}, f32[3,8,128]{2,1,0:T(8,128)S(1)}, f32[24,8,128]{2,1,0:T(8,128)S(1)}) custom-call(s32[16,128]{1,0:T(8,128)S(1)} %get-tuple-element.26.table, f32[640,128]{1,0:T(8,128)S(1)} %bitcast.7, ...), custom_call_target="tpu_custom_call" | custom-call | flops 3000000000 | bytes 18000000 | tf_op jit(solution)/shard_map/pallas_call | solution.py:490
  91.1 1.1 collective-permute-start.12
  92.2 2.8 %collective-permute-start.11 = (f32[24,8,128]{2,1,0:T(8,128)S(1)}, f32[24,8,128]{2,1,0:T(8,128)S(1)}, u32[]{:S(2)}, u32[]{:S(2)}) collective-permute-start(f32[24,8,128]{2,1,0:T(8,128)S(1)} %get-tuple-element.42.x_ref), channel_id=1, source_target_pairs={{0,1},{1,0},{2,3},{3,2},{4,5},{5,4},{6,7},{7,6},{8,9},{9,8},{10,11... | collective-permute-start | bytes 294920 | tf_op jit(solution)/shard_map/ppermute | solution.py:416
  95.0 0.2 collective-permute-done.12.b_ref
  95.2 0.7 collective-permute-done.11.a_ref
  96.0 1.8 %shard_map.101 = (f32[24,8,128]{2,1,0:T(8,128)S(1)}, f32[640,128]{1,0:T(8,128)}) custom-call(s32[16,128]{1,0:T(8,128)S(1)} %get-tuple-element.26.table, f32[24,8,128]{2,1,0:T(8,128)S(1)} %collective-permute-done.11.a_ref, f32[24,8,128]{2,1,0:T(8,128)S(1)} %get-tuple-element.42.x_ref, f32[24,8,128]{2,1,0:T(8,128)S(1)} %collective-permute-done.12.b_ref, ...), custom_call_target="tpu_custom_call" | custom-call | flops 1000000000 | bytes 6000000 | tf_op jit(solution)/shard_map/pallas_call | solution.py:498
  97.8 10.2 %all-to-all-start.2 = ((f32[128,1,640]{2,1,0:T(1,128)}), f32[128,1,640]{2,1,0:T(1,128)S(1)}, u32[]{:S(2)}, u32[]{:S(2)}) async-start(f32[128,1,640]{2,1,0:T(1,128)} %bitcast.5), calls=%async_computation.2 | async-start | bytes 655360 | tf_op jit(solution)/shard_map/all_to_all | solution.py:445
  108.0 2.8 %shard_map.102.x_ref = f32[24,8,128]{2,1,0:T(8,128)S(1)} custom-call(f32[24,8,128]{2,1,0:T(8,128)S(1)} %get-tuple-element.46.x_ref.v1_ref, f32[8,384,384]{2,1,0:T(8,128)} %matrix_ref.5), custom_call_target="tpu_custom_call" | custom-call | flops 1500000000 | bytes 9000000 | tf_op jit(solution)/shard_map/pallas_call | solution.py:448
  110.8 1.7 %collective-permute-start.14 = (f32[24,8,128]{2,1,0:T(8,128)S(1)}, f32[24,8,128]{2,1,0:T(8,128)S(1)}, u32[]{:S(2)}, u32[]{:S(2)}) collective-permute-start(f32[24,8,128]{2,1,0:T(8,128)S(1)} %shard_map.102.x_ref), channel_id=1, source_target_pairs={{0,31},{1,2},{2,1},{3,4},{4,3},{5,6},{6,5},{7,8},{8,7},{9,10},{10,... | collective-permute-start | bytes 294920 | tf_op jit(solution)/shard_map/ppermute | solution.py:416
  112.5 3.6 %collective-permute-start.13 = (f32[24,8,128]{2,1,0:T(8,128)S(1)}, f32[24,8,128]{2,1,0:T(8,128)S(1)}, u32[]{:S(2)}, u32[]{:S(2)}) collective-permute-start(f32[24,8,128]{2,1,0:T(8,128)S(1)} %shard_map.102.x_ref), channel_id=1, source_target_pairs={{0,1},{1,0},{2,3},{3,2},{4,5},{5,4},{6,7},{7,6},{8,9},{9,8},{10,11... | collective-permute-start | bytes 294920 | tf_op jit(solution)/shard_map/ppermute | solution.py:416
  116.1 0.0 collective-permute-done.14.b_ref
  116.1 0.9 collective-permute-done.13.a_ref
  117.0 2.6 %all-to-all-done.2 = f32[128,1,640]{2,1,0:T(1,128)S(1)} async-done(((f32[128,1,640]{2,1,0:T(1,128)}), f32[128,1,640]{2,1,0:T(1,128)S(1)}, u32[]{:S(2)}, u32[]{:S(2)}) %all-to-all-start.2) | async-done | bytes 327712 | tf_op jit(solution)/shard_map/all_to_all | solution.py:445
  119.6 6.8 %shard_map.103 = (f32[8,8,384]{2,1,0:T(8,128)}, f32[8,8,384]{2,1,0:T(8,128)}, f32[8,8,384]{2,1,0:T(8,128)}) custom-call(s32[16,128]{1,0:T(8,128)S(1)} %get-tuple-element.26.table, f32[640,128]{1,0:T(8,128)S(1)} %bitcast.10, bf16[8,384,1024]{2,1,0:T(8,128)(2,1)} %get-tuple-element.40.weights_ref, f32[8,8,384]{2,1,0:T(8,128)S(1)} %collective-permute-done.4.am_ref, ...), custom_call_target="tpu_custom_call" | custom-call | flops 2500000000 | bytes 15000000 | tf_op jit(solution)/shard_map/pallas_call | solution.py:504
  (2 shorter events, 0.0 us)
Async XLA Ops:
  0.6 10.1 %copy-start = (f32[8,8,384]{2,1,0:T(8,128)S(1)}, f32[8,8,384]{2,1,0:T(8,128)}, u32[]{:S(2)}) copy-start(f32[8,8,384]{2,1,0:T(8,128)} %m_ref.2) | copy-start | bytes 294916
  0.6 10.1 %copy-start.1 = (f32[64,64]{1,0:T(8,128)S(1)}, f32[64,64]{1,0:T(8,128)}, u32[]{:S(2)}) copy-start(f32[64,64]{1,0:T(8,128)} %inverse_ref.5) | copy-start | bytes 49156
  3.6 6.2 %collective-permute-start.1 = (f32[25,8,128]{2,1,0:T(8,128)S(1)}, f32[25,8,128]{2,1,0:T(8,128)S(1)}, u32[]{:S(2)}, u32[]{:S(2)}) collective-permute-start(f32[25,8,128]{2,1,0:T(8,128)S(1)} %get-tuple-element.27.x_ref.ix_ref), channel_id=1, source_target_pairs={{0,31},{1,2},{2,1},{3,4},{4,3},{5,6},{6,5},{7,8},{8,7},{9,10},{10,... | collective-permute-start | bytes 307208 | tf_op jit(solution)/shard_map/ppermute | solution.py:416
  6.3 4.5 %collective-permute-start = (f32[25,8,128]{2,1,0:T(8,128)S(1)}, f32[25,8,128]{2,1,0:T(8,128)S(1)}, u32[]{:S(2)}, u32[]{:S(2)}) collective-permute-start(f32[25,8,128]{2,1,0:T(8,128)S(1)} %get-tuple-element.27.x_ref.ix_ref), channel_id=1, source_target_pairs={{0,1},{1,0},{2,3},{3,2},{4,5},{5,4},{6,7},{7,6},{8,9},{9,8},{10,11... | collective-permute-start | bytes 307208 | tf_op jit(solution)/shard_map/ppermute | solution.py:416
  12.9 31.6 %all-to-all-start = ((f32[64,1,4736]{2,1,0:T(1,128)}), f32[64,1,4736]{2,1,0:T(1,128)S(1)}, u32[]{:S(2)}, u32[]{:S(2)}) async-start(f32[64,1,4736]{2,1,0:T(1,128)} %bitcast.1), calls=%async_computation | async-start | bytes 2424832 | tf_op jit(solution)/shard_map/all_to_all | solution.py:455
  24.8 14.2 %collective-permute-start.5 = (f32[8,8,384]{2,1,0:T(8,128)S(1)}, f32[8,8,384]{2,1,0:T(8,128)S(1)}, u32[]{:S(2)}, u32[]{:S(2)}) collective-permute-start(f32[8,8,384]{2,1,0:T(8,128)S(1)} %copy-done), channel_id=1, source_target_pairs={{0,31},{1,2},{2,1},{3,4},{4,3},{5,6},{6,5},{7,8},{8,7},{9,10},{10,... | collective-permute-start | bytes 294920 | tf_op jit(solution)/shard_map/ppermute | solution.py:416
  24.8 14.1 %collective-permute-start.4 = (f32[8,8,384]{2,1,0:T(8,128)S(1)}, f32[8,8,384]{2,1,0:T(8,128)S(1)}, u32[]{:S(2)}, u32[]{:S(2)}) collective-permute-start(f32[8,8,384]{2,1,0:T(8,128)S(1)} %copy-done), channel_id=1, source_target_pairs={{0,1},{1,0},{2,3},{3,2},{4,5},{5,4},{6,7},{7,6},{8,9},{9,8},{10,11... | collective-permute-start | bytes 294920 | tf_op jit(solution)/shard_map/ppermute | solution.py:416
  32.4 8.1 %collective-permute-start.3 = (f32[24,8,128]{2,1,0:T(8,128)S(1)}, f32[24,8,128]{2,1,0:T(8,128)S(1)}, u32[]{:S(2)}, u32[]{:S(2)}) collective-permute-start(f32[24,8,128]{2,1,0:T(8,128)S(1)} %shard_map.96.x_ref), channel_id=1, source_target_pairs={{0,31},{1,2},{2,1},{3,4},{4,3},{5,6},{6,5},{7,8},{8,7},{9,10},{10,... | collective-permute-start | bytes 294920 | tf_op jit(solution)/shard_map/ppermute | solution.py:416
  32.4 8.1 %collective-permute-start.2 = (f32[24,8,128]{2,1,0:T(8,128)S(1)}, f32[24,8,128]{2,1,0:T(8,128)S(1)}, u32[]{:S(2)}, u32[]{:S(2)}) collective-permute-start(f32[24,8,128]{2,1,0:T(8,128)S(1)} %shard_map.96.x_ref), channel_id=1, source_target_pairs={{0,1},{1,0},{2,3},{3,2},{4,5},{5,4},{6,7},{7,6},{8,9},{9,8},{10,11... | collective-permute-start | bytes 294920 | tf_op jit(solution)/shard_map/ppermute | solution.py:416
  44.5 2.9 %collective-permute-start.6 = (f32[2368,128]{1,0:T(8,128)S(1)}, f32[2368,128]{1,0:T(8,128)S(1)}, u32[]{:S(2)}, u32[]{:S(2)}) collective-permute-start(f32[2368,128]{1,0:T(8,128)S(1)} %bitcast.8), channel_id=1, source_target_pairs={{0,1},{1,0},{2,3},{3,2},{4,5},{5,4},{6,7},{7,6},{8,9},{9,8},{10,11... | collective-permute-start | bytes 3637256 | tf_op jit(solution)/shard_map/ppermute | solution.py:462
  57.4 4.1 %collective-permute-start.8 = (f32[24,8,128]{2,1,0:T(8,128)S(1)}, f32[24,8,128]{2,1,0:T(8,128)S(1)}, u32[]{:S(2)}, u32[]{:S(2)}) collective-permute-start(f32[24,8,128]{2,1,0:T(8,128)S(1)} %get-tuple-element.37.x_ref), channel_id=1, source_target_pairs={{0,31},{1,2},{2,1},{3,4},{4,3},{5,6},{6,5},{7,8},{8,7},{9,10},{10,... | collective-permute-start | bytes 294920 | tf_op jit(solution)/shard_map/ppermute | solution.py:416
  58.8 2.8 %collective-permute-start.7 = (f32[24,8,128]{2,1,0:T(8,128)S(1)}, f32[24,8,128]{2,1,0:T(8,128)S(1)}, u32[]{:S(2)}, u32[]{:S(2)}) collective-permute-start(f32[24,8,128]{2,1,0:T(8,128)S(1)} %get-tuple-element.37.x_ref), channel_id=1, source_target_pairs={{0,1},{1,0},{2,3},{3,2},{4,5},{5,4},{6,7},{7,6},{8,9},{9,8},{10,11... | collective-permute-start | bytes 294920 | tf_op jit(solution)/shard_map/ppermute | solution.py:416
  63.4 19.2 %all-to-all-start.1 = ((f32[128,1,640]{2,1,0:T(1,128)}), f32[128,1,640]{2,1,0:T(1,128)S(1)}, u32[]{:S(2)}, u32[]{:S(2)}) async-start(f32[128,1,640]{2,1,0:T(1,128)} %bitcast.3), calls=%async_computation.1 | async-start | bytes 655360 | tf_op jit(solution)/shard_map/all_to_all | solution.py:445
  73.7 5.3 %collective-permute-start.10 = (f32[24,8,128]{2,1,0:T(8,128)S(1)}, f32[24,8,128]{2,1,0:T(8,128)S(1)}, u32[]{:S(2)}, u32[]{:S(2)}) collective-permute-start(f32[24,8,128]{2,1,0:T(8,128)S(1)} %shard_map.99.x_ref), channel_id=1, source_target_pairs={{0,31},{1,2},{2,1},{3,4},{4,3},{5,6},{6,5},{7,8},{8,7},{9,10},{10,... | collective-permute-start | bytes 294920 | tf_op jit(solution)/shard_map/ppermute | solution.py:416
  75.4 4.5 %collective-permute-start.9 = (f32[24,8,128]{2,1,0:T(8,128)S(1)}, f32[24,8,128]{2,1,0:T(8,128)S(1)}, u32[]{:S(2)}, u32[]{:S(2)}) collective-permute-start(f32[24,8,128]{2,1,0:T(8,128)S(1)} %shard_map.99.x_ref), channel_id=1, source_target_pairs={{0,1},{1,0},{2,3},{3,2},{4,5},{5,4},{6,7},{7,6},{8,9},{9,8},{10,11... | collective-permute-start | bytes 294920 | tf_op jit(solution)/shard_map/ppermute | solution.py:416
  91.1 4.1 %collective-permute-start.12 = (f32[24,8,128]{2,1,0:T(8,128)S(1)}, f32[24,8,128]{2,1,0:T(8,128)S(1)}, u32[]{:S(2)}, u32[]{:S(2)}) collective-permute-start(f32[24,8,128]{2,1,0:T(8,128)S(1)} %get-tuple-element.42.x_ref), channel_id=1, source_target_pairs={{0,31},{1,2},{2,1},{3,4},{4,3},{5,6},{6,5},{7,8},{8,7},{9,10},{10,... | collective-permute-start | bytes 294920 | tf_op jit(solution)/shard_map/ppermute | solution.py:416
  92.2 3.7 %collective-permute-start.11 = (f32[24,8,128]{2,1,0:T(8,128)S(1)}, f32[24,8,128]{2,1,0:T(8,128)S(1)}, u32[]{:S(2)}, u32[]{:S(2)}) collective-permute-start(f32[24,8,128]{2,1,0:T(8,128)S(1)} %get-tuple-element.42.x_ref), channel_id=1, source_target_pairs={{0,1},{1,0},{2,3},{3,2},{4,5},{5,4},{6,7},{7,6},{8,9},{9,8},{10,11... | collective-permute-start | bytes 294920 | tf_op jit(solution)/shard_map/ppermute | solution.py:416
  97.8 21.9 %all-to-all-start.2 = ((f32[128,1,640]{2,1,0:T(1,128)}), f32[128,1,640]{2,1,0:T(1,128)S(1)}, u32[]{:S(2)}, u32[]{:S(2)}) async-start(f32[128,1,640]{2,1,0:T(1,128)} %bitcast.5), calls=%async_computation.2 | async-start | bytes 655360 | tf_op jit(solution)/shard_map/all_to_all | solution.py:445
  110.8 5.3 %collective-permute-start.14 = (f32[24,8,128]{2,1,0:T(8,128)S(1)}, f32[24,8,128]{2,1,0:T(8,128)S(1)}, u32[]{:S(2)}, u32[]{:S(2)}) collective-permute-start(f32[24,8,128]{2,1,0:T(8,128)S(1)} %shard_map.102.x_ref), channel_id=1, source_target_pairs={{0,31},{1,2},{2,1},{3,4},{4,3},{5,6},{6,5},{7,8},{8,7},{9,10},{10,... | collective-permute-start | bytes 294920 | tf_op jit(solution)/shard_map/ppermute | solution.py:416
  112.5 4.5 %collective-permute-start.13 = (f32[24,8,128]{2,1,0:T(8,128)S(1)}, f32[24,8,128]{2,1,0:T(8,128)S(1)}, u32[]{:S(2)}, u32[]{:S(2)}) collective-permute-start(f32[24,8,128]{2,1,0:T(8,128)S(1)} %shard_map.102.x_ref), channel_id=1, source_target_pairs={{0,1},{1,0},{2,3},{3,2},{4,5},{5,4},{6,7},{7,6},{8,9},{9,8},{10,11... | collective-permute-start | bytes 294920 | tf_op jit(solution)/shard_map/ppermute | solution.py:416

commit v5 on v4

--- a/solution.py
+++ b/solution.py
@@ -438,7 +438,10 @@
         ],
         us=4,
     )(core, in_hbm(loads), in_hbm(corner_index), in_hbm(partner), inverse)
+    ma, mb = both(corner_map)
+    maps = (ma, corner_map, mb)
     ua, ub = both(u)
+    maps, ua, ub = lax.optimization_barrier((maps, ua, ub))
     indices = (ua, u, ub)
 
     def spread(x):
@@ -456,9 +459,7 @@
         card.reshape(devices // 2, -1), GT, 0, 0, tiled=True, axis_index_groups=same_core
     ).reshape(-1, 128)
     pooled = through(r0)
-    ma, mb = both(corner_map)
-    maps = (ma, corner_map, mb)
-    own_cards, pooled, maps = lax.optimization_barrier((own_cards, pooled, maps))
+    own_cards, pooled = lax.optimization_barrier((own_cards, pooled))
     other_cards = lax.ppermute(own_cards, "tile", inner_swap)
     z0, u, weights = pl.pallas_call(
         solve_first_kernel,

time: 127 us -> 129 us (1.016)
  waiting for transfers between devices: 25.8 us -> 30 us
  starting transfers between devices: 57.5 us -> 55.7 us
    ppermute x7, waiting for transfers between devices: 10.1 us -> 15.1 us  [both(): lax.ppermute(x, 'tile', outer_swap)]
    all_to_all x1, starting transfers between devices: 11.8 us -> 9.78 us  [shards(): lax.all_to_all(card.reshape(devices // 2, -1), GT, 0, 0, tiled=True, axis...]
  transfers between devices with their start and end apart: 18 -> 18, of which waited for: 12 -> 11; matrix products, arithmetic and copies ran while one was open for 0% -> 0% of each run, Pallas kernels for 7% -> 6%
where the time goes in v5:
time: 129 us
  starting transfers between devices  55.7 us (43%)
  Pallas kernels  42.3 us (33%)
  waiting for transfers between devices  30 us (23%)
    ppermute x7, starting transfers between devices, both(): lax.ppermute(x, 'tile', inner_swap)  18.6 us
    all_to_all x2, starting transfers between devices, spread(): lax.all_to_all(x.reshape(devices, -1), GT, 0, 0, tiled=True)  17.3 us
    ppermute x7, waiting for transfers between devices, both(): lax.ppermute(x, 'tile', outer_swap)  15.1 us
    pallas_call x1, Pallas kernels, shards(): pl.pallas_call(solve_first_kernel, in_specs=[SMEM] * 2 + [ANY] * 3 + [VME...  9.97 us
    all_to_all x1, starting transfers between devices, shards(): lax.all_to_all(card.reshape(devices // 2, -1), GT, 0, 0, tiled=True, axis...  9.78 us
    ppermute x7, starting transfers between devices, both(): lax.ppermute(x, 'tile', outer_swap)  8.82 us
    pallas_call x1, Pallas kernels, shards(): call(solve_second_kernel, [field, field, field, shape(3, 8, 128), field],...  8.55 us
    pallas_call x3, Pallas kernels, through(): call(product_kernel, [field], [VMEM, ANY], [held, sems], us=3)(x, stiff)  8.34 us
  transfers between devices with their start and end apart: 18, of which 11 were waited for; matrix products, arithmetic and copies ran while one was open for 0% of the time, Pallas kernels for 6%

profile of v5, /device:TPU:1, one launch (start us, length us, event | category | flops | bytes accessed | tf_op | source)
XLA Modules:
  0.0 128.9 jit_solution(3164843771584129766)
XLA Ops:
  0.6 0.0 copy-start
  0.6 0.0 copy-start.1
  0.7 2.9 %shard_map.94 = (f32[25,8,128]{2,1,0:T(8,128)S(1)}, s32[16,128]{1,0:T(8,128)S(1)}) custom-call(s32[1]{0:T(128)} %bitcast.core, f32[8,8,384]{2,1,0:T(8,128)} %loads_ref.1, s32[8,8]{1,0:T(8,128)} %index_ref.1, s32[8,12]{1,0:T(8,128)} %partner_ref.1, f32[8,384,384]{2,1,0:T(8,128)} %inverse_ref.7), custom_call_target="tpu_custom_call" | custom-call | flops 2000000000 | bytes 12000000 | tf_op jit(solution)/shard_map/pallas_call | solution.py:428
  3.6 2.7 %collective-permute-start.3 = (f32[25,8,128]{2,1,0:T(8,128)S(1)}, f32[25,8,128]{2,1,0:T(8,128)S(1)}, u32[]{:S(2)}, u32[]{:S(2)}) collective-permute-start(f32[25,8,128]{2,1,0:T(8,128)S(1)} %get-tuple-element.29.x_ref.ix_ref), channel_id=1, source_target_pairs={{0,31},{1,2},{2,1},{3,4},{4,3},{5,6},{6,5},{7,8},{8,7},{9,10},{10,... | collective-permute-start | bytes 307208 | tf_op jit(solution)/shard_map/ppermute | solution.py:416
  6.3 3.6 %collective-permute-start.2 = (f32[25,8,128]{2,1,0:T(8,128)S(1)}, f32[25,8,128]{2,1,0:T(8,128)S(1)}, u32[]{:S(2)}, u32[]{:S(2)}) collective-permute-start(f32[25,8,128]{2,1,0:T(8,128)S(1)} %get-tuple-element.29.x_ref.ix_ref), channel_id=1, source_target_pairs={{0,1},{1,0},{2,3},{3,2},{4,5},{5,4},{6,7},{7,6},{8,9},{9,8},{10,11... | collective-permute-start | bytes 307208 | tf_op jit(solution)/shard_map/ppermute | solution.py:416
  9.8 0.0 collective-permute-start.1
  9.8 0.9 collective-permute-start
  10.8 3.1 %collective-permute-done.1.bm_ref = f32[8,8,384]{2,1,0:T(8,128)S(1)} collective-permute-done((f32[8,8,384]{2,1,0:T(8,128)S(1)}, f32[8,8,384]{2,1,0:T(8,128)S(1)}, u32[]{:S(2)}, u32[]{:S(2)}) %collective-permute-start.1) | collective-permute-done | bytes 98336 | tf_op jit(solution)/shard_map/ppermute | solution.py:416
  13.9 0.0 collective-permute-done.am_ref
  13.9 0.0 collective-permute-done.3.b_ref.ib_ref
  13.9 0.0 collective-permute-done.2.a_ref.ia_ref
  13.9 2.1 %shard_map.95 = (f32[24,8,128]{2,1,0:T(8,128)S(1)}, f32[2368,128]{1,0:T(8,128)}) custom-call(s32[16,128]{1,0:T(8,128)S(1)} %get-tuple-element.28.table, f32[25,8,128]{2,1,0:T(8,128)S(1)} %collective-permute-done.2.a_ref.ia_ref, f32[25,8,128]{2,1,0:T(8,128)S(1)} %get-tuple-element.29.x_ref.ix_ref, f32[25,8,128]{2,1,0:T(8,128)S(1)} %collective-permute-done.3.b_ref.ib_ref, ...), custom_call_target="tpu_custom_call" | custom-call | flops 1000000000 | bytes 6000000 | tf_op jit(solution)/shard_map/pallas_call | solution.py:455
  16.0 9.8 %all-to-all-start = ((f32[64,1,4736]{2,1,0:T(1,128)}), f32[64,1,4736]{2,1,0:T(1,128)S(1)}, u32[]{:S(2)}, u32[]{:S(2)}) async-start(f32[64,1,4736]{2,1,0:T(1,128)} %bitcast.1), calls=%async_computation | async-start | bytes 2424832 | tf_op jit(solution)/shard_map/all_to_all | solution.py:458
  25.8 2.8 %shard_map.96.x_ref = f32[24,8,128]{2,1,0:T(8,128)S(1)} custom-call(f32[24,8,128]{2,1,0:T(8,128)S(1)} %get-tuple-element.33.x_ref.r0_ref, f32[8,384,384]{2,1,0:T(8,128)} %matrix_ref.5), custom_call_target="tpu_custom_call" | custom-call | flops 1500000000 | bytes 9000000 | tf_op jit(solution)/shard_map/pallas_call | solution.py:451
  28.6 1.1 collective-permute-start.5
  29.7 3.7 %collective-permute-start.4 = (f32[24,8,128]{2,1,0:T(8,128)S(1)}, f32[24,8,128]{2,1,0:T(8,128)S(1)}, u32[]{:S(2)}, u32[]{:S(2)}) collective-permute-start(f32[24,8,128]{2,1,0:T(8,128)S(1)} %shard_map.96.x_ref), channel_id=1, source_target_pairs={{0,1},{1,0},{2,3},{3,2},{4,5},{5,4},{6,7},{7,6},{8,9},{9,8},{10,11... | collective-permute-start | bytes 294920 | tf_op jit(solution)/shard_map/ppermute | solution.py:416
  33.4 8.5 %collective-permute-done.5.b_ref = f32[24,8,128]{2,1,0:T(8,128)S(1)} collective-permute-done((f32[24,8,128]{2,1,0:T(8,128)S(1)}, f32[24,8,128]{2,1,0:T(8,128)S(1)}, u32[]{:S(2)}, u32[]{:S(2)}) %collective-permute-start.5) | collective-permute-done | bytes 98336 | tf_op jit(solution)/shard_map/ppermute | solution.py:416
  42.0 0.0 collective-permute-done.4.a_ref
  42.0 4.5 %all-to-all-done = f32[64,1,4736]{2,1,0:T(1,128)S(1)} async-done(((f32[64,1,4736]{2,1,0:T(1,128)}), f32[64,1,4736]{2,1,0:T(1,128)S(1)}, u32[]{:S(2)}, u32[]{:S(2)}) %all-to-all-start) | async-done | bytes 1212448 | tf_op jit(solution)/shard_map/all_to_all | solution.py:458
  46.5 1.1 collective-permute-start.6
  47.6 2.5 %collective-permute-done.6.other_ref = f32[2368,128]{1,0:T(8,128)S(1)} collective-permute-done((f32[2368,128]{1,0:T(8,128)S(1)}, f32[2368,128]{1,0:T(8,128)S(1)}, u32[]{:S(2)}, u32[]{:S(2)}) %collective-permute-start.6) | collective-permute-done | bytes 1212448 | tf_op jit(solution)/shard_map/ppermute | solution.py:463
  50.1 10.0 %shard_map.97 = (f32[24,8,128]{2,1,0:T(8,128)S(1)}, f32[24,8,128]{2,1,0:T(8,128)S(1)}, bf16[8,384,1024]{2,1,0:T(8,128)(2,1)}) custom-call(s32[1]{0:T(128)} %bitcast.core, s32[16,128]{1,0:T(8,128)S(1)} %get-tuple-element.28.table, f32[25,8,128]{2,1,0:T(8,128)S(1)} %collective-permute-done.2.a_ref.ia_ref, f32[25,8,128]{2,1,0:T(8,128)S(1)} %get-tuple-element.29.x_ref.ix_ref, ...), custom_call_target="tpu_custom_call" | custom-call | flops 4000000000 | bytes 20000000 | tf_op jit(solution)/shard_map/pallas_call | solution.py:464
  60.1 0.4 collective-permute-start.8
  60.5 0.4 collective-permute-start.7
  60.9 3.3 %collective-permute-done.8.b_ref = f32[24,8,128]{2,1,0:T(8,128)S(1)} collective-permute-done((f32[24,8,128]{2,1,0:T(8,128)S(1)}, f32[24,8,128]{2,1,0:T(8,128)S(1)}, u32[]{:S(2)}, u32[]{:S(2)}) %collective-permute-start.8) | collective-permute-done | bytes 98336 | tf_op jit(solution)/shard_map/ppermute | solution.py:416
  64.2 0.0 collective-permute-done.7.a_ref
  64.2 1.8 %shard_map.98 = (f32[24,8,128]{2,1,0:T(8,128)S(1)}, f32[640,128]{1,0:T(8,128)}) custom-call(s32[16,128]{1,0:T(8,128)S(1)} %get-tuple-element.28.table, f32[24,8,128]{2,1,0:T(8,128)S(1)} %collective-permute-done.7.a_ref, f32[24,8,128]{2,1,0:T(8,128)S(1)} %get-tuple-element.41.x_ref, f32[24,8,128]{2,1,0:T(8,128)S(1)} %collective-permute-done.8.b_ref, ...), custom_call_target="tpu_custom_call" | custom-call | flops 1000000000 | bytes 6000000 | tf_op jit(solution)/shard_map/pallas_call | solution.py:486
  66.0 7.1 %all-to-all-start.1 = ((f32[128,1,640]{2,1,0:T(1,128)}), f32[128,1,640]{2,1,0:T(1,128)S(1)}, u32[]{:S(2)}, u32[]{:S(2)}) async-start(f32[128,1,640]{2,1,0:T(1,128)} %bitcast.3), calls=%async_computation.1 | async-start | bytes 655360 | tf_op jit(solution)/shard_map/all_to_all | solution.py:448
  73.2 2.8 %shard_map.99.x_ref = f32[24,8,128]{2,1,0:T(8,128)S(1)} custom-call(f32[24,8,128]{2,1,0:T(8,128)S(1)} %get-tuple-element.45.x_ref.w0_ref, f32[8,384,384]{2,1,0:T(8,128)} %matrix_ref.5), custom_call_target="tpu_custom_call" | custom-call | flops 1500000000 | bytes 9000000 | tf_op jit(solution)/shard_map/pallas_call | solution.py:451
  75.9 1.7 %collective-permute-start.10 = (f32[24,8,128]{2,1,0:T(8,128)S(1)}, f32[24,8,128]{2,1,0:T(8,128)S(1)}, u32[]{:S(2)}, u32[]{:S(2)}) collective-permute-start(f32[24,8,128]{2,1,0:T(8,128)S(1)} %shard_map.99.x_ref), channel_id=1, source_target_pairs={{0,31},{1,2},{2,1},{3,4},{4,3},{5,6},{6,5},{7,8},{8,7},{9,10},{10,... | collective-permute-start | bytes 294920 | tf_op jit(solution)/shard_map/ppermute | solution.py:416
  77.7 3.7 %collective-permute-start.9 = (f32[24,8,128]{2,1,0:T(8,128)S(1)}, f32[24,8,128]{2,1,0:T(8,128)S(1)}, u32[]{:S(2)}, u32[]{:S(2)}) collective-permute-start(f32[24,8,128]{2,1,0:T(8,128)S(1)} %shard_map.99.x_ref), channel_id=1, source_target_pairs={{0,1},{1,0},{2,3},{3,2},{4,5},{5,4},{6,7},{7,6},{8,9},{9,8},{10,11... | collective-permute-start | bytes 294920 | tf_op jit(solution)/shard_map/ppermute | solution.py:416
  81.4 0.0 collective-permute-done.10.b_ref
  81.4 0.9 collective-permute-done.9.a_ref
  82.3 2.6 %all-to-all-done.1 = f32[128,1,640]{2,1,0:T(1,128)S(1)} async-done(((f32[128,1,640]{2,1,0:T(1,128)}), f32[128,1,640]{2,1,0:T(1,128)S(1)}, u32[]{:S(2)}, u32[]{:S(2)}) %all-to-all-start.1) | async-done | bytes 327712 | tf_op jit(solution)/shard_map/all_to_all | solution.py:448
  84.9 8.6 %shard_map.100 = (f32[24,8,128]{2,1,0:T(8,128)S(1)}, f32[24,8,128]{2,1,0:T(8,128)S(1)}, f32[24,8,128]{2,1,0:T(8,128)S(1)}, f32[3,8,128]{2,1,0:T(8,128)S(1)}, f32[24,8,128]{2,1,0:T(8,128)S(1)}) custom-call(s32[16,128]{1,0:T(8,128)S(1)} %get-tuple-element.28.table, f32[640,128]{1,0:T(8,128)S(1)} %bitcast.7, ...), custom_call_target="tpu_custom_call" | custom-call | flops 3000000000 | bytes 18000000 | tf_op jit(solution)/shard_map/pallas_call | solution.py:491
  93.5 1.1 collective-permute-start.12
  94.6 2.8 %collective-permute-start.11 = (f32[24,8,128]{2,1,0:T(8,128)S(1)}, f32[24,8,128]{2,1,0:T(8,128)S(1)}, u32[]{:S(2)}, u32[]{:S(2)}) collective-permute-start(f32[24,8,128]{2,1,0:T(8,128)S(1)} %get-tuple-element.46.x_ref), channel_id=1, source_target_pairs={{0,1},{1,0},{2,3},{3,2},{4,5},{5,4},{6,7},{7,6},{8,9},{9,8},{10,11... | collective-permute-start | bytes 294920 | tf_op jit(solution)/shard_map/ppermute | solution.py:416
  97.4 0.2 collective-permute-done.12.b_ref
  97.6 0.7 collective-permute-done.11.a_ref
  98.3 1.8 %shard_map.101 = (f32[24,8,128]{2,1,0:T(8,128)S(1)}, f32[640,128]{1,0:T(8,128)}) custom-call(s32[16,128]{1,0:T(8,128)S(1)} %get-tuple-element.28.table, f32[24,8,128]{2,1,0:T(8,128)S(1)} %collective-permute-done.11.a_ref, f32[24,8,128]{2,1,0:T(8,128)S(1)} %get-tuple-element.46.x_ref, f32[24,8,128]{2,1,0:T(8,128)S(1)} %collective-permute-done.12.b_ref, ...), custom_call_target="tpu_custom_call" | custom-call | flops 1000000000 | bytes 6000000 | tf_op jit(solution)/shard_map/pallas_call | solution.py:499
  100.1 10.2 %all-to-all-start.2 = ((f32[128,1,640]{2,1,0:T(1,128)}), f32[128,1,640]{2,1,0:T(1,128)S(1)}, u32[]{:S(2)}, u32[]{:S(2)}) async-start(f32[128,1,640]{2,1,0:T(1,128)} %bitcast.5), calls=%async_computation.2 | async-start | bytes 655360 | tf_op jit(solution)/shard_map/all_to_all | solution.py:448
  110.4 2.8 %shard_map.102.x_ref = f32[24,8,128]{2,1,0:T(8,128)S(1)} custom-call(f32[24,8,128]{2,1,0:T(8,128)S(1)} %get-tuple-element.50.x_ref.v1_ref, f32[8,384,384]{2,1,0:T(8,128)} %matrix_ref.5), custom_call_target="tpu_custom_call" | custom-call | flops 1500000000 | bytes 9000000 | tf_op jit(solution)/shard_map/pallas_call | solution.py:451
  113.2 1.7 %collective-permute-start.14 = (f32[24,8,128]{2,1,0:T(8,128)S(1)}, f32[24,8,128]{2,1,0:T(8,128)S(1)}, u32[]{:S(2)}, u32[]{:S(2)}) collective-permute-start(f32[24,8,128]{2,1,0:T(8,128)S(1)} %shard_map.102.x_ref), channel_id=1, source_target_pairs={{0,31},{1,2},{2,1},{3,4},{4,3},{5,6},{6,5},{7,8},{8,7},{9,10},{10,... | collective-permute-start | bytes 294920 | tf_op jit(solution)/shard_map/ppermute | solution.py:416
  114.9 3.6 %collective-permute-start.13 = (f32[24,8,128]{2,1,0:T(8,128)S(1)}, f32[24,8,128]{2,1,0:T(8,128)S(1)}, u32[]{:S(2)}, u32[]{:S(2)}) collective-permute-start(f32[24,8,128]{2,1,0:T(8,128)S(1)} %shard_map.102.x_ref), channel_id=1, source_target_pairs={{0,1},{1,0},{2,3},{3,2},{4,5},{5,4},{6,7},{7,6},{8,9},{9,8},{10,11... | collective-permute-start | bytes 294920 | tf_op jit(solution)/shard_map/ppermute | solution.py:416
  118.5 0.0 collective-permute-done.14.b_ref
  118.5 0.9 collective-permute-done.13.a_ref
  119.4 2.6 %all-to-all-done.2 = f32[128,1,640]{2,1,0:T(1,128)S(1)} async-done(((f32[128,1,640]{2,1,0:T(1,128)}), f32[128,1,640]{2,1,0:T(1,128)S(1)}, u32[]{:S(2)}, u32[]{:S(2)}) %all-to-all-start.2) | async-done | bytes 327712 | tf_op jit(solution)/shard_map/all_to_all | solution.py:448
  122.0 6.8 %shard_map.103 = (f32[8,8,384]{2,1,0:T(8,128)}, f32[8,8,384]{2,1,0:T(8,128)}, f32[8,8,384]{2,1,0:T(8,128)}) custom-call(s32[16,128]{1,0:T(8,128)S(1)} %get-tuple-element.28.table, f32[640,128]{1,0:T(8,128)S(1)} %bitcast.10, bf16[8,384,1024]{2,1,0:T(8,128)(2,1)} %get-tuple-element.44.weights_ref, f32[8,8,384]{2,1,0:T(8,128)S(1)} %collective-permute-done.am_ref, ...), custom_call_target="tpu_custom_call" | custom-call | flops 2500000000 | bytes 15000000 | tf_op jit(solution)/shard_map/pallas_call | solution.py:505
  (2 shorter events, 0.0 us)
Async XLA Ops:
  0.6 9.2 %copy-start = (f32[8,8,384]{2,1,0:T(8,128)S(1)}, f32[8,8,384]{2,1,0:T(8,128)}, u32[]{:S(2)}) copy-start(f32[8,8,384]{2,1,0:T(8,128)} %m_ref.2) | copy-start | bytes 294916
  0.6 13.2 %copy-start.1 = (f32[64,64]{1,0:T(8,128)S(1)}, f32[64,64]{1,0:T(8,128)}, u32[]{:S(2)}) copy-start(f32[64,64]{1,0:T(8,128)} %inverse_ref.5) | copy-start | bytes 49156
  3.6 10.3 %collective-permute-start.3 = (f32[25,8,128]{2,1,0:T(8,128)S(1)}, f32[25,8,128]{2,1,0:T(8,128)S(1)}, u32[]{:S(2)}, u32[]{:S(2)}) collective-permute-start(f32[25,8,128]{2,1,0:T(8,128)S(1)} %get-tuple-element.29.x_ref.ix_ref), channel_id=1, source_target_pairs={{0,31},{1,2},{2,1},{3,4},{4,3},{5,6},{6,5},{7,8},{8,7},{9,10},{10,... | collective-permute-start | bytes 307208 | tf_op jit(solution)/shard_map/ppermute | solution.py:416
  6.3 7.6 %collective-permute-start.2 = (f32[25,8,128]{2,1,0:T(8,128)S(1)}, f32[25,8,128]{2,1,0:T(8,128)S(1)}, u32[]{:S(2)}, u32[]{:S(2)}) collective-permute-start(f32[25,8,128]{2,1,0:T(8,128)S(1)} %get-tuple-element.29.x_ref.ix_ref), channel_id=1, source_target_pairs={{0,1},{1,0},{2,3},{3,2},{4,5},{5,4},{6,7},{7,6},{8,9},{9,8},{10,11... | collective-permute-start | bytes 307208 | tf_op jit(solution)/shard_map/ppermute | solution.py:416
  9.8 4.0 %collective-permute-start.1 = (f32[8,8,384]{2,1,0:T(8,128)S(1)}, f32[8,8,384]{2,1,0:T(8,128)S(1)}, u32[]{:S(2)}, u32[]{:S(2)}) collective-permute-start(f32[8,8,384]{2,1,0:T(8,128)S(1)} %copy-done), channel_id=1, source_target_pairs={{0,31},{1,2},{2,1},{3,4},{4,3},{5,6},{6,5},{7,8},{8,7},{9,10},{10,... | collective-permute-start | bytes 294920 | tf_op jit(solution)/shard_map/ppermute | solution.py:416
  9.8 4.0 %collective-permute-start = (f32[8,8,384]{2,1,0:T(8,128)S(1)}, f32[8,8,384]{2,1,0:T(8,128)S(1)}, u32[]{:S(2)}, u32[]{:S(2)}) collective-permute-start(f32[8,8,384]{2,1,0:T(8,128)S(1)} %copy-done), channel_id=1, source_target_pairs={{0,1},{1,0},{2,3},{3,2},{4,5},{5,4},{6,7},{7,6},{8,9},{9,8},{10,11... | collective-permute-start | bytes 294920 | tf_op jit(solution)/shard_map/ppermute | solution.py:416
  16.0 30.4 %all-to-all-start = ((f32[64,1,4736]{2,1,0:T(1,128)}), f32[64,1,4736]{2,1,0:T(1,128)S(1)}, u32[]{:S(2)}, u32[]{:S(2)}) async-start(f32[64,1,4736]{2,1,0:T(1,128)} %bitcast.1), calls=%async_computation | async-start | bytes 2424832 | tf_op jit(solution)/shard_map/all_to_all | solution.py:458
  28.6 13.4 %collective-permute-start.5 = (f32[24,8,128]{2,1,0:T(8,128)S(1)}, f32[24,8,128]{2,1,0:T(8,128)S(1)}, u32[]{:S(2)}, u32[]{:S(2)}) collective-permute-start(f32[24,8,128]{2,1,0:T(8,128)S(1)} %shard_map.96.x_ref), channel_id=1, source_target_pairs={{0,31},{1,2},{2,1},{3,4},{4,3},{5,6},{6,5},{7,8},{8,7},{9,10},{10,... | collective-permute-start | bytes 294920 | tf_op jit(solution)/shard_map/ppermute | solution.py:416
  29.7 12.2 %collective-permute-start.4 = (f32[24,8,128]{2,1,0:T(8,128)S(1)}, f32[24,8,128]{2,1,0:T(8,128)S(1)}, u32[]{:S(2)}, u32[]{:S(2)}) collective-permute-start(f32[24,8,128]{2,1,0:T(8,128)S(1)} %shard_map.96.x_ref), channel_id=1, source_target_pairs={{0,1},{1,0},{2,3},{3,2},{4,5},{5,4},{6,7},{7,6},{8,9},{9,8},{10,11... | collective-permute-start | bytes 294920 | tf_op jit(solution)/shard_map/ppermute | solution.py:416
  46.5 3.6 %collective-permute-start.6 = (f32[2368,128]{1,0:T(8,128)S(1)}, f32[2368,128]{1,0:T(8,128)S(1)}, u32[]{:S(2)}, u32[]{:S(2)}) collective-permute-start(f32[2368,128]{1,0:T(8,128)S(1)} %bitcast.8), channel_id=1, source_target_pairs={{0,1},{1,0},{2,3},{3,2},{4,5},{5,4},{6,7},{7,6},{8,9},{9,8},{10,11... | collective-permute-start | bytes 3637256 | tf_op jit(solution)/shard_map/ppermute | solution.py:463
  60.1 4.1 %collective-permute-start.8 = (f32[24,8,128]{2,1,0:T(8,128)S(1)}, f32[24,8,128]{2,1,0:T(8,128)S(1)}, u32[]{:S(2)}, u32[]{:S(2)}) collective-permute-start(f32[24,8,128]{2,1,0:T(8,128)S(1)} %get-tuple-element.41.x_ref), channel_id=1, source_target_pairs={{0,31},{1,2},{2,1},{3,4},{4,3},{5,6},{6,5},{7,8},{8,7},{9,10},{10,... | collective-permute-start | bytes 294920 | tf_op jit(solution)/shard_map/ppermute | solution.py:416
  60.5 3.7 %collective-permute-start.7 = (f32[24,8,128]{2,1,0:T(8,128)S(1)}, f32[24,8,128]{2,1,0:T(8,128)S(1)}, u32[]{:S(2)}, u32[]{:S(2)}) collective-permute-start(f32[24,8,128]{2,1,0:T(8,128)S(1)} %get-tuple-element.41.x_ref), channel_id=1, source_target_pairs={{0,1},{1,0},{2,3},{3,2},{4,5},{5,4},{6,7},{7,6},{8,9},{9,8},{10,11... | collective-permute-start | bytes 294920 | tf_op jit(solution)/shard_map/ppermute | solution.py:416
  66.0 18.9 %all-to-all-start.1 = ((f32[128,1,640]{2,1,0:T(1,128)}), f32[128,1,640]{2,1,0:T(1,128)S(1)}, u32[]{:S(2)}, u32[]{:S(2)}) async-start(f32[128,1,640]{2,1,0:T(1,128)} %bitcast.3), calls=%async_computation.1 | async-start | bytes 655360 | tf_op jit(solution)/shard_map/all_to_all | solution.py:448
  75.9 5.4 %collective-permute-start.10 = (f32[24,8,128]{2,1,0:T(8,128)S(1)}, f32[24,8,128]{2,1,0:T(8,128)S(1)}, u32[]{:S(2)}, u32[]{:S(2)}) collective-permute-start(f32[24,8,128]{2,1,0:T(8,128)S(1)} %shard_map.99.x_ref), channel_id=1, source_target_pairs={{0,31},{1,2},{2,1},{3,4},{4,3},{5,6},{6,5},{7,8},{8,7},{9,10},{10,... | collective-permute-start | bytes 294920 | tf_op jit(solution)/shard_map/ppermute | solution.py:416
  77.7 4.6 %collective-permute-start.9 = (f32[24,8,128]{2,1,0:T(8,128)S(1)}, f32[24,8,128]{2,1,0:T(8,128)S(1)}, u32[]{:S(2)}, u32[]{:S(2)}) collective-permute-start(f32[24,8,128]{2,1,0:T(8,128)S(1)} %shard_map.99.x_ref), channel_id=1, source_target_pairs={{0,1},{1,0},{2,3},{3,2},{4,5},{5,4},{6,7},{7,6},{8,9},{9,8},{10,11... | collective-permute-start | bytes 294920 | tf_op jit(solution)/shard_map/ppermute | solution.py:416
  93.5 4.1 %collective-permute-start.12 = (f32[24,8,128]{2,1,0:T(8,128)S(1)}, f32[24,8,128]{2,1,0:T(8,128)S(1)}, u32[]{:S(2)}, u32[]{:S(2)}) collective-permute-start(f32[24,8,128]{2,1,0:T(8,128)S(1)} %get-tuple-element.46.x_ref), channel_id=1, source_target_pairs={{0,31},{1,2},{2,1},{3,4},{4,3},{5,6},{6,5},{7,8},{8,7},{9,10},{10,... | collective-permute-start | bytes 294920 | tf_op jit(solution)/shard_map/ppermute | solution.py:416
  94.6 3.7 %collective-permute-start.11 = (f32[24,8,128]{2,1,0:T(8,128)S(1)}, f32[24,8,128]{2,1,0:T(8,128)S(1)}, u32[]{:S(2)}, u32[]{:S(2)}) collective-permute-start(f32[24,8,128]{2,1,0:T(8,128)S(1)} %get-tuple-element.46.x_ref), channel_id=1, source_target_pairs={{0,1},{1,0},{2,3},{3,2},{4,5},{5,4},{6,7},{7,6},{8,9},{9,8},{10,11... | collective-permute-start | bytes 294920 | tf_op jit(solution)/shard_map/ppermute | solution.py:416
  100.1 21.9 %all-to-all-start.2 = ((f32[128,1,640]{2,1,0:T(1,128)}), f32[128,1,640]{2,1,0:T(1,128)S(1)}, u32[]{:S(2)}, u32[]{:S(2)}) async-start(f32[128,1,640]{2,1,0:T(1,128)} %bitcast.5), calls=%async_computation.2 | async-start | bytes 655360 | tf_op jit(solution)/shard_map/all_to_all | solution.py:448
  113.2 5.3 %collective-permute-start.14 = (f32[24,8,128]{2,1,0:T(8,128)S(1)}, f32[24,8,128]{2,1,0:T(8,128)S(1)}, u32[]{:S(2)}, u32[]{:S(2)}) collective-permute-start(f32[24,8,128]{2,1,0:T(8,128)S(1)} %shard_map.102.x_ref), channel_id=1, source_target_pairs={{0,31},{1,2},{2,1},{3,4},{4,3},{5,6},{6,5},{7,8},{8,7},{9,10},{10,... | collective-permute-start | bytes 294920 | tf_op jit(solution)/shard_map/ppermute | solution.py:416
  114.9 4.5 %collective-permute-start.13 = (f32[24,8,128]{2,1,0:T(8,128)S(1)}, f32[24,8,128]{2,1,0:T(8,128)S(1)}, u32[]{:S(2)}, u32[]{:S(2)}) collective-permute-start(f32[24,8,128]{2,1,0:T(8,128)S(1)} %shard_map.102.x_ref), channel_id=1, source_target_pairs={{0,1},{1,0},{2,3},{3,2},{4,5},{5,4},{6,7},{7,6},{8,9},{9,8},{10,11... | collective-permute-start | bytes 294920 | tf_op jit(solution)/shard_map/ppermute | solution.py:416

commit v6 on v4

--- a/solution.py
+++ b/solution.py
@@ -200,16 +200,22 @@
         card_ref[at + 32 : at + CARD, :] = tail
 
 
-def send_second_kernel(table, a_ref, x_ref, b_ref, map_ref, r0_ref, z0_ref, w_ref, pay_ref, pool):
+def multiply_held(x, matrix_ref, out_ref):
+    for p in range(COUNT):
+        put_tiles(out_ref, p, product(get_row(x, p), matrix_ref[p]))
+
+
+def send_second_kernel(table, a_ref, x_ref, b_ref, map_ref, schur_ref, r0_ref, z0_ref, w_ref, pay_ref, q_ref, pool):
     fill_pool(pool, a_ref, x_ref, b_ref)
     w = jump(pool, table)
     for t in range(TILES):
         w_ref[t] = w[t]
     send(w, map_ref, [case_sum(r0_ref, z0_ref), case_sum(z0_ref, w)], pay_ref)
+    multiply_held(w, schur_ref, q_ref)
 
 
 def send_third_kernel(
-    table, a_ref, x_ref, b_ref, map_ref, r1_ref, z1_ref, z0_ref, w0_ref, v_ref, pay_ref, pool
+    table, a_ref, x_ref, b_ref, map_ref, schur_ref, r1_ref, z1_ref, z0_ref, w0_ref, v_ref, pay_ref, q_ref, pool
 ):
     fill_pool(pool, a_ref, x_ref, b_ref)
     v = jump(pool, table)
@@ -217,6 +223,7 @@
         v_ref[t] = v[t]
     columns = [case_sum(r1_ref, z1_ref), case_sum(z1_ref, v), case_sum(z0_ref, v), case_sum(z1_ref, w0_ref)]
     send(v, map_ref, columns, pay_ref)
+    multiply_held(v, schur_ref, q_ref)
 
 
 def gather_rows(mine, ids, own_ref, other_ref, rows, names):
@@ -271,17 +278,15 @@
                 pool[t] = pool[t] + full[p * 8 : (p + 1) * 8, c * 128 : (c + 1) * 128]
 
 
-def coarse_into_pool(got_ref, copies, weights, maps, pool, gathered, then=()):
-    sums = unpack(got_ref, gathered)
+def coarse_kernel(got_ref, weights_ref, out_ref, sums_ref, gathered, weights, sems):
+    copies = fetch(weights_ref, weights, sems)
+    sums_ref[...] = jnp.broadcast_to(unpack(got_ref, gathered), (8, 128))
     out = None
     for c in range(PARTS):
         copies[c].wait()
-        if then:
-            then[c].start()
         term = partial_solve(weights, gathered, c)
         out = term if out is None else out + term
-    into_pool(out, maps, pool)
-    return sums
+    out_ref[...] = out
 
 
 def totals(sums, count):
@@ -359,14 +364,12 @@
 
 
 def solve_second_kernel(
-    table, got_ref, weights_ref, am_ref, m_ref, bm_ref, a_ref, x_ref, b_ref, inverse_ref, r0_ref, z0_ref, w0_ref,
-    y_ref, r_ref, z_ref, scale_ref, u_ref, pool, gathered, weights, held, sems,
+    table, out_ref, sums_ref, am_ref, m_ref, bm_ref, a_ref, x_ref, b_ref, inverse_ref, r0_ref, z0_ref, w0_ref,
+    y_ref, r_ref, z_ref, scale_ref, u_ref, pool,
 ):
-    parts = fetch(weights_ref, weights, sems, COUNT)
-    copies = copies_of(inverse_ref, held, sems)
     fill_pool(pool, a_ref, x_ref, b_ref)
-    sums = coarse_into_pool(got_ref, parts, weights, (am_ref, m_ref, bm_ref), pool, gathered, copies)
-    energy, curve = totals(sums, 2)
+    into_pool(out_ref[...], (am_ref, m_ref, bm_ref), pool)
+    energy, curve = totals(sums_ref[0:1, :], 2)
     step = energy / curve
     scale_ref[0] = energy
     scale_ref[1] = curve
@@ -379,18 +382,17 @@
         r_ref[t] = r0_ref[t] - step * w0_ref[t]
         z.append(z0_ref[t] - step * half)
         z_ref[t] = z[t]
-    multiply(z, copies, held, u_ref)
+    multiply_held(z, inverse_ref, u_ref)
 
 
 def solve_third_kernel(
-    table, got_ref, weights_ref, am_ref, m_ref, bm_ref, a_ref, x_ref, b_ref,
+    table, out_ref, sums_ref, am_ref, m_ref, bm_ref, a_ref, x_ref, b_ref,
     scale_ref, z0_ref, w0_ref, y0_ref, r1_ref, z1_ref, v1_ref, multipliers_ref, residual_ref, preconditioned_ref,
-    pool, gathered, weights, sems,
+    pool,
 ):
-    parts = fetch(weights_ref, weights, sems)
     fill_pool(pool, a_ref, x_ref, b_ref)
-    sums = coarse_into_pool(got_ref, parts, weights, (am_ref, m_ref, bm_ref), pool, gathered)
-    energy, zv, pv, zw = totals(sums, 4)
+    into_pool(out_ref[...], (am_ref, m_ref, bm_ref), pool)
+    energy, zv, pv, zw = totals(sums_ref[0:1, :], 4)
     first = scale_ref[2]
     grow = energy / scale_ref[0]
     second = energy / (zv + grow * (pv + zw) + grow * grow * scale_ref[1])
@@ -480,34 +482,27 @@
         cost_estimate=pl.CostEstimate(flops=4_000_000_000, bytes_accessed=20_000_000, transcendentals=0),
     )(core, table, *indices, own_cards, other_cards, *maps, *pooled, inverse)
     weights = in_hbm(weights)
-    solve_scratch = [pool, gathered, solver, held, pltpu.SemaphoreType.DMA((COUNT + PARTS,))]
+    coarse_scratch = [gathered, solver, pltpu.SemaphoreType.DMA((PARTS,))]
+    coarse_out = [shape(6 * SLOTS, 16), shape(8, 128)]
     ua, ub = both(u)
-    w0, parts = call(send_second_kernel, [field, pay], [SMEM] + [VMEM] * 6, [pool])(
-        table, ua, u, ub, corner_map, r0, z0
+    w0, parts, q = call(send_second_kernel, [field, pay, field], [SMEM] + [VMEM] * 7, [pool], us=3)(
+        table, ua, u, ub, corner_map, schur, r0, z0
     )
-    got = spread(parts)
-    pooled = through(w0)
+    qa, qb = both(q)
+    out, sums = call(coarse_kernel, coarse_out, [VMEM, ANY], coarse_scratch, us=20)(spread(parts), weights)
     y0, r1, z1, scale, u = call(
-        solve_second_kernel,
-        [field, field, field, shape(3, 8, 128), field],
-        [SMEM, VMEM, ANY] + [VMEM] * 6 + [ANY] + [VMEM] * 3,
-        solve_scratch,
-        us=6,
-    )(table, got, weights, *maps, *pooled, inverse, r0, z0, w0)
+        solve_second_kernel, [field, field, field, shape(3, 8, 128), field], [SMEM] + [VMEM] * 12, [pool], us=3
+    )(table, out, sums, *maps, qa, q, qb, local_inverse, r0, z0, w0)
     ua, ub = both(u)
-    v1, parts = call(send_third_kernel, [field, pay], [SMEM] + [VMEM] * 8, [pool])(
-        table, ua, u, ub, corner_map, r1, z1, z0, w0
+    v1, parts, q = call(send_third_kernel, [field, pay, field], [SMEM] + [VMEM] * 9, [pool], us=3)(
+        table, ua, u, ub, corner_map, schur, r1, z1, z0, w0
     )
-    got = spread(parts)
-    pooled = through(v1)
+    qa, qb = both(q)
+    out, sums = call(coarse_kernel, coarse_out, [VMEM, ANY], coarse_scratch, us=20)(spread(parts), weights)
     return tuple(
-        call(
-            solve_third_kernel,
-            [shape(COUNT, CASES, WIDTH)] * 3,
-            [SMEM, VMEM, ANY] + [VMEM] * 13,
-            [pool, gathered, solver, pltpu.SemaphoreType.DMA((PARTS,))],
-            us=5,
-        )(table, got, weights, *maps, *pooled, scale, z0, w0, y0, r1, z1, v1)
+        call(solve_third_kernel, [shape(COUNT, CASES, WIDTH)] * 3, [SMEM] + [VMEM] * 15, [pool], us=2)(
+            table, out, sums, *maps, qa, q, qb, scale, z0, w0, y0, r1, z1, v1
+        )
     )
 
 

time: 127 us -> 124 us (0.976)
  waiting for transfers between devices: 25.8 us -> 33.1 us
  Pallas kernels: 42.3 us -> 36.3 us
  starting transfers between devices: 57.5 us -> 53.3 us
    all_to_all x2, waiting for transfers between devices: 5.2 us -> 13.2 us  [spread(): lax.all_to_all(x.reshape(devices, -1), GT, 0, 0, tiled=True)]
    pallas_call x1, Pallas kernels: 8.55 us -> 1.94 us  [shards(): call(solve_second_kernel, [field, field, field, shape(3, 8, 128), field],...]
    pallas_call x3 -> x5, Pallas kernels: 10.4 us -> 16.5 us  [the longest x2 10.1 us: shards(): call(coarse_kernel, coarse_out, [VMEM, ANY], coarse_scratch, us=20)]
    pallas_call x3 -> x1, Pallas kernels: 8.33 us -> 2.77 us  [through(): call(product_kernel, [field], [VMEM, ANY], [held, sems], us=3)(x, stiff)]
    ppermute x7, waiting for transfers between devices: 3.57 us -> 0.96 us  [both(): lax.ppermute(x, 'tile', inner_swap)]
    all_to_all x2, starting transfers between devices: 17.8 us -> 15.3 us  [spread(): lax.all_to_all(x.reshape(devices, -1), GT, 0, 0, tiled=True)]
    ppermute x7, waiting for transfers between devices: 10.1 us -> 12 us  [both(): lax.ppermute(x, 'tile', outer_swap)]
    ppermute x7, starting transfers between devices: 19.2 us -> 17.6 us  [both(): lax.ppermute(x, 'tile', inner_swap)]
  transfers between devices with their start and end apart: 18 -> 18, of which waited for: 12 -> 9; matrix products, arithmetic and copies ran while one was open for 0% -> 0% of each run, Pallas kernels for 7% -> 10%
where the time goes in v6:
time: 124 us
  starting transfers between devices  53.3 us (43%)
  Pallas kernels  36.3 us (29%)
  waiting for transfers between devices  33.1 us (27%)
    ppermute x7, starting transfers between devices, both(): lax.ppermute(x, 'tile', inner_swap)  17.6 us
    all_to_all x2, starting transfers between devices, spread(): lax.all_to_all(x.reshape(devices, -1), GT, 0, 0, tiled=True)  15.3 us
    all_to_all x2, waiting for transfers between devices, spread(): lax.all_to_all(x.reshape(devices, -1), GT, 0, 0, tiled=True)  13.2 us
    ppermute x7, waiting for transfers between devices, both(): lax.ppermute(x, 'tile', outer_swap)  12 us
    all_to_all x1, starting transfers between devices, shards(): lax.all_to_all(card.reshape(devices // 2, -1), GT, 0, 0, tiled=True, axis...  11.8 us
    pallas_call x2, Pallas kernels, shards(): call(coarse_kernel, coarse_out, [VMEM, ANY], coarse_scratch, us=20)  10.1 us
    pallas_call x1, Pallas kernels, shards(): pl.pallas_call(solve_first_kernel, in_specs=[SMEM] * 2 + [ANY] * 3 + [VME...  9.98 us
    ppermute x7, starting transfers between devices, both(): lax.ppermute(x, 'tile', outer_swap)  8.5 us
  transfers between devices with their start and end apart: 18, of which 9 were waited for; matrix products, arithmetic and copies ran while one was open for 0% of the time, Pallas kernels for 10%

profile of v6, /device:TPU:1, one launch (start us, length us, event | category | flops | bytes accessed | tf_op | source)
XLA Modules:
  0.0 123.8 jit_solution(1147613352938195598)
XLA Ops:
  0.7 2.9 %shard_map.94 = (f32[25,8,128]{2,1,0:T(8,128)S(1)}, s32[16,128]{1,0:T(8,128)S(1)}) custom-call(s32[1]{0:T(128)} %bitcast.core, f32[8,8,384]{2,1,0:T(8,128)} %loads_ref.1, s32[8,8]{1,0:T(8,128)} %index_ref.1, s32[8,12]{1,0:T(8,128)} %partner_ref.1, f32[8,384,384]{2,1,0:T(8,128)} %inverse_ref.7), custom_call_target="tpu_custom_call" | custom-call | flops 2000000000 | bytes 12000000 | tf_op jit(solution)/shard_map/pallas_call | solution.py:430
  3.6 2.7 %collective-permute-start.1 = (f32[25,8,128]{2,1,0:T(8,128)S(1)}, f32[25,8,128]{2,1,0:T(8,128)S(1)}, u32[]{:S(2)}, u32[]{:S(2)}) collective-permute-start(f32[25,8,128]{2,1,0:T(8,128)S(1)} %get-tuple-element.33.x_ref.ix_ref), channel_id=1, source_target_pairs={{0,31},{1,2},{2,1},{3,4},{4,3},{5,6},{6,5},{7,8},{8,7},{9,10},{10,... | collective-permute-start | bytes 307208 | tf_op jit(solution)/shard_map/ppermute | solution.py:418
  6.3 3.6 %collective-permute-start = (f32[25,8,128]{2,1,0:T(8,128)S(1)}, f32[25,8,128]{2,1,0:T(8,128)S(1)}, u32[]{:S(2)}, u32[]{:S(2)}) collective-permute-start(f32[25,8,128]{2,1,0:T(8,128)S(1)} %get-tuple-element.33.x_ref.ix_ref), channel_id=1, source_target_pairs={{0,1},{1,0},{2,3},{3,2},{4,5},{5,4},{6,7},{7,6},{8,9},{9,8},{10,11... | collective-permute-start | bytes 307208 | tf_op jit(solution)/shard_map/ppermute | solution.py:418
  9.8 0.0 collective-permute-done.1.b_ref.ib_ref
  9.8 0.9 collective-permute-done.a_ref.ia_ref
  10.8 2.1 %shard_map.95 = (f32[24,8,128]{2,1,0:T(8,128)S(1)}, f32[2368,128]{1,0:T(8,128)}) custom-call(s32[16,128]{1,0:T(8,128)S(1)} %get-tuple-element.32.table, f32[25,8,128]{2,1,0:T(8,128)S(1)} %collective-permute-done.a_ref.ia_ref, f32[25,8,128]{2,1,0:T(8,128)S(1)} %get-tuple-element.33.x_ref.ix_ref, f32[25,8,128]{2,1,0:T(8,128)S(1)} %collective-permute-done.1.b_ref.ib_ref, ...), custom_call_target="tpu_custom_call" | custom-call | flops 1000000000 | bytes 6000000 | tf_op jit(solution)/shard_map/pallas_call | solution.py:454
  12.9 11.8 %all-to-all-start = ((f32[64,1,4736]{2,1,0:T(1,128)}), f32[64,1,4736]{2,1,0:T(1,128)S(1)}, u32[]{:S(2)}, u32[]{:S(2)}) async-start(f32[64,1,4736]{2,1,0:T(1,128)} %bitcast.1), calls=%async_computation | async-start | bytes 2424832 | tf_op jit(solution)/shard_map/all_to_all | solution.py:457
  24.8 0.1 collective-permute-start.5
  24.9 4.7 %collective-permute-start.4 = (f32[8,8,384]{2,1,0:T(8,128)S(1)}, f32[8,8,384]{2,1,0:T(8,128)S(1)}, u32[]{:S(2)}, u32[]{:S(2)}) collective-permute-start(f32[8,8,384]{2,1,0:T(8,128)S(1)} %copy-done), channel_id=1, source_target_pairs={{0,1},{1,0},{2,3},{3,2},{4,5},{5,4},{6,7},{7,6},{8,9},{9,8},{10,11... | collective-permute-start | bytes 294920 | tf_op jit(solution)/shard_map/ppermute | solution.py:418
  29.6 2.8 %shard_map.96.x_ref = f32[24,8,128]{2,1,0:T(8,128)S(1)} custom-call(f32[24,8,128]{2,1,0:T(8,128)S(1)} %get-tuple-element.35.x_ref.r0_ref, f32[8,384,384]{2,1,0:T(8,128)} %schur_ref.3), custom_call_target="tpu_custom_call" | custom-call | flops 1500000000 | bytes 9000000 | tf_op jit(solution)/shard_map/pallas_call | solution.py:450
  32.4 0.1 collective-permute-start.3
  32.4 1.0 collective-permute-start.2
  33.4 5.6 %collective-permute-done.5.bm_ref = f32[8,8,384]{2,1,0:T(8,128)S(1)} collective-permute-done((f32[8,8,384]{2,1,0:T(8,128)S(1)}, f32[8,8,384]{2,1,0:T(8,128)S(1)}, u32[]{:S(2)}, u32[]{:S(2)}) %collective-permute-start.5) | collective-permute-done | bytes 98336 | tf_op jit(solution)/shard_map/ppermute | solution.py:418
  39.0 0.0 collective-permute-done.4.am_ref
  39.0 1.5 %collective-permute-done.3.b_ref = f32[24,8,128]{2,1,0:T(8,128)S(1)} collective-permute-done((f32[24,8,128]{2,1,0:T(8,128)S(1)}, f32[24,8,128]{2,1,0:T(8,128)S(1)}, u32[]{:S(2)}, u32[]{:S(2)}) %collective-permute-start.3) | collective-permute-done | bytes 98336 | tf_op jit(solution)/shard_map/ppermute | solution.py:418
  40.5 0.0 collective-permute-done.2.a_ref
  40.5 4.0 %all-to-all-done = f32[64,1,4736]{2,1,0:T(1,128)S(1)} async-done(((f32[64,1,4736]{2,1,0:T(1,128)}), f32[64,1,4736]{2,1,0:T(1,128)S(1)}, u32[]{:S(2)}, u32[]{:S(2)}) %all-to-all-start) | async-done | bytes 1212448 | tf_op jit(solution)/shard_map/all_to_all | solution.py:457
  44.5 0.1 collective-permute-start.6
  44.6 2.8 %collective-permute-done.6.other_ref = f32[2368,128]{1,0:T(8,128)S(1)} collective-permute-done((f32[2368,128]{1,0:T(8,128)S(1)}, f32[2368,128]{1,0:T(8,128)S(1)}, u32[]{:S(2)}, u32[]{:S(2)}) %collective-permute-start.6) | collective-permute-done | bytes 1212448 | tf_op jit(solution)/shard_map/ppermute | solution.py:464
  47.4 10.0 %shard_map.97 = (f32[24,8,128]{2,1,0:T(8,128)S(1)}, f32[24,8,128]{2,1,0:T(8,128)S(1)}, bf16[8,384,1024]{2,1,0:T(8,128)(2,1)}) custom-call(s32[1]{0:T(128)} %bitcast.core, s32[16,128]{1,0:T(8,128)S(1)} %get-tuple-element.32.table, f32[25,8,128]{2,1,0:T(8,128)S(1)} %collective-permute-done.a_ref.ia_ref, f32[25,8,128]{2,1,0:T(8,128)S(1)} %get-tuple-element.33.x_ref.ix_ref, ...), custom_call_target="tpu_custom_call" | custom-call | flops 4000000000 | bytes 20000000 | tf_op jit(solution)/shard_map/pallas_call | solution.py:465
  57.4 1.4 %collective-permute-start.8 = (f32[24,8,128]{2,1,0:T(8,128)S(1)}, f32[24,8,128]{2,1,0:T(8,128)S(1)}, u32[]{:S(2)}, u32[]{:S(2)}) collective-permute-start(f32[24,8,128]{2,1,0:T(8,128)S(1)} %get-tuple-element.43.x_ref), channel_id=1, source_target_pairs={{0,31},{1,2},{2,1},{3,4},{4,3},{5,6},{6,5},{7,8},{8,7},{9,10},{10,... | collective-permute-start | bytes 294920 | tf_op jit(solution)/shard_map/ppermute | solution.py:418
  58.8 0.0 collective-permute-start.7
  58.8 2.8 %collective-permute-done.8.b_ref = f32[24,8,128]{2,1,0:T(8,128)S(1)} collective-permute-done((f32[24,8,128]{2,1,0:T(8,128)S(1)}, f32[24,8,128]{2,1,0:T(8,128)S(1)}, u32[]{:S(2)}, u32[]{:S(2)}) %collective-permute-start.8) | collective-permute-done | bytes 98336 | tf_op jit(solution)/shard_map/ppermute | solution.py:418
  61.5 0.0 collective-permute-done.7.a_ref
  61.6 0.0 slice-start
  61.6 2.3 %shard_map.98 = (f32[24,8,128]{2,1,0:T(8,128)S(1)}, f32[640,128]{1,0:T(8,128)}, f32[24,8,128]{2,1,0:T(8,128)S(1)}) custom-call(s32[16,128]{1,0:T(8,128)S(1)} %get-tuple-element.32.table, f32[24,8,128]{2,1,0:T(8,128)S(1)} %collective-permute-done.7.a_ref, f32[24,8,128]{2,1,0:T(8,128)S(1)} %get-tuple-element.43.x_ref, ...), custom_call_target="tpu_custom_call" | custom-call | flops 1500000000 | bytes 9000000 | tf_op jit(solution)/shard_map/pallas_call | solution.py:488
  63.9 7.5 %all-to-all-start.1 = ((f32[128,1,640]{2,1,0:T(1,128)}), f32[128,1,640]{2,1,0:T(1,128)S(1)}, u32[]{:S(2)}, u32[]{:S(2)}) async-start(f32[128,1,640]{2,1,0:T(1,128)} %bitcast.3), calls=%async_computation.1 | async-start | bytes 655360 | tf_op jit(solution)/shard_map/all_to_all | solution.py:447
  71.4 1.7 %collective-permute-start.10 = (f32[24,8,128]{2,1,0:T(8,128)S(1)}, f32[24,8,128]{2,1,0:T(8,128)S(1)}, u32[]{:S(2)}, u32[]{:S(2)}) collective-permute-start(f32[24,8,128]{2,1,0:T(8,128)S(1)} %get-tuple-element.49.x_ref), channel_id=1, source_target_pairs={{0,31},{1,2},{2,1},{3,4},{4,3},{5,6},{6,5},{7,8},{8,7},{9,10},{10,... | collective-permute-start | bytes 294920 | tf_op jit(solution)/shard_map/ppermute | solution.py:418
  73.2 3.6 %collective-permute-start.9 = (f32[24,8,128]{2,1,0:T(8,128)S(1)}, f32[24,8,128]{2,1,0:T(8,128)S(1)}, u32[]{:S(2)}, u32[]{:S(2)}) collective-permute-start(f32[24,8,128]{2,1,0:T(8,128)S(1)} %get-tuple-element.49.x_ref), channel_id=1, source_target_pairs={{0,1},{1,0},{2,3},{3,2},{4,5},{5,4},{6,7},{7,6},{8,9},{9,8},{10,11... | collective-permute-start | bytes 294920 | tf_op jit(solution)/shard_map/ppermute | solution.py:418
  76.7 6.6 %all-to-all-done.1 = f32[128,1,640]{2,1,0:T(1,128)S(1)} async-done(((f32[128,1,640]{2,1,0:T(1,128)}), f32[128,1,640]{2,1,0:T(1,128)S(1)}, u32[]{:S(2)}, u32[]{:S(2)}) %all-to-all-start.1) | async-done | bytes 327712 | tf_op jit(solution)/shard_map/all_to_all | solution.py:447
  83.3 5.1 %shard_map.99 = (f32[384,16]{1,0:T(8,128)S(1)}, f32[8,128]{1,0:T(8,128)S(1)}) custom-call(f32[640,128]{1,0:T(8,128)S(1)} %bitcast.11, bf16[8,384,1024]{2,1,0:T(8,128)(2,1)} %get-tuple-element.46.weights_ref), custom_call_target="tpu_custom_call" | custom-call | flops 10000000000 | bytes 60000000 | tf_op jit(solution)/shard_map/pallas_call | solution.py:492
  88.5 0.0 collective-permute-done.10.b_ref
  88.5 0.0 collective-permute-done.9.a_ref
  88.5 0.2 slice-done.1
  88.7 1.9 %shard_map.100 = (f32[24,8,128]{2,1,0:T(8,128)S(1)}, f32[24,8,128]{2,1,0:T(8,128)S(1)}, f32[24,8,128]{2,1,0:T(8,128)S(1)}, f32[3,8,128]{2,1,0:T(8,128)S(1)}, f32[24,8,128]{2,1,0:T(8,128)S(1)}) custom-call(s32[16,128]{1,0:T(8,128)S(1)} %get-tuple-element.32.table, f32[384,16]{1,0:T(8,128)S(1)} %get-tuple-element.47.out_ref, ...), custom_call_target="tpu_custom_call" | custom-call | flops 1500000000 | bytes 9000000 | tf_op jit(solution)/shard_map/pallas_call | solution.py:493
  90.6 0.9 collective-permute-start.12
  91.5 1.1 collective-permute-start.11
  92.5 2.2 %collective-permute-done.12.b_ref = f32[24,8,128]{2,1,0:T(8,128)S(1)} collective-permute-done((f32[24,8,128]{2,1,0:T(8,128)S(1)}, f32[24,8,128]{2,1,0:T(8,128)S(1)}, u32[]{:S(2)}, u32[]{:S(2)}) %collective-permute-start.12) | collective-permute-done | bytes 98336 | tf_op jit(solution)/shard_map/ppermute | solution.py:418
  94.7 0.0 collective-permute-done.11.a_ref
  94.8 2.3 %shard_map.101 = (f32[24,8,128]{2,1,0:T(8,128)S(1)}, f32[640,128]{1,0:T(8,128)}, f32[24,8,128]{2,1,0:T(8,128)S(1)}) custom-call(s32[16,128]{1,0:T(8,128)S(1)} %get-tuple-element.32.table, f32[24,8,128]{2,1,0:T(8,128)S(1)} %collective-permute-done.11.a_ref, f32[24,8,128]{2,1,0:T(8,128)S(1)} %get-tuple-element.51.x_ref, ...), custom_call_target="tpu_custom_call" | custom-call | flops 1500000000 | bytes 9000000 | tf_op jit(solution)/shard_map/pallas_call | solution.py:497
  97.0 7.8 %all-to-all-start.2 = ((f32[128,1,640]{2,1,0:T(1,128)}), f32[128,1,640]{2,1,0:T(1,128)S(1)}, u32[]{:S(2)}, u32[]{:S(2)}) async-start(f32[128,1,640]{2,1,0:T(1,128)} %bitcast.5), calls=%async_computation.2 | async-start | bytes 655360 | tf_op jit(solution)/shard_map/all_to_all | solution.py:447
  104.8 1.7 %collective-permute-start.14 = (f32[24,8,128]{2,1,0:T(8,128)S(1)}, f32[24,8,128]{2,1,0:T(8,128)S(1)}, u32[]{:S(2)}, u32[]{:S(2)}) collective-permute-start(f32[24,8,128]{2,1,0:T(8,128)S(1)} %get-tuple-element.57.x_ref), channel_id=1, source_target_pairs={{0,31},{1,2},{2,1},{3,4},{4,3},{5,6},{6,5},{7,8},{8,7},{9,10},{10,... | collective-permute-start | bytes 294920 | tf_op jit(solution)/shard_map/ppermute | solution.py:418
  106.5 3.7 %collective-permute-start.13 = (f32[24,8,128]{2,1,0:T(8,128)S(1)}, f32[24,8,128]{2,1,0:T(8,128)S(1)}, u32[]{:S(2)}, u32[]{:S(2)}) collective-permute-start(f32[24,8,128]{2,1,0:T(8,128)S(1)} %get-tuple-element.57.x_ref), channel_id=1, source_target_pairs={{0,1},{1,0},{2,3},{3,2},{4,5},{5,4},{6,7},{7,6},{8,9},{9,8},{10,11... | collective-permute-start | bytes 294920 | tf_op jit(solution)/shard_map/ppermute | solution.py:418
  110.2 6.6 %all-to-all-done.2 = f32[128,1,640]{2,1,0:T(1,128)S(1)} async-done(((f32[128,1,640]{2,1,0:T(1,128)}), f32[128,1,640]{2,1,0:T(1,128)S(1)}, u32[]{:S(2)}, u32[]{:S(2)}) %all-to-all-start.2) | async-done | bytes 327712 | tf_op jit(solution)/shard_map/all_to_all | solution.py:447
  116.9 5.0 %shard_map.102 = (f32[384,16]{1,0:T(8,128)S(1)}, f32[8,128]{1,0:T(8,128)S(1)}) custom-call(f32[640,128]{1,0:T(8,128)S(1)} %bitcast.12, bf16[8,384,1024]{2,1,0:T(8,128)(2,1)} %get-tuple-element.46.weights_ref), custom_call_target="tpu_custom_call" | custom-call | flops 10000000000 | bytes 60000000 | tf_op jit(solution)/shard_map/pallas_call | solution.py:501
  121.8 0.0 collective-permute-done.14.b_ref
  121.8 0.0 collective-permute-done.13.a_ref
  121.8 1.9 %shard_map.103 = (f32[8,8,384]{2,1,0:T(8,128)}, f32[8,8,384]{2,1,0:T(8,128)}, f32[8,8,384]{2,1,0:T(8,128)}) custom-call(s32[16,128]{1,0:T(8,128)S(1)} %get-tuple-element.32.table, f32[384,16]{1,0:T(8,128)S(1)} %get-tuple-element.55.out_ref, f32[8,128]{1,0:T(8,128)S(1)} %get-tuple-element.56.sums_ref, f32[8,8,384]{2,1,0:T(8,128)S(1)} %collective-permute-done.4.am_ref, ...), custom_call_target="tpu_custom_call" | custom-call | flops 1000000000 | bytes 6000000 | tf_op jit(solution)/shard_map/pallas_call | solution.py:503
  (17 shorter events, 0.0 us)
Async XLA Ops:
  0.6 10.1 %copy-start = (f32[8,8,384]{2,1,0:T(8,128)S(1)}, f32[8,8,384]{2,1,0:T(8,128)}, u32[]{:S(2)}) copy-start(f32[8,8,384]{2,1,0:T(8,128)} %m_ref.2) | copy-start | bytes 294916
  0.6 10.1 %copy-start.1 = (f32[64,64]{1,0:T(8,128)S(1)}, f32[64,64]{1,0:T(8,128)}, u32[]{:S(2)}) copy-start(f32[64,64]{1,0:T(8,128)} %inverse_ref.5) | copy-start | bytes 49156
  3.6 6.2 %collective-permute-start.1 = (f32[25,8,128]{2,1,0:T(8,128)S(1)}, f32[25,8,128]{2,1,0:T(8,128)S(1)}, u32[]{:S(2)}, u32[]{:S(2)}) collective-permute-start(f32[25,8,128]{2,1,0:T(8,128)S(1)} %get-tuple-element.33.x_ref.ix_ref), channel_id=1, source_target_pairs={{0,31},{1,2},{2,1},{3,4},{4,3},{5,6},{6,5},{7,8},{8,7},{9,10},{10,... | collective-permute-start | bytes 307208 | tf_op jit(solution)/shard_map/ppermute | solution.py:418
  6.3 4.5 %collective-permute-start = (f32[25,8,128]{2,1,0:T(8,128)S(1)}, f32[25,8,128]{2,1,0:T(8,128)S(1)}, u32[]{:S(2)}, u32[]{:S(2)}) collective-permute-start(f32[25,8,128]{2,1,0:T(8,128)S(1)} %get-tuple-element.33.x_ref.ix_ref), channel_id=1, source_target_pairs={{0,1},{1,0},{2,3},{3,2},{4,5},{5,4},{6,7},{7,6},{8,9},{9,8},{10,11... | collective-permute-start | bytes 307208 | tf_op jit(solution)/shard_map/ppermute | solution.py:418
  12.9 31.6 %all-to-all-start = ((f32[64,1,4736]{2,1,0:T(1,128)}), f32[64,1,4736]{2,1,0:T(1,128)S(1)}, u32[]{:S(2)}, u32[]{:S(2)}) async-start(f32[64,1,4736]{2,1,0:T(1,128)} %bitcast.1), calls=%async_computation | async-start | bytes 2424832 | tf_op jit(solution)/shard_map/all_to_all | solution.py:457
  24.8 14.2 %collective-permute-start.5 = (f32[8,8,384]{2,1,0:T(8,128)S(1)}, f32[8,8,384]{2,1,0:T(8,128)S(1)}, u32[]{:S(2)}, u32[]{:S(2)}) collective-permute-start(f32[8,8,384]{2,1,0:T(8,128)S(1)} %copy-done), channel_id=1, source_target_pairs={{0,31},{1,2},{2,1},{3,4},{4,3},{5,6},{6,5},{7,8},{8,7},{9,10},{10,... | collective-permute-start | bytes 294920 | tf_op jit(solution)/shard_map/ppermute | solution.py:418
  24.9 14.1 %collective-permute-start.4 = (f32[8,8,384]{2,1,0:T(8,128)S(1)}, f32[8,8,384]{2,1,0:T(8,128)S(1)}, u32[]{:S(2)}, u32[]{:S(2)}) collective-permute-start(f32[8,8,384]{2,1,0:T(8,128)S(1)} %copy-done), channel_id=1, source_target_pairs={{0,1},{1,0},{2,3},{3,2},{4,5},{5,4},{6,7},{7,6},{8,9},{9,8},{10,11... | collective-permute-start | bytes 294920 | tf_op jit(solution)/shard_map/ppermute | solution.py:418
  32.4 8.1 %collective-permute-start.3 = (f32[24,8,128]{2,1,0:T(8,128)S(1)}, f32[24,8,128]{2,1,0:T(8,128)S(1)}, u32[]{:S(2)}, u32[]{:S(2)}) collective-permute-start(f32[24,8,128]{2,1,0:T(8,128)S(1)} %shard_map.96.x_ref), channel_id=1, source_target_pairs={{0,31},{1,2},{2,1},{3,4},{4,3},{5,6},{6,5},{7,8},{8,7},{9,10},{10,... | collective-permute-start | bytes 294920 | tf_op jit(solution)/shard_map/ppermute | solution.py:418
  32.4 8.0 %collective-permute-start.2 = (f32[24,8,128]{2,1,0:T(8,128)S(1)}, f32[24,8,128]{2,1,0:T(8,128)S(1)}, u32[]{:S(2)}, u32[]{:S(2)}) collective-permute-start(f32[24,8,128]{2,1,0:T(8,128)S(1)} %shard_map.96.x_ref), channel_id=1, source_target_pairs={{0,1},{1,0},{2,3},{3,2},{4,5},{5,4},{6,7},{7,6},{8,9},{9,8},{10,11... | collective-permute-start | bytes 294920 | tf_op jit(solution)/shard_map/ppermute | solution.py:418
  44.5 17.0 %slice-start.2 = ((s8[4718592]{0:T(1024)(128)(4,1)}), s8[4194304]{0:T(1024)(128)(4,1)S(1)}, s32[]{:S(2)}) async-start(s8[4718592]{0:T(1024)(128)(4,1)} %bitcast.13), calls=%async_computation.5 | async-start | bytes 8388608
  44.5 17.0 %slice-start.3 = ((s8[4718592]{0:T(1024)(128)(4,1)}), s8[524288]{0:T(1024)(128)(4,1)S(1)}, s32[]{:S(2)}) async-start(s8[4718592]{0:T(1024)(128)(4,1)} %bitcast.13), calls=%async_computation.6 | async-start | bytes 1048576
  44.5 2.9 %collective-permute-start.6 = (f32[2368,128]{1,0:T(8,128)S(1)}, f32[2368,128]{1,0:T(8,128)S(1)}, u32[]{:S(2)}, u32[]{:S(2)}) collective-permute-start(f32[2368,128]{1,0:T(8,128)S(1)} %bitcast.9), channel_id=1, source_target_pairs={{0,1},{1,0},{2,3},{3,2},{4,5},{5,4},{6,7},{7,6},{8,9},{9,8},{10,11... | collective-permute-start | bytes 3637256 | tf_op jit(solution)/shard_map/ppermute | solution.py:464
  57.4 4.1 %collective-permute-start.8 = (f32[24,8,128]{2,1,0:T(8,128)S(1)}, f32[24,8,128]{2,1,0:T(8,128)S(1)}, u32[]{:S(2)}, u32[]{:S(2)}) collective-permute-start(f32[24,8,128]{2,1,0:T(8,128)S(1)} %get-tuple-element.43.x_ref), channel_id=1, source_target_pairs={{0,31},{1,2},{2,1},{3,4},{4,3},{5,6},{6,5},{7,8},{8,7},{9,10},{10,... | collective-permute-start | bytes 294920 | tf_op jit(solution)/shard_map/ppermute | solution.py:418
  58.8 2.8 %collective-permute-start.7 = (f32[24,8,128]{2,1,0:T(8,128)S(1)}, f32[24,8,128]{2,1,0:T(8,128)S(1)}, u32[]{:S(2)}, u32[]{:S(2)}) collective-permute-start(f32[24,8,128]{2,1,0:T(8,128)S(1)} %get-tuple-element.43.x_ref), channel_id=1, source_target_pairs={{0,1},{1,0},{2,3},{3,2},{4,5},{5,4},{6,7},{7,6},{8,9},{9,8},{10,11... | collective-permute-start | bytes 294920 | tf_op jit(solution)/shard_map/ppermute | solution.py:418
  61.6 26.9 %slice-start = ((s8[4718592]{0:T(1024)(128)(4,1)}), s8[524288]{0:T(1024)(128)(4,1)S(1)}, s32[]{:S(2)}) async-start(s8[4718592]{0:T(1024)(128)(4,1)} %bitcast.7), calls=%async_computation.3 | async-start | bytes 1048576
  63.9 19.5 %all-to-all-start.1 = ((f32[128,1,640]{2,1,0:T(1,128)}), f32[128,1,640]{2,1,0:T(1,128)S(1)}, u32[]{:S(2)}, u32[]{:S(2)}) async-start(f32[128,1,640]{2,1,0:T(1,128)} %bitcast.3), calls=%async_computation.1 | async-start | bytes 655360 | tf_op jit(solution)/shard_map/all_to_all | solution.py:447
  71.4 17.0 %collective-permute-start.10 = (f32[24,8,128]{2,1,0:T(8,128)S(1)}, f32[24,8,128]{2,1,0:T(8,128)S(1)}, u32[]{:S(2)}, u32[]{:S(2)}) collective-permute-start(f32[24,8,128]{2,1,0:T(8,128)S(1)} %get-tuple-element.49.x_ref), channel_id=1, source_target_pairs={{0,31},{1,2},{2,1},{3,4},{4,3},{5,6},{6,5},{7,8},{8,7},{9,10},{10,... | collective-permute-start | bytes 294920 | tf_op jit(solution)/shard_map/ppermute | solution.py:418
  73.2 15.3 %collective-permute-start.9 = (f32[24,8,128]{2,1,0:T(8,128)S(1)}, f32[24,8,128]{2,1,0:T(8,128)S(1)}, u32[]{:S(2)}, u32[]{:S(2)}) collective-permute-start(f32[24,8,128]{2,1,0:T(8,128)S(1)} %get-tuple-element.49.x_ref), channel_id=1, source_target_pairs={{0,1},{1,0},{2,3},{3,2},{4,5},{5,4},{6,7},{7,6},{8,9},{9,8},{10,11... | collective-permute-start | bytes 294920 | tf_op jit(solution)/shard_map/ppermute | solution.py:418
  83.3 11.4 %slice-start.4 = ((s8[4718592]{0:T(1024)(128)(4,1)}), s8[4194304]{0:T(1024)(128)(4,1)S(1)}, s32[]{:S(2)}) async-start(s8[4718592]{0:T(1024)(128)(4,1)} %bitcast.15), calls=%async_computation.7 | async-start | bytes 8388608
  83.3 5.3 %slice-start.1 = ((s8[4718592]{0:T(1024)(128)(4,1)}), s8[4194304]{0:T(1024)(128)(4,1)S(1)}, s32[]{:S(2)}) async-start(s8[4718592]{0:T(1024)(128)(4,1)} %bitcast.7), calls=%async_computation.4 | async-start | bytes 8388608
  83.3 11.4 %slice-start.5 = ((s8[4718592]{0:T(1024)(128)(4,1)}), s8[524288]{0:T(1024)(128)(4,1)S(1)}, s32[]{:S(2)}) async-start(s8[4718592]{0:T(1024)(128)(4,1)} %bitcast.15), calls=%async_computation.8 | async-start | bytes 1048576
  90.6 4.1 %collective-permute-start.12 = (f32[24,8,128]{2,1,0:T(8,128)S(1)}, f32[24,8,128]{2,1,0:T(8,128)S(1)}, u32[]{:S(2)}, u32[]{:S(2)}) collective-permute-start(f32[24,8,128]{2,1,0:T(8,128)S(1)} %get-tuple-element.51.x_ref), channel_id=1, source_target_pairs={{0,31},{1,2},{2,1},{3,4},{4,3},{5,6},{6,5},{7,8},{8,7},{9,10},{10,... | collective-permute-start | bytes 294920 | tf_op jit(solution)/shard_map/ppermute | solution.py:418
  91.5 3.3 %collective-permute-start.11 = (f32[24,8,128]{2,1,0:T(8,128)S(1)}, f32[24,8,128]{2,1,0:T(8,128)S(1)}, u32[]{:S(2)}, u32[]{:S(2)}) collective-permute-start(f32[24,8,128]{2,1,0:T(8,128)S(1)} %get-tuple-element.51.x_ref), channel_id=1, source_target_pairs={{0,1},{1,0},{2,3},{3,2},{4,5},{5,4},{6,7},{7,6},{8,9},{9,8},{10,11... | collective-permute-start | bytes 294920 | tf_op jit(solution)/shard_map/ppermute | solution.py:418
  97.0 19.8 %all-to-all-start.2 = ((f32[128,1,640]{2,1,0:T(1,128)}), f32[128,1,640]{2,1,0:T(1,128)S(1)}, u32[]{:S(2)}, u32[]{:S(2)}) async-start(f32[128,1,640]{2,1,0:T(1,128)} %bitcast.5), calls=%async_computation.2 | async-start | bytes 655360 | tf_op jit(solution)/shard_map/all_to_all | solution.py:447
  104.8 17.0 %collective-permute-start.14 = (f32[24,8,128]{2,1,0:T(8,128)S(1)}, f32[24,8,128]{2,1,0:T(8,128)S(1)}, u32[]{:S(2)}, u32[]{:S(2)}) collective-permute-start(f32[24,8,128]{2,1,0:T(8,128)S(1)} %get-tuple-element.57.x_ref), channel_id=1, source_target_pairs={{0,31},{1,2},{2,1},{3,4},{4,3},{5,6},{6,5},{7,8},{8,7},{9,10},{10,... | collective-permute-start | bytes 294920 | tf_op jit(solution)/shard_map/ppermute | solution.py:418
  106.5 15.3 %collective-permute-start.13 = (f32[24,8,128]{2,1,0:T(8,128)S(1)}, f32[24,8,128]{2,1,0:T(8,128)S(1)}, u32[]{:S(2)}, u32[]{:S(2)}) collective-permute-start(f32[24,8,128]{2,1,0:T(8,128)S(1)} %get-tuple-element.57.x_ref), channel_id=1, source_target_pairs={{0,1},{1,0},{2,3},{3,2},{4,5},{5,4},{6,7},{7,6},{8,9},{9,8},{10,11... | collective-permute-start | bytes 294920 | tf_op jit(solution)/shard_map/ppermute | solution.py:418

commit v7 on v6

--- a/solution.py
+++ b/solution.py
@@ -19,7 +19,7 @@
 TILES = COUNT * CHUNKS
 SLOTS = COUNT * CORNERS
 CARD = 37
-PARTS, PART = 8, 1024
+PARTS, PART, KEEP = 8, 1024, 2
 
 
 def call(kernel, outs, specs, scratch=(), us=2):
@@ -205,18 +205,30 @@
         put_tiles(out_ref, p, product(get_row(x, p), matrix_ref[p]))
 
 
-def send_second_kernel(table, a_ref, x_ref, b_ref, map_ref, schur_ref, r0_ref, z0_ref, w_ref, pay_ref, q_ref, pool):
+def send_second_kernel(
+    table, a_ref, x_ref, b_ref, map_ref, schur_ref, r0_ref, z0_ref, weights_ref, w_ref, pay_ref, q_ref, kept_ref,
+    pool, sems,
+):
+    keeps = [pltpu.make_async_copy(weights_ref.at[c], kept_ref.at[c], sems.at[c]) for c in range(KEEP)]
+    for keep in keeps:
+        keep.start()
     fill_pool(pool, a_ref, x_ref, b_ref)
     w = jump(pool, table)
     for t in range(TILES):
         w_ref[t] = w[t]
     send(w, map_ref, [case_sum(r0_ref, z0_ref), case_sum(z0_ref, w)], pay_ref)
     multiply_held(w, schur_ref, q_ref)
+    for keep in keeps:
+        keep.wait()
 
 
 def send_third_kernel(
-    table, a_ref, x_ref, b_ref, map_ref, schur_ref, r1_ref, z1_ref, z0_ref, w0_ref, v_ref, pay_ref, q_ref, pool
+    table, a_ref, x_ref, b_ref, map_ref, schur_ref, r1_ref, z1_ref, z0_ref, w0_ref, weights_ref,
+    v_ref, pay_ref, q_ref, kept_ref, pool, sems,
 ):
+    keeps = [pltpu.make_async_copy(weights_ref.at[c], kept_ref.at[c], sems.at[c]) for c in range(KEEP)]
+    for keep in keeps:
+        keep.start()
     fill_pool(pool, a_ref, x_ref, b_ref)
     v = jump(pool, table)
     for t in range(TILES):
@@ -224,6 +236,8 @@
     columns = [case_sum(r1_ref, z1_ref), case_sum(z1_ref, v), case_sum(z0_ref, v), case_sum(z1_ref, w0_ref)]
     send(v, map_ref, columns, pay_ref)
     multiply_held(v, schur_ref, q_ref)
+    for keep in keeps:
+        keep.wait()
 
 
 def gather_rows(mine, ids, own_ref, other_ref, rows, names):
@@ -256,7 +270,7 @@
 
 
 def partial_solve(weights, gathered, c):
-    return lax.dot_general(weights[c], gathered[:, c * PART : (c + 1) * PART], NT, preferred_element_type=F32)
+    return lax.dot_general(weights[...], gathered[:, c * PART : (c + 1) * PART], NT, preferred_element_type=F32)
 
 
 def into_pool(out, maps, pool):
@@ -278,14 +292,18 @@
                 pool[t] = pool[t] + full[p * 8 : (p + 1) * 8, c * 128 : (c + 1) * 128]
 
 
-def coarse_kernel(got_ref, weights_ref, out_ref, sums_ref, gathered, weights, sems):
-    copies = fetch(weights_ref, weights, sems)
+def coarse_kernel(got_ref, kept_ref, weights_ref, out_ref, sums_ref, gathered, weights, sems):
+    copies = [
+        pltpu.make_async_copy(weights_ref.at[c], weights.at[c - KEEP], sems.at[c - KEEP]) for c in range(KEEP, PARTS)
+    ]
+    for copy in copies:
+        copy.start()
     sums_ref[...] = jnp.broadcast_to(unpack(got_ref, gathered), (8, 128))
-    out = None
-    for c in range(PARTS):
-        copies[c].wait()
-        term = partial_solve(weights, gathered, c)
-        out = term if out is None else out + term
+    out = partial_solve(kept_ref.at[0], gathered, 0)
+    for c in range(1, PARTS):
+        if c >= KEEP:
+            copies[c - KEEP].wait()
+        out = out + partial_solve(kept_ref.at[c] if c < KEEP else weights.at[c - KEEP], gathered, c)
     out_ref[...] = out
 
 
@@ -352,7 +370,7 @@
         store = pltpu.make_async_copy(weights.at[part], weights_ref.at[part], sems.at[COUNT + part])
         store.start()
         stores.append(store)
-        term = partial_solve(weights, gathered, part)
+        term = partial_solve(weights.at[part], gathered, part)
         out = term if out is None else out + term
     into_pool(out, (am_ref, m_ref, bm_ref), pool)
     z = [0.5 * t for t in jump(pool, table)]
@@ -482,23 +500,30 @@
         cost_estimate=pl.CostEstimate(flops=4_000_000_000, bytes_accessed=20_000_000, transcendentals=0),
     )(core, table, *indices, own_cards, other_cards, *maps, *pooled, inverse)
     weights = in_hbm(weights)
-    coarse_scratch = [gathered, solver, pltpu.SemaphoreType.DMA((PARTS,))]
+    rest = pltpu.VMEM((PARTS - KEEP, 6 * SLOTS, PART), BF16)
+    kept_shape = jax.ShapeDtypeStruct((KEEP, 6 * SLOTS, PART), BF16)
+    keep_scratch = [pool, pltpu.SemaphoreType.DMA((KEEP,))]
+    coarse_scratch = [gathered, rest, pltpu.SemaphoreType.DMA((PARTS - KEEP,))]
     coarse_out = [shape(6 * SLOTS, 16), shape(8, 128)]
     ua, ub = both(u)
-    w0, parts, q = call(send_second_kernel, [field, pay, field], [SMEM] + [VMEM] * 7, [pool], us=3)(
-        table, ua, u, ub, corner_map, schur, r0, z0
+    w0, parts, q, kept = call(
+        send_second_kernel, [field, pay, field, kept_shape], [SMEM] + [VMEM] * 7 + [ANY], keep_scratch, us=3
+    )(
+        table, ua, u, ub, corner_map, schur, r0, z0, weights
     )
     qa, qb = both(q)
-    out, sums = call(coarse_kernel, coarse_out, [VMEM, ANY], coarse_scratch, us=20)(spread(parts), weights)
+    out, sums = call(coarse_kernel, coarse_out, [VMEM, VMEM, ANY], coarse_scratch, us=20)(spread(parts), kept, weights)
     y0, r1, z1, scale, u = call(
         solve_second_kernel, [field, field, field, shape(3, 8, 128), field], [SMEM] + [VMEM] * 12, [pool], us=3
     )(table, out, sums, *maps, qa, q, qb, local_inverse, r0, z0, w0)
     ua, ub = both(u)
-    v1, parts, q = call(send_third_kernel, [field, pay, field], [SMEM] + [VMEM] * 9, [pool], us=3)(
-        table, ua, u, ub, corner_map, schur, r1, z1, z0, w0
+    v1, parts, q, kept = call(
+        send_third_kernel, [field, pay, field, kept_shape], [SMEM] + [VMEM] * 9 + [ANY], keep_scratch, us=3
+    )(
+        table, ua, u, ub, corner_map, schur, r1, z1, z0, w0, weights
     )
     qa, qb = both(q)
-    out, sums = call(coarse_kernel, coarse_out, [VMEM, ANY], coarse_scratch, us=20)(spread(parts), weights)
+    out, sums = call(coarse_kernel, coarse_out, [VMEM, VMEM, ANY], coarse_scratch, us=20)(spread(parts), kept, weights)
     return tuple(
         call(solve_third_kernel, [shape(COUNT, CASES, WIDTH)] * 3, [SMEM] + [VMEM] * 15, [pool], us=2)(
             table, out, sums, *maps, qa, q, qb, scale, z0, w0, y0, r1, z1, v1

time: 124 us -> 125 us (level)
  no operation moved by 1% of the time
where the time goes in v7:
time: 125 us; the launch traced here: 124 us
  starting transfers between devices  53.3 us (43%)
  Pallas kernels  36.9 us (30%)
  waiting for transfers between devices  33.1 us (26%)
    ppermute x7, starting transfers between devices, both(): lax.ppermute(x, 'tile', inner_swap)  17.6 us
    all_to_all x2, starting transfers between devices, spread(): lax.all_to_all(x.reshape(devices, -1), GT, 0, 0, tiled=True)  15.4 us
    all_to_all x2, waiting for transfers between devices, spread(): lax.all_to_all(x.reshape(devices, -1), GT, 0, 0, tiled=True)  13.2 us
    ppermute x7, waiting for transfers between devices, both(): lax.ppermute(x, 'tile', outer_swap)  12 us
    all_to_all x1, starting transfers between devices, shards(): lax.all_to_all(card.reshape(devices // 2, -1), GT, 0, 0, tiled=True, axis...  11.8 us
    pallas_call x1, Pallas kernels, shards(): pl.pallas_call(solve_first_kernel, in_specs=[SMEM] * 2 + [ANY] * 3 + [VME...  9.98 us
    pallas_call x2, Pallas kernels, shards(): call(coarse_kernel, coarse_out, [VMEM, VMEM, ANY], coarse_scratch, us=20)  9.12 us
    ppermute x7, starting transfers between devices, both(): lax.ppermute(x, 'tile', outer_swap)  8.49 us
  transfers between devices with their start and end apart: 18, of which 9 were waited for; matrix products, arithmetic and copies ran while one was open for 0% of the time, Pallas kernels for 10%

profile of v7, /device:TPU:1, one launch (start us, length us, event | category | flops | bytes accessed | tf_op | source)
XLA Modules:
  0.0 124.3 jit_solution(11830503184648498452)
XLA Ops:
  0.7 2.9 %shard_map.94 = (f32[25,8,128]{2,1,0:T(8,128)S(1)}, s32[16,128]{1,0:T(8,128)S(1)}) custom-call(s32[1]{0:T(128)} %bitcast.core, f32[8,8,384]{2,1,0:T(8,128)} %loads_ref.1, s32[8,8]{1,0:T(8,128)} %index_ref.1, s32[8,12]{1,0:T(8,128)} %partner_ref.1, f32[8,384,384]{2,1,0:T(8,128)} %inverse_ref.7), custom_call_target="tpu_custom_call" | custom-call | flops 2000000000 | bytes 12000000 | tf_op jit(solution)/shard_map/pallas_call | solution.py:448
  3.6 2.7 %collective-permute-start.1 = (f32[25,8,128]{2,1,0:T(8,128)S(1)}, f32[25,8,128]{2,1,0:T(8,128)S(1)}, u32[]{:S(2)}, u32[]{:S(2)}) collective-permute-start(f32[25,8,128]{2,1,0:T(8,128)S(1)} %get-tuple-element.35.x_ref.ix_ref), channel_id=1, source_target_pairs={{0,31},{1,2},{2,1},{3,4},{4,3},{5,6},{6,5},{7,8},{8,7},{9,10},{10,... | collective-permute-start | bytes 307208 | tf_op jit(solution)/shard_map/ppermute | solution.py:436
  6.3 3.6 %collective-permute-start = (f32[25,8,128]{2,1,0:T(8,128)S(1)}, f32[25,8,128]{2,1,0:T(8,128)S(1)}, u32[]{:S(2)}, u32[]{:S(2)}) collective-permute-start(f32[25,8,128]{2,1,0:T(8,128)S(1)} %get-tuple-element.35.x_ref.ix_ref), channel_id=1, source_target_pairs={{0,1},{1,0},{2,3},{3,2},{4,5},{5,4},{6,7},{7,6},{8,9},{9,8},{10,11... | collective-permute-start | bytes 307208 | tf_op jit(solution)/shard_map/ppermute | solution.py:436
  9.8 0.0 collective-permute-done.1.b_ref.ib_ref
  9.8 0.9 collective-permute-done.a_ref.ia_ref
  10.8 2.1 %shard_map.95 = (f32[24,8,128]{2,1,0:T(8,128)S(1)}, f32[2368,128]{1,0:T(8,128)}) custom-call(s32[16,128]{1,0:T(8,128)S(1)} %get-tuple-element.34.table, f32[25,8,128]{2,1,0:T(8,128)S(1)} %collective-permute-done.a_ref.ia_ref, f32[25,8,128]{2,1,0:T(8,128)S(1)} %get-tuple-element.35.x_ref.ix_ref, f32[25,8,128]{2,1,0:T(8,128)S(1)} %collective-permute-done.1.b_ref.ib_ref, ...), custom_call_target="tpu_custom_call" | custom-call | flops 1000000000 | bytes 6000000 | tf_op jit(solution)/shard_map/pallas_call | solution.py:472
  12.9 11.8 %all-to-all-start = ((f32[64,1,4736]{2,1,0:T(1,128)}), f32[64,1,4736]{2,1,0:T(1,128)S(1)}, u32[]{:S(2)}, u32[]{:S(2)}) async-start(f32[64,1,4736]{2,1,0:T(1,128)} %bitcast.1), calls=%async_computation | async-start | bytes 2424832 | tf_op jit(solution)/shard_map/all_to_all | solution.py:475
  24.8 0.1 collective-permute-start.5
  24.9 4.7 %collective-permute-start.4 = (f32[8,8,384]{2,1,0:T(8,128)S(1)}, f32[8,8,384]{2,1,0:T(8,128)S(1)}, u32[]{:S(2)}, u32[]{:S(2)}) collective-permute-start(f32[8,8,384]{2,1,0:T(8,128)S(1)} %copy-done), channel_id=1, source_target_pairs={{0,1},{1,0},{2,3},{3,2},{4,5},{5,4},{6,7},{7,6},{8,9},{9,8},{10,11... | collective-permute-start | bytes 294920 | tf_op jit(solution)/shard_map/ppermute | solution.py:436
  29.6 2.8 %shard_map.96.x_ref = f32[24,8,128]{2,1,0:T(8,128)S(1)} custom-call(f32[24,8,128]{2,1,0:T(8,128)S(1)} %get-tuple-element.37.x_ref.r0_ref, f32[8,384,384]{2,1,0:T(8,128)} %schur_ref.3), custom_call_target="tpu_custom_call" | custom-call | flops 1500000000 | bytes 9000000 | tf_op jit(solution)/shard_map/pallas_call | solution.py:468
  32.4 0.1 collective-permute-start.3
  32.4 1.0 collective-permute-start.2
  33.4 5.6 %collective-permute-done.5.bm_ref = f32[8,8,384]{2,1,0:T(8,128)S(1)} collective-permute-done((f32[8,8,384]{2,1,0:T(8,128)S(1)}, f32[8,8,384]{2,1,0:T(8,128)S(1)}, u32[]{:S(2)}, u32[]{:S(2)}) %collective-permute-start.5) | collective-permute-done | bytes 98336 | tf_op jit(solution)/shard_map/ppermute | solution.py:436
  39.0 0.0 collective-permute-done.4.am_ref
  39.0 1.5 %collective-permute-done.3.b_ref = f32[24,8,128]{2,1,0:T(8,128)S(1)} collective-permute-done((f32[24,8,128]{2,1,0:T(8,128)S(1)}, f32[24,8,128]{2,1,0:T(8,128)S(1)}, u32[]{:S(2)}, u32[]{:S(2)}) %collective-permute-start.3) | collective-permute-done | bytes 98336 | tf_op jit(solution)/shard_map/ppermute | solution.py:436
  40.5 0.0 collective-permute-done.2.a_ref
  40.5 4.0 %all-to-all-done = f32[64,1,4736]{2,1,0:T(1,128)S(1)} async-done(((f32[64,1,4736]{2,1,0:T(1,128)}), f32[64,1,4736]{2,1,0:T(1,128)S(1)}, u32[]{:S(2)}, u32[]{:S(2)}) %all-to-all-start) | async-done | bytes 1212448 | tf_op jit(solution)/shard_map/all_to_all | solution.py:475
  44.5 0.1 collective-permute-start.6
  44.6 2.8 %collective-permute-done.6.other_ref = f32[2368,128]{1,0:T(8,128)S(1)} collective-permute-done((f32[2368,128]{1,0:T(8,128)S(1)}, f32[2368,128]{1,0:T(8,128)S(1)}, u32[]{:S(2)}, u32[]{:S(2)}) %collective-permute-start.6) | collective-permute-done | bytes 1212448 | tf_op jit(solution)/shard_map/ppermute | solution.py:482
  47.4 10.0 %shard_map.97 = (f32[24,8,128]{2,1,0:T(8,128)S(1)}, f32[24,8,128]{2,1,0:T(8,128)S(1)}, bf16[8,384,1024]{2,1,0:T(8,128)(2,1)}) custom-call(s32[1]{0:T(128)} %bitcast.core, s32[16,128]{1,0:T(8,128)S(1)} %get-tuple-element.34.table, f32[25,8,128]{2,1,0:T(8,128)S(1)} %collective-permute-done.a_ref.ia_ref, f32[25,8,128]{2,1,0:T(8,128)S(1)} %get-tuple-element.35.x_ref.ix_ref, ...), custom_call_target="tpu_custom_call" | custom-call | flops 4000000000 | bytes 20000000 | tf_op jit(solution)/shard_map/pallas_call | solution.py:483
  57.4 1.4 %collective-permute-start.8 = (f32[24,8,128]{2,1,0:T(8,128)S(1)}, f32[24,8,128]{2,1,0:T(8,128)S(1)}, u32[]{:S(2)}, u32[]{:S(2)}) collective-permute-start(f32[24,8,128]{2,1,0:T(8,128)S(1)} %get-tuple-element.45.x_ref), channel_id=1, source_target_pairs={{0,31},{1,2},{2,1},{3,4},{4,3},{5,6},{6,5},{7,8},{8,7},{9,10},{10,... | collective-permute-start | bytes 294920 | tf_op jit(solution)/shard_map/ppermute | solution.py:436
  58.8 0.0 collective-permute-start.7
  58.8 2.8 %collective-permute-done.8.b_ref = f32[24,8,128]{2,1,0:T(8,128)S(1)} collective-permute-done((f32[24,8,128]{2,1,0:T(8,128)S(1)}, f32[24,8,128]{2,1,0:T(8,128)S(1)}, u32[]{:S(2)}, u32[]{:S(2)}) %collective-permute-start.8) | collective-permute-done | bytes 98336 | tf_op jit(solution)/shard_map/ppermute | solution.py:436
  61.5 0.0 collective-permute-done.7.a_ref
  61.6 0.0 slice-start.4
  61.6 3.0 %shard_map.98 = (f32[24,8,128]{2,1,0:T(8,128)S(1)}, f32[640,128]{1,0:T(8,128)}, f32[24,8,128]{2,1,0:T(8,128)S(1)}, bf16[2,384,1024]{2,1,0:T(8,128)(2,1)S(1)}) custom-call(s32[16,128]{1,0:T(8,128)S(1)} %get-tuple-element.34.table, f32[24,8,128]{2,1,0:T(8,128)S(1)} %collective-permute-done.7.a_ref, f32[24,8,128]{2,1,0:T(8,128)S(1)} %get-tuple-element.45.x_ref, ...), custom_call_target="tpu_custom_call" | custom-call | flops 1500000000 | bytes 9000000 | tf_op jit(solution)/shard_map/pallas_call | solution.py:509
  64.6 7.5 %all-to-all-start.1 = ((f32[128,1,640]{2,1,0:T(1,128)}), f32[128,1,640]{2,1,0:T(1,128)S(1)}, u32[]{:S(2)}, u32[]{:S(2)}) async-start(f32[128,1,640]{2,1,0:T(1,128)} %bitcast.3), calls=%async_computation.1 | async-start | bytes 655360 | tf_op jit(solution)/shard_map/all_to_all | solution.py:465
  72.2 1.7 %collective-permute-start.10 = (f32[24,8,128]{2,1,0:T(8,128)S(1)}, f32[24,8,128]{2,1,0:T(8,128)S(1)}, u32[]{:S(2)}, u32[]{:S(2)}) collective-permute-start(f32[24,8,128]{2,1,0:T(8,128)S(1)} %get-tuple-element.52.x_ref), channel_id=1, source_target_pairs={{0,31},{1,2},{2,1},{3,4},{4,3},{5,6},{6,5},{7,8},{8,7},{9,10},{10,... | collective-permute-start | bytes 294920 | tf_op jit(solution)/shard_map/ppermute | solution.py:436
  73.9 3.6 %collective-permute-start.9 = (f32[24,8,128]{2,1,0:T(8,128)S(1)}, f32[24,8,128]{2,1,0:T(8,128)S(1)}, u32[]{:S(2)}, u32[]{:S(2)}) collective-permute-start(f32[24,8,128]{2,1,0:T(8,128)S(1)} %get-tuple-element.52.x_ref), channel_id=1, source_target_pairs={{0,1},{1,0},{2,3},{3,2},{4,5},{5,4},{6,7},{7,6},{8,9},{9,8},{10,11... | collective-permute-start | bytes 294920 | tf_op jit(solution)/shard_map/ppermute | solution.py:436
  77.5 6.6 %all-to-all-done.1 = f32[128,1,640]{2,1,0:T(1,128)S(1)} async-done(((f32[128,1,640]{2,1,0:T(1,128)}), f32[128,1,640]{2,1,0:T(1,128)S(1)}, u32[]{:S(2)}, u32[]{:S(2)}) %all-to-all-start.1) | async-done | bytes 327712 | tf_op jit(solution)/shard_map/all_to_all | solution.py:465
  84.1 4.8 %shard_map.99 = (f32[384,16]{1,0:T(8,128)S(1)}, f32[8,128]{1,0:T(8,128)S(1)}) custom-call(f32[640,128]{1,0:T(8,128)S(1)} %bitcast.16, bf16[2,384,1024]{2,1,0:T(8,128)(2,1)S(1)} %get-tuple-element.49.kept_ref, bf16[8,384,1024]{2,1,0:T(8,128)(2,1)} %get-tuple-element.47.weights_ref), custom_call_target="tpu_custom_call" | custom-call | flops 10000000000 | bytes 60000000 | tf_op jit(solution)/shard_map/pallas_call | solution.py:515
  88.9 0.0 collective-permute-done.10.b_ref
  88.9 0.0 collective-permute-done.9.a_ref
  88.9 0.1 slice-done.5
  89.0 1.9 %shard_map.100 = (f32[24,8,128]{2,1,0:T(8,128)S(1)}, f32[24,8,128]{2,1,0:T(8,128)S(1)}, f32[24,8,128]{2,1,0:T(8,128)S(1)}, f32[3,8,128]{2,1,0:T(8,128)S(1)}, f32[24,8,128]{2,1,0:T(8,128)S(1)}) custom-call(s32[16,128]{1,0:T(8,128)S(1)} %get-tuple-element.34.table, f32[384,16]{1,0:T(8,128)S(1)} %get-tuple-element.50.out_ref, ...), custom_call_target="tpu_custom_call" | custom-call | flops 1500000000 | bytes 9000000 | tf_op jit(solution)/shard_map/pallas_call | solution.py:516
  90.9 0.9 collective-permute-start.12
  91.8 1.1 collective-permute-start.11
  92.8 2.2 %collective-permute-done.12.b_ref = f32[24,8,128]{2,1,0:T(8,128)S(1)} collective-permute-done((f32[24,8,128]{2,1,0:T(8,128)S(1)}, f32[24,8,128]{2,1,0:T(8,128)S(1)}, u32[]{:S(2)}, u32[]{:S(2)}) %collective-permute-start.12) | collective-permute-done | bytes 98336 | tf_op jit(solution)/shard_map/ppermute | solution.py:436
  95.0 0.0 collective-permute-done.11.a_ref
  95.0 3.1 %shard_map.101 = (f32[24,8,128]{2,1,0:T(8,128)S(1)}, f32[640,128]{1,0:T(8,128)}, f32[24,8,128]{2,1,0:T(8,128)S(1)}, bf16[2,384,1024]{2,1,0:T(8,128)(2,1)S(1)}) custom-call(s32[16,128]{1,0:T(8,128)S(1)} %get-tuple-element.34.table, f32[24,8,128]{2,1,0:T(8,128)S(1)} %collective-permute-done.11.a_ref, f32[24,8,128]{2,1,0:T(8,128)S(1)} %get-tuple-element.54.x_ref, ...), custom_call_target="tpu_custom_call" | custom-call | flops 1500000000 | bytes 9000000 | tf_op jit(solution)/shard_map/pallas_call | solution.py:520
  98.2 7.8 %all-to-all-start.2 = ((f32[128,1,640]{2,1,0:T(1,128)}), f32[128,1,640]{2,1,0:T(1,128)S(1)}, u32[]{:S(2)}, u32[]{:S(2)}) async-start(f32[128,1,640]{2,1,0:T(1,128)} %bitcast.5), calls=%async_computation.2 | async-start | bytes 655360 | tf_op jit(solution)/shard_map/all_to_all | solution.py:465
  106.0 1.7 %collective-permute-start.14 = (f32[24,8,128]{2,1,0:T(8,128)S(1)}, f32[24,8,128]{2,1,0:T(8,128)S(1)}, u32[]{:S(2)}, u32[]{:S(2)}) collective-permute-start(f32[24,8,128]{2,1,0:T(8,128)S(1)} %get-tuple-element.61.x_ref), channel_id=1, source_target_pairs={{0,31},{1,2},{2,1},{3,4},{4,3},{5,6},{6,5},{7,8},{8,7},{9,10},{10,... | collective-permute-start | bytes 294920 | tf_op jit(solution)/shard_map/ppermute | solution.py:436
  107.7 3.7 %collective-permute-start.13 = (f32[24,8,128]{2,1,0:T(8,128)S(1)}, f32[24,8,128]{2,1,0:T(8,128)S(1)}, u32[]{:S(2)}, u32[]{:S(2)}) collective-permute-start(f32[24,8,128]{2,1,0:T(8,128)S(1)} %get-tuple-element.61.x_ref), channel_id=1, source_target_pairs={{0,1},{1,0},{2,3},{3,2},{4,5},{5,4},{6,7},{7,6},{8,9},{9,8},{10,11... | collective-permute-start | bytes 294920 | tf_op jit(solution)/shard_map/ppermute | solution.py:436
  111.4 6.6 %all-to-all-done.2 = f32[128,1,640]{2,1,0:T(1,128)S(1)} async-done(((f32[128,1,640]{2,1,0:T(1,128)}), f32[128,1,640]{2,1,0:T(1,128)S(1)}, u32[]{:S(2)}, u32[]{:S(2)}) %all-to-all-start.2) | async-done | bytes 327712 | tf_op jit(solution)/shard_map/all_to_all | solution.py:465
  118.0 4.4 %shard_map.102 = (f32[384,16]{1,0:T(8,128)S(1)}, f32[8,128]{1,0:T(8,128)S(1)}) custom-call(f32[640,128]{1,0:T(8,128)S(1)} %bitcast.15, bf16[2,384,1024]{2,1,0:T(8,128)(2,1)S(1)} %get-tuple-element.58.kept_ref, bf16[8,384,1024]{2,1,0:T(8,128)(2,1)} %get-tuple-element.47.weights_ref), custom_call_target="tpu_custom_call" | custom-call | flops 10000000000 | bytes 60000000 | tf_op jit(solution)/shard_map/pallas_call | solution.py:526
  122.4 0.0 collective-permute-done.14.b_ref
  122.4 0.0 collective-permute-done.13.a_ref
  122.4 1.9 %shard_map.103 = (f32[8,8,384]{2,1,0:T(8,128)}, f32[8,8,384]{2,1,0:T(8,128)}, f32[8,8,384]{2,1,0:T(8,128)}) custom-call(s32[16,128]{1,0:T(8,128)S(1)} %get-tuple-element.34.table, f32[384,16]{1,0:T(8,128)S(1)} %get-tuple-element.59.out_ref, f32[8,128]{1,0:T(8,128)S(1)} %get-tuple-element.60.sums_ref, f32[8,8,384]{2,1,0:T(8,128)S(1)} %collective-permute-done.4.am_ref, ...), custom_call_target="tpu_custom_call" | custom-call | flops 1000000000 | bytes 6000000 | tf_op jit(solution)/shard_map/pallas_call | solution.py:528
  (17 shorter events, 0.0 us)
Async XLA Ops:
  0.6 10.1 %copy-start = (f32[8,8,384]{2,1,0:T(8,128)S(1)}, f32[8,8,384]{2,1,0:T(8,128)}, u32[]{:S(2)}) copy-start(f32[8,8,384]{2,1,0:T(8,128)} %m_ref.2) | copy-start | bytes 294916
  0.7 10.1 %copy-start.1 = (f32[64,64]{1,0:T(8,128)S(1)}, f32[64,64]{1,0:T(8,128)}, u32[]{:S(2)}) copy-start(f32[64,64]{1,0:T(8,128)} %inverse_ref.5) | copy-start | bytes 49156
  3.6 6.2 %collective-permute-start.1 = (f32[25,8,128]{2,1,0:T(8,128)S(1)}, f32[25,8,128]{2,1,0:T(8,128)S(1)}, u32[]{:S(2)}, u32[]{:S(2)}) collective-permute-start(f32[25,8,128]{2,1,0:T(8,128)S(1)} %get-tuple-element.35.x_ref.ix_ref), channel_id=1, source_target_pairs={{0,31},{1,2},{2,1},{3,4},{4,3},{5,6},{6,5},{7,8},{8,7},{9,10},{10,... | collective-permute-start | bytes 307208 | tf_op jit(solution)/shard_map/ppermute | solution.py:436
  6.3 4.5 %collective-permute-start = (f32[25,8,128]{2,1,0:T(8,128)S(1)}, f32[25,8,128]{2,1,0:T(8,128)S(1)}, u32[]{:S(2)}, u32[]{:S(2)}) collective-permute-start(f32[25,8,128]{2,1,0:T(8,128)S(1)} %get-tuple-element.35.x_ref.ix_ref), channel_id=1, source_target_pairs={{0,1},{1,0},{2,3},{3,2},{4,5},{5,4},{6,7},{7,6},{8,9},{9,8},{10,11... | collective-permute-start | bytes 307208 | tf_op jit(solution)/shard_map/ppermute | solution.py:436
  12.9 31.6 %all-to-all-start = ((f32[64,1,4736]{2,1,0:T(1,128)}), f32[64,1,4736]{2,1,0:T(1,128)S(1)}, u32[]{:S(2)}, u32[]{:S(2)}) async-start(f32[64,1,4736]{2,1,0:T(1,128)} %bitcast.1), calls=%async_computation | async-start | bytes 2424832 | tf_op jit(solution)/shard_map/all_to_all | solution.py:475
  24.8 14.2 %collective-permute-start.5 = (f32[8,8,384]{2,1,0:T(8,128)S(1)}, f32[8,8,384]{2,1,0:T(8,128)S(1)}, u32[]{:S(2)}, u32[]{:S(2)}) collective-permute-start(f32[8,8,384]{2,1,0:T(8,128)S(1)} %copy-done), channel_id=1, source_target_pairs={{0,31},{1,2},{2,1},{3,4},{4,3},{5,6},{6,5},{7,8},{8,7},{9,10},{10,... | collective-permute-start | bytes 294920 | tf_op jit(solution)/shard_map/ppermute | solution.py:436
  24.9 14.1 %collective-permute-start.4 = (f32[8,8,384]{2,1,0:T(8,128)S(1)}, f32[8,8,384]{2,1,0:T(8,128)S(1)}, u32[]{:S(2)}, u32[]{:S(2)}) collective-permute-start(f32[8,8,384]{2,1,0:T(8,128)S(1)} %copy-done), channel_id=1, source_target_pairs={{0,1},{1,0},{2,3},{3,2},{4,5},{5,4},{6,7},{7,6},{8,9},{9,8},{10,11... | collective-permute-start | bytes 294920 | tf_op jit(solution)/shard_map/ppermute | solution.py:436
  32.4 8.1 %collective-permute-start.3 = (f32[24,8,128]{2,1,0:T(8,128)S(1)}, f32[24,8,128]{2,1,0:T(8,128)S(1)}, u32[]{:S(2)}, u32[]{:S(2)}) collective-permute-start(f32[24,8,128]{2,1,0:T(8,128)S(1)} %shard_map.96.x_ref), channel_id=1, source_target_pairs={{0,31},{1,2},{2,1},{3,4},{4,3},{5,6},{6,5},{7,8},{8,7},{9,10},{10,... | collective-permute-start | bytes 294920 | tf_op jit(solution)/shard_map/ppermute | solution.py:436
  32.4 8.0 %collective-permute-start.2 = (f32[24,8,128]{2,1,0:T(8,128)S(1)}, f32[24,8,128]{2,1,0:T(8,128)S(1)}, u32[]{:S(2)}, u32[]{:S(2)}) collective-permute-start(f32[24,8,128]{2,1,0:T(8,128)S(1)} %shard_map.96.x_ref), channel_id=1, source_target_pairs={{0,1},{1,0},{2,3},{3,2},{4,5},{5,4},{6,7},{7,6},{8,9},{9,8},{10,11... | collective-permute-start | bytes 294920 | tf_op jit(solution)/shard_map/ppermute | solution.py:436
  44.5 17.0 %slice-start = ((s8[4718592]{0:T(1024)(128)(4,1)}), s8[4194304]{0:T(1024)(128)(4,1)S(1)}, s32[]{:S(2)}) async-start(s8[4718592]{0:T(1024)(128)(4,1)} %bitcast.7), calls=%async_computation.3 | async-start | bytes 8388608
  44.5 17.0 %slice-start.1 = ((s8[4718592]{0:T(1024)(128)(4,1)}), s8[524288]{0:T(1024)(128)(4,1)S(1)}, s32[]{:S(2)}) async-start(s8[4718592]{0:T(1024)(128)(4,1)} %bitcast.7), calls=%async_computation.4 | async-start | bytes 1048576
  44.5 2.9 %collective-permute-start.6 = (f32[2368,128]{1,0:T(8,128)S(1)}, f32[2368,128]{1,0:T(8,128)S(1)}, u32[]{:S(2)}, u32[]{:S(2)}) collective-permute-start(f32[2368,128]{1,0:T(8,128)S(1)} %bitcast.13), channel_id=1, source_target_pairs={{0,1},{1,0},{2,3},{3,2},{4,5},{5,4},{6,7},{7,6},{8,9},{9,8},{10,11... | collective-permute-start | bytes 3637256 | tf_op jit(solution)/shard_map/ppermute | solution.py:482
  57.4 4.1 %collective-permute-start.8 = (f32[24,8,128]{2,1,0:T(8,128)S(1)}, f32[24,8,128]{2,1,0:T(8,128)S(1)}, u32[]{:S(2)}, u32[]{:S(2)}) collective-permute-start(f32[24,8,128]{2,1,0:T(8,128)S(1)} %get-tuple-element.45.x_ref), channel_id=1, source_target_pairs={{0,31},{1,2},{2,1},{3,4},{4,3},{5,6},{6,5},{7,8},{8,7},{9,10},{10,... | collective-permute-start | bytes 294920 | tf_op jit(solution)/shard_map/ppermute | solution.py:436
  58.8 2.8 %collective-permute-start.7 = (f32[24,8,128]{2,1,0:T(8,128)S(1)}, f32[24,8,128]{2,1,0:T(8,128)S(1)}, u32[]{:S(2)}, u32[]{:S(2)}) collective-permute-start(f32[24,8,128]{2,1,0:T(8,128)S(1)} %get-tuple-element.45.x_ref), channel_id=1, source_target_pairs={{0,1},{1,0},{2,3},{3,2},{4,5},{5,4},{6,7},{7,6},{8,9},{9,8},{10,11... | collective-permute-start | bytes 294920 | tf_op jit(solution)/shard_map/ppermute | solution.py:436
  61.6 27.3 %slice-start.4 = ((s8[4718592]{0:T(1024)(128)(4,1)}), s8[524288]{0:T(1024)(128)(4,1)S(1)}, s32[]{:S(2)}) async-start(s8[4718592]{0:T(1024)(128)(4,1)} %bitcast.11), calls=%async_computation.7 | async-start | bytes 1048576
  64.6 19.5 %all-to-all-start.1 = ((f32[128,1,640]{2,1,0:T(1,128)}), f32[128,1,640]{2,1,0:T(1,128)S(1)}, u32[]{:S(2)}, u32[]{:S(2)}) async-start(f32[128,1,640]{2,1,0:T(1,128)} %bitcast.3), calls=%async_computation.1 | async-start | bytes 655360 | tf_op jit(solution)/shard_map/all_to_all | solution.py:465
  72.2 16.7 %collective-permute-start.10 = (f32[24,8,128]{2,1,0:T(8,128)S(1)}, f32[24,8,128]{2,1,0:T(8,128)S(1)}, u32[]{:S(2)}, u32[]{:S(2)}) collective-permute-start(f32[24,8,128]{2,1,0:T(8,128)S(1)} %get-tuple-element.52.x_ref), channel_id=1, source_target_pairs={{0,31},{1,2},{2,1},{3,4},{4,3},{5,6},{6,5},{7,8},{8,7},{9,10},{10,... | collective-permute-start | bytes 294920 | tf_op jit(solution)/shard_map/ppermute | solution.py:436
  73.9 15.0 %collective-permute-start.9 = (f32[24,8,128]{2,1,0:T(8,128)S(1)}, f32[24,8,128]{2,1,0:T(8,128)S(1)}, u32[]{:S(2)}, u32[]{:S(2)}) collective-permute-start(f32[24,8,128]{2,1,0:T(8,128)S(1)} %get-tuple-element.52.x_ref), channel_id=1, source_target_pairs={{0,1},{1,0},{2,3},{3,2},{4,5},{5,4},{6,7},{7,6},{8,9},{9,8},{10,11... | collective-permute-start | bytes 294920 | tf_op jit(solution)/shard_map/ppermute | solution.py:436
  84.1 10.9 %slice-start.2 = ((s8[4718592]{0:T(1024)(128)(4,1)}), s8[4194304]{0:T(1024)(128)(4,1)S(1)}, s32[]{:S(2)}) async-start(s8[4718592]{0:T(1024)(128)(4,1)} %bitcast.9), calls=%async_computation.5 | async-start | bytes 8388608
  84.1 4.9 %slice-start.5 = ((s8[4718592]{0:T(1024)(128)(4,1)}), s8[4194304]{0:T(1024)(128)(4,1)S(1)}, s32[]{:S(2)}) async-start(s8[4718592]{0:T(1024)(128)(4,1)} %bitcast.11), calls=%async_computation.8 | async-start | bytes 8388608
  84.1 10.9 %slice-start.3 = ((s8[4718592]{0:T(1024)(128)(4,1)}), s8[524288]{0:T(1024)(128)(4,1)S(1)}, s32[]{:S(2)}) async-start(s8[4718592]{0:T(1024)(128)(4,1)} %bitcast.9), calls=%async_computation.6 | async-start | bytes 1048576
  90.9 4.1 %collective-permute-start.12 = (f32[24,8,128]{2,1,0:T(8,128)S(1)}, f32[24,8,128]{2,1,0:T(8,128)S(1)}, u32[]{:S(2)}, u32[]{:S(2)}) collective-permute-start(f32[24,8,128]{2,1,0:T(8,128)S(1)} %get-tuple-element.54.x_ref), channel_id=1, source_target_pairs={{0,31},{1,2},{2,1},{3,4},{4,3},{5,6},{6,5},{7,8},{8,7},{9,10},{10,... | collective-permute-start | bytes 294920 | tf_op jit(solution)/shard_map/ppermute | solution.py:436
  91.8 3.3 %collective-permute-start.11 = (f32[24,8,128]{2,1,0:T(8,128)S(1)}, f32[24,8,128]{2,1,0:T(8,128)S(1)}, u32[]{:S(2)}, u32[]{:S(2)}) collective-permute-start(f32[24,8,128]{2,1,0:T(8,128)S(1)} %get-tuple-element.54.x_ref), channel_id=1, source_target_pairs={{0,1},{1,0},{2,3},{3,2},{4,5},{5,4},{6,7},{7,6},{8,9},{9,8},{10,11... | collective-permute-start | bytes 294920 | tf_op jit(solution)/shard_map/ppermute | solution.py:436
  98.2 19.9 %all-to-all-start.2 = ((f32[128,1,640]{2,1,0:T(1,128)}), f32[128,1,640]{2,1,0:T(1,128)S(1)}, u32[]{:S(2)}, u32[]{:S(2)}) async-start(f32[128,1,640]{2,1,0:T(1,128)} %bitcast.5), calls=%async_computation.2 | async-start | bytes 655360 | tf_op jit(solution)/shard_map/all_to_all | solution.py:465
  106.0 16.4 %collective-permute-start.14 = (f32[24,8,128]{2,1,0:T(8,128)S(1)}, f32[24,8,128]{2,1,0:T(8,128)S(1)}, u32[]{:S(2)}, u32[]{:S(2)}) collective-permute-start(f32[24,8,128]{2,1,0:T(8,128)S(1)} %get-tuple-element.61.x_ref), channel_id=1, source_target_pairs={{0,31},{1,2},{2,1},{3,4},{4,3},{5,6},{6,5},{7,8},{8,7},{9,10},{10,... | collective-permute-start | bytes 294920 | tf_op jit(solution)/shard_map/ppermute | solution.py:436
  107.7 14.7 %collective-permute-start.13 = (f32[24,8,128]{2,1,0:T(8,128)S(1)}, f32[24,8,128]{2,1,0:T(8,128)S(1)}, u32[]{:S(2)}, u32[]{:S(2)}) collective-permute-start(f32[24,8,128]{2,1,0:T(8,128)S(1)} %get-tuple-element.61.x_ref), channel_id=1, source_target_pairs={{0,1},{1,0},{2,3},{3,2},{4,5},{5,4},{6,7},{7,6},{8,9},{9,8},{10,11... | collective-permute-start | bytes 294920 | tf_op jit(solution)/shard_map/ppermute | solution.py:436

commit v8 on v7

--- a/solution.py
+++ b/solution.py
@@ -205,30 +205,18 @@
         put_tiles(out_ref, p, product(get_row(x, p), matrix_ref[p]))
 
 
-def send_second_kernel(
-    table, a_ref, x_ref, b_ref, map_ref, schur_ref, r0_ref, z0_ref, weights_ref, w_ref, pay_ref, q_ref, kept_ref,
-    pool, sems,
-):
-    keeps = [pltpu.make_async_copy(weights_ref.at[c], kept_ref.at[c], sems.at[c]) for c in range(KEEP)]
-    for keep in keeps:
-        keep.start()
+def send_second_kernel(table, a_ref, x_ref, b_ref, map_ref, schur_ref, r0_ref, z0_ref, w_ref, pay_ref, q_ref, pool):
     fill_pool(pool, a_ref, x_ref, b_ref)
     w = jump(pool, table)
     for t in range(TILES):
         w_ref[t] = w[t]
     send(w, map_ref, [case_sum(r0_ref, z0_ref), case_sum(z0_ref, w)], pay_ref)
     multiply_held(w, schur_ref, q_ref)
-    for keep in keeps:
-        keep.wait()
 
 
 def send_third_kernel(
-    table, a_ref, x_ref, b_ref, map_ref, schur_ref, r1_ref, z1_ref, z0_ref, w0_ref, weights_ref,
-    v_ref, pay_ref, q_ref, kept_ref, pool, sems,
+    table, a_ref, x_ref, b_ref, map_ref, schur_ref, r1_ref, z1_ref, z0_ref, w0_ref, v_ref, pay_ref, q_ref, pool
 ):
-    keeps = [pltpu.make_async_copy(weights_ref.at[c], kept_ref.at[c], sems.at[c]) for c in range(KEEP)]
-    for keep in keeps:
-        keep.start()
     fill_pool(pool, a_ref, x_ref, b_ref)
     v = jump(pool, table)
     for t in range(TILES):
@@ -236,8 +224,6 @@
     columns = [case_sum(r1_ref, z1_ref), case_sum(z1_ref, v), case_sum(z0_ref, v), case_sum(z1_ref, w0_ref)]
     send(v, map_ref, columns, pay_ref)
     multiply_held(v, schur_ref, q_ref)
-    for keep in keeps:
-        keep.wait()
 
 
 def gather_rows(mine, ids, own_ref, other_ref, rows, names):
@@ -290,6 +276,21 @@
             for c in range(CHUNKS):
                 t = e * TILES + p * CHUNKS + c
                 pool[t] = pool[t] + full[p * 8 : (p + 1) * 8, c * 128 : (c + 1) * 128]
+
+
+def hold_kernel(after_ref, source_ref, held_ref, sems):
+    del after_ref
+    for copy in fetch(source_ref, held_ref, sems):
+        copy.wait()
+
+
+def keep_kernel(after_ref, weights_ref, kept_ref, sems):
+    del after_ref
+    copies = [pltpu.make_async_copy(weights_ref.at[c], kept_ref.at[c], sems.at[c]) for c in range(KEEP)]
+    for copy in copies:
+        copy.start()
+    for copy in copies:
+        copy.wait()
 
 
 def coarse_kernel(got_ref, kept_ref, weights_ref, out_ref, sums_ref, gathered, weights, sems):
@@ -502,28 +503,30 @@
     weights = in_hbm(weights)
     rest = pltpu.VMEM((PARTS - KEEP, 6 * SLOTS, PART), BF16)
     kept_shape = jax.ShapeDtypeStruct((KEEP, 6 * SLOTS, PART), BF16)
-    keep_scratch = [pool, pltpu.SemaphoreType.DMA((KEEP,))]
     coarse_scratch = [gathered, rest, pltpu.SemaphoreType.DMA((PARTS - KEEP,))]
+
+    def hold(after):
+        return call(hold_kernel, [shape(COUNT, WIDTH, WIDTH)], [ANY] * 2, [sems], us=2)(after, stiff)[0]
+
+    def keep(after):
+        return call(keep_kernel, [kept_shape], [ANY] * 2, [pltpu.SemaphoreType.DMA((KEEP,))], us=2)(after, weights)[0]
+
     coarse_out = [shape(6 * SLOTS, 16), shape(8, 128)]
     ua, ub = both(u)
-    w0, parts, q, kept = call(
-        send_second_kernel, [field, pay, field, kept_shape], [SMEM] + [VMEM] * 7 + [ANY], keep_scratch, us=3
-    )(
-        table, ua, u, ub, corner_map, schur, r0, z0, weights
+    w0, parts, q = call(send_second_kernel, [field, pay, field], [SMEM] + [VMEM] * 7, [pool], us=3)(
+        table, ua, u, ub, corner_map, hold(u), r0, z0
     )
     qa, qb = both(q)
-    out, sums = call(coarse_kernel, coarse_out, [VMEM, VMEM, ANY], coarse_scratch, us=20)(spread(parts), kept, weights)
+    out, sums = call(coarse_kernel, coarse_out, [VMEM, VMEM, ANY], coarse_scratch, us=20)(spread(parts), keep(qb), weights)
     y0, r1, z1, scale, u = call(
         solve_second_kernel, [field, field, field, shape(3, 8, 128), field], [SMEM] + [VMEM] * 12, [pool], us=3
     )(table, out, sums, *maps, qa, q, qb, local_inverse, r0, z0, w0)
     ua, ub = both(u)
-    v1, parts, q, kept = call(
-        send_third_kernel, [field, pay, field, kept_shape], [SMEM] + [VMEM] * 9 + [ANY], keep_scratch, us=3
-    )(
-        table, ua, u, ub, corner_map, schur, r1, z1, z0, w0, weights
+    v1, parts, q = call(send_third_kernel, [field, pay, field], [SMEM] + [VMEM] * 9, [pool], us=3)(
+        table, ua, u, ub, corner_map, hold(u), r1, z1, z0, w0
     )
     qa, qb = both(q)
-    out, sums = call(coarse_kernel, coarse_out, [VMEM, VMEM, ANY], coarse_scratch, us=20)(spread(parts), kept, weights)
+    out, sums = call(coarse_kernel, coarse_out, [VMEM, VMEM, ANY], coarse_scratch, us=20)(spread(parts), keep(qb), weights)
     return tuple(
         call(solve_third_kernel, [shape(COUNT, CASES, WIDTH)] * 3, [SMEM] + [VMEM] * 15, [pool], us=2)(
             table, out, sums, *maps, qa, q, qb, scale, z0, w0, y0, r1, z1, v1

time: 125 us -> 124 us (level)
  waiting for transfers between devices: 33.1 us -> 25.7 us
  Pallas kernels: 36.9 us -> 42.6 us
    pallas_call x2 -> x6, Pallas kernels: 6.15 us -> 12.2 us  [the longest x2 4.75 us: hold(): call(hold_kernel, [shape(COUNT, WIDTH, WIDTH)], [ANY] * 2, [sems], us=2)]
    all_to_all x2, waiting for transfers between devices: 13.2 us -> 7.88 us  [spread(): lax.all_to_all(x.reshape(devices, -1), GT, 0, 0, tiled=True)]
    ppermute x7, waiting for transfers between devices: 12 us -> 9.95 us  [both(): lax.ppermute(x, 'tile', outer_swap)]
  transfers between devices with their start and end apart: 18 -> 18, of which waited for: 9 -> 10; matrix products, arithmetic and copies ran while one was open for 0% -> 0% of each run, Pallas kernels for 10% -> 15%
where the time goes in v8:
time: 124 us
  starting transfers between devices  54.4 us (44%)
  Pallas kernels  42.6 us (34%)
  waiting for transfers between devices  25.7 us (21%)
    ppermute x7, starting transfers between devices, both(): lax.ppermute(x, 'tile', inner_swap)  18.1 us
    all_to_all x2, starting transfers between devices, spread(): lax.all_to_all(x.reshape(devices, -1), GT, 0, 0, tiled=True)  16 us
    all_to_all x1, starting transfers between devices, shards(): lax.all_to_all(card.reshape(devices // 2, -1), GT, 0, 0, tiled=True, axis...  11.8 us
    pallas_call x1, Pallas kernels, shards(): pl.pallas_call(solve_first_kernel, in_specs=[SMEM] * 2 + [ANY] * 3 + [VME...  9.98 us
    ppermute x7, waiting for transfers between devices, both(): lax.ppermute(x, 'tile', outer_swap)  9.95 us
    pallas_call x2, Pallas kernels, shards(): call(coarse_kernel, coarse_out, [VMEM, VMEM, ANY], coarse_scratch, us=20)  8.78 us
    ppermute x7, starting transfers between devices, both(): lax.ppermute(x, 'tile', outer_swap)  8.49 us
    all_to_all x2, waiting for transfers between devices, spread(): lax.all_to_all(x.reshape(devices, -1), GT, 0, 0, tiled=True)  7.88 us
  transfers between devices with their start and end apart: 18, of which 10 were waited for; matrix products, arithmetic and copies ran while one was open for 0% of the time, Pallas kernels for 15%

profile of v8, /device:TPU:1, one launch (start us, length us, event | category | flops | bytes accessed | tf_op | source)
XLA Modules:
  0.0 123.7 jit_solution(4510553325143088450)
XLA Ops:
  0.7 2.9 %shard_map.94 = (f32[25,8,128]{2,1,0:T(8,128)S(1)}, s32[16,128]{1,0:T(8,128)S(1)}) custom-call(s32[1]{0:T(128)} %bitcast.core, f32[8,8,384]{2,1,0:T(8,128)} %loads_ref.1, s32[8,8]{1,0:T(8,128)} %index_ref.1, s32[8,12]{1,0:T(8,128)} %partner_ref.1, f32[8,384,384]{2,1,0:T(8,128)} %inverse_ref.7), custom_call_target="tpu_custom_call" | custom-call | flops 2000000000 | bytes 12000000 | tf_op jit(solution)/shard_map/pallas_call | solution.py:449
  3.6 2.7 %collective-permute-start.1 = (f32[25,8,128]{2,1,0:T(8,128)S(1)}, f32[25,8,128]{2,1,0:T(8,128)S(1)}, u32[]{:S(2)}, u32[]{:S(2)}) collective-permute-start(f32[25,8,128]{2,1,0:T(8,128)S(1)} %get-tuple-element.33.x_ref.ix_ref), channel_id=1, source_target_pairs={{0,31},{1,2},{2,1},{3,4},{4,3},{5,6},{6,5},{7,8},{8,7},{9,10},{10,... | collective-permute-start | bytes 307208 | tf_op jit(solution)/shard_map/ppermute | solution.py:437
  6.3 3.6 %collective-permute-start = (f32[25,8,128]{2,1,0:T(8,128)S(1)}, f32[25,8,128]{2,1,0:T(8,128)S(1)}, u32[]{:S(2)}, u32[]{:S(2)}) collective-permute-start(f32[25,8,128]{2,1,0:T(8,128)S(1)} %get-tuple-element.33.x_ref.ix_ref), channel_id=1, source_target_pairs={{0,1},{1,0},{2,3},{3,2},{4,5},{5,4},{6,7},{7,6},{8,9},{9,8},{10,11... | collective-permute-start | bytes 307208 | tf_op jit(solution)/shard_map/ppermute | solution.py:437
  9.8 0.9 collective-permute-done.a_ref.ia_ref
  10.8 2.1 %shard_map.95 = (f32[24,8,128]{2,1,0:T(8,128)S(1)}, f32[2368,128]{1,0:T(8,128)}) custom-call(s32[16,128]{1,0:T(8,128)S(1)} %get-tuple-element.32.table, f32[25,8,128]{2,1,0:T(8,128)S(1)} %collective-permute-done.a_ref.ia_ref, f32[25,8,128]{2,1,0:T(8,128)S(1)} %get-tuple-element.33.x_ref.ix_ref, f32[25,8,128]{2,1,0:T(8,128)S(1)} %collective-permute-done.1.b_ref.ib_ref, ...), custom_call_target="tpu_custom_call" | custom-call | flops 1000000000 | bytes 6000000 | tf_op jit(solution)/shard_map/pallas_call | solution.py:473
  12.9 11.8 %all-to-all-start = ((f32[64,1,4736]{2,1,0:T(1,128)}), f32[64,1,4736]{2,1,0:T(1,128)S(1)}, u32[]{:S(2)}, u32[]{:S(2)}) async-start(f32[64,1,4736]{2,1,0:T(1,128)} %bitcast.1), calls=%async_computation | async-start | bytes 2424832 | tf_op jit(solution)/shard_map/all_to_all | solution.py:476
  24.7 0.1 collective-permute-start.5
  24.8 4.7 %collective-permute-start.4 = (f32[8,8,384]{2,1,0:T(8,128)S(1)}, f32[8,8,384]{2,1,0:T(8,128)S(1)}, u32[]{:S(2)}, u32[]{:S(2)}) collective-permute-start(f32[8,8,384]{2,1,0:T(8,128)S(1)} %copy-done), channel_id=1, source_target_pairs={{0,1},{1,0},{2,3},{3,2},{4,5},{5,4},{6,7},{7,6},{8,9},{9,8},{10,11... | collective-permute-start | bytes 294920 | tf_op jit(solution)/shard_map/ppermute | solution.py:437
  29.6 2.8 %shard_map.96.x_ref = f32[24,8,128]{2,1,0:T(8,128)S(1)} custom-call(f32[24,8,128]{2,1,0:T(8,128)S(1)} %get-tuple-element.35.x_ref.r0_ref, f32[8,384,384]{2,1,0:T(8,128)} %source_ref.3), custom_call_target="tpu_custom_call" | custom-call | flops 1500000000 | bytes 9000000 | tf_op jit(solution)/shard_map/pallas_call | solution.py:469
  32.3 0.1 collective-permute-start.3
  32.4 1.0 collective-permute-start.2
  33.4 5.6 %collective-permute-done.5.bm_ref = f32[8,8,384]{2,1,0:T(8,128)S(1)} collective-permute-done((f32[8,8,384]{2,1,0:T(8,128)S(1)}, f32[8,8,384]{2,1,0:T(8,128)S(1)}, u32[]{:S(2)}, u32[]{:S(2)}) %collective-permute-start.5) | collective-permute-done | bytes 98336 | tf_op jit(solution)/shard_map/ppermute | solution.py:437
  39.0 0.0 collective-permute-done.4.am_ref
  39.0 1.5 %collective-permute-done.3.b_ref = f32[24,8,128]{2,1,0:T(8,128)S(1)} collective-permute-done((f32[24,8,128]{2,1,0:T(8,128)S(1)}, f32[24,8,128]{2,1,0:T(8,128)S(1)}, u32[]{:S(2)}, u32[]{:S(2)}) %collective-permute-start.3) | collective-permute-done | bytes 98336 | tf_op jit(solution)/shard_map/ppermute | solution.py:437
  40.5 0.0 collective-permute-done.2.a_ref
  40.5 4.0 %all-to-all-done = f32[64,1,4736]{2,1,0:T(1,128)S(1)} async-done(((f32[64,1,4736]{2,1,0:T(1,128)}), f32[64,1,4736]{2,1,0:T(1,128)S(1)}, u32[]{:S(2)}, u32[]{:S(2)}) %all-to-all-start) | async-done | bytes 1212448 | tf_op jit(solution)/shard_map/all_to_all | solution.py:476
  44.5 2.9 %collective-permute-done.6.other_ref = f32[2368,128]{1,0:T(8,128)S(1)} collective-permute-done((f32[2368,128]{1,0:T(8,128)S(1)}, f32[2368,128]{1,0:T(8,128)S(1)}, u32[]{:S(2)}, u32[]{:S(2)}) %collective-permute-start.6) | collective-permute-done | bytes 1212448 | tf_op jit(solution)/shard_map/ppermute | solution.py:483
  47.4 10.0 %shard_map.97 = (f32[24,8,128]{2,1,0:T(8,128)S(1)}, f32[24,8,128]{2,1,0:T(8,128)S(1)}, bf16[8,384,1024]{2,1,0:T(8,128)(2,1)}) custom-call(s32[1]{0:T(128)} %bitcast.core, s32[16,128]{1,0:T(8,128)S(1)} %get-tuple-element.32.table, f32[25,8,128]{2,1,0:T(8,128)S(1)} %collective-permute-done.a_ref.ia_ref, f32[25,8,128]{2,1,0:T(8,128)S(1)} %get-tuple-element.33.x_ref.ix_ref, ...), custom_call_target="tpu_custom_call" | custom-call | flops 4000000000 | bytes 20000000 | tf_op jit(solution)/shard_map/pallas_call | solution.py:484
  57.4 1.4 %collective-permute-start.8 = (f32[24,8,128]{2,1,0:T(8,128)S(1)}, f32[24,8,128]{2,1,0:T(8,128)S(1)}, u32[]{:S(2)}, u32[]{:S(2)}) collective-permute-start(f32[24,8,128]{2,1,0:T(8,128)S(1)} %get-tuple-element.43.after_ref.x_ref), channel_id=1, source_target_pairs={{0,31},{1,2},{2,1},{3,4},{4,3},{5,6},{6,5},{7,8},{8,7},{9,10},{10,... | collective-permute-start | bytes 294920 | tf_op jit(solution)/shard_map/ppermute | solution.py:437
  58.8 0.0 collective-permute-start.7
  58.8 2.4 %shard_map.98.schur_ref = f32[8,384,384]{2,1,0:T(8,128)S(1)} custom-call(f32[24,8,128]{2,1,0:T(8,128)S(1)} %get-tuple-element.43.after_ref.x_ref, f32[8,384,384]{2,1,0:T(8,128)} %source_ref.3), custom_call_target="tpu_custom_call" | custom-call | flops 1000000000 | bytes 6000000 | tf_op jit(solution)/shard_map/pallas_call | solution.py:509
  61.1 0.4 collective-permute-done.8.b_ref
  61.5 0.0 collective-permute-done.7.a_ref
  61.5 2.3 %shard_map.99 = (f32[24,8,128]{2,1,0:T(8,128)S(1)}, f32[640,128]{1,0:T(8,128)}, f32[24,8,128]{2,1,0:T(8,128)S(1)}) custom-call(s32[16,128]{1,0:T(8,128)S(1)} %get-tuple-element.32.table, f32[24,8,128]{2,1,0:T(8,128)S(1)} %collective-permute-done.7.a_ref, f32[24,8,128]{2,1,0:T(8,128)S(1)} %get-tuple-element.43.after_ref.x_ref, ...), custom_call_target="tpu_custom_call" | custom-call | flops 1500000000 | bytes 9000000 | tf_op jit(solution)/shard_map/pallas_call | solution.py:516
  63.8 7.5 %all-to-all-start.1 = ((f32[128,1,640]{2,1,0:T(1,128)}), f32[128,1,640]{2,1,0:T(1,128)S(1)}, u32[]{:S(2)}, u32[]{:S(2)}) async-start(f32[128,1,640]{2,1,0:T(1,128)} %bitcast.3), calls=%async_computation.1 | async-start | bytes 655360 | tf_op jit(solution)/shard_map/all_to_all | solution.py:466
  71.4 1.7 %collective-permute-start.9 = (f32[24,8,128]{2,1,0:T(8,128)S(1)}, f32[24,8,128]{2,1,0:T(8,128)S(1)}, u32[]{:S(2)}, u32[]{:S(2)}) collective-permute-start(f32[24,8,128]{2,1,0:T(8,128)S(1)} %get-tuple-element.46.x_ref), channel_id=1, source_target_pairs={{0,31},{1,2},{2,1},{3,4},{4,3},{5,6},{6,5},{7,8},{8,7},{9,10},{10,... | collective-permute-start | bytes 294920 | tf_op jit(solution)/shard_map/ppermute | solution.py:437
  73.1 3.6 %collective-permute-start.10 = (f32[24,8,128]{2,1,0:T(8,128)S(1)}, f32[24,8,128]{2,1,0:T(8,128)S(1)}, u32[]{:S(2)}, u32[]{:S(2)}) collective-permute-start(f32[24,8,128]{2,1,0:T(8,128)S(1)} %get-tuple-element.46.x_ref), channel_id=1, source_target_pairs={{0,1},{1,0},{2,3},{3,2},{4,5},{5,4},{6,7},{7,6},{8,9},{9,8},{10,11... | collective-permute-start | bytes 294920 | tf_op jit(solution)/shard_map/ppermute | solution.py:437
  76.7 1.2 %collective-permute-done.9.after_ref.b_ref = f32[24,8,128]{2,1,0:T(8,128)S(1)} collective-permute-done((f32[24,8,128]{2,1,0:T(8,128)S(1)}, f32[24,8,128]{2,1,0:T(8,128)S(1)}, u32[]{:S(2)}, u32[]{:S(2)}) %collective-permute-start.9) | collective-permute-done | bytes 98336 | tf_op jit(solution)/shard_map/ppermute | solution.py:437
  77.9 1.4 %shard_map.100.kept_ref = bf16[2,384,1024]{2,1,0:T(8,128)(2,1)S(1)} custom-call(f32[24,8,128]{2,1,0:T(8,128)S(1)} %collective-permute-done.9.after_ref.b_ref, bf16[8,384,1024]{2,1,0:T(8,128)(2,1)} %get-tuple-element.47.weights_ref), custom_call_target="tpu_custom_call" | custom-call | flops 1000000000 | bytes 6000000 | tf_op jit(solution)/shard_map/pallas_call | solution.py:512
  79.4 3.9 %all-to-all-done.1 = f32[128,1,640]{2,1,0:T(1,128)S(1)} async-done(((f32[128,1,640]{2,1,0:T(1,128)}), f32[128,1,640]{2,1,0:T(1,128)S(1)}, u32[]{:S(2)}, u32[]{:S(2)}) %all-to-all-start.1) | async-done | bytes 327712 | tf_op jit(solution)/shard_map/all_to_all | solution.py:466
  83.3 4.4 %shard_map.101 = (f32[384,16]{1,0:T(8,128)S(1)}, f32[8,128]{1,0:T(8,128)S(1)}) custom-call(f32[640,128]{1,0:T(8,128)S(1)} %bitcast.11, bf16[2,384,1024]{2,1,0:T(8,128)(2,1)S(1)} %shard_map.100.kept_ref, bf16[8,384,1024]{2,1,0:T(8,128)(2,1)} %get-tuple-element.47.weights_ref), custom_call_target="tpu_custom_call" | custom-call | flops 10000000000 | bytes 60000000 | tf_op jit(solution)/shard_map/pallas_call | solution.py:520
  87.7 0.0 collective-permute-done.10.a_ref
  87.7 2.0 %shard_map.102 = (f32[24,8,128]{2,1,0:T(8,128)S(1)}, f32[24,8,128]{2,1,0:T(8,128)S(1)}, f32[24,8,128]{2,1,0:T(8,128)S(1)}, f32[3,8,128]{2,1,0:T(8,128)S(1)}, f32[24,8,128]{2,1,0:T(8,128)S(1)}) custom-call(s32[16,128]{1,0:T(8,128)S(1)} %get-tuple-element.32.table, f32[384,16]{1,0:T(8,128)S(1)} %get-tuple-element.48.out_ref, ...), custom_call_target="tpu_custom_call" | custom-call | flops 1500000000 | bytes 9000000 | tf_op jit(solution)/shard_map/pallas_call | solution.py:521
  89.7 0.9 collective-permute-start.12
  90.5 1.7 %collective-permute-start.11 = (f32[24,8,128]{2,1,0:T(8,128)S(1)}, f32[24,8,128]{2,1,0:T(8,128)S(1)}, u32[]{:S(2)}, u32[]{:S(2)}) collective-permute-start(f32[24,8,128]{2,1,0:T(8,128)S(1)} %get-tuple-element.51.after_ref.x_ref), channel_id=1, source_target_pairs={{0,1},{1,0},{2,3},{3,2},{4,5},{5,4},{6,7},{7,6},{8,9},{9,8},{10,11... | collective-permute-start | bytes 294920 | tf_op jit(solution)/shard_map/ppermute | solution.py:437
  92.3 2.4 %shard_map.103.schur_ref = f32[8,384,384]{2,1,0:T(8,128)S(1)} custom-call(f32[24,8,128]{2,1,0:T(8,128)S(1)} %get-tuple-element.51.after_ref.x_ref, f32[8,384,384]{2,1,0:T(8,128)} %source_ref.3), custom_call_target="tpu_custom_call" | custom-call | flops 1000000000 | bytes 6000000 | tf_op jit(solution)/shard_map/pallas_call | solution.py:509
  94.7 0.0 collective-permute-done.12.b_ref
  94.7 0.0 collective-permute-done.11.a_ref
  94.7 2.3 %shard_map.104 = (f32[24,8,128]{2,1,0:T(8,128)S(1)}, f32[640,128]{1,0:T(8,128)}, f32[24,8,128]{2,1,0:T(8,128)S(1)}) custom-call(s32[16,128]{1,0:T(8,128)S(1)} %get-tuple-element.32.table, f32[24,8,128]{2,1,0:T(8,128)S(1)} %collective-permute-done.11.a_ref, f32[24,8,128]{2,1,0:T(8,128)S(1)} %get-tuple-element.51.after_ref.x_ref, ...), custom_call_target="tpu_custom_call" | custom-call | flops 1500000000 | bytes 9000000 | tf_op jit(solution)/shard_map/pallas_call | solution.py:525
  97.0 8.5 %all-to-all-start.2 = ((f32[128,1,640]{2,1,0:T(1,128)}), f32[128,1,640]{2,1,0:T(1,128)S(1)}, u32[]{:S(2)}, u32[]{:S(2)}) async-start(f32[128,1,640]{2,1,0:T(1,128)} %bitcast.5), calls=%async_computation.2 | async-start | bytes 655360 | tf_op jit(solution)/shard_map/all_to_all | solution.py:466
  105.5 1.7 %collective-permute-start.13 = (f32[24,8,128]{2,1,0:T(8,128)S(1)}, f32[24,8,128]{2,1,0:T(8,128)S(1)}, u32[]{:S(2)}, u32[]{:S(2)}) collective-permute-start(f32[24,8,128]{2,1,0:T(8,128)S(1)} %get-tuple-element.55.x_ref), channel_id=1, source_target_pairs={{0,31},{1,2},{2,1},{3,4},{4,3},{5,6},{6,5},{7,8},{8,7},{9,10},{10,... | collective-permute-start | bytes 294920 | tf_op jit(solution)/shard_map/ppermute | solution.py:437
  107.2 3.6 %collective-permute-start.14 = (f32[24,8,128]{2,1,0:T(8,128)S(1)}, f32[24,8,128]{2,1,0:T(8,128)S(1)}, u32[]{:S(2)}, u32[]{:S(2)}) collective-permute-start(f32[24,8,128]{2,1,0:T(8,128)S(1)} %get-tuple-element.55.x_ref), channel_id=1, source_target_pairs={{0,1},{1,0},{2,3},{3,2},{4,5},{5,4},{6,7},{7,6},{8,9},{9,8},{10,11... | collective-permute-start | bytes 294920 | tf_op jit(solution)/shard_map/ppermute | solution.py:437
  110.8 1.2 %collective-permute-done.13.after_ref.b_ref = f32[24,8,128]{2,1,0:T(8,128)S(1)} collective-permute-done((f32[24,8,128]{2,1,0:T(8,128)S(1)}, f32[24,8,128]{2,1,0:T(8,128)S(1)}, u32[]{:S(2)}, u32[]{:S(2)}) %collective-permute-start.13) | collective-permute-done | bytes 98336 | tf_op jit(solution)/shard_map/ppermute | solution.py:437
  112.0 1.4 %shard_map.105.kept_ref = bf16[2,384,1024]{2,1,0:T(8,128)(2,1)S(1)} custom-call(f32[24,8,128]{2,1,0:T(8,128)S(1)} %collective-permute-done.13.after_ref.b_ref, bf16[8,384,1024]{2,1,0:T(8,128)(2,1)} %get-tuple-element.47.weights_ref), custom_call_target="tpu_custom_call" | custom-call | flops 1000000000 | bytes 6000000 | tf_op jit(solution)/shard_map/pallas_call | solution.py:512
  113.4 4.0 %all-to-all-done.2 = f32[128,1,640]{2,1,0:T(1,128)S(1)} async-done(((f32[128,1,640]{2,1,0:T(1,128)}), f32[128,1,640]{2,1,0:T(1,128)S(1)}, u32[]{:S(2)}, u32[]{:S(2)}) %all-to-all-start.2) | async-done | bytes 327712 | tf_op jit(solution)/shard_map/all_to_all | solution.py:466
  117.4 4.4 %shard_map.106 = (f32[384,16]{1,0:T(8,128)S(1)}, f32[8,128]{1,0:T(8,128)S(1)}) custom-call(f32[640,128]{1,0:T(8,128)S(1)} %bitcast.12, bf16[2,384,1024]{2,1,0:T(8,128)(2,1)S(1)} %shard_map.105.kept_ref, bf16[8,384,1024]{2,1,0:T(8,128)(2,1)} %get-tuple-element.47.weights_ref), custom_call_target="tpu_custom_call" | custom-call | flops 10000000000 | bytes 60000000 | tf_op jit(solution)/shard_map/pallas_call | solution.py:529
  121.8 0.0 collective-permute-done.14.a_ref
  121.8 1.9 %shard_map.107 = (f32[8,8,384]{2,1,0:T(8,128)}, f32[8,8,384]{2,1,0:T(8,128)}, f32[8,8,384]{2,1,0:T(8,128)}) custom-call(s32[16,128]{1,0:T(8,128)S(1)} %get-tuple-element.32.table, f32[384,16]{1,0:T(8,128)S(1)} %get-tuple-element.56.out_ref, f32[8,128]{1,0:T(8,128)S(1)} %get-tuple-element.57.sums_ref, f32[8,8,384]{2,1,0:T(8,128)S(1)} %collective-permute-done.4.am_ref, ...), custom_call_target="tpu_custom_call" | custom-call | flops 1000000000 | bytes 6000000 | tf_op jit(solution)/shard_map/pallas_call | solution.py:531
  (11 shorter events, 0.0 us)
Async XLA Ops:
  0.6 10.1 %copy-start = (f32[8,8,384]{2,1,0:T(8,128)S(1)}, f32[8,8,384]{2,1,0:T(8,128)}, u32[]{:S(2)}) copy-start(f32[8,8,384]{2,1,0:T(8,128)} %m_ref.2) | copy-start | bytes 294916
  0.6 10.1 %copy-start.1 = (f32[64,64]{1,0:T(8,128)S(1)}, f32[64,64]{1,0:T(8,128)}, u32[]{:S(2)}) copy-start(f32[64,64]{1,0:T(8,128)} %inverse_ref.5) | copy-start | bytes 49156
  3.6 6.2 %collective-permute-start.1 = (f32[25,8,128]{2,1,0:T(8,128)S(1)}, f32[25,8,128]{2,1,0:T(8,128)S(1)}, u32[]{:S(2)}, u32[]{:S(2)}) collective-permute-start(f32[25,8,128]{2,1,0:T(8,128)S(1)} %get-tuple-element.33.x_ref.ix_ref), channel_id=1, source_target_pairs={{0,31},{1,2},{2,1},{3,4},{4,3},{5,6},{6,5},{7,8},{8,7},{9,10},{10,... | collective-permute-start | bytes 307208 | tf_op jit(solution)/shard_map/ppermute | solution.py:437
  6.3 4.5 %collective-permute-start = (f32[25,8,128]{2,1,0:T(8,128)S(1)}, f32[25,8,128]{2,1,0:T(8,128)S(1)}, u32[]{:S(2)}, u32[]{:S(2)}) collective-permute-start(f32[25,8,128]{2,1,0:T(8,128)S(1)} %get-tuple-element.33.x_ref.ix_ref), channel_id=1, source_target_pairs={{0,1},{1,0},{2,3},{3,2},{4,5},{5,4},{6,7},{7,6},{8,9},{9,8},{10,11... | collective-permute-start | bytes 307208 | tf_op jit(solution)/shard_map/ppermute | solution.py:437
  12.9 31.6 %all-to-all-start = ((f32[64,1,4736]{2,1,0:T(1,128)}), f32[64,1,4736]{2,1,0:T(1,128)S(1)}, u32[]{:S(2)}, u32[]{:S(2)}) async-start(f32[64,1,4736]{2,1,0:T(1,128)} %bitcast.1), calls=%async_computation | async-start | bytes 2424832 | tf_op jit(solution)/shard_map/all_to_all | solution.py:476
  24.7 14.2 %collective-permute-start.5 = (f32[8,8,384]{2,1,0:T(8,128)S(1)}, f32[8,8,384]{2,1,0:T(8,128)S(1)}, u32[]{:S(2)}, u32[]{:S(2)}) collective-permute-start(f32[8,8,384]{2,1,0:T(8,128)S(1)} %copy-done), channel_id=1, source_target_pairs={{0,31},{1,2},{2,1},{3,4},{4,3},{5,6},{6,5},{7,8},{8,7},{9,10},{10,... | collective-permute-start | bytes 294920 | tf_op jit(solution)/shard_map/ppermute | solution.py:437
  24.8 14.1 %collective-permute-start.4 = (f32[8,8,384]{2,1,0:T(8,128)S(1)}, f32[8,8,384]{2,1,0:T(8,128)S(1)}, u32[]{:S(2)}, u32[]{:S(2)}) collective-permute-start(f32[8,8,384]{2,1,0:T(8,128)S(1)} %copy-done), channel_id=1, source_target_pairs={{0,1},{1,0},{2,3},{3,2},{4,5},{5,4},{6,7},{7,6},{8,9},{9,8},{10,11... | collective-permute-start | bytes 294920 | tf_op jit(solution)/shard_map/ppermute | solution.py:437
  32.3 8.1 %collective-permute-start.3 = (f32[24,8,128]{2,1,0:T(8,128)S(1)}, f32[24,8,128]{2,1,0:T(8,128)S(1)}, u32[]{:S(2)}, u32[]{:S(2)}) collective-permute-start(f32[24,8,128]{2,1,0:T(8,128)S(1)} %shard_map.96.x_ref), channel_id=1, source_target_pairs={{0,31},{1,2},{2,1},{3,4},{4,3},{5,6},{6,5},{7,8},{8,7},{9,10},{10,... | collective-permute-start | bytes 294920 | tf_op jit(solution)/shard_map/ppermute | solution.py:437
  32.4 8.0 %collective-permute-start.2 = (f32[24,8,128]{2,1,0:T(8,128)S(1)}, f32[24,8,128]{2,1,0:T(8,128)S(1)}, u32[]{:S(2)}, u32[]{:S(2)}) collective-permute-start(f32[24,8,128]{2,1,0:T(8,128)S(1)} %shard_map.96.x_ref), channel_id=1, source_target_pairs={{0,1},{1,0},{2,3},{3,2},{4,5},{5,4},{6,7},{7,6},{8,9},{9,8},{10,11... | collective-permute-start | bytes 294920 | tf_op jit(solution)/shard_map/ppermute | solution.py:437
  44.5 2.9 %collective-permute-start.6 = (f32[2368,128]{1,0:T(8,128)S(1)}, f32[2368,128]{1,0:T(8,128)S(1)}, u32[]{:S(2)}, u32[]{:S(2)}) collective-permute-start(f32[2368,128]{1,0:T(8,128)S(1)} %bitcast.9), channel_id=1, source_target_pairs={{0,1},{1,0},{2,3},{3,2},{4,5},{5,4},{6,7},{7,6},{8,9},{9,8},{10,11... | collective-permute-start | bytes 3637256 | tf_op jit(solution)/shard_map/ppermute | solution.py:483
  57.4 4.1 %collective-permute-start.8 = (f32[24,8,128]{2,1,0:T(8,128)S(1)}, f32[24,8,128]{2,1,0:T(8,128)S(1)}, u32[]{:S(2)}, u32[]{:S(2)}) collective-permute-start(f32[24,8,128]{2,1,0:T(8,128)S(1)} %get-tuple-element.43.after_ref.x_ref), channel_id=1, source_target_pairs={{0,31},{1,2},{2,1},{3,4},{4,3},{5,6},{6,5},{7,8},{8,7},{9,10},{10,... | collective-permute-start | bytes 294920 | tf_op jit(solution)/shard_map/ppermute | solution.py:437
  58.8 2.8 %collective-permute-start.7 = (f32[24,8,128]{2,1,0:T(8,128)S(1)}, f32[24,8,128]{2,1,0:T(8,128)S(1)}, u32[]{:S(2)}, u32[]{:S(2)}) collective-permute-start(f32[24,8,128]{2,1,0:T(8,128)S(1)} %get-tuple-element.43.after_ref.x_ref), channel_id=1, source_target_pairs={{0,1},{1,0},{2,3},{3,2},{4,5},{5,4},{6,7},{7,6},{8,9},{9,8},{10,11... | collective-permute-start | bytes 294920 | tf_op jit(solution)/shard_map/ppermute | solution.py:437
  63.8 19.4 %all-to-all-start.1 = ((f32[128,1,640]{2,1,0:T(1,128)}), f32[128,1,640]{2,1,0:T(1,128)S(1)}, u32[]{:S(2)}, u32[]{:S(2)}) async-start(f32[128,1,640]{2,1,0:T(1,128)} %bitcast.3), calls=%async_computation.1 | async-start | bytes 655360 | tf_op jit(solution)/shard_map/all_to_all | solution.py:466
  71.4 6.5 %collective-permute-start.9 = (f32[24,8,128]{2,1,0:T(8,128)S(1)}, f32[24,8,128]{2,1,0:T(8,128)S(1)}, u32[]{:S(2)}, u32[]{:S(2)}) collective-permute-start(f32[24,8,128]{2,1,0:T(8,128)S(1)} %get-tuple-element.46.x_ref), channel_id=1, source_target_pairs={{0,31},{1,2},{2,1},{3,4},{4,3},{5,6},{6,5},{7,8},{8,7},{9,10},{10,... | collective-permute-start | bytes 294920 | tf_op jit(solution)/shard_map/ppermute | solution.py:437
  73.1 14.6 %collective-permute-start.10 = (f32[24,8,128]{2,1,0:T(8,128)S(1)}, f32[24,8,128]{2,1,0:T(8,128)S(1)}, u32[]{:S(2)}, u32[]{:S(2)}) collective-permute-start(f32[24,8,128]{2,1,0:T(8,128)S(1)} %get-tuple-element.46.x_ref), channel_id=1, source_target_pairs={{0,1},{1,0},{2,3},{3,2},{4,5},{5,4},{6,7},{7,6},{8,9},{9,8},{10,11... | collective-permute-start | bytes 294920 | tf_op jit(solution)/shard_map/ppermute | solution.py:437
  77.9 9.8 %slice-start = ((s8[4718592]{0:T(1024)(128)(4,1)}), s8[524288]{0:T(1024)(128)(4,1)S(1)}, s32[]{:S(2)}) async-start(s8[4718592]{0:T(1024)(128)(4,1)} %bitcast.7), calls=%async_computation.3 | async-start | bytes 1048576
  83.3 4.5 %slice-start.1 = ((s8[4718592]{0:T(1024)(128)(4,1)}), s8[4194304]{0:T(1024)(128)(4,1)S(1)}, s32[]{:S(2)}) async-start(s8[4718592]{0:T(1024)(128)(4,1)} %bitcast.7), calls=%async_computation.4 | async-start | bytes 8388608
  89.7 5.0 %collective-permute-start.12 = (f32[24,8,128]{2,1,0:T(8,128)S(1)}, f32[24,8,128]{2,1,0:T(8,128)S(1)}, u32[]{:S(2)}, u32[]{:S(2)}) collective-permute-start(f32[24,8,128]{2,1,0:T(8,128)S(1)} %get-tuple-element.51.after_ref.x_ref), channel_id=1, source_target_pairs={{0,31},{1,2},{2,1},{3,4},{4,3},{5,6},{6,5},{7,8},{8,7},{9,10},{10,... | collective-permute-start | bytes 294920 | tf_op jit(solution)/shard_map/ppermute | solution.py:437
  90.5 4.1 %collective-permute-start.11 = (f32[24,8,128]{2,1,0:T(8,128)S(1)}, f32[24,8,128]{2,1,0:T(8,128)S(1)}, u32[]{:S(2)}, u32[]{:S(2)}) collective-permute-start(f32[24,8,128]{2,1,0:T(8,128)S(1)} %get-tuple-element.51.after_ref.x_ref), channel_id=1, source_target_pairs={{0,1},{1,0},{2,3},{3,2},{4,5},{5,4},{6,7},{7,6},{8,9},{9,8},{10,11... | collective-permute-start | bytes 294920 | tf_op jit(solution)/shard_map/ppermute | solution.py:437
  97.0 20.4 %all-to-all-start.2 = ((f32[128,1,640]{2,1,0:T(1,128)}), f32[128,1,640]{2,1,0:T(1,128)S(1)}, u32[]{:S(2)}, u32[]{:S(2)}) async-start(f32[128,1,640]{2,1,0:T(1,128)} %bitcast.5), calls=%async_computation.2 | async-start | bytes 655360 | tf_op jit(solution)/shard_map/all_to_all | solution.py:466
  105.5 6.5 %collective-permute-start.13 = (f32[24,8,128]{2,1,0:T(8,128)S(1)}, f32[24,8,128]{2,1,0:T(8,128)S(1)}, u32[]{:S(2)}, u32[]{:S(2)}) collective-permute-start(f32[24,8,128]{2,1,0:T(8,128)S(1)} %get-tuple-element.55.x_ref), channel_id=1, source_target_pairs={{0,31},{1,2},{2,1},{3,4},{4,3},{5,6},{6,5},{7,8},{8,7},{9,10},{10,... | collective-permute-start | bytes 294920 | tf_op jit(solution)/shard_map/ppermute | solution.py:437
  107.2 14.6 %collective-permute-start.14 = (f32[24,8,128]{2,1,0:T(8,128)S(1)}, f32[24,8,128]{2,1,0:T(8,128)S(1)}, u32[]{:S(2)}, u32[]{:S(2)}) collective-permute-start(f32[24,8,128]{2,1,0:T(8,128)S(1)} %get-tuple-element.55.x_ref), channel_id=1, source_target_pairs={{0,1},{1,0},{2,3},{3,2},{4,5},{5,4},{6,7},{7,6},{8,9},{9,8},{10,11... | collective-permute-start | bytes 294920 | tf_op jit(solution)/shard_map/ppermute | solution.py:437

commit v9 on v8

--- a/solution.py
+++ b/solution.py
@@ -479,7 +479,9 @@
     pooled = through(r0)
     ma, mb = both(corner_map)
     maps = (ma, corner_map, mb)
-    own_cards, pooled, maps = lax.optimization_barrier((own_cards, pooled, maps))
+    qa, q, qb = pooled
+    own_cards, q = lax.optimization_barrier((own_cards, q))
+    pooled = (qa, q, qb)
     other_cards = lax.ppermute(own_cards, "tile", inner_swap)
     z0, u, weights = pl.pallas_call(
         solve_first_kernel,
@@ -517,7 +519,7 @@
         table, ua, u, ub, corner_map, hold(u), r0, z0
     )
     qa, qb = both(q)
-    out, sums = call(coarse_kernel, coarse_out, [VMEM, VMEM, ANY], coarse_scratch, us=20)(spread(parts), keep(qb), weights)
+    out, sums = call(coarse_kernel, coarse_out, [VMEM, VMEM, ANY], coarse_scratch, us=20)(spread(parts), keep(q), weights)
     y0, r1, z1, scale, u = call(
         solve_second_kernel, [field, field, field, shape(3, 8, 128), field], [SMEM] + [VMEM] * 12, [pool], us=3
     )(table, out, sums, *maps, qa, q, qb, local_inverse, r0, z0, w0)
@@ -526,7 +528,7 @@
         table, ua, u, ub, corner_map, hold(u), r1, z1, z0, w0
     )
     qa, qb = both(q)
-    out, sums = call(coarse_kernel, coarse_out, [VMEM, VMEM, ANY], coarse_scratch, us=20)(spread(parts), keep(qb), weights)
+    out, sums = call(coarse_kernel, coarse_out, [VMEM, VMEM, ANY], coarse_scratch, us=20)(spread(parts), keep(q), weights)
     return tuple(
         call(solve_third_kernel, [shape(COUNT, CASES, WIDTH)] * 3, [SMEM] + [VMEM] * 15, [pool], us=2)(
             table, out, sums, *maps, qa, q, qb, scale, z0, w0, y0, r1, z1, v1

time: 124 us -> 129 us (1.040)
  waiting for transfers between devices: 25.7 us -> 28.9 us
  starting transfers between devices: 54.4 us -> 56.4 us
    all_to_all x1, waiting for transfers between devices: 4.04 us -> 16.6 us  [shards(): lax.all_to_all(card.reshape(devices // 2, -1), GT, 0, 0, tiled=True, axis...]
    ppermute x7, waiting for transfers between devices: 9.95 us -> 0.02 us  [both(): lax.ppermute(x, 'tile', outer_swap)]
    ppermute x7, starting transfers between devices: 18.1 us -> 22.4 us  [both(): lax.ppermute(x, 'tile', inner_swap)]
    ppermute x1, waiting for transfers between devices: 2.89 us -> 0.01 us  [shards(): other_cards = lax.ppermute(own_cards, 'tile', inner_swap)]
    all_to_all x2, waiting for transfers between devices: 7.88 us -> 10.4 us  [spread(): lax.all_to_all(x.reshape(devices, -1), GT, 0, 0, tiled=True)]
    all_to_all x2, starting transfers between devices: 16 us -> 13.6 us  [spread(): lax.all_to_all(x.reshape(devices, -1), GT, 0, 0, tiled=True)]
  transfers between devices with their start and end apart: 18 -> 18, of which waited for: 10 -> 5; matrix products, arithmetic and copies ran while one was open for 0% -> 0% of each run, Pallas kernels for 15% -> 15%
where the time goes in v9:
time: 129 us
  starting transfers between devices  56.4 us (44%)
  Pallas kernels  42.6 us (33%)
  waiting for transfers between devices  28.9 us (22%)
    ppermute x7, starting transfers between devices, both(): lax.ppermute(x, 'tile', inner_swap)  22.4 us
    all_to_all x1, waiting for transfers between devices, shards(): lax.all_to_all(card.reshape(devices // 2, -1), GT, 0, 0, tiled=True, axis...  16.6 us
    all_to_all x2, starting transfers between devices, spread(): lax.all_to_all(x.reshape(devices, -1), GT, 0, 0, tiled=True)  13.6 us
    all_to_all x1, starting transfers between devices, shards(): lax.all_to_all(card.reshape(devices // 2, -1), GT, 0, 0, tiled=True, axis...  11.8 us
    all_to_all x2, waiting for transfers between devices, spread(): lax.all_to_all(x.reshape(devices, -1), GT, 0, 0, tiled=True)  10.4 us
    pallas_call x1, Pallas kernels, shards(): pl.pallas_call(solve_first_kernel, in_specs=[SMEM] * 2 + [ANY] * 3 + [VME...  9.98 us
    pallas_call x2, Pallas kernels, shards(): call(coarse_kernel, coarse_out, [VMEM, VMEM, ANY], coarse_scratch, us=20)  8.78 us
    ppermute x7, starting transfers between devices, both(): lax.ppermute(x, 'tile', outer_swap)  8.52 us
  transfers between devices with their start and end apart: 18, of which 5 were waited for; matrix products, arithmetic and copies ran while one was open for 0% of the time, Pallas kernels for 15%

profile of v9, /device:TPU:1, one launch (start us, length us, event | category | flops | bytes accessed | tf_op | source)
XLA Modules:
  0.0 128.8 jit_solution(2013534480273991394)
XLA Ops:
  0.7 2.9 %shard_map.94 = (f32[25,8,128]{2,1,0:T(8,128)S(1)}, s32[16,128]{1,0:T(8,128)S(1)}) custom-call(s32[1]{0:T(128)} %bitcast.core, f32[8,8,384]{2,1,0:T(8,128)} %loads_ref.1, s32[8,8]{1,0:T(8,128)} %index_ref.1, s32[8,12]{1,0:T(8,128)} %partner_ref.1, f32[8,384,384]{2,1,0:T(8,128)} %inverse_ref.7), custom_call_target="tpu_custom_call" | custom-call | flops 2000000000 | bytes 12000000 | tf_op jit(solution)/shard_map/pallas_call | solution.py:449
  3.6 2.7 %collective-permute-start.1 = (f32[25,8,128]{2,1,0:T(8,128)S(1)}, f32[25,8,128]{2,1,0:T(8,128)S(1)}, u32[]{:S(2)}, u32[]{:S(2)}) collective-permute-start(f32[25,8,128]{2,1,0:T(8,128)S(1)} %get-tuple-element.28.x_ref.ix_ref), channel_id=1, source_target_pairs={{0,31},{1,2},{2,1},{3,4},{4,3},{5,6},{6,5},{7,8},{8,7},{9,10},{10,... | collective-permute-start | bytes 307208 | tf_op jit(solution)/shard_map/ppermute | solution.py:437
  6.3 3.6 %collective-permute-start = (f32[25,8,128]{2,1,0:T(8,128)S(1)}, f32[25,8,128]{2,1,0:T(8,128)S(1)}, u32[]{:S(2)}, u32[]{:S(2)}) collective-permute-start(f32[25,8,128]{2,1,0:T(8,128)S(1)} %get-tuple-element.28.x_ref.ix_ref), channel_id=1, source_target_pairs={{0,1},{1,0},{2,3},{3,2},{4,5},{5,4},{6,7},{7,6},{8,9},{9,8},{10,11... | collective-permute-start | bytes 307208 | tf_op jit(solution)/shard_map/ppermute | solution.py:437
  9.8 0.0 collective-permute-done.1.b_ref.ib_ref
  9.8 0.9 collective-permute-done.a_ref.ia_ref
  10.8 2.1 %shard_map.95 = (f32[24,8,128]{2,1,0:T(8,128)S(1)}, f32[2368,128]{1,0:T(8,128)}) custom-call(s32[16,128]{1,0:T(8,128)S(1)} %get-tuple-element.27.table, f32[25,8,128]{2,1,0:T(8,128)S(1)} %collective-permute-done.a_ref.ia_ref, f32[25,8,128]{2,1,0:T(8,128)S(1)} %get-tuple-element.28.x_ref.ix_ref, f32[25,8,128]{2,1,0:T(8,128)S(1)} %collective-permute-done.1.b_ref.ib_ref, ...), custom_call_target="tpu_custom_call" | custom-call | flops 1000000000 | bytes 6000000 | tf_op jit(solution)/shard_map/pallas_call | solution.py:473
  12.9 11.8 %all-to-all-start = ((f32[64,1,4736]{2,1,0:T(1,128)}), f32[64,1,4736]{2,1,0:T(1,128)S(1)}, u32[]{:S(2)}, u32[]{:S(2)}) async-start(f32[64,1,4736]{2,1,0:T(1,128)} %bitcast.1), calls=%async_computation | async-start | bytes 2424832 | tf_op jit(solution)/shard_map/all_to_all | solution.py:476
  24.7 2.8 %shard_map.96.x_ref = f32[24,8,128]{2,1,0:T(8,128)S(1)} custom-call(f32[24,8,128]{2,1,0:T(8,128)S(1)} %get-tuple-element.30.x_ref.r0_ref, f32[8,384,384]{2,1,0:T(8,128)} %source_ref.3), custom_call_target="tpu_custom_call" | custom-call | flops 1500000000 | bytes 9000000 | tf_op jit(solution)/shard_map/pallas_call | solution.py:469
  27.5 16.6 %all-to-all-done = f32[64,1,4736]{2,1,0:T(1,128)S(1)} async-done(((f32[64,1,4736]{2,1,0:T(1,128)}), f32[64,1,4736]{2,1,0:T(1,128)S(1)}, u32[]{:S(2)}, u32[]{:S(2)}) %all-to-all-start) | async-done | bytes 1212448 | tf_op jit(solution)/shard_map/all_to_all | solution.py:476
  44.2 0.0 collective-permute-start.2
  44.2 0.7 collective-permute-start.4
  44.9 0.3 collective-permute-start.3
  45.1 0.8 collective-permute-start.6
  45.9 3.8 %collective-permute-start.5 = (f32[24,8,128]{2,1,0:T(8,128)S(1)}, f32[24,8,128]{2,1,0:T(8,128)S(1)}, u32[]{:S(2)}, u32[]{:S(2)}) collective-permute-start(f32[24,8,128]{2,1,0:T(8,128)S(1)} %shard_map.96.x_ref), channel_id=1, source_target_pairs={{0,1},{1,0},{2,3},{3,2},{4,5},{5,4},{6,7},{7,6},{8,9},{9,8},{10,11... | collective-permute-start | bytes 294920 | tf_op jit(solution)/shard_map/ppermute | solution.py:437
  49.8 0.0 collective-permute-done.4.bm_ref
  49.8 0.0 collective-permute-done.3.am_ref
  49.8 0.0 collective-permute-done.6.b_ref
  49.8 0.9 collective-permute-done.5.a_ref
  50.7 0.0 collective-permute-done.2.other_ref
  50.7 10.0 %shard_map.97 = (f32[24,8,128]{2,1,0:T(8,128)S(1)}, f32[24,8,128]{2,1,0:T(8,128)S(1)}, bf16[8,384,1024]{2,1,0:T(8,128)(2,1)}) custom-call(s32[1]{0:T(128)} %bitcast.core, s32[16,128]{1,0:T(8,128)S(1)} %get-tuple-element.27.table, f32[25,8,128]{2,1,0:T(8,128)S(1)} %collective-permute-done.a_ref.ia_ref, f32[25,8,128]{2,1,0:T(8,128)S(1)} %get-tuple-element.28.x_ref.ix_ref, ...), custom_call_target="tpu_custom_call" | custom-call | flops 4000000000 | bytes 20000000 | tf_op jit(solution)/shard_map/pallas_call | solution.py:486
  60.7 0.1 collective-permute-start.8
  60.8 6.4 %collective-permute-start.7 = (f32[24,8,128]{2,1,0:T(8,128)S(1)}, f32[24,8,128]{2,1,0:T(8,128)S(1)}, u32[]{:S(2)}, u32[]{:S(2)}) collective-permute-start(f32[24,8,128]{2,1,0:T(8,128)S(1)} %get-tuple-element.33.after_ref.x_ref), channel_id=1, source_target_pairs={{0,1},{1,0},{2,3},{3,2},{4,5},{5,4},{6,7},{7,6},{8,9},{9,8},{10,11... | collective-permute-start | bytes 294920 | tf_op jit(solution)/shard_map/ppermute | solution.py:437
  67.2 2.4 %shard_map.98.schur_ref = f32[8,384,384]{2,1,0:T(8,128)S(1)} custom-call(f32[24,8,128]{2,1,0:T(8,128)S(1)} %get-tuple-element.33.after_ref.x_ref, f32[8,384,384]{2,1,0:T(8,128)} %source_ref.3), custom_call_target="tpu_custom_call" | custom-call | flops 1000000000 | bytes 6000000 | tf_op jit(solution)/shard_map/pallas_call | solution.py:511
  69.6 0.0 collective-permute-done.8.b_ref
  69.6 0.0 collective-permute-done.7.a_ref
  69.6 2.3 %shard_map.99 = (f32[24,8,128]{2,1,0:T(8,128)S(1)}, f32[640,128]{1,0:T(8,128)}, f32[24,8,128]{2,1,0:T(8,128)S(1)}) custom-call(s32[16,128]{1,0:T(8,128)S(1)} %get-tuple-element.27.table, f32[24,8,128]{2,1,0:T(8,128)S(1)} %collective-permute-done.7.a_ref, f32[24,8,128]{2,1,0:T(8,128)S(1)} %get-tuple-element.33.after_ref.x_ref, ...), custom_call_target="tpu_custom_call" | custom-call | flops 1500000000 | bytes 9000000 | tf_op jit(solution)/shard_map/pallas_call | solution.py:518
  71.9 6.0 %all-to-all-start.1 = ((f32[128,1,640]{2,1,0:T(1,128)}), f32[128,1,640]{2,1,0:T(1,128)S(1)}, u32[]{:S(2)}, u32[]{:S(2)}) async-start(f32[128,1,640]{2,1,0:T(1,128)} %bitcast.3), calls=%async_computation.1 | async-start | bytes 655360 | tf_op jit(solution)/shard_map/all_to_all | solution.py:466
  77.9 1.7 %collective-permute-start.10 = (f32[24,8,128]{2,1,0:T(8,128)S(1)}, f32[24,8,128]{2,1,0:T(8,128)S(1)}, u32[]{:S(2)}, u32[]{:S(2)}) collective-permute-start(f32[24,8,128]{2,1,0:T(8,128)S(1)} %get-tuple-element.36.after_ref.x_ref), channel_id=1, source_target_pairs={{0,31},{1,2},{2,1},{3,4},{4,3},{5,6},{6,5},{7,8},{8,7},{9,10},{10,... | collective-permute-start | bytes 294920 | tf_op jit(solution)/shard_map/ppermute | solution.py:437
  79.6 3.6 %collective-permute-start.9 = (f32[24,8,128]{2,1,0:T(8,128)S(1)}, f32[24,8,128]{2,1,0:T(8,128)S(1)}, u32[]{:S(2)}, u32[]{:S(2)}) collective-permute-start(f32[24,8,128]{2,1,0:T(8,128)S(1)} %get-tuple-element.36.after_ref.x_ref), channel_id=1, source_target_pairs={{0,1},{1,0},{2,3},{3,2},{4,5},{5,4},{6,7},{7,6},{8,9},{9,8},{10,11... | collective-permute-start | bytes 294920 | tf_op jit(solution)/shard_map/ppermute | solution.py:437
  83.2 1.4 %shard_map.100.kept_ref = bf16[2,384,1024]{2,1,0:T(8,128)(2,1)S(1)} custom-call(f32[24,8,128]{2,1,0:T(8,128)S(1)} %get-tuple-element.36.after_ref.x_ref, bf16[8,384,1024]{2,1,0:T(8,128)(2,1)} %get-tuple-element.37.weights_ref), custom_call_target="tpu_custom_call" | custom-call | flops 1000000000 | bytes 6000000 | tf_op jit(solution)/shard_map/pallas_call | solution.py:514
  84.7 5.2 %all-to-all-done.1 = f32[128,1,640]{2,1,0:T(1,128)S(1)} async-done(((f32[128,1,640]{2,1,0:T(1,128)}), f32[128,1,640]{2,1,0:T(1,128)S(1)}, u32[]{:S(2)}, u32[]{:S(2)}) %all-to-all-start.1) | async-done | bytes 327712 | tf_op jit(solution)/shard_map/all_to_all | solution.py:466
  89.8 4.4 %shard_map.101 = (f32[384,16]{1,0:T(8,128)S(1)}, f32[8,128]{1,0:T(8,128)S(1)}) custom-call(f32[640,128]{1,0:T(8,128)S(1)} %bitcast.11, bf16[2,384,1024]{2,1,0:T(8,128)(2,1)S(1)} %shard_map.100.kept_ref, bf16[8,384,1024]{2,1,0:T(8,128)(2,1)} %get-tuple-element.37.weights_ref), custom_call_target="tpu_custom_call" | custom-call | flops 10000000000 | bytes 60000000 | tf_op jit(solution)/shard_map/pallas_call | solution.py:522
  94.3 0.0 collective-permute-done.10.b_ref
  94.3 0.0 collective-permute-done.9.a_ref
  94.3 2.0 %shard_map.102 = (f32[24,8,128]{2,1,0:T(8,128)S(1)}, f32[24,8,128]{2,1,0:T(8,128)S(1)}, f32[24,8,128]{2,1,0:T(8,128)S(1)}, f32[3,8,128]{2,1,0:T(8,128)S(1)}, f32[24,8,128]{2,1,0:T(8,128)S(1)}) custom-call(s32[16,128]{1,0:T(8,128)S(1)} %get-tuple-element.27.table, f32[384,16]{1,0:T(8,128)S(1)} %get-tuple-element.38.out_ref, ...), custom_call_target="tpu_custom_call" | custom-call | flops 1500000000 | bytes 9000000 | tf_op jit(solution)/shard_map/pallas_call | solution.py:523
  96.3 0.9 collective-permute-start.12
  97.1 1.1 collective-permute-start.11
  98.2 2.4 %shard_map.103.schur_ref = f32[8,384,384]{2,1,0:T(8,128)S(1)} custom-call(f32[24,8,128]{2,1,0:T(8,128)S(1)} %get-tuple-element.41.after_ref.x_ref, f32[8,384,384]{2,1,0:T(8,128)} %source_ref.3), custom_call_target="tpu_custom_call" | custom-call | flops 1000000000 | bytes 6000000 | tf_op jit(solution)/shard_map/pallas_call | solution.py:511
  100.6 0.0 collective-permute-done.12.b_ref
  100.6 0.0 collective-permute-done.11.a_ref
  100.6 2.3 %shard_map.104 = (f32[24,8,128]{2,1,0:T(8,128)S(1)}, f32[640,128]{1,0:T(8,128)}, f32[24,8,128]{2,1,0:T(8,128)S(1)}) custom-call(s32[16,128]{1,0:T(8,128)S(1)} %get-tuple-element.27.table, f32[24,8,128]{2,1,0:T(8,128)S(1)} %collective-permute-done.11.a_ref, f32[24,8,128]{2,1,0:T(8,128)S(1)} %get-tuple-element.41.after_ref.x_ref, ...), custom_call_target="tpu_custom_call" | custom-call | flops 1500000000 | bytes 9000000 | tf_op jit(solution)/shard_map/pallas_call | solution.py:527
  102.9 7.6 %all-to-all-start.2 = ((f32[128,1,640]{2,1,0:T(1,128)}), f32[128,1,640]{2,1,0:T(1,128)S(1)}, u32[]{:S(2)}, u32[]{:S(2)}) async-start(f32[128,1,640]{2,1,0:T(1,128)} %bitcast.5), calls=%async_computation.2 | async-start | bytes 655360 | tf_op jit(solution)/shard_map/all_to_all | solution.py:466
  110.5 1.7 %collective-permute-start.14 = (f32[24,8,128]{2,1,0:T(8,128)S(1)}, f32[24,8,128]{2,1,0:T(8,128)S(1)}, u32[]{:S(2)}, u32[]{:S(2)}) collective-permute-start(f32[24,8,128]{2,1,0:T(8,128)S(1)} %get-tuple-element.45.after_ref.x_ref), channel_id=1, source_target_pairs={{0,31},{1,2},{2,1},{3,4},{4,3},{5,6},{6,5},{7,8},{8,7},{9,10},{10,... | collective-permute-start | bytes 294920 | tf_op jit(solution)/shard_map/ppermute | solution.py:437
  112.2 3.7 %collective-permute-start.13 = (f32[24,8,128]{2,1,0:T(8,128)S(1)}, f32[24,8,128]{2,1,0:T(8,128)S(1)}, u32[]{:S(2)}, u32[]{:S(2)}) collective-permute-start(f32[24,8,128]{2,1,0:T(8,128)S(1)} %get-tuple-element.45.after_ref.x_ref), channel_id=1, source_target_pairs={{0,1},{1,0},{2,3},{3,2},{4,5},{5,4},{6,7},{7,6},{8,9},{9,8},{10,11... | collective-permute-start | bytes 294920 | tf_op jit(solution)/shard_map/ppermute | solution.py:437
  115.9 1.4 %shard_map.105.kept_ref = bf16[2,384,1024]{2,1,0:T(8,128)(2,1)S(1)} custom-call(f32[24,8,128]{2,1,0:T(8,128)S(1)} %get-tuple-element.45.after_ref.x_ref, bf16[8,384,1024]{2,1,0:T(8,128)(2,1)} %get-tuple-element.37.weights_ref), custom_call_target="tpu_custom_call" | custom-call | flops 1000000000 | bytes 6000000 | tf_op jit(solution)/shard_map/pallas_call | solution.py:514
  117.3 5.2 %all-to-all-done.2 = f32[128,1,640]{2,1,0:T(1,128)S(1)} async-done(((f32[128,1,640]{2,1,0:T(1,128)}), f32[128,1,640]{2,1,0:T(1,128)S(1)}, u32[]{:S(2)}, u32[]{:S(2)}) %all-to-all-start.2) | async-done | bytes 327712 | tf_op jit(solution)/shard_map/all_to_all | solution.py:466
  122.5 4.4 %shard_map.106 = (f32[384,16]{1,0:T(8,128)S(1)}, f32[8,128]{1,0:T(8,128)S(1)}) custom-call(f32[640,128]{1,0:T(8,128)S(1)} %bitcast.12, bf16[2,384,1024]{2,1,0:T(8,128)(2,1)S(1)} %shard_map.105.kept_ref, bf16[8,384,1024]{2,1,0:T(8,128)(2,1)} %get-tuple-element.37.weights_ref), custom_call_target="tpu_custom_call" | custom-call | flops 10000000000 | bytes 60000000 | tf_op jit(solution)/shard_map/pallas_call | solution.py:531
  126.9 1.9 %shard_map.107 = (f32[8,8,384]{2,1,0:T(8,128)}, f32[8,8,384]{2,1,0:T(8,128)}, f32[8,8,384]{2,1,0:T(8,128)}) custom-call(s32[16,128]{1,0:T(8,128)S(1)} %get-tuple-element.27.table, f32[384,16]{1,0:T(8,128)S(1)} %get-tuple-element.46.out_ref, f32[8,128]{1,0:T(8,128)S(1)} %get-tuple-element.47.sums_ref, f32[8,8,384]{2,1,0:T(8,128)S(1)} %collective-permute-done.3.am_ref, ...), custom_call_target="tpu_custom_call" | custom-call | flops 1000000000 | bytes 6000000 | tf_op jit(solution)/shard_map/pallas_call | solution.py:533
  (11 shorter events, 0.0 us)
Async XLA Ops:
  0.6 10.1 %copy-start = (f32[8,8,384]{2,1,0:T(8,128)S(1)}, f32[8,8,384]{2,1,0:T(8,128)}, u32[]{:S(2)}) copy-start(f32[8,8,384]{2,1,0:T(8,128)} %m_ref.5) | copy-start | bytes 294916
  0.6 10.1 %copy-start.1 = (f32[64,64]{1,0:T(8,128)S(1)}, f32[64,64]{1,0:T(8,128)}, u32[]{:S(2)}) copy-start(f32[64,64]{1,0:T(8,128)} %inverse_ref.5) | copy-start | bytes 49156
  3.6 6.2 %collective-permute-start.1 = (f32[25,8,128]{2,1,0:T(8,128)S(1)}, f32[25,8,128]{2,1,0:T(8,128)S(1)}, u32[]{:S(2)}, u32[]{:S(2)}) collective-permute-start(f32[25,8,128]{2,1,0:T(8,128)S(1)} %get-tuple-element.28.x_ref.ix_ref), channel_id=1, source_target_pairs={{0,31},{1,2},{2,1},{3,4},{4,3},{5,6},{6,5},{7,8},{8,7},{9,10},{10,... | collective-permute-start | bytes 307208 | tf_op jit(solution)/shard_map/ppermute | solution.py:437
  6.3 4.5 %collective-permute-start = (f32[25,8,128]{2,1,0:T(8,128)S(1)}, f32[25,8,128]{2,1,0:T(8,128)S(1)}, u32[]{:S(2)}, u32[]{:S(2)}) collective-permute-start(f32[25,8,128]{2,1,0:T(8,128)S(1)} %get-tuple-element.28.x_ref.ix_ref), channel_id=1, source_target_pairs={{0,1},{1,0},{2,3},{3,2},{4,5},{5,4},{6,7},{7,6},{8,9},{9,8},{10,11... | collective-permute-start | bytes 307208 | tf_op jit(solution)/shard_map/ppermute | solution.py:437
  12.9 31.3 %all-to-all-start = ((f32[64,1,4736]{2,1,0:T(1,128)}), f32[64,1,4736]{2,1,0:T(1,128)S(1)}, u32[]{:S(2)}, u32[]{:S(2)}) async-start(f32[64,1,4736]{2,1,0:T(1,128)} %bitcast.1), calls=%async_computation | async-start | bytes 2424832 | tf_op jit(solution)/shard_map/all_to_all | solution.py:476
  44.2 6.5 %collective-permute-start.2 = (f32[2368,128]{1,0:T(8,128)S(1)}, f32[2368,128]{1,0:T(8,128)S(1)}, u32[]{:S(2)}, u32[]{:S(2)}) collective-permute-start(f32[2368,128]{1,0:T(8,128)S(1)} %bitcast.9), channel_id=1, source_target_pairs={{0,1},{1,0},{2,3},{3,2},{4,5},{5,4},{6,7},{7,6},{8,9},{9,8},{10,11... | collective-permute-start | bytes 3637256 | tf_op jit(solution)/shard_map/ppermute | solution.py:485
  44.2 5.6 %collective-permute-start.4 = (f32[8,8,384]{2,1,0:T(8,128)S(1)}, f32[8,8,384]{2,1,0:T(8,128)S(1)}, u32[]{:S(2)}, u32[]{:S(2)}) collective-permute-start(f32[8,8,384]{2,1,0:T(8,128)S(1)} %copy-done), channel_id=1, source_target_pairs={{0,31},{1,2},{2,1},{3,4},{4,3},{5,6},{6,5},{7,8},{8,7},{9,10},{10,... | collective-permute-start | bytes 294920 | tf_op jit(solution)/shard_map/ppermute | solution.py:437
  44.9 4.9 %collective-permute-start.3 = (f32[8,8,384]{2,1,0:T(8,128)S(1)}, f32[8,8,384]{2,1,0:T(8,128)S(1)}, u32[]{:S(2)}, u32[]{:S(2)}) collective-permute-start(f32[8,8,384]{2,1,0:T(8,128)S(1)} %copy-done), channel_id=1, source_target_pairs={{0,1},{1,0},{2,3},{3,2},{4,5},{5,4},{6,7},{7,6},{8,9},{9,8},{10,11... | collective-permute-start | bytes 294920 | tf_op jit(solution)/shard_map/ppermute | solution.py:437
  45.1 4.6 %collective-permute-start.6 = (f32[24,8,128]{2,1,0:T(8,128)S(1)}, f32[24,8,128]{2,1,0:T(8,128)S(1)}, u32[]{:S(2)}, u32[]{:S(2)}) collective-permute-start(f32[24,8,128]{2,1,0:T(8,128)S(1)} %shard_map.96.x_ref), channel_id=1, source_target_pairs={{0,31},{1,2},{2,1},{3,4},{4,3},{5,6},{6,5},{7,8},{8,7},{9,10},{10,... | collective-permute-start | bytes 294920 | tf_op jit(solution)/shard_map/ppermute | solution.py:437
  45.9 4.8 %collective-permute-start.5 = (f32[24,8,128]{2,1,0:T(8,128)S(1)}, f32[24,8,128]{2,1,0:T(8,128)S(1)}, u32[]{:S(2)}, u32[]{:S(2)}) collective-permute-start(f32[24,8,128]{2,1,0:T(8,128)S(1)} %shard_map.96.x_ref), channel_id=1, source_target_pairs={{0,1},{1,0},{2,3},{3,2},{4,5},{5,4},{6,7},{7,6},{8,9},{9,8},{10,11... | collective-permute-start | bytes 294920 | tf_op jit(solution)/shard_map/ppermute | solution.py:437
  60.7 8.9 %collective-permute-start.8 = (f32[24,8,128]{2,1,0:T(8,128)S(1)}, f32[24,8,128]{2,1,0:T(8,128)S(1)}, u32[]{:S(2)}, u32[]{:S(2)}) collective-permute-start(f32[24,8,128]{2,1,0:T(8,128)S(1)} %get-tuple-element.33.after_ref.x_ref), channel_id=1, source_target_pairs={{0,31},{1,2},{2,1},{3,4},{4,3},{5,6},{6,5},{7,8},{8,7},{9,10},{10,... | collective-permute-start | bytes 294920 | tf_op jit(solution)/shard_map/ppermute | solution.py:437
  60.8 8.8 %collective-permute-start.7 = (f32[24,8,128]{2,1,0:T(8,128)S(1)}, f32[24,8,128]{2,1,0:T(8,128)S(1)}, u32[]{:S(2)}, u32[]{:S(2)}) collective-permute-start(f32[24,8,128]{2,1,0:T(8,128)S(1)} %get-tuple-element.33.after_ref.x_ref), channel_id=1, source_target_pairs={{0,1},{1,0},{2,3},{3,2},{4,5},{5,4},{6,7},{7,6},{8,9},{9,8},{10,11... | collective-permute-start | bytes 294920 | tf_op jit(solution)/shard_map/ppermute | solution.py:437
  71.9 17.9 %all-to-all-start.1 = ((f32[128,1,640]{2,1,0:T(1,128)}), f32[128,1,640]{2,1,0:T(1,128)S(1)}, u32[]{:S(2)}, u32[]{:S(2)}) async-start(f32[128,1,640]{2,1,0:T(1,128)} %bitcast.3), calls=%async_computation.1 | async-start | bytes 655360 | tf_op jit(solution)/shard_map/all_to_all | solution.py:466
  77.9 16.3 %collective-permute-start.10 = (f32[24,8,128]{2,1,0:T(8,128)S(1)}, f32[24,8,128]{2,1,0:T(8,128)S(1)}, u32[]{:S(2)}, u32[]{:S(2)}) collective-permute-start(f32[24,8,128]{2,1,0:T(8,128)S(1)} %get-tuple-element.36.after_ref.x_ref), channel_id=1, source_target_pairs={{0,31},{1,2},{2,1},{3,4},{4,3},{5,6},{6,5},{7,8},{8,7},{9,10},{10,... | collective-permute-start | bytes 294920 | tf_op jit(solution)/shard_map/ppermute | solution.py:437
  79.6 14.6 %collective-permute-start.9 = (f32[24,8,128]{2,1,0:T(8,128)S(1)}, f32[24,8,128]{2,1,0:T(8,128)S(1)}, u32[]{:S(2)}, u32[]{:S(2)}) collective-permute-start(f32[24,8,128]{2,1,0:T(8,128)S(1)} %get-tuple-element.36.after_ref.x_ref), channel_id=1, source_target_pairs={{0,1},{1,0},{2,3},{3,2},{4,5},{5,4},{6,7},{7,6},{8,9},{9,8},{10,11... | collective-permute-start | bytes 294920 | tf_op jit(solution)/shard_map/ppermute | solution.py:437
  83.2 11.1 %slice-start = ((s8[4718592]{0:T(1024)(128)(4,1)}), s8[524288]{0:T(1024)(128)(4,1)S(1)}, s32[]{:S(2)}) async-start(s8[4718592]{0:T(1024)(128)(4,1)} %bitcast.7), calls=%async_computation.3 | async-start | bytes 1048576
  89.8 4.5 %slice-start.1 = ((s8[4718592]{0:T(1024)(128)(4,1)}), s8[4194304]{0:T(1024)(128)(4,1)S(1)}, s32[]{:S(2)}) async-start(s8[4718592]{0:T(1024)(128)(4,1)} %bitcast.7), calls=%async_computation.4 | async-start | bytes 8388608
  96.3 4.3 %collective-permute-start.12 = (f32[24,8,128]{2,1,0:T(8,128)S(1)}, f32[24,8,128]{2,1,0:T(8,128)S(1)}, u32[]{:S(2)}, u32[]{:S(2)}) collective-permute-start(f32[24,8,128]{2,1,0:T(8,128)S(1)} %get-tuple-element.41.after_ref.x_ref), channel_id=1, source_target_pairs={{0,31},{1,2},{2,1},{3,4},{4,3},{5,6},{6,5},{7,8},{8,7},{9,10},{10,... | collective-permute-start | bytes 294920 | tf_op jit(solution)/shard_map/ppermute | solution.py:437
  97.1 3.5 %collective-permute-start.11 = (f32[24,8,128]{2,1,0:T(8,128)S(1)}, f32[24,8,128]{2,1,0:T(8,128)S(1)}, u32[]{:S(2)}, u32[]{:S(2)}) collective-permute-start(f32[24,8,128]{2,1,0:T(8,128)S(1)} %get-tuple-element.41.after_ref.x_ref), channel_id=1, source_target_pairs={{0,1},{1,0},{2,3},{3,2},{4,5},{5,4},{6,7},{7,6},{8,9},{9,8},{10,11... | collective-permute-start | bytes 294920 | tf_op jit(solution)/shard_map/ppermute | solution.py:437
  102.9 19.6 %all-to-all-start.2 = ((f32[128,1,640]{2,1,0:T(1,128)}), f32[128,1,640]{2,1,0:T(1,128)S(1)}, u32[]{:S(2)}, u32[]{:S(2)}) async-start(f32[128,1,640]{2,1,0:T(1,128)} %bitcast.5), calls=%async_computation.2 | async-start | bytes 655360 | tf_op jit(solution)/shard_map/all_to_all | solution.py:466
  110.5 16.4 %collective-permute-start.14 = (f32[24,8,128]{2,1,0:T(8,128)S(1)}, f32[24,8,128]{2,1,0:T(8,128)S(1)}, u32[]{:S(2)}, u32[]{:S(2)}) collective-permute-start(f32[24,8,128]{2,1,0:T(8,128)S(1)} %get-tuple-element.45.after_ref.x_ref), channel_id=1, source_target_pairs={{0,31},{1,2},{2,1},{3,4},{4,3},{5,6},{6,5},{7,8},{8,7},{9,10},{10,... | collective-permute-start | bytes 294920 | tf_op jit(solution)/shard_map/ppermute | solution.py:437
  112.2 14.7 %collective-permute-start.13 = (f32[24,8,128]{2,1,0:T(8,128)S(1)}, f32[24,8,128]{2,1,0:T(8,128)S(1)}, u32[]{:S(2)}, u32[]{:S(2)}) collective-permute-start(f32[24,8,128]{2,1,0:T(8,128)S(1)} %get-tuple-element.45.after_ref.x_ref), channel_id=1, source_target_pairs={{0,1},{1,0},{2,3},{3,2},{4,5},{5,4},{6,7},{7,6},{8,9},{9,8},{10,11... | collective-permute-start | bytes 294920 | tf_op jit(solution)/shard_map/ppermute | solution.py:437

commit v10 on v9

--- a/solution.py
+++ b/solution.py
@@ -479,9 +479,7 @@
     pooled = through(r0)
     ma, mb = both(corner_map)
     maps = (ma, corner_map, mb)
-    qa, q, qb = pooled
-    own_cards, q = lax.optimization_barrier((own_cards, q))
-    pooled = (qa, q, qb)
+    own_cards, pooled, maps = lax.optimization_barrier((own_cards, pooled, maps))
     other_cards = lax.ppermute(own_cards, "tile", inner_swap)
     z0, u, weights = pl.pallas_call(
         solve_first_kernel,

time: 129 us -> 123 us (0.953)
  starting transfers between devices: 56.4 us -> 53 us
  waiting for transfers between devices: 28.9 us -> 25.7 us
    all_to_all x1, waiting for transfers between devices: 16.6 us -> 4.04 us  [shards(): lax.all_to_all(card.reshape(devices // 2, -1), GT, 0, 0, tiled=True, axis...]
    ppermute x7, waiting for transfers between devices: 0.02 us -> 7.47 us  [both(): lax.ppermute(x, 'tile', outer_swap)]
    ppermute x7, starting transfers between devices: 22.4 us -> 17.6 us  [both(): lax.ppermute(x, 'tile', inner_swap)]
    ppermute x1, waiting for transfers between devices: 0.01 us -> 2.89 us  [shards(): other_cards = lax.ppermute(own_cards, 'tile', inner_swap)]
    all_to_all x2, starting transfers between devices: 13.6 us -> 15.1 us  [spread(): lax.all_to_all(x.reshape(devices, -1), GT, 0, 0, tiled=True)]
  transfers between devices with their start and end apart: 18 -> 18, of which waited for: 5 -> 8; matrix products, arithmetic and copies ran while one was open for 0% -> 0% of each run, Pallas kernels for 15% -> 16%
where the time goes in v10:
time: 123 us; the launch traced here: 122 us
  starting transfers between devices  53 us (43%)
  Pallas kernels  42.6 us (35%)
  waiting for transfers between devices  25.7 us (21%)
    ppermute x7, starting transfers between devices, both(): lax.ppermute(x, 'tile', inner_swap)  17.6 us
    all_to_all x2, starting transfers between devices, spread(): lax.all_to_all(x.reshape(devices, -1), GT, 0, 0, tiled=True)  15.1 us
    all_to_all x1, starting transfers between devices, shards(): lax.all_to_all(card.reshape(devices // 2, -1), GT, 0, 0, tiled=True, axis...  11.8 us
    all_to_all x2, waiting for transfers between devices, spread(): lax.all_to_all(x.reshape(devices, -1), GT, 0, 0, tiled=True)  10.4 us
    pallas_call x1, Pallas kernels, shards(): pl.pallas_call(solve_first_kernel, in_specs=[SMEM] * 2 + [ANY] * 3 + [VME...  9.98 us
    pallas_call x2, Pallas kernels, shards(): call(coarse_kernel, coarse_out, [VMEM, VMEM, ANY], coarse_scratch, us=20)  8.77 us
    ppermute x7, starting transfers between devices, both(): lax.ppermute(x, 'tile', outer_swap)  8.5 us
    ppermute x7, waiting for transfers between devices, both(): lax.ppermute(x, 'tile', outer_swap)  7.47 us
  transfers between devices with their start and end apart: 18, of which 8 were waited for; matrix products, arithmetic and copies ran while one was open for 0% of the time, Pallas kernels for 16%

profile of v10, /device:TPU:1, one launch (start us, length us, event | category | flops | bytes accessed | tf_op | source)
XLA Modules:
  0.0 122.3 jit_solution(12010995009876086303)
XLA Ops:
  0.7 2.9 %shard_map.94 = (f32[25,8,128]{2,1,0:T(8,128)S(1)}, s32[16,128]{1,0:T(8,128)S(1)}) custom-call(s32[1]{0:T(128)} %bitcast.core, f32[8,8,384]{2,1,0:T(8,128)} %loads_ref.1, s32[8,8]{1,0:T(8,128)} %index_ref.1, s32[8,12]{1,0:T(8,128)} %partner_ref.1, f32[8,384,384]{2,1,0:T(8,128)} %inverse_ref.7), custom_call_target="tpu_custom_call" | custom-call | flops 2000000000 | bytes 12000000 | tf_op jit(solution)/shard_map/pallas_call | solution.py:449
  3.6 2.7 %collective-permute-start.1 = (f32[25,8,128]{2,1,0:T(8,128)S(1)}, f32[25,8,128]{2,1,0:T(8,128)S(1)}, u32[]{:S(2)}, u32[]{:S(2)}) collective-permute-start(f32[25,8,128]{2,1,0:T(8,128)S(1)} %get-tuple-element.33.x_ref.ix_ref), channel_id=1, source_target_pairs={{0,31},{1,2},{2,1},{3,4},{4,3},{5,6},{6,5},{7,8},{8,7},{9,10},{10,... | collective-permute-start | bytes 307208 | tf_op jit(solution)/shard_map/ppermute | solution.py:437
  6.3 3.6 %collective-permute-start = (f32[25,8,128]{2,1,0:T(8,128)S(1)}, f32[25,8,128]{2,1,0:T(8,128)S(1)}, u32[]{:S(2)}, u32[]{:S(2)}) collective-permute-start(f32[25,8,128]{2,1,0:T(8,128)S(1)} %get-tuple-element.33.x_ref.ix_ref), channel_id=1, source_target_pairs={{0,1},{1,0},{2,3},{3,2},{4,5},{5,4},{6,7},{7,6},{8,9},{9,8},{10,11... | collective-permute-start | bytes 307208 | tf_op jit(solution)/shard_map/ppermute | solution.py:437
  9.8 0.0 collective-permute-done.1.b_ref.ib_ref
  9.8 0.9 collective-permute-done.a_ref.ia_ref
  10.8 2.1 %shard_map.95 = (f32[24,8,128]{2,1,0:T(8,128)S(1)}, f32[2368,128]{1,0:T(8,128)}) custom-call(s32[16,128]{1,0:T(8,128)S(1)} %get-tuple-element.32.table, f32[25,8,128]{2,1,0:T(8,128)S(1)} %collective-permute-done.a_ref.ia_ref, f32[25,8,128]{2,1,0:T(8,128)S(1)} %get-tuple-element.33.x_ref.ix_ref, f32[25,8,128]{2,1,0:T(8,128)S(1)} %collective-permute-done.1.b_ref.ib_ref, ...), custom_call_target="tpu_custom_call" | custom-call | flops 1000000000 | bytes 6000000 | tf_op jit(solution)/shard_map/pallas_call | solution.py:473
  12.9 11.8 %all-to-all-start = ((f32[64,1,4736]{2,1,0:T(1,128)}), f32[64,1,4736]{2,1,0:T(1,128)S(1)}, u32[]{:S(2)}, u32[]{:S(2)}) async-start(f32[64,1,4736]{2,1,0:T(1,128)} %bitcast.1), calls=%async_computation | async-start | bytes 2424832 | tf_op jit(solution)/shard_map/all_to_all | solution.py:476
  24.7 0.1 collective-permute-start.5
  24.8 4.7 %collective-permute-start.4 = (f32[8,8,384]{2,1,0:T(8,128)S(1)}, f32[8,8,384]{2,1,0:T(8,128)S(1)}, u32[]{:S(2)}, u32[]{:S(2)}) collective-permute-start(f32[8,8,384]{2,1,0:T(8,128)S(1)} %copy-done), channel_id=1, source_target_pairs={{0,1},{1,0},{2,3},{3,2},{4,5},{5,4},{6,7},{7,6},{8,9},{9,8},{10,11... | collective-permute-start | bytes 294920 | tf_op jit(solution)/shard_map/ppermute | solution.py:437
  29.6 2.8 %shard_map.96.x_ref = f32[24,8,128]{2,1,0:T(8,128)S(1)} custom-call(f32[24,8,128]{2,1,0:T(8,128)S(1)} %get-tuple-element.35.x_ref.r0_ref, f32[8,384,384]{2,1,0:T(8,128)} %source_ref.3), custom_call_target="tpu_custom_call" | custom-call | flops 1500000000 | bytes 9000000 | tf_op jit(solution)/shard_map/pallas_call | solution.py:469
  32.3 0.1 collective-permute-start.3
  32.4 1.0 collective-permute-start.2
  33.4 5.6 %collective-permute-done.5.bm_ref = f32[8,8,384]{2,1,0:T(8,128)S(1)} collective-permute-done((f32[8,8,384]{2,1,0:T(8,128)S(1)}, f32[8,8,384]{2,1,0:T(8,128)S(1)}, u32[]{:S(2)}, u32[]{:S(2)}) %collective-permute-start.5) | collective-permute-done | bytes 98336 | tf_op jit(solution)/shard_map/ppermute | solution.py:437
  39.0 0.0 collective-permute-done.4.am_ref
  39.0 1.5 %collective-permute-done.3.b_ref = f32[24,8,128]{2,1,0:T(8,128)S(1)} collective-permute-done((f32[24,8,128]{2,1,0:T(8,128)S(1)}, f32[24,8,128]{2,1,0:T(8,128)S(1)}, u32[]{:S(2)}, u32[]{:S(2)}) %collective-permute-start.3) | collective-permute-done | bytes 98336 | tf_op jit(solution)/shard_map/ppermute | solution.py:437
  40.5 0.0 collective-permute-done.2.a_ref
  40.5 4.0 %all-to-all-done = f32[64,1,4736]{2,1,0:T(1,128)S(1)} async-done(((f32[64,1,4736]{2,1,0:T(1,128)}), f32[64,1,4736]{2,1,0:T(1,128)S(1)}, u32[]{:S(2)}, u32[]{:S(2)}) %all-to-all-start) | async-done | bytes 1212448 | tf_op jit(solution)/shard_map/all_to_all | solution.py:476
  44.5 0.0 collective-permute-start.6
  44.5 2.9 %collective-permute-done.6.other_ref = f32[2368,128]{1,0:T(8,128)S(1)} collective-permute-done((f32[2368,128]{1,0:T(8,128)S(1)}, f32[2368,128]{1,0:T(8,128)S(1)}, u32[]{:S(2)}, u32[]{:S(2)}) %collective-permute-start.6) | collective-permute-done | bytes 1212448 | tf_op jit(solution)/shard_map/ppermute | solution.py:483
  47.4 10.0 %shard_map.97 = (f32[24,8,128]{2,1,0:T(8,128)S(1)}, f32[24,8,128]{2,1,0:T(8,128)S(1)}, bf16[8,384,1024]{2,1,0:T(8,128)(2,1)}) custom-call(s32[1]{0:T(128)} %bitcast.core, s32[16,128]{1,0:T(8,128)S(1)} %get-tuple-element.32.table, f32[25,8,128]{2,1,0:T(8,128)S(1)} %collective-permute-done.a_ref.ia_ref, f32[25,8,128]{2,1,0:T(8,128)S(1)} %get-tuple-element.33.x_ref.ix_ref, ...), custom_call_target="tpu_custom_call" | custom-call | flops 4000000000 | bytes 20000000 | tf_op jit(solution)/shard_map/pallas_call | solution.py:484
  57.4 1.4 %collective-permute-start.8 = (f32[24,8,128]{2,1,0:T(8,128)S(1)}, f32[24,8,128]{2,1,0:T(8,128)S(1)}, u32[]{:S(2)}, u32[]{:S(2)}) collective-permute-start(f32[24,8,128]{2,1,0:T(8,128)S(1)} %get-tuple-element.43.after_ref.x_ref), channel_id=1, source_target_pairs={{0,31},{1,2},{2,1},{3,4},{4,3},{5,6},{6,5},{7,8},{8,7},{9,10},{10,... | collective-permute-start | bytes 294920 | tf_op jit(solution)/shard_map/ppermute | solution.py:437
  58.8 0.0 collective-permute-start.7
  58.8 2.4 %shard_map.98.schur_ref = f32[8,384,384]{2,1,0:T(8,128)S(1)} custom-call(f32[24,8,128]{2,1,0:T(8,128)S(1)} %get-tuple-element.43.after_ref.x_ref, f32[8,384,384]{2,1,0:T(8,128)} %source_ref.3), custom_call_target="tpu_custom_call" | custom-call | flops 1000000000 | bytes 6000000 | tf_op jit(solution)/shard_map/pallas_call | solution.py:509
  61.1 0.4 collective-permute-done.8.b_ref
  61.5 0.0 collective-permute-done.7.a_ref
  61.5 2.3 %shard_map.99 = (f32[24,8,128]{2,1,0:T(8,128)S(1)}, f32[640,128]{1,0:T(8,128)}, f32[24,8,128]{2,1,0:T(8,128)S(1)}) custom-call(s32[16,128]{1,0:T(8,128)S(1)} %get-tuple-element.32.table, f32[24,8,128]{2,1,0:T(8,128)S(1)} %collective-permute-done.7.a_ref, f32[24,8,128]{2,1,0:T(8,128)S(1)} %get-tuple-element.43.after_ref.x_ref, ...), custom_call_target="tpu_custom_call" | custom-call | flops 1500000000 | bytes 9000000 | tf_op jit(solution)/shard_map/pallas_call | solution.py:516
  63.8 7.5 %all-to-all-start.1 = ((f32[128,1,640]{2,1,0:T(1,128)}), f32[128,1,640]{2,1,0:T(1,128)S(1)}, u32[]{:S(2)}, u32[]{:S(2)}) async-start(f32[128,1,640]{2,1,0:T(1,128)} %bitcast.3), calls=%async_computation.1 | async-start | bytes 655360 | tf_op jit(solution)/shard_map/all_to_all | solution.py:466
  71.4 1.7 %collective-permute-start.10 = (f32[24,8,128]{2,1,0:T(8,128)S(1)}, f32[24,8,128]{2,1,0:T(8,128)S(1)}, u32[]{:S(2)}, u32[]{:S(2)}) collective-permute-start(f32[24,8,128]{2,1,0:T(8,128)S(1)} %get-tuple-element.46.after_ref.x_ref), channel_id=1, source_target_pairs={{0,31},{1,2},{2,1},{3,4},{4,3},{5,6},{6,5},{7,8},{8,7},{9,10},{10,... | collective-permute-start | bytes 294920 | tf_op jit(solution)/shard_map/ppermute | solution.py:437
  73.1 3.6 %collective-permute-start.9 = (f32[24,8,128]{2,1,0:T(8,128)S(1)}, f32[24,8,128]{2,1,0:T(8,128)S(1)}, u32[]{:S(2)}, u32[]{:S(2)}) collective-permute-start(f32[24,8,128]{2,1,0:T(8,128)S(1)} %get-tuple-element.46.after_ref.x_ref), channel_id=1, source_target_pairs={{0,1},{1,0},{2,3},{3,2},{4,5},{5,4},{6,7},{7,6},{8,9},{9,8},{10,11... | collective-permute-start | bytes 294920 | tf_op jit(solution)/shard_map/ppermute | solution.py:437
  76.7 1.4 %shard_map.100.kept_ref = bf16[2,384,1024]{2,1,0:T(8,128)(2,1)S(1)} custom-call(f32[24,8,128]{2,1,0:T(8,128)S(1)} %get-tuple-element.46.after_ref.x_ref, bf16[8,384,1024]{2,1,0:T(8,128)(2,1)} %get-tuple-element.47.weights_ref), custom_call_target="tpu_custom_call" | custom-call | flops 1000000000 | bytes 6000000 | tf_op jit(solution)/shard_map/pallas_call | solution.py:512
  78.1 5.2 %all-to-all-done.1 = f32[128,1,640]{2,1,0:T(1,128)S(1)} async-done(((f32[128,1,640]{2,1,0:T(1,128)}), f32[128,1,640]{2,1,0:T(1,128)S(1)}, u32[]{:S(2)}, u32[]{:S(2)}) %all-to-all-start.1) | async-done | bytes 327712 | tf_op jit(solution)/shard_map/all_to_all | solution.py:466
  83.3 4.4 %shard_map.101 = (f32[384,16]{1,0:T(8,128)S(1)}, f32[8,128]{1,0:T(8,128)S(1)}) custom-call(f32[640,128]{1,0:T(8,128)S(1)} %bitcast.11, bf16[2,384,1024]{2,1,0:T(8,128)(2,1)S(1)} %shard_map.100.kept_ref, bf16[8,384,1024]{2,1,0:T(8,128)(2,1)} %get-tuple-element.47.weights_ref), custom_call_target="tpu_custom_call" | custom-call | flops 10000000000 | bytes 60000000 | tf_op jit(solution)/shard_map/pallas_call | solution.py:520
  87.8 2.0 %shard_map.102 = (f32[24,8,128]{2,1,0:T(8,128)S(1)}, f32[24,8,128]{2,1,0:T(8,128)S(1)}, f32[24,8,128]{2,1,0:T(8,128)S(1)}, f32[3,8,128]{2,1,0:T(8,128)S(1)}, f32[24,8,128]{2,1,0:T(8,128)S(1)}) custom-call(s32[16,128]{1,0:T(8,128)S(1)} %get-tuple-element.32.table, f32[384,16]{1,0:T(8,128)S(1)} %get-tuple-element.48.out_ref, ...), custom_call_target="tpu_custom_call" | custom-call | flops 1500000000 | bytes 9000000 | tf_op jit(solution)/shard_map/pallas_call | solution.py:521
  89.7 0.9 collective-permute-start.12
  90.6 1.1 collective-permute-start.11
  91.6 2.4 %shard_map.103.schur_ref = f32[8,384,384]{2,1,0:T(8,128)S(1)} custom-call(f32[24,8,128]{2,1,0:T(8,128)S(1)} %get-tuple-element.51.after_ref.x_ref, f32[8,384,384]{2,1,0:T(8,128)} %source_ref.3), custom_call_target="tpu_custom_call" | custom-call | flops 1000000000 | bytes 6000000 | tf_op jit(solution)/shard_map/pallas_call | solution.py:509
  94.0 0.0 collective-permute-done.12.b_ref
  94.0 0.0 collective-permute-done.11.a_ref
  94.0 2.3 %shard_map.104 = (f32[24,8,128]{2,1,0:T(8,128)S(1)}, f32[640,128]{1,0:T(8,128)}, f32[24,8,128]{2,1,0:T(8,128)S(1)}) custom-call(s32[16,128]{1,0:T(8,128)S(1)} %get-tuple-element.32.table, f32[24,8,128]{2,1,0:T(8,128)S(1)} %collective-permute-done.11.a_ref, f32[24,8,128]{2,1,0:T(8,128)S(1)} %get-tuple-element.51.after_ref.x_ref, ...), custom_call_target="tpu_custom_call" | custom-call | flops 1500000000 | bytes 9000000 | tf_op jit(solution)/shard_map/pallas_call | solution.py:525
  96.3 7.6 %all-to-all-start.2 = ((f32[128,1,640]{2,1,0:T(1,128)}), f32[128,1,640]{2,1,0:T(1,128)S(1)}, u32[]{:S(2)}, u32[]{:S(2)}) async-start(f32[128,1,640]{2,1,0:T(1,128)} %bitcast.5), calls=%async_computation.2 | async-start | bytes 655360 | tf_op jit(solution)/shard_map/all_to_all | solution.py:466
  103.9 1.7 %collective-permute-start.14 = (f32[24,8,128]{2,1,0:T(8,128)S(1)}, f32[24,8,128]{2,1,0:T(8,128)S(1)}, u32[]{:S(2)}, u32[]{:S(2)}) collective-permute-start(f32[24,8,128]{2,1,0:T(8,128)S(1)} %get-tuple-element.55.after_ref.x_ref), channel_id=1, source_target_pairs={{0,31},{1,2},{2,1},{3,4},{4,3},{5,6},{6,5},{7,8},{8,7},{9,10},{10,... | collective-permute-start | bytes 294920 | tf_op jit(solution)/shard_map/ppermute | solution.py:437
  105.7 3.7 %collective-permute-start.13 = (f32[24,8,128]{2,1,0:T(8,128)S(1)}, f32[24,8,128]{2,1,0:T(8,128)S(1)}, u32[]{:S(2)}, u32[]{:S(2)}) collective-permute-start(f32[24,8,128]{2,1,0:T(8,128)S(1)} %get-tuple-element.55.after_ref.x_ref), channel_id=1, source_target_pairs={{0,1},{1,0},{2,3},{3,2},{4,5},{5,4},{6,7},{7,6},{8,9},{9,8},{10,11... | collective-permute-start | bytes 294920 | tf_op jit(solution)/shard_map/ppermute | solution.py:437
  109.4 1.4 %shard_map.105.kept_ref = bf16[2,384,1024]{2,1,0:T(8,128)(2,1)S(1)} custom-call(f32[24,8,128]{2,1,0:T(8,128)S(1)} %get-tuple-element.55.after_ref.x_ref, bf16[8,384,1024]{2,1,0:T(8,128)(2,1)} %get-tuple-element.47.weights_ref), custom_call_target="tpu_custom_call" | custom-call | flops 1000000000 | bytes 6000000 | tf_op jit(solution)/shard_map/pallas_call | solution.py:512
  110.8 5.2 %all-to-all-done.2 = f32[128,1,640]{2,1,0:T(1,128)S(1)} async-done(((f32[128,1,640]{2,1,0:T(1,128)}), f32[128,1,640]{2,1,0:T(1,128)S(1)}, u32[]{:S(2)}, u32[]{:S(2)}) %all-to-all-start.2) | async-done | bytes 327712 | tf_op jit(solution)/shard_map/all_to_all | solution.py:466
  116.0 4.4 %shard_map.106 = (f32[384,16]{1,0:T(8,128)S(1)}, f32[8,128]{1,0:T(8,128)S(1)}) custom-call(f32[640,128]{1,0:T(8,128)S(1)} %bitcast.12, bf16[2,384,1024]{2,1,0:T(8,128)(2,1)S(1)} %shard_map.105.kept_ref, bf16[8,384,1024]{2,1,0:T(8,128)(2,1)} %get-tuple-element.47.weights_ref), custom_call_target="tpu_custom_call" | custom-call | flops 10000000000 | bytes 60000000 | tf_op jit(solution)/shard_map/pallas_call | solution.py:529
  120.3 0.0 collective-permute-done.14.b_ref
  120.3 0.0 collective-permute-done.13.a_ref
  120.4 1.9 %shard_map.107 = (f32[8,8,384]{2,1,0:T(8,128)}, f32[8,8,384]{2,1,0:T(8,128)}, f32[8,8,384]{2,1,0:T(8,128)}) custom-call(s32[16,128]{1,0:T(8,128)S(1)} %get-tuple-element.32.table, f32[384,16]{1,0:T(8,128)S(1)} %get-tuple-element.56.out_ref, f32[8,128]{1,0:T(8,128)S(1)} %get-tuple-element.57.sums_ref, f32[8,8,384]{2,1,0:T(8,128)S(1)} %collective-permute-done.4.am_ref, ...), custom_call_target="tpu_custom_call" | custom-call | flops 1000000000 | bytes 6000000 | tf_op jit(solution)/shard_map/pallas_call | solution.py:531
  (11 shorter events, 0.0 us)
Async XLA Ops:
  0.6 10.1 %copy-start = (f32[8,8,384]{2,1,0:T(8,128)S(1)}, f32[8,8,384]{2,1,0:T(8,128)}, u32[]{:S(2)}) copy-start(f32[8,8,384]{2,1,0:T(8,128)} %m_ref.2) | copy-start | bytes 294916
  0.6 10.1 %copy-start.1 = (f32[64,64]{1,0:T(8,128)S(1)}, f32[64,64]{1,0:T(8,128)}, u32[]{:S(2)}) copy-start(f32[64,64]{1,0:T(8,128)} %inverse_ref.5) | copy-start | bytes 49156
  3.6 6.2 %collective-permute-start.1 = (f32[25,8,128]{2,1,0:T(8,128)S(1)}, f32[25,8,128]{2,1,0:T(8,128)S(1)}, u32[]{:S(2)}, u32[]{:S(2)}) collective-permute-start(f32[25,8,128]{2,1,0:T(8,128)S(1)} %get-tuple-element.33.x_ref.ix_ref), channel_id=1, source_target_pairs={{0,31},{1,2},{2,1},{3,4},{4,3},{5,6},{6,5},{7,8},{8,7},{9,10},{10,... | collective-permute-start | bytes 307208 | tf_op jit(solution)/shard_map/ppermute | solution.py:437
  6.3 4.5 %collective-permute-start = (f32[25,8,128]{2,1,0:T(8,128)S(1)}, f32[25,8,128]{2,1,0:T(8,128)S(1)}, u32[]{:S(2)}, u32[]{:S(2)}) collective-permute-start(f32[25,8,128]{2,1,0:T(8,128)S(1)} %get-tuple-element.33.x_ref.ix_ref), channel_id=1, source_target_pairs={{0,1},{1,0},{2,3},{3,2},{4,5},{5,4},{6,7},{7,6},{8,9},{9,8},{10,11... | collective-permute-start | bytes 307208 | tf_op jit(solution)/shard_map/ppermute | solution.py:437
  12.9 31.6 %all-to-all-start = ((f32[64,1,4736]{2,1,0:T(1,128)}), f32[64,1,4736]{2,1,0:T(1,128)S(1)}, u32[]{:S(2)}, u32[]{:S(2)}) async-start(f32[64,1,4736]{2,1,0:T(1,128)} %bitcast.1), calls=%async_computation | async-start | bytes 2424832 | tf_op jit(solution)/shard_map/all_to_all | solution.py:476
  24.7 14.2 %collective-permute-start.5 = (f32[8,8,384]{2,1,0:T(8,128)S(1)}, f32[8,8,384]{2,1,0:T(8,128)S(1)}, u32[]{:S(2)}, u32[]{:S(2)}) collective-permute-start(f32[8,8,384]{2,1,0:T(8,128)S(1)} %copy-done), channel_id=1, source_target_pairs={{0,31},{1,2},{2,1},{3,4},{4,3},{5,6},{6,5},{7,8},{8,7},{9,10},{10,... | collective-permute-start | bytes 294920 | tf_op jit(solution)/shard_map/ppermute | solution.py:437
  24.8 14.1 %collective-permute-start.4 = (f32[8,8,384]{2,1,0:T(8,128)S(1)}, f32[8,8,384]{2,1,0:T(8,128)S(1)}, u32[]{:S(2)}, u32[]{:S(2)}) collective-permute-start(f32[8,8,384]{2,1,0:T(8,128)S(1)} %copy-done), channel_id=1, source_target_pairs={{0,1},{1,0},{2,3},{3,2},{4,5},{5,4},{6,7},{7,6},{8,9},{9,8},{10,11... | collective-permute-start | bytes 294920 | tf_op jit(solution)/shard_map/ppermute | solution.py:437
  32.3 8.1 %collective-permute-start.3 = (f32[24,8,128]{2,1,0:T(8,128)S(1)}, f32[24,8,128]{2,1,0:T(8,128)S(1)}, u32[]{:S(2)}, u32[]{:S(2)}) collective-permute-start(f32[24,8,128]{2,1,0:T(8,128)S(1)} %shard_map.96.x_ref), channel_id=1, source_target_pairs={{0,31},{1,2},{2,1},{3,4},{4,3},{5,6},{6,5},{7,8},{8,7},{9,10},{10,... | collective-permute-start | bytes 294920 | tf_op jit(solution)/shard_map/ppermute | solution.py:437
  32.4 8.0 %collective-permute-start.2 = (f32[24,8,128]{2,1,0:T(8,128)S(1)}, f32[24,8,128]{2,1,0:T(8,128)S(1)}, u32[]{:S(2)}, u32[]{:S(2)}) collective-permute-start(f32[24,8,128]{2,1,0:T(8,128)S(1)} %shard_map.96.x_ref), channel_id=1, source_target_pairs={{0,1},{1,0},{2,3},{3,2},{4,5},{5,4},{6,7},{7,6},{8,9},{9,8},{10,11... | collective-permute-start | bytes 294920 | tf_op jit(solution)/shard_map/ppermute | solution.py:437
  44.5 2.9 %collective-permute-start.6 = (f32[2368,128]{1,0:T(8,128)S(1)}, f32[2368,128]{1,0:T(8,128)S(1)}, u32[]{:S(2)}, u32[]{:S(2)}) collective-permute-start(f32[2368,128]{1,0:T(8,128)S(1)} %bitcast.9), channel_id=1, source_target_pairs={{0,1},{1,0},{2,3},{3,2},{4,5},{5,4},{6,7},{7,6},{8,9},{9,8},{10,11... | collective-permute-start | bytes 3637256 | tf_op jit(solution)/shard_map/ppermute | solution.py:483
  57.4 4.1 %collective-permute-start.8 = (f32[24,8,128]{2,1,0:T(8,128)S(1)}, f32[24,8,128]{2,1,0:T(8,128)S(1)}, u32[]{:S(2)}, u32[]{:S(2)}) collective-permute-start(f32[24,8,128]{2,1,0:T(8,128)S(1)} %get-tuple-element.43.after_ref.x_ref), channel_id=1, source_target_pairs={{0,31},{1,2},{2,1},{3,4},{4,3},{5,6},{6,5},{7,8},{8,7},{9,10},{10,... | collective-permute-start | bytes 294920 | tf_op jit(solution)/shard_map/ppermute | solution.py:437
  58.8 2.8 %collective-permute-start.7 = (f32[24,8,128]{2,1,0:T(8,128)S(1)}, f32[24,8,128]{2,1,0:T(8,128)S(1)}, u32[]{:S(2)}, u32[]{:S(2)}) collective-permute-start(f32[24,8,128]{2,1,0:T(8,128)S(1)} %get-tuple-element.43.after_ref.x_ref), channel_id=1, source_target_pairs={{0,1},{1,0},{2,3},{3,2},{4,5},{5,4},{6,7},{7,6},{8,9},{9,8},{10,11... | collective-permute-start | bytes 294920 | tf_op jit(solution)/shard_map/ppermute | solution.py:437
  63.8 19.5 %all-to-all-start.1 = ((f32[128,1,640]{2,1,0:T(1,128)}), f32[128,1,640]{2,1,0:T(1,128)S(1)}, u32[]{:S(2)}, u32[]{:S(2)}) async-start(f32[128,1,640]{2,1,0:T(1,128)} %bitcast.3), calls=%async_computation.1 | async-start | bytes 655360 | tf_op jit(solution)/shard_map/all_to_all | solution.py:466
  71.4 16.3 %collective-permute-start.10 = (f32[24,8,128]{2,1,0:T(8,128)S(1)}, f32[24,8,128]{2,1,0:T(8,128)S(1)}, u32[]{:S(2)}, u32[]{:S(2)}) collective-permute-start(f32[24,8,128]{2,1,0:T(8,128)S(1)} %get-tuple-element.46.after_ref.x_ref), channel_id=1, source_target_pairs={{0,31},{1,2},{2,1},{3,4},{4,3},{5,6},{6,5},{7,8},{8,7},{9,10},{10,... | collective-permute-start | bytes 294920 | tf_op jit(solution)/shard_map/ppermute | solution.py:437
  73.1 14.6 %collective-permute-start.9 = (f32[24,8,128]{2,1,0:T(8,128)S(1)}, f32[24,8,128]{2,1,0:T(8,128)S(1)}, u32[]{:S(2)}, u32[]{:S(2)}) collective-permute-start(f32[24,8,128]{2,1,0:T(8,128)S(1)} %get-tuple-element.46.after_ref.x_ref), channel_id=1, source_target_pairs={{0,1},{1,0},{2,3},{3,2},{4,5},{5,4},{6,7},{7,6},{8,9},{9,8},{10,11... | collective-permute-start | bytes 294920 | tf_op jit(solution)/shard_map/ppermute | solution.py:437
  76.7 11.1 %slice-start = ((s8[4718592]{0:T(1024)(128)(4,1)}), s8[524288]{0:T(1024)(128)(4,1)S(1)}, s32[]{:S(2)}) async-start(s8[4718592]{0:T(1024)(128)(4,1)} %bitcast.7), calls=%async_computation.3 | async-start | bytes 1048576
  83.3 4.5 %slice-start.1 = ((s8[4718592]{0:T(1024)(128)(4,1)}), s8[4194304]{0:T(1024)(128)(4,1)S(1)}, s32[]{:S(2)}) async-start(s8[4718592]{0:T(1024)(128)(4,1)} %bitcast.7), calls=%async_computation.4 | async-start | bytes 8388608
  89.7 4.3 %collective-permute-start.12 = (f32[24,8,128]{2,1,0:T(8,128)S(1)}, f32[24,8,128]{2,1,0:T(8,128)S(1)}, u32[]{:S(2)}, u32[]{:S(2)}) collective-permute-start(f32[24,8,128]{2,1,0:T(8,128)S(1)} %get-tuple-element.51.after_ref.x_ref), channel_id=1, source_target_pairs={{0,31},{1,2},{2,1},{3,4},{4,3},{5,6},{6,5},{7,8},{8,7},{9,10},{10,... | collective-permute-start | bytes 294920 | tf_op jit(solution)/shard_map/ppermute | solution.py:437
  90.6 3.5 %collective-permute-start.11 = (f32[24,8,128]{2,1,0:T(8,128)S(1)}, f32[24,8,128]{2,1,0:T(8,128)S(1)}, u32[]{:S(2)}, u32[]{:S(2)}) collective-permute-start(f32[24,8,128]{2,1,0:T(8,128)S(1)} %get-tuple-element.51.after_ref.x_ref), channel_id=1, source_target_pairs={{0,1},{1,0},{2,3},{3,2},{4,5},{5,4},{6,7},{7,6},{8,9},{9,8},{10,11... | collective-permute-start | bytes 294920 | tf_op jit(solution)/shard_map/ppermute | solution.py:437
  96.3 19.6 %all-to-all-start.2 = ((f32[128,1,640]{2,1,0:T(1,128)}), f32[128,1,640]{2,1,0:T(1,128)S(1)}, u32[]{:S(2)}, u32[]{:S(2)}) async-start(f32[128,1,640]{2,1,0:T(1,128)} %bitcast.5), calls=%async_computation.2 | async-start | bytes 655360 | tf_op jit(solution)/shard_map/all_to_all | solution.py:466
  103.9 16.4 %collective-permute-start.14 = (f32[24,8,128]{2,1,0:T(8,128)S(1)}, f32[24,8,128]{2,1,0:T(8,128)S(1)}, u32[]{:S(2)}, u32[]{:S(2)}) collective-permute-start(f32[24,8,128]{2,1,0:T(8,128)S(1)} %get-tuple-element.55.after_ref.x_ref), channel_id=1, source_target_pairs={{0,31},{1,2},{2,1},{3,4},{4,3},{5,6},{6,5},{7,8},{8,7},{9,10},{10,... | collective-permute-start | bytes 294920 | tf_op jit(solution)/shard_map/ppermute | solution.py:437
  105.7 14.7 %collective-permute-start.13 = (f32[24,8,128]{2,1,0:T(8,128)S(1)}, f32[24,8,128]{2,1,0:T(8,128)S(1)}, u32[]{:S(2)}, u32[]{:S(2)}) collective-permute-start(f32[24,8,128]{2,1,0:T(8,128)S(1)} %get-tuple-element.55.after_ref.x_ref), channel_id=1, source_target_pairs={{0,1},{1,0},{2,3},{3,2},{4,5},{5,4},{6,7},{7,6},{8,9},{9,8},{10,11... | collective-permute-start | bytes 294920 | tf_op jit(solution)/shard_map/ppermute | solution.py:437

commit v11 on v10

--- a/solution.py
+++ b/solution.py
@@ -19,7 +19,7 @@
 TILES = COUNT * CHUNKS
 SLOTS = COUNT * CORNERS
 CARD = 37
-PARTS, PART, KEEP = 8, 1024, 2
+PARTS, PART, KEEP = 8, 1024, 3
 
 
 def call(kernel, outs, specs, scratch=(), us=2):

time: 123 us -> 124 us (level)
  local copies, waits for them, and re-layouts: 0.02 us -> 1.33 us
    unnamed x8 -> x34, local copies, waits for them, and re-layouts: 0.02 us -> 1.33 us
where the time goes in v11:
time: 124 us
  starting transfers between devices  53 us (43%)
  Pallas kernels  43.4 us (35%)
  waiting for transfers between devices  25.2 us (20%)
  local copies, waits for them, and re-layouts  1.33 us (1%)
    ppermute x7, starting transfers between devices, both(): lax.ppermute(x, 'tile', inner_swap)  17.6 us
    all_to_all x2, starting transfers between devices, spread(): lax.all_to_all(x.reshape(devices, -1), GT, 0, 0, tiled=True)  15.1 us
    all_to_all x1, starting transfers between devices, shards(): lax.all_to_all(card.reshape(devices // 2, -1), GT, 0, 0, tiled=True, axis...  11.8 us
    pallas_call x1, Pallas kernels, shards(): pl.pallas_call(solve_first_kernel, in_specs=[SMEM] * 2 + [ANY] * 3 + [VME...  9.97 us
    all_to_all x2, waiting for transfers between devices, spread(): lax.all_to_all(x.reshape(devices, -1), GT, 0, 0, tiled=True)  9.89 us
    pallas_call x2, Pallas kernels, shards(): call(coarse_kernel, coarse_out, [VMEM, VMEM, ANY], coarse_scratch, us=20)  8.7 us
    ppermute x7, starting transfers between devices, both(): lax.ppermute(x, 'tile', outer_swap)  8.5 us
    ppermute x7, waiting for transfers between devices, both(): lax.ppermute(x, 'tile', outer_swap)  7.46 us
  transfers between devices with their start and end apart: 18, of which 8 were waited for; matrix products, arithmetic and copies ran while one was open for 0% of the time, Pallas kernels for 16%

profile of v11, /device:TPU:1, one launch (start us, length us, event | category | flops | bytes accessed | tf_op | source)
XLA Modules:
  0.0 124.0 jit_solution(5303059884393138360)
XLA Ops:
  0.7 2.9 %shard_map.94 = (f32[25,8,128]{2,1,0:T(8,128)S(1)}, s32[16,128]{1,0:T(8,128)S(1)}) custom-call(s32[1]{0:T(128)} %bitcast.core, f32[8,8,384]{2,1,0:T(8,128)} %loads_ref.1, s32[8,8]{1,0:T(8,128)} %index_ref.1, s32[8,12]{1,0:T(8,128)} %partner_ref.1, f32[8,384,384]{2,1,0:T(8,128)} %inverse_ref.7), custom_call_target="tpu_custom_call" | custom-call | flops 2000000000 | bytes 12000000 | tf_op jit(solution)/shard_map/pallas_call | solution.py:449
  3.6 2.7 %collective-permute-start.1 = (f32[25,8,128]{2,1,0:T(8,128)S(1)}, f32[25,8,128]{2,1,0:T(8,128)S(1)}, u32[]{:S(2)}, u32[]{:S(2)}) collective-permute-start(f32[25,8,128]{2,1,0:T(8,128)S(1)} %get-tuple-element.33.x_ref.ix_ref), channel_id=1, source_target_pairs={{0,31},{1,2},{2,1},{3,4},{4,3},{5,6},{6,5},{7,8},{8,7},{9,10},{10,... | collective-permute-start | bytes 307208 | tf_op jit(solution)/shard_map/ppermute | solution.py:437
  6.3 3.6 %collective-permute-start = (f32[25,8,128]{2,1,0:T(8,128)S(1)}, f32[25,8,128]{2,1,0:T(8,128)S(1)}, u32[]{:S(2)}, u32[]{:S(2)}) collective-permute-start(f32[25,8,128]{2,1,0:T(8,128)S(1)} %get-tuple-element.33.x_ref.ix_ref), channel_id=1, source_target_pairs={{0,1},{1,0},{2,3},{3,2},{4,5},{5,4},{6,7},{7,6},{8,9},{9,8},{10,11... | collective-permute-start | bytes 307208 | tf_op jit(solution)/shard_map/ppermute | solution.py:437
  9.8 0.0 collective-permute-done.1.b_ref.ib_ref
  9.8 0.9 collective-permute-done.a_ref.ia_ref
  10.8 2.2 %shard_map.95 = (f32[24,8,128]{2,1,0:T(8,128)S(1)}, f32[2368,128]{1,0:T(8,128)}) custom-call(s32[16,128]{1,0:T(8,128)S(1)} %get-tuple-element.32.table, f32[25,8,128]{2,1,0:T(8,128)S(1)} %collective-permute-done.a_ref.ia_ref, f32[25,8,128]{2,1,0:T(8,128)S(1)} %get-tuple-element.33.x_ref.ix_ref, f32[25,8,128]{2,1,0:T(8,128)S(1)} %collective-permute-done.1.b_ref.ib_ref, ...), custom_call_target="tpu_custom_call" | custom-call | flops 1000000000 | bytes 6000000 | tf_op jit(solution)/shard_map/pallas_call | solution.py:473
  12.9 11.8 %all-to-all-start = ((f32[64,1,4736]{2,1,0:T(1,128)}), f32[64,1,4736]{2,1,0:T(1,128)S(1)}, u32[]{:S(2)}, u32[]{:S(2)}) async-start(f32[64,1,4736]{2,1,0:T(1,128)} %bitcast.1), calls=%async_computation | async-start | bytes 2424832 | tf_op jit(solution)/shard_map/all_to_all | solution.py:476
  24.8 0.1 collective-permute-start.5
  24.9 4.7 %collective-permute-start.4 = (f32[8,8,384]{2,1,0:T(8,128)S(1)}, f32[8,8,384]{2,1,0:T(8,128)S(1)}, u32[]{:S(2)}, u32[]{:S(2)}) collective-permute-start(f32[8,8,384]{2,1,0:T(8,128)S(1)} %copy-done), channel_id=1, source_target_pairs={{0,1},{1,0},{2,3},{3,2},{4,5},{5,4},{6,7},{7,6},{8,9},{9,8},{10,11... | collective-permute-start | bytes 294920 | tf_op jit(solution)/shard_map/ppermute | solution.py:437
  29.6 2.8 %shard_map.96.x_ref = f32[24,8,128]{2,1,0:T(8,128)S(1)} custom-call(f32[24,8,128]{2,1,0:T(8,128)S(1)} %get-tuple-element.35.x_ref.r0_ref, f32[8,384,384]{2,1,0:T(8,128)} %source_ref.3), custom_call_target="tpu_custom_call" | custom-call | flops 1500000000 | bytes 9000000 | tf_op jit(solution)/shard_map/pallas_call | solution.py:469
  32.4 0.1 collective-permute-start.3
  32.5 1.0 collective-permute-start.2
  33.4 5.6 %collective-permute-done.5.bm_ref = f32[8,8,384]{2,1,0:T(8,128)S(1)} collective-permute-done((f32[8,8,384]{2,1,0:T(8,128)S(1)}, f32[8,8,384]{2,1,0:T(8,128)S(1)}, u32[]{:S(2)}, u32[]{:S(2)}) %collective-permute-start.5) | collective-permute-done | bytes 98336 | tf_op jit(solution)/shard_map/ppermute | solution.py:437
  39.0 0.0 collective-permute-done.4.am_ref
  39.0 1.5 %collective-permute-done.3.b_ref = f32[24,8,128]{2,1,0:T(8,128)S(1)} collective-permute-done((f32[24,8,128]{2,1,0:T(8,128)S(1)}, f32[24,8,128]{2,1,0:T(8,128)S(1)}, u32[]{:S(2)}, u32[]{:S(2)}) %collective-permute-start.3) | collective-permute-done | bytes 98336 | tf_op jit(solution)/shard_map/ppermute | solution.py:437
  40.5 0.0 collective-permute-done.2.a_ref
  40.5 4.0 %all-to-all-done = f32[64,1,4736]{2,1,0:T(1,128)S(1)} async-done(((f32[64,1,4736]{2,1,0:T(1,128)}), f32[64,1,4736]{2,1,0:T(1,128)S(1)}, u32[]{:S(2)}, u32[]{:S(2)}) %all-to-all-start) | async-done | bytes 1212448 | tf_op jit(solution)/shard_map/all_to_all | solution.py:476
  44.5 0.0 collective-permute-start.6
  44.6 2.9 %collective-permute-done.6.other_ref = f32[2368,128]{1,0:T(8,128)S(1)} collective-permute-done((f32[2368,128]{1,0:T(8,128)S(1)}, f32[2368,128]{1,0:T(8,128)S(1)}, u32[]{:S(2)}, u32[]{:S(2)}) %collective-permute-start.6) | collective-permute-done | bytes 1212448 | tf_op jit(solution)/shard_map/ppermute | solution.py:483
  47.4 10.0 %shard_map.97 = (f32[24,8,128]{2,1,0:T(8,128)S(1)}, f32[24,8,128]{2,1,0:T(8,128)S(1)}, bf16[8,384,1024]{2,1,0:T(8,128)(2,1)}) custom-call(s32[1]{0:T(128)} %bitcast.core, s32[16,128]{1,0:T(8,128)S(1)} %get-tuple-element.32.table, f32[25,8,128]{2,1,0:T(8,128)S(1)} %collective-permute-done.a_ref.ia_ref, f32[25,8,128]{2,1,0:T(8,128)S(1)} %get-tuple-element.33.x_ref.ix_ref, ...), custom_call_target="tpu_custom_call" | custom-call | flops 4000000000 | bytes 20000000 | tf_op jit(solution)/shard_map/pallas_call | solution.py:484
  57.4 0.0 copy-start.4
  57.4 1.4 %collective-permute-start.8 = (f32[24,8,128]{2,1,0:T(8,128)S(1)}, f32[24,8,128]{2,1,0:T(8,128)S(1)}, u32[]{:S(2)}, u32[]{:S(2)}) collective-permute-start(f32[24,8,128]{2,1,0:T(8,128)S(1)} %get-tuple-element.43.after_ref.x_ref), channel_id=1, source_target_pairs={{0,31},{1,2},{2,1},{3,4},{4,3},{5,6},{6,5},{7,8},{8,7},{9,10},{10,... | collective-permute-start | bytes 294920 | tf_op jit(solution)/shard_map/ppermute | solution.py:437
  58.8 0.0 collective-permute-start.7
  58.8 2.4 %shard_map.98.schur_ref = f32[8,384,384]{2,1,0:T(8,128)S(1)} custom-call(f32[24,8,128]{2,1,0:T(8,128)S(1)} %get-tuple-element.43.after_ref.x_ref, f32[8,384,384]{2,1,0:T(8,128)} %source_ref.3), custom_call_target="tpu_custom_call" | custom-call | flops 1000000000 | bytes 6000000 | tf_op jit(solution)/shard_map/pallas_call | solution.py:509
  61.2 0.4 collective-permute-done.8.b_ref
  61.6 0.0 collective-permute-done.7.a_ref
  61.6 2.3 %shard_map.99 = (f32[24,8,128]{2,1,0:T(8,128)S(1)}, f32[640,128]{1,0:T(8,128)}, f32[24,8,128]{2,1,0:T(8,128)S(1)}) custom-call(s32[16,128]{1,0:T(8,128)S(1)} %get-tuple-element.32.table, f32[24,8,128]{2,1,0:T(8,128)S(1)} %collective-permute-done.7.a_ref, f32[24,8,128]{2,1,0:T(8,128)S(1)} %get-tuple-element.43.after_ref.x_ref, ...), custom_call_target="tpu_custom_call" | custom-call | flops 1500000000 | bytes 9000000 | tf_op jit(solution)/shard_map/pallas_call | solution.py:516
  63.9 0.6 copy-done.9
  64.5 7.5 %all-to-all-start.1 = ((f32[128,1,640]{2,1,0:T(1,128)}), f32[128,1,640]{2,1,0:T(1,128)S(1)}, u32[]{:S(2)}, u32[]{:S(2)}) async-start(f32[128,1,640]{2,1,0:T(1,128)} %bitcast.3), calls=%async_computation.1 | async-start | bytes 655360 | tf_op jit(solution)/shard_map/all_to_all | solution.py:466
  72.1 1.7 %collective-permute-start.10 = (f32[24,8,128]{2,1,0:T(8,128)S(1)}, f32[24,8,128]{2,1,0:T(8,128)}, u32[]{:S(2)}, u32[]{:S(2)}) collective-permute-start(f32[24,8,128]{2,1,0:T(8,128)S(1)} %get-tuple-element.46.after_ref.x_ref), channel_id=1, source_target_pairs={{0,31},{1,2},{2,1},{3,4},{4,3},{5,6},{6,5},{7,8},{8,7},{9,10},{10,... | collective-permute-start | bytes 294920 | tf_op jit(solution)/shard_map/ppermute | solution.py:437
  73.8 3.6 %collective-permute-start.9 = (f32[24,8,128]{2,1,0:T(8,128)S(1)}, f32[24,8,128]{2,1,0:T(8,128)}, u32[]{:S(2)}, u32[]{:S(2)}) collective-permute-start(f32[24,8,128]{2,1,0:T(8,128)S(1)} %get-tuple-element.46.after_ref.x_ref), channel_id=1, source_target_pairs={{0,1},{1,0},{2,3},{3,2},{4,5},{5,4},{6,7},{7,6},{8,9},{9,8},{10,11... | collective-permute-start | bytes 294920 | tf_op jit(solution)/shard_map/ppermute | solution.py:437
  77.4 1.7 %shard_map.100.kept_ref = bf16[3,384,1024]{2,1,0:T(8,128)(2,1)S(1)} custom-call(f32[24,8,128]{2,1,0:T(8,128)S(1)} %get-tuple-element.46.after_ref.x_ref, bf16[8,384,1024]{2,1,0:T(8,128)(2,1)} %get-tuple-element.47.weights_ref), custom_call_target="tpu_custom_call" | custom-call | flops 1000000000 | bytes 6000000 | tf_op jit(solution)/shard_map/pallas_call | solution.py:512
  79.1 4.9 %all-to-all-done.1 = f32[128,1,640]{2,1,0:T(1,128)S(1)} async-done(((f32[128,1,640]{2,1,0:T(1,128)}), f32[128,1,640]{2,1,0:T(1,128)S(1)}, u32[]{:S(2)}, u32[]{:S(2)}) %all-to-all-start.1) | async-done | bytes 327712 | tf_op jit(solution)/shard_map/all_to_all | solution.py:466
  84.0 4.5 %shard_map.101 = (f32[384,16]{1,0:T(8,128)S(1)}, f32[8,128]{1,0:T(8,128)S(1)}) custom-call(f32[640,128]{1,0:T(8,128)S(1)} %bitcast.11, bf16[3,384,1024]{2,1,0:T(8,128)(2,1)S(1)} %shard_map.100.kept_ref, bf16[8,384,1024]{2,1,0:T(8,128)(2,1)} %get-tuple-element.47.weights_ref), custom_call_target="tpu_custom_call" | custom-call | flops 10000000000 | bytes 60000000 | tf_op jit(solution)/shard_map/pallas_call | solution.py:520
  88.5 0.0 collective-permute-done.10.b_ref
  88.6 2.2 %shard_map.102 = (f32[24,8,128]{2,1,0:T(8,128)S(1)}, f32[24,8,128]{2,1,0:T(8,128)S(1)}, f32[24,8,128]{2,1,0:T(8,128)S(1)}, f32[3,8,128]{2,1,0:T(8,128)S(1)}, f32[24,8,128]{2,1,0:T(8,128)S(1)}) custom-call(s32[16,128]{1,0:T(8,128)S(1)} %get-tuple-element.32.table, f32[384,16]{1,0:T(8,128)S(1)} %get-tuple-element.48.out_ref, ...), custom_call_target="tpu_custom_call" | custom-call | flops 1500000000 | bytes 9000000 | tf_op jit(solution)/shard_map/pallas_call | solution.py:521
  90.9 0.9 collective-permute-start.12
  91.7 1.1 collective-permute-start.11
  92.8 2.4 %shard_map.103.schur_ref = f32[8,384,384]{2,1,0:T(8,128)S(1)} custom-call(f32[24,8,128]{2,1,0:T(8,128)S(1)} %get-tuple-element.51.after_ref.x_ref, f32[8,384,384]{2,1,0:T(8,128)} %source_ref.3), custom_call_target="tpu_custom_call" | custom-call | flops 1000000000 | bytes 6000000 | tf_op jit(solution)/shard_map/pallas_call | solution.py:509
  95.2 2.3 %shard_map.104 = (f32[24,8,128]{2,1,0:T(8,128)S(1)}, f32[640,128]{1,0:T(8,128)}, f32[24,8,128]{2,1,0:T(8,128)S(1)}) custom-call(s32[16,128]{1,0:T(8,128)S(1)} %get-tuple-element.32.table, f32[24,8,128]{2,1,0:T(8,128)S(1)} %collective-permute-done.11.a_ref, f32[24,8,128]{2,1,0:T(8,128)S(1)} %get-tuple-element.51.after_ref.x_ref, ...), custom_call_target="tpu_custom_call" | custom-call | flops 1500000000 | bytes 9000000 | tf_op jit(solution)/shard_map/pallas_call | solution.py:525
  97.6 0.6 copy-done.13
  98.2 7.6 %all-to-all-start.2 = ((f32[128,1,640]{2,1,0:T(1,128)}), f32[128,1,640]{2,1,0:T(1,128)S(1)}, u32[]{:S(2)}, u32[]{:S(2)}) async-start(f32[128,1,640]{2,1,0:T(1,128)} %bitcast.5), calls=%async_computation.2 | async-start | bytes 655360 | tf_op jit(solution)/shard_map/all_to_all | solution.py:466
  105.8 1.7 %collective-permute-start.14 = (f32[24,8,128]{2,1,0:T(8,128)S(1)}, f32[24,8,128]{2,1,0:T(8,128)S(1)}, u32[]{:S(2)}, u32[]{:S(2)}) collective-permute-start(f32[24,8,128]{2,1,0:T(8,128)S(1)} %get-tuple-element.55.after_ref.x_ref), channel_id=1, source_target_pairs={{0,31},{1,2},{2,1},{3,4},{4,3},{5,6},{6,5},{7,8},{8,7},{9,10},{10,... | collective-permute-start | bytes 294920 | tf_op jit(solution)/shard_map/ppermute | solution.py:437
  107.5 3.7 %collective-permute-start.13 = (f32[24,8,128]{2,1,0:T(8,128)S(1)}, f32[24,8,128]{2,1,0:T(8,128)S(1)}, u32[]{:S(2)}, u32[]{:S(2)}) collective-permute-start(f32[24,8,128]{2,1,0:T(8,128)S(1)} %get-tuple-element.55.after_ref.x_ref), channel_id=1, source_target_pairs={{0,1},{1,0},{2,3},{3,2},{4,5},{5,4},{6,7},{7,6},{8,9},{9,8},{10,11... | collective-permute-start | bytes 294920 | tf_op jit(solution)/shard_map/ppermute | solution.py:437
  111.2 1.6 %shard_map.105.kept_ref = bf16[3,384,1024]{2,1,0:T(8,128)(2,1)S(1)} custom-call(f32[24,8,128]{2,1,0:T(8,128)S(1)} %get-tuple-element.55.after_ref.x_ref, bf16[8,384,1024]{2,1,0:T(8,128)(2,1)} %get-tuple-element.47.weights_ref), custom_call_target="tpu_custom_call" | custom-call | flops 1000000000 | bytes 6000000 | tf_op jit(solution)/shard_map/pallas_call | solution.py:512
  112.9 5.0 %all-to-all-done.2 = f32[128,1,640]{2,1,0:T(1,128)S(1)} async-done(((f32[128,1,640]{2,1,0:T(1,128)}), f32[128,1,640]{2,1,0:T(1,128)S(1)}, u32[]{:S(2)}, u32[]{:S(2)}) %all-to-all-start.2) | async-done | bytes 327712 | tf_op jit(solution)/shard_map/all_to_all | solution.py:466
  117.8 4.2 %shard_map.106 = (f32[384,16]{1,0:T(8,128)S(1)}, f32[8,128]{1,0:T(8,128)S(1)}) custom-call(f32[640,128]{1,0:T(8,128)S(1)} %bitcast.12, bf16[3,384,1024]{2,1,0:T(8,128)(2,1)S(1)} %shard_map.105.kept_ref, bf16[8,384,1024]{2,1,0:T(8,128)(2,1)} %get-tuple-element.47.weights_ref), custom_call_target="tpu_custom_call" | custom-call | flops 10000000000 | bytes 60000000 | tf_op jit(solution)/shard_map/pallas_call | solution.py:529
  122.1 1.9 %shard_map.107 = (f32[8,8,384]{2,1,0:T(8,128)}, f32[8,8,384]{2,1,0:T(8,128)}, f32[8,8,384]{2,1,0:T(8,128)}) custom-call(s32[16,128]{1,0:T(8,128)S(1)} %get-tuple-element.32.table, f32[384,16]{1,0:T(8,128)S(1)} %get-tuple-element.56.out_ref, f32[8,128]{1,0:T(8,128)S(1)} %get-tuple-element.57.sums_ref, f32[8,8,384]{2,1,0:T(8,128)S(1)} %copy-done.3, ...), custom_call_target="tpu_custom_call" | custom-call | flops 1000000000 | bytes 6000000 | tf_op jit(solution)/shard_map/pallas_call | solution.py:531
  (37 shorter events, 0.1 us)
Async XLA Ops:
  0.6 10.1 %copy-start = (f32[8,8,384]{2,1,0:T(8,128)S(1)}, f32[8,8,384]{2,1,0:T(8,128)}, u32[]{:S(2)}) copy-start(f32[8,8,384]{2,1,0:T(8,128)} %m_ref.2) | copy-start | bytes 294916
  0.6 10.1 %copy-start.12 = (f32[64,64]{1,0:T(8,128)S(1)}, f32[64,64]{1,0:T(8,128)}, u32[]{:S(2)}) copy-start(f32[64,64]{1,0:T(8,128)} %inverse_ref.5) | copy-start | bytes 49156
  3.6 6.2 %collective-permute-start.1 = (f32[25,8,128]{2,1,0:T(8,128)S(1)}, f32[25,8,128]{2,1,0:T(8,128)S(1)}, u32[]{:S(2)}, u32[]{:S(2)}) collective-permute-start(f32[25,8,128]{2,1,0:T(8,128)S(1)} %get-tuple-element.33.x_ref.ix_ref), channel_id=1, source_target_pairs={{0,31},{1,2},{2,1},{3,4},{4,3},{5,6},{6,5},{7,8},{8,7},{9,10},{10,... | collective-permute-start | bytes 307208 | tf_op jit(solution)/shard_map/ppermute | solution.py:437
  6.3 4.5 %collective-permute-start = (f32[25,8,128]{2,1,0:T(8,128)S(1)}, f32[25,8,128]{2,1,0:T(8,128)S(1)}, u32[]{:S(2)}, u32[]{:S(2)}) collective-permute-start(f32[25,8,128]{2,1,0:T(8,128)S(1)} %get-tuple-element.33.x_ref.ix_ref), channel_id=1, source_target_pairs={{0,1},{1,0},{2,3},{3,2},{4,5},{5,4},{6,7},{7,6},{8,9},{9,8},{10,11... | collective-permute-start | bytes 307208 | tf_op jit(solution)/shard_map/ppermute | solution.py:437
  12.9 48.6 %copy-start.7 = (f32[24,8,128]{2,1,0:T(8,128)}, f32[24,8,128]{2,1,0:T(8,128)S(1)}, u32[]{:S(2)}) copy-start(f32[24,8,128]{2,1,0:T(8,128)S(1)} %get-tuple-element.35.x_ref.r0_ref) | copy-start | bytes 294916
  12.9 31.6 %all-to-all-start = ((f32[64,1,4736]{2,1,0:T(1,128)}), f32[64,1,4736]{2,1,0:T(1,128)S(1)}, u32[]{:S(2)}, u32[]{:S(2)}) async-start(f32[64,1,4736]{2,1,0:T(1,128)} %bitcast.1), calls=%async_computation | async-start | bytes 2424832 | tf_op jit(solution)/shard_map/all_to_all | solution.py:476
  24.8 14.2 %collective-permute-start.5 = (f32[8,8,384]{2,1,0:T(8,128)S(1)}, f32[8,8,384]{2,1,0:T(8,128)S(1)}, u32[]{:S(2)}, u32[]{:S(2)}) collective-permute-start(f32[8,8,384]{2,1,0:T(8,128)S(1)} %copy-done), channel_id=1, source_target_pairs={{0,31},{1,2},{2,1},{3,4},{4,3},{5,6},{6,5},{7,8},{8,7},{9,10},{10,... | collective-permute-start | bytes 294920 | tf_op jit(solution)/shard_map/ppermute | solution.py:437
  24.9 14.1 %collective-permute-start.4 = (f32[8,8,384]{2,1,0:T(8,128)S(1)}, f32[8,8,384]{2,1,0:T(8,128)S(1)}, u32[]{:S(2)}, u32[]{:S(2)}) collective-permute-start(f32[8,8,384]{2,1,0:T(8,128)S(1)} %copy-done), channel_id=1, source_target_pairs={{0,1},{1,0},{2,3},{3,2},{4,5},{5,4},{6,7},{7,6},{8,9},{9,8},{10,11... | collective-permute-start | bytes 294920 | tf_op jit(solution)/shard_map/ppermute | solution.py:437
  32.4 8.1 %collective-permute-start.3 = (f32[24,8,128]{2,1,0:T(8,128)S(1)}, f32[24,8,128]{2,1,0:T(8,128)S(1)}, u32[]{:S(2)}, u32[]{:S(2)}) collective-permute-start(f32[24,8,128]{2,1,0:T(8,128)S(1)} %shard_map.96.x_ref), channel_id=1, source_target_pairs={{0,31},{1,2},{2,1},{3,4},{4,3},{5,6},{6,5},{7,8},{8,7},{9,10},{10,... | collective-permute-start | bytes 294920 | tf_op jit(solution)/shard_map/ppermute | solution.py:437
  32.5 8.0 %collective-permute-start.2 = (f32[24,8,128]{2,1,0:T(8,128)S(1)}, f32[24,8,128]{2,1,0:T(8,128)S(1)}, u32[]{:S(2)}, u32[]{:S(2)}) collective-permute-start(f32[24,8,128]{2,1,0:T(8,128)S(1)} %shard_map.96.x_ref), channel_id=1, source_target_pairs={{0,1},{1,0},{2,3},{3,2},{4,5},{5,4},{6,7},{7,6},{8,9},{9,8},{10,11... | collective-permute-start | bytes 294920 | tf_op jit(solution)/shard_map/ppermute | solution.py:437
  39.0 18.4 %copy-start.1 = (f32[8,8,384]{2,1,0:T(8,128)}, f32[8,8,384]{2,1,0:T(8,128)S(1)}, u32[]{:S(2)}) copy-start(f32[8,8,384]{2,1,0:T(8,128)S(1)} %collective-permute-done.4.am_ref) | copy-start | bytes 294916
  44.5 2.9 %collective-permute-start.6 = (f32[2368,128]{1,0:T(8,128)S(1)}, f32[2368,128]{1,0:T(8,128)S(1)}, u32[]{:S(2)}, u32[]{:S(2)}) collective-permute-start(f32[2368,128]{1,0:T(8,128)S(1)} %bitcast.9), channel_id=1, source_target_pairs={{0,1},{1,0},{2,3},{3,2},{4,5},{5,4},{6,7},{7,6},{8,9},{9,8},{10,11... | collective-permute-start | bytes 3637256 | tf_op jit(solution)/shard_map/ppermute | solution.py:483
  57.4 4.1 %copy-start.4 = (f32[24,8,128]{2,1,0:T(8,128)}, f32[24,8,128]{2,1,0:T(8,128)S(1)}, u32[]{:S(2)}) copy-start(f32[24,8,128]{2,1,0:T(8,128)S(1)} %get-tuple-element.44.z0_ref) | copy-start | bytes 294916
  57.4 4.1 %collective-permute-start.8 = (f32[24,8,128]{2,1,0:T(8,128)S(1)}, f32[24,8,128]{2,1,0:T(8,128)S(1)}, u32[]{:S(2)}, u32[]{:S(2)}) collective-permute-start(f32[24,8,128]{2,1,0:T(8,128)S(1)} %get-tuple-element.43.after_ref.x_ref), channel_id=1, source_target_pairs={{0,31},{1,2},{2,1},{3,4},{4,3},{5,6},{6,5},{7,8},{8,7},{9,10},{10,... | collective-permute-start | bytes 294920 | tf_op jit(solution)/shard_map/ppermute | solution.py:437
  58.8 2.8 %collective-permute-start.7 = (f32[24,8,128]{2,1,0:T(8,128)S(1)}, f32[24,8,128]{2,1,0:T(8,128)S(1)}, u32[]{:S(2)}, u32[]{:S(2)}) collective-permute-start(f32[24,8,128]{2,1,0:T(8,128)S(1)} %get-tuple-element.43.after_ref.x_ref), channel_id=1, source_target_pairs={{0,1},{1,0},{2,3},{3,2},{4,5},{5,4},{6,7},{7,6},{8,9},{9,8},{10,11... | collective-permute-start | bytes 294920 | tf_op jit(solution)/shard_map/ppermute | solution.py:437
  63.9 0.6 copy-start.9
  64.5 19.4 %all-to-all-start.1 = ((f32[128,1,640]{2,1,0:T(1,128)}), f32[128,1,640]{2,1,0:T(1,128)S(1)}, u32[]{:S(2)}, u32[]{:S(2)}) async-start(f32[128,1,640]{2,1,0:T(1,128)} %bitcast.3), calls=%async_computation.1 | async-start | bytes 655360 | tf_op jit(solution)/shard_map/all_to_all | solution.py:466
  72.1 16.5 %collective-permute-start.10 = (f32[24,8,128]{2,1,0:T(8,128)S(1)}, f32[24,8,128]{2,1,0:T(8,128)}, u32[]{:S(2)}, u32[]{:S(2)}) collective-permute-start(f32[24,8,128]{2,1,0:T(8,128)S(1)} %get-tuple-element.46.after_ref.x_ref), channel_id=1, source_target_pairs={{0,31},{1,2},{2,1},{3,4},{4,3},{5,6},{6,5},{7,8},{8,7},{9,10},{10,... | collective-permute-start | bytes 294920 | tf_op jit(solution)/shard_map/ppermute | solution.py:437
  73.8 14.8 %collective-permute-start.9 = (f32[24,8,128]{2,1,0:T(8,128)S(1)}, f32[24,8,128]{2,1,0:T(8,128)}, u32[]{:S(2)}, u32[]{:S(2)}) collective-permute-start(f32[24,8,128]{2,1,0:T(8,128)S(1)} %get-tuple-element.46.after_ref.x_ref), channel_id=1, source_target_pairs={{0,1},{1,0},{2,3},{3,2},{4,5},{5,4},{6,7},{7,6},{8,9},{9,8},{10,11... | collective-permute-start | bytes 294920 | tf_op jit(solution)/shard_map/ppermute | solution.py:437
  77.4 11.2 %slice-start = ((s8[4718592]{0:T(1024)(128)(4,1)}), s8[524288]{0:T(1024)(128)(4,1)S(1)}, s32[]{:S(2)}) async-start(s8[4718592]{0:T(1024)(128)(4,1)} %bitcast.7), calls=%async_computation.3 | async-start | bytes 1048576
  84.0 4.6 %slice-start.1 = ((s8[4718592]{0:T(1024)(128)(4,1)}), s8[4194304]{0:T(1024)(128)(4,1)S(1)}, s32[]{:S(2)}) async-start(s8[4718592]{0:T(1024)(128)(4,1)} %bitcast.7), calls=%async_computation.4 | async-start | bytes 8388608
  84.0 4.6 %copy-start.2 = (f32[8,8,384]{2,1,0:T(8,128)S(1)}, f32[8,8,384]{2,1,0:T(8,128)}, u32[]{:S(2)}) copy-start(f32[8,8,384]{2,1,0:T(8,128)} %copy-done.1) | copy-start | bytes 294916
  84.0 4.6 %copy-start.5 = (f32[24,8,128]{2,1,0:T(8,128)S(1)}, f32[24,8,128]{2,1,0:T(8,128)}, u32[]{:S(2)}) copy-start(f32[24,8,128]{2,1,0:T(8,128)} %copy-done.4) | copy-start | bytes 294916
  84.0 4.6 %copy-start.8 = (f32[24,8,128]{2,1,0:T(8,128)S(1)}, f32[24,8,128]{2,1,0:T(8,128)}, u32[]{:S(2)}) copy-start(f32[24,8,128]{2,1,0:T(8,128)} %copy-done.7) | copy-start | bytes 294916
  84.0 4.6 %copy-start.10 = (f32[24,8,128]{2,1,0:T(8,128)S(1)}, f32[24,8,128]{2,1,0:T(8,128)}, u32[]{:S(2)}) copy-start(f32[24,8,128]{2,1,0:T(8,128)} %copy-done.9) | copy-start | bytes 294916
  90.9 4.3 %collective-permute-start.12 = (f32[24,8,128]{2,1,0:T(8,128)S(1)}, f32[24,8,128]{2,1,0:T(8,128)S(1)}, u32[]{:S(2)}, u32[]{:S(2)}) collective-permute-start(f32[24,8,128]{2,1,0:T(8,128)S(1)} %get-tuple-element.51.after_ref.x_ref), channel_id=1, source_target_pairs={{0,31},{1,2},{2,1},{3,4},{4,3},{5,6},{6,5},{7,8},{8,7},{9,10},{10,... | collective-permute-start | bytes 294920 | tf_op jit(solution)/shard_map/ppermute | solution.py:437
  91.7 3.5 %collective-permute-start.11 = (f32[24,8,128]{2,1,0:T(8,128)S(1)}, f32[24,8,128]{2,1,0:T(8,128)S(1)}, u32[]{:S(2)}, u32[]{:S(2)}) collective-permute-start(f32[24,8,128]{2,1,0:T(8,128)S(1)} %get-tuple-element.51.after_ref.x_ref), channel_id=1, source_target_pairs={{0,1},{1,0},{2,3},{3,2},{4,5},{5,4},{6,7},{7,6},{8,9},{9,8},{10,11... | collective-permute-start | bytes 294920 | tf_op jit(solution)/shard_map/ppermute | solution.py:437
  97.6 0.6 copy-start.13
  98.2 19.6 %all-to-all-start.2 = ((f32[128,1,640]{2,1,0:T(1,128)}), f32[128,1,640]{2,1,0:T(1,128)S(1)}, u32[]{:S(2)}, u32[]{:S(2)}) async-start(f32[128,1,640]{2,1,0:T(1,128)} %bitcast.5), calls=%async_computation.2 | async-start | bytes 655360 | tf_op jit(solution)/shard_map/all_to_all | solution.py:466
  105.8 16.2 %collective-permute-start.14 = (f32[24,8,128]{2,1,0:T(8,128)S(1)}, f32[24,8,128]{2,1,0:T(8,128)S(1)}, u32[]{:S(2)}, u32[]{:S(2)}) collective-permute-start(f32[24,8,128]{2,1,0:T(8,128)S(1)} %get-tuple-element.55.after_ref.x_ref), channel_id=1, source_target_pairs={{0,31},{1,2},{2,1},{3,4},{4,3},{5,6},{6,5},{7,8},{8,7},{9,10},{10,... | collective-permute-start | bytes 294920 | tf_op jit(solution)/shard_map/ppermute | solution.py:437
  107.5 14.5 %collective-permute-start.13 = (f32[24,8,128]{2,1,0:T(8,128)S(1)}, f32[24,8,128]{2,1,0:T(8,128)S(1)}, u32[]{:S(2)}, u32[]{:S(2)}) collective-permute-start(f32[24,8,128]{2,1,0:T(8,128)S(1)} %get-tuple-element.55.after_ref.x_ref), channel_id=1, source_target_pairs={{0,1},{1,0},{2,3},{3,2},{4,5},{5,4},{6,7},{7,6},{8,9},{9,8},{10,11... | collective-permute-start | bytes 294920 | tf_op jit(solution)/shard_map/ppermute | solution.py:437
  117.8 4.2 %copy-start.3 = (f32[8,8,384]{2,1,0:T(8,128)S(1)}, f32[8,8,384]{2,1,0:T(8,128)}, u32[]{:S(2)}) copy-start(f32[8,8,384]{2,1,0:T(8,128)} %copy-done.1) | copy-start | bytes 294916
  117.8 4.2 %copy-start.6 = (f32[24,8,128]{2,1,0:T(8,128)S(1)}, f32[24,8,128]{2,1,0:T(8,128)}, u32[]{:S(2)}) copy-start(f32[24,8,128]{2,1,0:T(8,128)} %copy-done.4) | copy-start | bytes 294916
  117.8 4.2 %copy-start.11 = (f32[24,8,128]{2,1,0:T(8,128)S(1)}, f32[24,8,128]{2,1,0:T(8,128)}, u32[]{:S(2)}) copy-start(f32[24,8,128]{2,1,0:T(8,128)} %copy-done.9) | copy-start | bytes 294916
  117.8 4.2 %copy-start.14 = (f32[24,8,128]{2,1,0:T(8,128)S(1)}, f32[24,8,128]{2,1,0:T(8,128)}, u32[]{:S(2)}) copy-start(f32[24,8,128]{2,1,0:T(8,128)} %copy-done.13) | copy-start | bytes 294916
